TPU v7x, 32 devices: a whole 2x2x4 slice. The times are simulated.
32 devices in a mesh: row: 4 (over z), col: 8 (over y, x, core).
Axes of the slice: x: 2, y: 2, z: 4, core: 2. Of those that a mesh axis runs over, the one named last changes fastest.
Arguments:
- iterate: bfloat16 [3584, 18432], P('row', 'col'), as said below
Outputs:
- update: bfloat16 [3584, 18432], P('row', 'col')
Inputs may be any that keep to these rules, and one draw needn't show every extreme that they name: An iterate of the orthogonalization, with spectral norm of order one.
All inputs are finite; a program needn't handle non-finite values.
Results may differ from a plain program's by a relative error of at most 0.018.
Values may be sent and summed in bfloat16 or wider, within the bound.
No kernel may reach another device: no remote copies, remote signals or barrier semaphores. Data moves between devices by JAX's collectives and lax.ppermute only.
A program may use at most 64 MiB of HBM per device.

v0:
```python
import math

import jax
import jax.numpy as jnp
from jax import lax
from jax.sharding import PartitionSpec as P

N = 18432


coef_a = 3.4445
coef_b = -4.775
coef_c = 2.0315


def per_device(iterate):
    contract = (((1,), (1,)), ((), ()))
    partial_value = lax.dot_general(
        iterate,
        lax.all_gather(iterate, "row", axis=0, tiled=True),
        contract,
        preferred_element_type=jnp.float32,
    )
    partial_value = partial_value.astype(jnp.bfloat16)
    gram_tile = (
        lax.psum_scatter(partial_value, "col", scatter_dimension=1, tiled=True)
        .astype(jnp.float32)
        .astype(jnp.bfloat16)
    )
    gram_panel = lax.all_gather(gram_tile, "col", axis=1, tiled=True)
    squared = jnp.dot(
        gram_panel,
        lax.all_gather(gram_tile, "row", axis=0, tiled=True),
        preferred_element_type=jnp.float32,
    )
    factor = (coef_b * gram_tile.astype(jnp.float32) + coef_c * squared).astype(jnp.bfloat16)
    factor_panel = lax.all_gather(factor, "col", axis=1, tiled=True)
    product = jnp.dot(
        factor_panel,
        lax.all_gather(iterate, "row", axis=0, tiled=True),
        preferred_element_type=jnp.float32,
    )
    result = coef_a * iterate.astype(jnp.float32) + product
    return (math.sqrt(N) * result).astype(jnp.bfloat16)


def solution(mesh):
    return jax.shard_map(
        per_device,
        mesh=mesh,
        in_specs=(P("row", "col"),),
        out_specs=P("row", "col"),
        check_vma=False,
    )
```

profile of v0, /device:TPU:0, one launch (start us, length us, event | category | flops | bytes accessed | tf_op | source)
XLA Modules:
  0.0 573.0 jit_solution(9806608487441506420)
XLA Ops:
  6.5 0.0 all-gather.5.cloned.1.call-start
  6.5 0.7 all-gather.5.cloned.1.call-update
  7.3 0.0 reduce-scatter.2.cloned.1.call-start
  7.3 286.8 %all-gather.5.cloned.1.call-done = bf16[3584,2304]{1,0:T(8,128)(2,1)} async-done(((bf16[896,2304]{1,0:T(8,128)(2,1)}), bf16[3584,2304]{1,0:T(8,128)(2,1)}) %all-gather.5.cloned.1.call-update) | async-done | bytes 16515088 | tf_op jit(solution)/shard_map/all_gather | solution.py:20
  294.2 22.4 %convolution_convert_fusion = bf16[896,3584]{0,1:T(8,128)(2,1)} fusion(bf16[896,2304]{1,0:T(8,128)(2,1)} %param.1, bf16[3584,2304]{1,0:T(8,128)(2,1)} %all-gather.5.cloned.1.call-done), kind=kOutput, calls=%fused_computation.1 | convolution fusion | flops 14800715776 | bytes 27066368 | tf_op jit(solution)/shard_map/dot_general | solution.py:18
  316.6 0.0 reduce-scatter.2.cloned.1.call-update
  316.6 0.0 all-gather.9.cloned.1.call-start
  316.7 60.7 %reduce-scatter.2.cloned.1.call-done = bf16[896,448]{0,1:T(8,128)(2,1)} async-done(((bf16[896,3584]{0,1:T(8,128)(2,1)}), bf16[896,448]{0,1:T(8,128)(2,1)}) %reduce-scatter.2.cloned.1.call-update) | async-done | bytes 802832 | tf_op jit(solution)/shard_map/reduce_scatter | solution.py:26
  377.4 0.0 all-gather.9.cloned.1.call-update
  377.4 0.0 all-gather.7.cloned.1.call-start
  377.4 0.5 all-gather.7.cloned.1.call-update
  378.0 0.0 all-gather.11.cloned.1.call-start
  378.0 65.5 %all-gather.9.cloned.1.call-done = bf16[3584,448]{0,1:T(8,128)(2,1)} async-done(((bf16[896,448]{0,1:T(8,128)(2,1)}), bf16[3584,448]{0,1:T(8,128)(2,1)}) %all-gather.9.cloned.1.call-update) | async-done | bytes 3211280 | tf_op jit(solution)/shard_map/all_gather | solution.py:33
  443.5 46.6 %all-gather.7.cloned.1.call-done = bf16[896,3584]{0,1:T(8,128)(2,1)} async-done(((bf16[896,448]{0,1:T(8,128)(2,1)}), bf16[896,3584]{0,1:T(8,128)(2,1)}) %all-gather.7.cloned.1.call-update) | async-done | bytes 6422544 | tf_op jit(solution)/shard_map/all_gather | solution.py:30
  490.1 8.3 %add_convert_fusion = bf16[896,448]{0,1:T(8,128)(2,1)} fusion(bf16[896,448]{0,1:T(8,128)(2,1)} %reduce-scatter.2.cloned.1.call-done, bf16[3584,448]{0,1:T(8,128)(2,1)} %all-gather.9.cloned.1.call-done, bf16[896,3584]{0,1:T(8,128)(2,1)} %all-gather.7.cloned.1.call-done), kind=kOutput, calls=%fused_computation.2 | convolution fusion | flops 2879299584 | bytes 11239424 | tf_op jit(solution)/shard_map/dot_general | solution.py:31
  498.3 0.0 all-gather.11.cloned.1.call-update
  498.4 46.2 %all-gather.11.cloned.1.call-done = bf16[896,3584]{0,1:T(8,128)(2,1)} async-done(((bf16[896,448]{0,1:T(8,128)(2,1)}), bf16[896,3584]{0,1:T(8,128)(2,1)}) %all-gather.11.cloned.1.call-update) | async-done | bytes 6422544 | tf_op jit(solution)/shard_map/all_gather | solution.py:37
  544.6 21.9 %multiply_convert_fusion = bf16[896,2304]{1,0:T(8,128)(2,1)} fusion(bf16[896,2304]{1,0:T(8,128)(2,1)} %param.1, bf16[896,3584]{0,1:T(8,128)(2,1)} %all-gather.11.cloned.1.call-done, bf16[3584,2304]{1,0:T(8,128)(2,1)} %all-gather.5.cloned.1.call-done), kind=kOutput, calls=%fused_computation | convolution fusion | flops 14807826432 | bytes 31195136 | tf_op jit(solution)/shard_map/dot_general | solution.py:38
Async XLA Ops:
  6.5 287.6 %all-gather.5.cloned.1.call-start = ((), (), s32[]{:S(2)}) async-start(), calls=%async_computation.1 | async-start | bytes 20643840 | tf_op jit(solution)/shard_map/all_gather | solution.py:20
  7.3 370.1 %reduce-scatter.2.cloned.1.call-start = ((), (), s32[]{:S(2)}) async-start(), calls=%async_computation.2 | async-start | bytes 7225344 | tf_op jit(solution)/shard_map/reduce_scatter | solution.py:26
  316.6 126.9 %all-gather.9.cloned.1.call-start = ((), (), s32[]{:S(2)}) async-start(), calls=%async_computation.4 | async-start | bytes 4014080 | tf_op jit(solution)/shard_map/all_gather | solution.py:33
  377.4 112.7 %all-gather.7.cloned.1.call-start = ((), (), s32[]{:S(2)}) async-start(), calls=%async_computation.3 | async-start | bytes 7225344 | tf_op jit(solution)/shard_map/all_gather | solution.py:30
  378.0 166.6 %all-gather.11.cloned.1.call-start = ((), (), s32[]{:S(2)}) async-start(), calls=%async_computation.5 | async-start | bytes 7225344 | tf_op jit(solution)/shard_map/all_gather | solution.py:37
Sparse Core Ops, SparseCore 0:
  8.9 285.1 all-gather.4
  316.7 60.5 reduce-scatter.1
  379.0 64.4 all-gather.8
  445.2 44.7 all-gather.6
  498.5 46.0 all-gather.10
where the time goes:
time: 573 us
  waiting for transfers between devices  507 us (88%)
  matrix products  52.6 us (9%)
  between operations  13.1 us (2%)
    all_gather x1, waiting for transfers between devices, per_device(): lax.all_gather(iterate, 'row', axis=0, tiled=True)  287 us
    all_gather x1, waiting for transfers between devices, per_device(): lax.all_gather(gram_tile, 'row', axis=0, tiled=True)  65.5 us
    reduce_scatter x1, waiting for transfers between devices, per_device(): lax.psum_scatter(partial_value, 'col', scatter_dimension=1, tiled=True)  60.7 us
    all_gather x1, waiting for transfers between devices, per_device(): gram_panel = lax.all_gather(gram_tile, 'col', axis=1, tiled=True)  46.6 us
    all_gather x1, waiting for transfers between devices, per_device(): factor_panel = lax.all_gather(factor, 'col', axis=1, tiled=True)  46.2 us
    dot_general x1, matrix products, per_device(): lax.dot_general(iterate, lax.all_gather(iterate, 'row', axis=0, tiled=Tru...  22.4 us
    dot_general x1, matrix products, per_device(): jnp.dot(factor_panel, lax.all_gather(iterate, 'row', axis=0, tiled=True),...  21.9 us
  transfers between devices with their start and end apart: 5, of which 5 were waited for; matrix products, arithmetic and copies ran while one was open for 0% of the time, Pallas kernels for 0%

commit v1 on v0

v1 whole, which is shorter than its diff:
```python
import math

import jax
import jax.numpy as jnp
from jax import lax
from jax.sharding import PartitionSpec as P

N = 18432


coef_a = 3.4445
coef_b = -4.775
coef_c = 2.0315


def dot_rows(left, right):
    return lax.dot_general(
        left, right, (((1,), (1,)), ((), ())), preferred_element_type=jnp.float32
    )


def per_device(iterate):
    contract = (((1,), (1,)), ((), ()))
    gathered = lax.all_gather(iterate, "row", axis=0, tiled=True)
    partial_value = lax.dot_general(
        iterate, gathered, contract, preferred_element_type=jnp.float32
    )
    partial_value = partial_value.astype(jnp.bfloat16)
    gram_tile = lax.psum_scatter(partial_value, "col", scatter_dimension=1, tiled=True)
    gram_panel = lax.all_gather(gram_tile, "col", axis=1, tiled=True)
    squared = jnp.dot(
        gram_panel,
        lax.all_gather(gram_tile, "row", axis=0, tiled=True),
        preferred_element_type=jnp.float32,
    )
    factor = (coef_b * gram_tile.astype(jnp.float32) + coef_c * squared).astype(jnp.bfloat16)
    factor_panel = lax.all_gather(factor, "col", axis=1, tiled=True)
    product = jnp.dot(factor_panel, gathered, preferred_element_type=jnp.float32)
    result = coef_a * iterate.astype(jnp.float32) + product
    return (math.sqrt(N) * result).astype(jnp.bfloat16)


def per_device_line(n_col, x):
    rows = x.shape[0]
    z = lax.axis_index("row")
    right, left = [(0, 1), (1, 2), (2, 3)], [(3, 2), (2, 1), (1, 0)]

    def gram_block(one, other):
        return dot_rows(one, other).astype(jnp.bfloat16)

    def scatter(blocks):
        return lax.psum_scatter(jnp.stack(blocks), "col", scatter_dimension=1, tiled=True)

    r1 = lax.ppermute(x, "row", right)
    l1 = lax.ppermute(x, "row", left)
    r2 = lax.ppermute(r1, "row", right[1:])
    l2 = lax.ppermute(l1, "row", left[1:])

    first = scatter([gram_block(x, other) for other in (x, l1, r1)])
    first, r2, l2 = lax.optimization_barrier((first, r2, l2))

    width = x.shape[1] // 3
    pieces = [slice(0, width), slice(width, 2 * width), slice(2 * width, None)]
    r3 = [lax.ppermute(r2[:, piece], "row", right[2:]) for piece in pieces]
    l3 = [lax.ppermute(l2[:, piece], "row", left[2:]) for piece in pieces]

    across = l2 + r2
    inner = jnp.where(z == 1, r1, l1)
    second = scatter([gram_block(x, across), gram_block(inner, across)])
    second, r3[0], l3[0] = lax.optimization_barrier((second, r3[0], l3[0]))
    corner = lax.ppermute(second[1], "row", [(1, 0), (2, 3)])
    tile = jnp.concatenate(
        [
            first[0],
            jnp.where(z == 3, corner, first[1]),
            second[0],
            jnp.where(z == 0, corner, first[2]),
        ],
        axis=1,
    )

    panel = lax.all_gather(tile, "col", axis=0, tiled=True)
    tr1 = lax.ppermute(tile, "row", right)
    tl1 = lax.ppermute(tile, "row", left)
    tr2 = lax.ppermute(tr1, "row", right[1:])
    tl2 = lax.ppermute(tl1, "row", left[1:])
    tr3 = lax.ppermute(tr2, "row", right[2:])
    tl3 = lax.ppermute(tl2, "row", left[2:])
    strips = [tile, tl1 + tr3, tl2 + tr2, tr1 + tl3]
    strips = [jnp.roll(strip, d * rows, axis=1) for d, strip in enumerate(strips)]
    strip = jnp.concatenate(strips, axis=0)
    panel, strip, r3[1], l3[1] = lax.optimization_barrier((panel, strip, r3[1], l3[1]))
    squared = dot_rows(strip, panel)
    factor = (coef_b * strip[:, :rows].astype(jnp.float32) + coef_c * squared).astype(jnp.bfloat16)
    factor = lax.all_gather(factor.reshape(4, -1, rows), "col", axis=1, tiled=True)

    def term(d, block):
        return lax.dot_general(
            factor[d], block, (((0,), (0,)), ((), ())), preferred_element_type=jnp.float32
        )

    r3, l3 = jnp.concatenate(r3, axis=1), jnp.concatenate(l3, axis=1)
    product = term(0, x) + term(2, across) + term(1, l1 + r3) + term(3, r1 + l3)
    result = coef_a * x.astype(jnp.float32) + product
    return (math.sqrt(N) * result).astype(jnp.bfloat16)


def solution(mesh):
    n_row, n_col = mesh.shape["row"], mesh.shape["col"]

    def body(iterate):
        if n_row == 4 and iterate.shape[0] % (16 * n_col) == 0:
            return per_device_line(n_col, iterate)
        return per_device(iterate)

    return jax.shard_map(
        body,
        mesh=mesh,
        in_specs=(P("row", "col"),),
        out_specs=P("row", "col"),
        check_vma=False,
    )
```

time: 573 us -> 486 us (0.85); the launches traced: 573 us -> 480 us
  waiting for transfers between devices: 507 us -> 319 us
  other arithmetic: 0 us -> 29.7 us
  starting transfers between devices: 0.16 us -> 27.7 us
  matrix products: 52.6 us -> 78.2 us
  local copies, waits for them, and re-layouts: 0 us -> 11 us
    all_gather x4 -> x2, waiting for transfers between devices: 445 us -> 41.2 us  [the longest x1 41.2 us: per_device_line(): lax.all_gather(factor.reshape(4, -1, rows), 'col', axis=1, tiled=True)]
    ppermute x0 -> x17, waiting for transfers between devices: none -> 267 us  [the longest x1 93.9 us: per_device_line(): l2 = lax.ppermute(l1, 'row', left[1:])]
    reduce_scatter x1 -> x2, waiting for transfers between devices: 60.7 us -> 10.8 us  [scatter(): lax.psum_scatter(jnp.stack(blocks), 'col', scatter_dimension=1, tiled=True)]
    ppermute x0 -> x17, starting transfers between devices: none -> 27.6 us  [the longest x1 5.45 us: per_device_line(): r1 = lax.ppermute(x, 'row', right)]
    dot_general x3 -> x10, matrix products: 52.6 us -> 78.2 us  [the longest x4 45.3 us: term(): lax.dot_general(factor[d], block, (((0,), (0,)), ((), ())), preferred_ele...]
    concatenate x0 -> x2, other arithmetic: none -> 20.1 us  [the longest x1 19.1 us: per_device_line(): strip = jnp.concatenate(strips, axis=0)]
    slice x0 -> x7, local copies, waits for them, and re-layouts: none -> 8.64 us  [the longest x1 4.45 us: per_device_line(): r3 = [lax.ppermute(r2[:, piece], 'row', right[2:]) for piece in pieces]]
  transfers between devices with their start and end apart: 5 -> 21, of which waited for: 5 -> 11; matrix products, arithmetic and copies ran while one was open for 0% -> 13% of each run, Pallas kernels for 0% -> 0%
where the time goes in v1:
time: 486 us; the launch traced here: 480 us
  waiting for transfers between devices  319 us (66%)
  matrix products  78.2 us (16%)
  other arithmetic  29.7 us (6%)
  starting transfers between devices  27.7 us (6%)
  between operations  14.1 us (3%)
  local copies, waits for them, and re-layouts  11 us (2%)
    ppermute x1, waiting for transfers between devices, per_device_line(): l2 = lax.ppermute(l1, 'row', left[1:])  93.9 us
    ppermute x1, waiting for transfers between devices, per_device_line(): r1 = lax.ppermute(x, 'row', right)  79.3 us
    dot_general x4, matrix products, term(): lax.dot_general(factor[d], block, (((0,), (0,)), ((), ())), preferred_ele...  45.3 us
    all_gather x1, waiting for transfers between devices, per_device_line(): lax.all_gather(factor.reshape(4, -1, rows), 'col', axis=1, tiled=True)  41.2 us
    dot_general x6, matrix products, dot_rows(): lax.dot_general(left, right, (((1,), (1,)), ((), ())), preferred_element_...  32.9 us
    ppermute x3, waiting for transfers between devices, per_device_line(): l3 = [lax.ppermute(l2[:, piece], 'row', left[2:]) for piece in pieces]  31.3 us
    concatenate x1, other arithmetic, per_device_line(): strip = jnp.concatenate(strips, axis=0)  19.1 us
    ppermute x1, waiting for transfers between devices, per_device_line(): tl2 = lax.ppermute(tl1, 'row', left[1:])  18.4 us
  transfers between devices with their start and end apart: 21, of which 11 were waited for; matrix products, arithmetic and copies ran while one was open for 13% of the time, Pallas kernels for 0%

profile of v1, /device:TPU:0, one launch (start us, length us, event | category | flops | bytes accessed | tf_op | source)
XLA Modules:
  0.0 479.8 jit_solution(3094032977492197696)
XLA Ops:
  6.5 5.4 %collective-permute-start.1 = (bf16[896,2304]{1,0:T(8,128)(2,1)}, bf16[896,2304]{1,0:T(8,128)(2,1)S(1)}, u32[]{:S(2)}, u32[]{:S(2)}) collective-permute-start(bf16[896,2304]{1,0:T(8,128)(2,1)} %param.1), channel_id=1, source_target_pairs={{0,8},{8,16},{16,24},{1,9},{9,17},{17,25},{2,10},{10,18},{18,26},{... | collective-permute-start | bytes 12386312 | tf_op jit(solution)/shard_map/ppermute | solution.py:54
  13.3 7.9 %fusion.17 = bf16[1,896,896]{2,1,0:T(8,128)(2,1)S(1)} fusion(bf16[896,2304]{1,0:T(8,128)(2,1)} %param.1), kind=kOutput, calls=%fused_computation.30 | convolution fusion | flops 3700178944 | bytes 5734400 | tf_op jit(solution)/shard_map/dot_general | solution.py:17
  21.2 79.3 %collective-permute-done.1 = bf16[896,2304]{1,0:T(8,128)(2,1)S(1)} collective-permute-done((bf16[896,2304]{1,0:T(8,128)(2,1)}, bf16[896,2304]{1,0:T(8,128)(2,1)S(1)}, u32[]{:S(2)}, u32[]{:S(2)}) %collective-permute-start.1) | collective-permute-done | bytes 4128800 | tf_op jit(solution)/shard_map/ppermute | solution.py:54
  100.5 4.4 fusion.19
  104.9 4.4 fusion.18
  109.4 2.5 pad_maximum_fusion
  112.0 2.7 collective-permute-start.2
  116.1 93.9 %collective-permute-done.3 = bf16[896,2304]{1,0:T(8,128)(2,1)} collective-permute-done((bf16[896,2304]{1,0:T(8,128)(2,1)}, bf16[896,2304]{1,0:T(8,128)(2,1)}, u32[]{:S(2)}, u32[]{:S(2)}) %collective-permute-start.3) | collective-permute-done | bytes 4128800 | tf_op jit(solution)/shard_map/ppermute | solution.py:57
  210.0 4.6 add.37
  214.6 4.4 fusion.20
  219.5 4.5 fusion.21
  224.0 2.0 pad_maximum_fusion.1
  226.0 4.0 fusion.27
  231.5 4.4 fusion.26
  235.9 1.8 collective-permute-start.4
  237.7 24.6 %collective-permute-done.5 = bf16[896,768]{1,0:T(8,128)(2,1)} collective-permute-done((bf16[896,768]{1,0:T(8,128)(2,1)S(1)}, bf16[896,768]{1,0:T(8,128)(2,1)}, u32[]{:S(2)}, u32[]{:S(2)}) %collective-permute-start.5) | collective-permute-done | bytes 1376288 | tf_op jit(solution)/shard_map/ppermute | solution.py:65
  262.3 10.8 %reduce-scatter.5.cloned.1.call-done = bf16[2,112,896]{2,1,0:T(8,128)(2,1)} async-done(((bf16[2,896,896]{2,1,0:T(8,128)(2,1)}), bf16[2,112,896]{2,1,0:T(8,128)(2,1)}) %reduce-scatter.5.cloned.1.call-update) | async-done | bytes 401424 | tf_op jit(solution)/shard_map/reduce_scatter | solution.py:52
  275.6 7.3 %collective-permute-done.6 = bf16[112,896]{1,0:T(8,128)(2,1)S(1)} collective-permute-done((bf16[112,896]{1,0:T(8,128)(2,1)S(1)}, bf16[112,896]{1,0:T(8,128)(2,1)S(1)}, u32[]{:S(2)}, u32[]{:S(2)}) %collective-permute-start.6) | collective-permute-done | bytes 200736 | tf_op jit(solution)/shard_map/ppermute | solution.py:71
  284.7 1.5 collective-permute-start.8
  287.5 15.3 %collective-permute-done.8 = bf16[112,3584]{1,0:T(8,128)(2,1)S(1)} collective-permute-done((bf16[112,3584]{1,0:T(8,128)(2,1)}, bf16[112,3584]{1,0:T(8,128)(2,1)S(1)}, u32[]{:S(2)}, u32[]{:S(2)}) %collective-permute-start.8) | collective-permute-done | bytes 802848 | tf_op jit(solution)/shard_map/ppermute | solution.py:83
  303.6 3.9 collective-permute-done.7
  309.5 18.4 %collective-permute-done.11 = bf16[112,3584]{1,0:T(8,128)(2,1)S(1)} collective-permute-done((bf16[112,3584]{1,0:T(8,128)(2,1)S(1)}, bf16[112,3584]{1,0:T(8,128)(2,1)S(1)}, u32[]{:S(2)}, u32[]{:S(2)}) %collective-permute-start.11) | collective-permute-done | bytes 802848 | tf_op jit(solution)/shard_map/ppermute | solution.py:86
  330.5 1.9 collective-permute-start.13
  333.0 17.6 %collective-permute-done.12 = bf16[112,3584]{1,0:T(8,128)(2,1)S(1)} collective-permute-done((bf16[112,3584]{1,0:T(8,128)(2,1)S(1)}, bf16[112,3584]{1,0:T(8,128)(2,1)S(1)}, u32[]{:S(2)}, u32[]{:S(2)}) %collective-permute-start.12) | collective-permute-done | bytes 802848 | tf_op jit(solution)/shard_map/ppermute | solution.py:88
  350.9 19.1 %maximum_maximum_fusion = bf16[448,3584]{1,0:T(8,128)(2,1)S(1)} fusion(bf16[112,896]{1,0:T(8,128)(2,1)S(1)} %slice.99, bf16[112,2688]{1,0:T(8,128)(2,1)S(1)} %slice.98, bf16[112,1792]{1,0:T(8,128)(2,1)S(1)} %get-tuple-element.32, bf16[112,1792]{1,0:T(8,128)(2,1)S(1)} %get-tuple-element.31, bf16[112,2688]{1,0:T(8,128)(2,1)S(1)} %slice.95, ...), kind=kLoop, calls=%fused_computation.18 | loop fusion | flops 32112640 | bytes 6422528 | tf_op jit(solution)/shard_map/concatenate | solution.py:91
  370.0 6.7 %collective-permute-done.14 = bf16[896,768]{1,0:T(8,128)(2,1)} collective-permute-done((bf16[896,768]{1,0:T(8,128)(2,1)}, bf16[896,768]{1,0:T(8,128)(2,1)}, u32[]{:S(2)}, u32[]{:S(2)}) %collective-permute-start.14) | collective-permute-done | bytes 1376288 | tf_op jit(solution)/shard_map/ppermute | solution.py:65
  376.7 7.3 %add_convert_fusion = bf16[448,896]{1,0:T(8,128)(2,1)} fusion(bf16[448,3584]{1,0:T(8,128)(2,1)S(1)} %maximum_maximum_fusion, bf16[896,3584]{1,0:T(8,128)(2,1)} %all-gather.3.cloned.1.call-done), kind=kOutput, calls=%fused_computation.29 | convolution fusion | flops 2879299584 | bytes 11239424 | tf_op jit(solution)/shard_map/dot_general | solution.py:17
  386.3 41.2 %all-gather.5.cloned.1.call-done = bf16[4,896,896]{2,1,0:T(8,128)(2,1)} async-done(((bf16[4,112,896]{2,1,0:T(8,128)(2,1)}), bf16[4,896,896]{2,1,0:T(8,128)(2,1)}) %all-gather.5.cloned.1.call-update) | async-done | bytes 6422544 | tf_op jit(solution)/shard_map/all_gather | solution.py:95
  427.4 10.5 %fusion.16 = f32[896,2304]{1,0:T(8,128)} fusion(bf16[896,2304]{1,0:T(8,128)(2,1)} %param.1, bf16[4,896,896]{2,1,0:T(8,128)(2,1)} %all-gather.5.cloned.1.call-done), kind=kOutput, calls=%fused_computation.28 | convolution fusion | flops 3699376128 | bytes 13991936 | tf_op jit(solution)/shard_map/dot_general | solution.py:98
  438.0 10.1 %fusion.5 = f32[896,2304]{1,0:T(8,128)} fusion(bf16[896,2304]{1,0:T(8,128)(2,1)S(1)} %copy-done.17, bf16[896,768]{1,0:T(8,128)(2,1)} %collective-permute-done.16, bf16[896,768]{1,0:T(8,128)(2,1)} %collective-permute-done.14, bf16[896,768]{1,0:T(8,128)(2,1)} %collective-permute-done.5, bf16[4,896,896]{2,1,0:T(8,128)(2,1)S(1)} %copy-done.11), kind=kOutput, calls=%fused_computation.9 | convolution fusion | flops 3715891200 | bytes 18120704 | tf_op jit(solution)/shard_map/dot_general | solution.py:98
  448.1 10.0 %fusion = f32[896,2304]{1,0:T(8,128)} fusion(bf16[896,2304]{1,0:T(8,128)(2,1)S(1)} %copy-done.14, bf16[896,768]{1,0:T(8,128)(2,1)S(1)} %collective-permute-done.15, bf16[896,768]{1,0:T(8,128)(2,1)} %collective-permute-done.13, bf16[896,768]{1,0:T(8,128)(2,1)} %collective-permute-done.4, bf16[4,896,896]{2,1,0:T(8,128)(2,1)S(1)} %copy-done.11), kind=kOutput, calls=%fused_computation.3 | convolution fusion | flops 3715891200 | bytes 18120704 | tf_op jit(solution)/shard_map/dot_general | solution.py:98
  458.1 14.6 %multiply_convert_fusion = bf16[896,2304]{1,0:T(8,128)(2,1)} fusion(f32[896,2304]{1,0:T(8,128)} %fusion.5, f32[896,2304]{1,0:T(8,128)} %fusion, f32[896,2304]{1,0:T(8,128)} %fusion.16, bf16[896,2304]{1,0:T(8,128)(2,1)} %param.1, bf16[896,2304]{1,0:T(8,128)(2,1)S(1)} %copy-done.1, bf16[4,896,896]{2,1,0:T(8,128)(2,1)} %all-gather.5.cloned.1.call-done), kind=kOutput, calls=%fused_computation | convolution fusion | flops 3715891200 | bytes 38764544 | tf_op jit(solution)/shard_map/dot_general | solution.py:98
  (78 shorter events, 18.6 us)
Async XLA Ops:
  6.5 203.5 %reduce-scatter.3.cloned.1.call-start = ((), (), s32[]{:S(2)}) async-start(), calls=%async_computation.2 | async-start | bytes 5419008 | tf_op jit(solution)/shard_map/reduce_scatter | solution.py:52
  6.5 93.9 %copy-start.2 = (bf16[896,2304]{1,0:T(8,128)(2,1)S(1)}, bf16[896,2304]{1,0:T(8,128)(2,1)}, u32[]{:S(2)}) copy-start(bf16[896,2304]{1,0:T(8,128)(2,1)} %param.1) | copy-start | bytes 12386308
  6.5 93.9 %collective-permute-start.1 = (bf16[896,2304]{1,0:T(8,128)(2,1)}, bf16[896,2304]{1,0:T(8,128)(2,1)S(1)}, u32[]{:S(2)}, u32[]{:S(2)}) collective-permute-start(bf16[896,2304]{1,0:T(8,128)(2,1)} %param.1), channel_id=1, source_target_pairs={{0,8},{8,16},{16,24},{1,9},{9,17},{17,25},{2,10},{10,18},{18,26},{... | collective-permute-start | bytes 12386312 | tf_op jit(solution)/shard_map/ppermute | solution.py:54
  12.0 92.9 %collective-permute-start = (bf16[896,2304]{1,0:T(8,128)(2,1)}, bf16[896,2304]{1,0:T(8,128)(2,1)S(1)}, u32[]{:S(2)}, u32[]{:S(2)}) collective-permute-start(bf16[896,2304]{1,0:T(8,128)(2,1)} %param.1), channel_id=1, source_target_pairs={{24,16},{16,8},{8,0},{25,17},{17,9},{9,1},{26,18},{18,10},{10,2},{... | collective-permute-start | bytes 12386312 | tf_op jit(solution)/shard_map/ppermute | solution.py:55
  111.9 161.2 %reduce-scatter.5.cloned.1.call-start = ((), (), s32[]{:S(2)}) async-start(), calls=%async_computation.3 | async-start | bytes 3612672 | tf_op jit(solution)/shard_map/reduce_scatter | solution.py:52
  112.0 4.1 collective-permute-start.2
  114.6 95.4 %collective-permute-start.3 = (bf16[896,2304]{1,0:T(8,128)(2,1)}, bf16[896,2304]{1,0:T(8,128)(2,1)}, u32[]{:S(2)}, u32[]{:S(2)}) collective-permute-start(bf16[896,2304]{1,0:T(8,128)(2,1)} %copy-done.12), channel_id=1, source_target_pairs={{16,8},{8,0},{17,9},{9,1},{18,10},{10,2},{19,11},{11,3},{20,12},{1... | collective-permute-start | bytes 12386312 | tf_op jit(solution)/shard_map/ppermute | solution.py:57
  214.6 4.9 %copy-start.16 = (bf16[896,2304]{1,0:T(8,128)(2,1)S(1)}, bf16[896,2304]{1,0:T(8,128)(2,1)}, u32[]{:S(2)}) copy-start(bf16[896,2304]{1,0:T(8,128)(2,1)} %copy-done.15) | copy-start | bytes 12386308
  226.0 150.7 %all-gather.3.cloned.1.call-start = ((), (), s32[]{:S(2)}) async-start(), calls=%async_computation.4 | async-start | bytes 7225344 | tf_op jit(solution)/shard_map/all_gather | solution.py:82
  230.1 45.5 %copy-start.10 = (bf16[3,112,896]{2,1,0:T(8,128)(2,1)S(1)}, bf16[3,112,896]{2,1,0:T(8,128)(2,1)}, u32[]{:S(2)}) copy-start(bf16[3,112,896]{2,1,0:T(8,128)(2,1)} %reduce-scatter.3.cloned.1.call-done) | copy-start | bytes 1806340
  230.1 32.2 %collective-permute-start.5 = (bf16[896,768]{1,0:T(8,128)(2,1)S(1)}, bf16[896,768]{1,0:T(8,128)(2,1)}, u32[]{:S(2)}, u32[]{:S(2)}) collective-permute-start(bf16[896,768]{1,0:T(8,128)(2,1)S(1)} %get-tuple-element.30), channel_id=1, source_target_pairs={{8,0},{9,1},{10,2},{11,3},{12,4},{13,5},{14,6},{15,7}} | collective-permute-start | bytes 4128776 | tf_op jit(solution)/shard_map/ppermute | solution.py:65
  235.9 26.4 %collective-permute-start.4 = (bf16[896,768]{1,0:T(8,128)(2,1)S(1)}, bf16[896,768]{1,0:T(8,128)(2,1)}, u32[]{:S(2)}, u32[]{:S(2)}) collective-permute-start(bf16[896,768]{1,0:T(8,128)(2,1)S(1)} %get-tuple-element.27), channel_id=1, source_target_pairs={{16,24},{17,25},{18,26},{19,27},{20,28},{21,29},{22,30},{23,31}} | collective-permute-start | bytes 4128776 | tf_op jit(solution)/shard_map/ppermute | solution.py:64
  274.2 8.6 %collective-permute-start.6 = (bf16[112,896]{1,0:T(8,128)(2,1)S(1)}, bf16[112,896]{1,0:T(8,128)(2,1)S(1)}, u32[]{:S(2)}, u32[]{:S(2)}) collective-permute-start(bf16[112,896]{1,0:T(8,128)(2,1)S(1)} %get-tuple-element.36), channel_id=1, source_target_pairs={{8,0},{16,24},{9,1},{17,25},{10,2},{18,26},{11,3},{19,27},{12,4},{... | collective-permute-start | bytes 602120 | tf_op jit(solution)/shard_map/ppermute | solution.py:71
  275.5 7.4 %copy-start.4 = (bf16[112,896]{1,0:T(8,128)(2,1)}, bf16[112,896]{1,0:T(8,128)(2,1)S(1)}, u32[]{:S(2)}) copy-start(bf16[112,896]{1,0:T(8,128)(2,1)S(1)} %slice_bitcast_fusion.10) | copy-start | bytes 602116
  284.7 142.8 %all-gather.5.cloned.1.call-start = ((), (), s32[]{:S(2)}) async-start(), calls=%async_computation.5 | async-start | bytes 7225344 | tf_op jit(solution)/shard_map/all_gather | solution.py:95
  284.7 18.1 %collective-permute-start.8 = (bf16[112,3584]{1,0:T(8,128)(2,1)}, bf16[112,3584]{1,0:T(8,128)(2,1)S(1)}, u32[]{:S(2)}, u32[]{:S(2)}) collective-permute-start(bf16[112,3584]{1,0:T(8,128)(2,1)} %pad_maximum_fusion.2), channel_id=1, source_target_pairs={{0,8},{8,16},{16,24},{1,9},{9,17},{17,25},{2,10},{10,18},{18,26},{... | collective-permute-start | bytes 2408456 | tf_op jit(solution)/shard_map/ppermute | solution.py:83
  286.2 21.2 %collective-permute-start.7 = (bf16[112,3584]{1,0:T(8,128)(2,1)}, bf16[112,3584]{1,0:T(8,128)(2,1)S(1)}, u32[]{:S(2)}, u32[]{:S(2)}) collective-permute-start(bf16[112,3584]{1,0:T(8,128)(2,1)} %pad_maximum_fusion.2), channel_id=1, source_target_pairs={{24,16},{16,8},{8,0},{25,17},{17,9},{9,1},{26,18},{18,10},{10,2},{... | collective-permute-start | bytes 2408456 | tf_op jit(solution)/shard_map/ppermute | solution.py:84
  302.9 5.9 %collective-permute-start.9 = (bf16[112,3584]{1,0:T(8,128)(2,1)S(1)}, bf16[112,3584]{1,0:T(8,128)(2,1)S(1)}, u32[]{:S(2)}, u32[]{:S(2)}) collective-permute-start(bf16[112,3584]{1,0:T(8,128)(2,1)S(1)} %collective-permute-done.8), channel_id=1, source_target_pairs={{8,16},{16,24},{9,17},{17,25},{10,18},{18,26},{11,19},{19,27},{12,... | collective-permute-start | bytes 2408456 | tf_op jit(solution)/shard_map/ppermute | solution.py:85
  307.4 20.5 %collective-permute-start.11 = (bf16[112,3584]{1,0:T(8,128)(2,1)S(1)}, bf16[112,3584]{1,0:T(8,128)(2,1)S(1)}, u32[]{:S(2)}, u32[]{:S(2)}) collective-permute-start(bf16[112,3584]{1,0:T(8,128)(2,1)S(1)} %collective-permute-done.7), channel_id=1, source_target_pairs={{16,8},{8,0},{17,9},{9,1},{18,10},{10,2},{19,11},{11,3},{20,12},{1... | collective-permute-start | bytes 2408456 | tf_op jit(solution)/shard_map/ppermute | solution.py:86
  308.7 24.0 %collective-permute-start.10 = (bf16[112,3584]{1,0:T(8,128)(2,1)S(1)}, bf16[112,3584]{1,0:T(8,128)(2,1)S(1)}, u32[]{:S(2)}, u32[]{:S(2)}) collective-permute-start(bf16[112,3584]{1,0:T(8,128)(2,1)S(1)} %collective-permute-done.9), channel_id=1, source_target_pairs={{16,24},{17,25},{18,26},{19,27},{20,28},{21,29},{22,30},{23,31}} | collective-permute-start | bytes 2408456 | tf_op jit(solution)/shard_map/ppermute | solution.py:87
  327.9 22.7 %collective-permute-start.12 = (bf16[112,3584]{1,0:T(8,128)(2,1)S(1)}, bf16[112,3584]{1,0:T(8,128)(2,1)S(1)}, u32[]{:S(2)}, u32[]{:S(2)}) collective-permute-start(bf16[112,3584]{1,0:T(8,128)(2,1)S(1)} %collective-permute-done.11), channel_id=1, source_target_pairs={{8,0},{9,1},{10,2},{11,3},{12,4},{13,5},{14,6},{15,7}} | collective-permute-start | bytes 2408456 | tf_op jit(solution)/shard_map/ppermute | solution.py:88
  329.2 47.5 %collective-permute-start.14 = (bf16[896,768]{1,0:T(8,128)(2,1)}, bf16[896,768]{1,0:T(8,128)(2,1)}, u32[]{:S(2)}, u32[]{:S(2)}) collective-permute-start(bf16[896,768]{1,0:T(8,128)(2,1)} %get-tuple-element.28), channel_id=1, source_target_pairs={{8,0},{9,1},{10,2},{11,3},{12,4},{13,5},{14,6},{15,7}} | collective-permute-start | bytes 4128776 | tf_op jit(solution)/shard_map/ppermute | solution.py:65
  330.5 46.2 %collective-permute-start.13 = (bf16[896,768]{1,0:T(8,128)(2,1)}, bf16[896,768]{1,0:T(8,128)(2,1)}, u32[]{:S(2)}, u32[]{:S(2)}) collective-permute-start(bf16[896,768]{1,0:T(8,128)(2,1)} %get-tuple-element.26), channel_id=1, source_target_pairs={{16,24},{17,25},{18,26},{19,27},{20,28},{21,29},{22,30},{23,31}} | collective-permute-start | bytes 4128776 | tf_op jit(solution)/shard_map/ppermute | solution.py:64
  332.7 18.2 %copy-start.5 = (bf16[112,896]{1,0:T(8,128)(2,1)S(1)}, bf16[112,896]{1,0:T(8,128)(2,1)}, u32[]{:S(2)}) copy-start(bf16[112,896]{1,0:T(8,128)(2,1)} %copy-done.4) | copy-start | bytes 602116
  332.7 18.2 %copy-start.7 = (bf16[112,896]{1,0:T(8,128)(2,1)S(1)}, bf16[112,896]{1,0:T(8,128)(2,1)}, u32[]{:S(2)}) copy-start(bf16[112,896]{1,0:T(8,128)(2,1)} %copy-done.6) | copy-start | bytes 602116
  332.7 18.2 %copy-start.9 = (bf16[112,896]{1,0:T(8,128)(2,1)S(1)}, bf16[112,896]{1,0:T(8,128)(2,1)}, u32[]{:S(2)}) copy-start(bf16[112,896]{1,0:T(8,128)(2,1)} %copy-done.8) | copy-start | bytes 602116
  384.0 54.0 %collective-permute-start.16 = (bf16[896,768]{1,0:T(8,128)(2,1)}, bf16[896,768]{1,0:T(8,128)(2,1)}, u32[]{:S(2)}, u32[]{:S(2)}) collective-permute-start(bf16[896,768]{1,0:T(8,128)(2,1)} %get-tuple-element.29), channel_id=1, source_target_pairs={{8,0},{9,1},{10,2},{11,3},{12,4},{13,5},{14,6},{15,7}} | collective-permute-start | bytes 4128776 | tf_op jit(solution)/shard_map/ppermute | solution.py:65
  385.3 62.8 %collective-permute-start.15 = (bf16[896,768]{1,0:T(8,128)(2,1)}, bf16[896,768]{1,0:T(8,128)(2,1)S(1)}, u32[]{:S(2)}, u32[]{:S(2)}) collective-permute-start(bf16[896,768]{1,0:T(8,128)(2,1)} %get-tuple-element.25), channel_id=1, source_target_pairs={{16,24},{17,25},{18,26},{19,27},{20,28},{21,29},{22,30},{23,31}} | collective-permute-start | bytes 4128776 | tf_op jit(solution)/shard_map/ppermute | solution.py:64
  427.4 10.5 %copy-start.11 = (bf16[4,896,896]{2,1,0:T(8,128)(2,1)S(1)}, bf16[4,896,896]{2,1,0:T(8,128)(2,1)}, u32[]{:S(2)}) copy-start(bf16[4,896,896]{2,1,0:T(8,128)(2,1)} %all-gather.5.cloned.1.call-done) | copy-start | bytes 19267588
  427.4 10.5 %copy-start.17 = (bf16[896,2304]{1,0:T(8,128)(2,1)S(1)}, bf16[896,2304]{1,0:T(8,128)(2,1)}, u32[]{:S(2)}) copy-start(bf16[896,2304]{1,0:T(8,128)(2,1)} %copy-done.15) | copy-start | bytes 12386308
  438.0 10.1 %copy-start.14 = (bf16[896,2304]{1,0:T(8,128)(2,1)S(1)}, bf16[896,2304]{1,0:T(8,128)(2,1)}, u32[]{:S(2)}) copy-start(bf16[896,2304]{1,0:T(8,128)(2,1)} %copy-done.12) | copy-start | bytes 12386308
  448.1 10.1 %copy-start.1 = (bf16[896,2304]{1,0:T(8,128)(2,1)S(1)}, bf16[896,2304]{1,0:T(8,128)(2,1)}, u32[]{:S(2)}) copy-start(bf16[896,2304]{1,0:T(8,128)(2,1)} %copy-done) | copy-start | bytes 12386308
  (7 other events, 23.9 us)
Sparse Core Ops, SparseCore 0:
  112.0 56.8 reduce-scatter.2
  226.1 46.9 reduce-scatter.4
  284.8 46.0 all-gather.2
  384.1 43.2 all-gather.4

commit v2 on v0

v2 whole, which is shorter than its diff:
```python
import functools
import math

import jax
import jax.numpy as jnp
from jax import lax
from jax.experimental import pallas as pl
from jax.experimental.pallas import tpu as pltpu
from jax.sharding import PartitionSpec as P

N = 18432


coef_a = 3.4445
coef_b = -4.775
coef_c = 2.0315


def dot_rows(left, right):
    return lax.dot_general(
        left, right, (((1,), (1,)), ((), ())), preferred_element_type=jnp.float32
    )


def per_device(iterate):
    contract = (((1,), (1,)), ((), ()))
    gathered = lax.all_gather(iterate, "row", axis=0, tiled=True)
    partial_value = lax.dot_general(
        iterate, gathered, contract, preferred_element_type=jnp.float32
    )
    partial_value = partial_value.astype(jnp.bfloat16)
    gram_tile = lax.psum_scatter(partial_value, "col", scatter_dimension=1, tiled=True)
    gram_panel = lax.all_gather(gram_tile, "col", axis=1, tiled=True)
    squared = jnp.dot(
        gram_panel,
        lax.all_gather(gram_tile, "row", axis=0, tiled=True),
        preferred_element_type=jnp.float32,
    )
    factor = (coef_b * gram_tile.astype(jnp.float32) + coef_c * squared).astype(jnp.bfloat16)
    factor_panel = lax.all_gather(factor, "col", axis=1, tiled=True)
    product = jnp.dot(factor_panel, gathered, preferred_element_type=jnp.float32)
    result = coef_a * iterate.astype(jnp.float32) + product
    return (math.sqrt(N) * result).astype(jnp.bfloat16)


def square_kernel(z_ref, panel, far_panel, own, l1, r3, l2, r2, r1, l3, corner, pair, end, last, out):
    z = z_ref[0]
    part = own.shape[1]
    rows = panel.shape[1]
    at_end = jnp.logical_or(z == 0, z == 3)
    near = jnp.where(at_end, end[...], corner[...])
    far = jnp.where(at_end, last[...], pair[...])
    low = jnp.where(z < 2, near, far)
    high = jnp.where(z < 2, far, near)
    zero = jnp.zeros_like(low)

    def strip(e, block):
        if e == 0:
            value = own[block]
        else:
            one, other = {1: (l1, r3), 2: (l2, r2), 3: (r1, l3)}[e]
            value = one[block] + other[block]
        if block == 3:
            value = value + jnp.where((z + e) % 4 == 0, low, zero)
        if block == 1:
            value = value + jnp.where((z + e) % 4 == 3, high, zero)
        return value

    total = jnp.zeros((rows, 4 * part), jnp.float32)
    for d in range(4):
        right = jnp.concatenate([strip(e, (d - e) % 4) for e in range(4)], axis=0)
        left = panel[d]
        if d == 1:
            left = left + jnp.where(z == 3, far_panel[...], jnp.zeros_like(left))
        if d == 3:
            left = left + jnp.where(z == 0, far_panel[...], jnp.zeros_like(left))
        total = total + dot_rows(left, right)
    index = lax.broadcasted_iota(jnp.int32, (rows, rows), 0)
    other = lax.broadcasted_iota(jnp.int32, (rows, rows), 1)
    unit = jnp.where(index == other, 1.0, 0.0).astype(jnp.bfloat16)
    linear = dot_rows(unit, jnp.concatenate([strip(e, (-e) % 4) for e in range(4)], axis=0))
    out[...] = (coef_b * linear + coef_c * total).astype(out.dtype)


def square(z, panel, *others):
    rows = panel.shape[1]
    part = others[1].shape[1]
    vmem = pl.BlockSpec(memory_space=pltpu.VMEM)
    return pl.pallas_call(
        square_kernel,
        out_shape=jax.ShapeDtypeStruct((rows, 4 * part), jnp.bfloat16),
        in_specs=[pl.BlockSpec(memory_space=pltpu.SMEM)] + [vmem] * (1 + len(others)),
        out_specs=vmem,
        compiler_params=pltpu.CompilerParams(vmem_limit_bytes=48 * 2**20),
        cost_estimate=pl.CostEstimate(
            flops=2 * rows * rows * 4 * 4 * part, bytes_accessed=2 * 5 * rows * rows, transcendentals=0
        ),
    )(z.reshape(1).astype(jnp.int32), panel, *others)


def product_kernel(starts, f, x, *rest):
    n_piece = len(starts) - 1
    groups = [rest[g * n_piece : (g + 1) * n_piece] for g in range(6)]
    l1, r3, l2, r2, r1, l3 = groups
    out, wide = rest[6 * n_piece :]
    n_col, part, width = x.shape
    step = pl.program_id(0)
    wide[:, :part, :] = x[...]
    for p in range(n_piece):

        @pl.when(jnp.logical_and(step >= starts[p], step < starts[p + 1]))
        def _(p=p):
            wide[:, part : 2 * part, :] = l1[p][...] + r3[p][...]
            wide[:, 2 * part : 3 * part, :] = l2[p][...] + r2[p][...]
            wide[:, 3 * part :, :] = r1[p][...] + l3[p][...]

    total = coef_a * x[...].reshape(n_col * part, width).astype(jnp.float32)
    for c in range(n_col):
        total = total + jnp.dot(f[c], wide[c], preferred_element_type=jnp.float32)
    out[...] = (math.sqrt(N) * total).astype(out.dtype)


def product(f, x, groups, tile):
    n_col, rows, depth = f.shape
    part = rows // n_col
    columns = x.shape[1]

    def split(value):
        return value.reshape(n_col, part, value.shape[1])

    starts = [0]
    for piece in groups[0]:
        starts.append(starts[-1] + piece.shape[1] // tile)

    def piece_spec(p):
        first, count = starts[p], starts[p + 1] - starts[p]
        return pl.BlockSpec((n_col, part, tile), lambda i: (0, 0, jnp.clip(i - first, 0, count - 1)))

    pieces = [piece_spec(p) for p in range(len(groups[0]))]
    return pl.pallas_call(
        functools.partial(product_kernel, tuple(starts)),
        grid=(columns // tile,),
        out_shape=jax.ShapeDtypeStruct((rows, columns), jnp.bfloat16),
        in_specs=[
            pl.BlockSpec((n_col, rows, depth), lambda i: (0, 0, 0), pipeline_mode=pl.Buffered(1)),
            pl.BlockSpec((n_col, part, tile), lambda i: (0, 0, i)),
        ]
        + pieces * 6,
        out_specs=pl.BlockSpec((rows, tile), lambda i: (0, i)),
        scratch_shapes=[pltpu.VMEM((n_col, depth, tile), jnp.bfloat16)],
        compiler_params=pltpu.CompilerParams(vmem_limit_bytes=56 * 2**20),
        cost_estimate=pl.CostEstimate(
            flops=2 * rows * n_col * depth * columns, bytes_accessed=2 * 12 * rows * columns, transcendentals=0
        ),
    )(f, *(split(value) for value in (x, *(piece for group in groups for piece in group))))


def sum_scatter(value, n_col):
    c = lax.axis_index("col")
    value = value.reshape(n_col, value.shape[0] // n_col, value.shape[1])
    bit = 1
    while bit < n_col:
        here = (c // bit) % 2
        value = value.reshape(-1, 2, *value.shape[1:])
        keep = lax.dynamic_index_in_dim(value, here, axis=1, keepdims=False)
        send = lax.dynamic_index_in_dim(value, 1 - here, axis=1, keepdims=False)
        other = lax.ppermute(send, "col", [(i, i ^ bit) for i in range(n_col)])
        value = (keep.astype(jnp.float32) + other.astype(jnp.float32)).astype(jnp.bfloat16)
        bit *= 2
    return value[0]


def per_device_line(n_col, x):
    z = lax.axis_index("row")
    right, left = [(0, 1), (1, 2), (2, 3)], [(3, 2), (2, 1), (1, 0)]
    unit = 256
    marks = [0, x.shape[1] - 2 * unit, x.shape[1]]

    def send(pieces, pairs):
        return [lax.ppermute(piece, "row", pairs) for piece in pieces]

    def gram_block(one, other):
        total = sum(dot_rows(a, b) for a, b in zip(one, other))
        return total.astype(jnp.bfloat16)

    def scatter(blocks):
        return lax.psum_scatter(jnp.stack(blocks), "col", scatter_dimension=1, tiled=True)

    xs = [x[:, a:b] for a, b in zip(marks, marks[1:])]
    r1, l1 = send(xs, right), send(xs, left)
    r2, l2 = send(r1, right[1:]), send(l1, left[1:])
    r1, l1 = list(r1), list(l1)

    own = scatter([gram_block(xs, xs)])
    own, r1[1], l1[1] = lax.optimization_barrier((own, r1[1], l1[1]))
    first = scatter([gram_block(xs, l1), gram_block(xs, r1), gram_block(r1, l1), gram_block(l1, r1)])
    second = lax.ppermute(first[2], "row", left[1:]) + lax.ppermute(first[3], "row", right[1:])
    tile = jnp.stack([own[0], first[0], second, first[1]])
    tile, r2, l2 = lax.optimization_barrier((tile, r2, l2))
    panel = lax.all_gather(tile, "col", axis=1, tiled=True)
    r3, l3 = send(r2, right[2:]), send(l2, left[2:])

    corner = gram_block(
        [jnp.where(z == 1, a, b) for a, b in zip(r1, l1)], [a + b for a, b in zip(l2, r2)]
    )

    tr1 = lax.ppermute(tile, "row", right)
    tl1 = lax.ppermute(tile, "row", left)
    tr2 = lax.ppermute(tr1, "row", right[1:])
    tl2 = lax.ppermute(tl1, "row", left[1:])
    tr3 = lax.ppermute(tr2, "row", right[2:])
    tl3 = lax.ppermute(tl2, "row", left[2:])

    corner, tr1, tl1 = lax.optimization_barrier((corner, tr1, tl1))
    corner = sum_scatter(corner, n_col)
    end = lax.ppermute(corner, "row", [(1, 0), (2, 3)])
    pair = lax.ppermute(corner, "row", [(1, 2), (2, 1)])
    last = lax.ppermute(pair, "row", [(1, 0), (2, 3)])
    panel, end = lax.optimization_barrier((panel, end))
    far_panel = lax.all_gather(end, "col", axis=0, tiled=True)
    far_panel, r3[0], l3[0] = lax.optimization_barrier((far_panel, r3[0], l3[0]))

    factor = square(z, panel, far_panel, tile, tl1, tr3, tl2, tr2, tr1, tl3, corner, pair, end, last)
    factor = lax.all_gather(factor, "col", axis=0, tiled=False)
    return product(factor, x, [l1, r3, l2, r2, r1, l3], unit)


def solution(mesh):
    n_row, n_col = mesh.shape["row"], mesh.shape["col"]

    def body(iterate):
        if (n_row, n_col) == (4, 8) and iterate.shape == (896, 2304):
            return per_device_line(n_col, iterate)
        return per_device(iterate)

    return jax.shard_map(
        body,
        mesh=mesh,
        in_specs=(P("row", "col"),),
        out_specs=P("row", "col"),
        check_vma=False,
    )
```

time: 573 us -> 528 us (0.921)
  waiting for transfers between devices: 507 us -> 361 us
  starting transfers between devices: 0.16 us -> 46.6 us
  Pallas kernels: 0 us -> 36.6 us
  local copies, waits for them, and re-layouts: 0 us -> 10.6 us
  other arithmetic: 0 us -> 9.29 us
    all_gather x4 -> x3, waiting for transfers between devices: 445 us -> 25.9 us  [the longest x1 25.9 us: per_device_line(): factor = lax.all_gather(factor, 'col', axis=0, tiled=False)]
    ppermute x0 -> x26, waiting for transfers between devices: none -> 275 us  [the longest x12 101 us: send(): return [lax.ppermute(piece, 'row', pairs) for piece in pieces]]
    ppermute x0 -> x26, starting transfers between devices: none -> 46.4 us  [the longest x12 23.6 us: send(): return [lax.ppermute(piece, 'row', pairs) for piece in pieces]]
    pallas_call x0 -> x2, Pallas kernels: none -> 36.6 us  [the longest x1 26.6 us: product(): pl.pallas_call(functools.partial(product_kernel, tuple(starts)), grid=(co...]
    slice x0 -> x3, local copies, waits for them, and re-layouts: none -> 6.36 us  [the longest x2 5.07 us: per_device_line(): xs = [x[:, a:b] for a, b in zip(marks, marks[1:])]]
    dot_general x3 -> x12, matrix products: 52.6 us -> 48.9 us  [dot_rows(): lax.dot_general(left, right, (((1,), (1,)), ((), ())), preferred_element_...]
    reduce_scatter x1 -> x2, waiting for transfers between devices: 60.7 us -> 60.8 us  [scatter(): lax.psum_scatter(jnp.stack(blocks), 'col', scatter_dimension=1, tiled=True)]
  transfers between devices with their start and end apart: 5 -> 31, of which waited for: 5 -> 14; matrix products, arithmetic and copies ran while one was open for 0% -> 5% of each run, Pallas kernels for 0% -> 0%
where the time goes in v2:
time: 528 us; the launch traced here: 527 us
  waiting for transfers between devices  361 us (68%)
  matrix products  48.9 us (9%)
  starting transfers between devices  46.6 us (9%)
  Pallas kernels  36.6 us (7%)
  between operations  13.6 us (3%)
  local copies, waits for them, and re-layouts  10.6 us (2%)
  other arithmetic  9.29 us (2%)
    ppermute x12, waiting for transfers between devices, send(): return [lax.ppermute(piece, 'row', pairs) for piece in pieces]  101 us
    ppermute x1, waiting for transfers between devices, per_device_line(): end = lax.ppermute(corner, 'row', [(1, 0), (2, 3)])  72.2 us
    reduce_scatter x2, waiting for transfers between devices, scatter(): lax.psum_scatter(jnp.stack(blocks), 'col', scatter_dimension=1, tiled=True)  60.8 us
    dot_general x12, matrix products, dot_rows(): lax.dot_general(left, right, (((1,), (1,)), ((), ())), preferred_element_...  48.9 us
    ppermute x1, waiting for transfers between devices, per_device_line(): lax.ppermute(first[2], 'row', left[1:])  33.6 us
    pallas_call x1, Pallas kernels, product(): pl.pallas_call(functools.partial(product_kernel, tuple(starts)), grid=(co...  26.6 us
    all_gather x1, waiting for transfers between devices, per_device_line(): factor = lax.all_gather(factor, 'col', axis=0, tiled=False)  25.9 us
    ppermute x12, starting transfers between devices, send(): return [lax.ppermute(piece, 'row', pairs) for piece in pieces]  23.6 us
  transfers between devices with their start and end apart: 31, of which 14 were waited for; matrix products, arithmetic and copies ran while one was open for 5% of the time, Pallas kernels for 0%

profile of v2, /device:TPU:0, one launch (start us, length us, event | category | flops | bytes accessed | tf_op | source)
XLA Modules:
  0.0 527.1 jit_solution(11024150198975895130)
XLA Ops:
  6.5 6.5 %fusion.24 = f32[896,896]{1,0:T(8,128)S(1)} fusion(bf16[896,2304]{1,0:T(8,128)(2,1)} %param.1), kind=kOutput, calls=%fused_computation.41 | convolution fusion | flops 2877292544 | bytes 6422528 | tf_op jit(solution)/shard_map/dot_general | solution.py:20
  13.0 4.0 fusion.7
  17.1 3.8 slice.18
  22.2 7.3 %collective-permute-start.3 = (bf16[896,1792]{1,0:T(8,128)(2,1)}, bf16[896,1792]{1,0:T(8,128)(2,1)}, u32[]{:S(2)}, u32[]{:S(2)}) collective-permute-start(bf16[896,1792]{1,0:T(8,128)(2,1)} %slice.18), channel_id=1, source_target_pairs={{0,8},{8,16},{16,24},{1,9},{9,17},{17,25},{2,10},{10,18},{18,26},{... | collective-permute-start | bytes 9633800 | tf_op jit(solution)/shard_map/ppermute | solution.py:180
  30.7 2.3 collective-permute-start
  34.6 81.8 %collective-permute-done = bf16[896,512]{1,0:T(8,128)(2,1)S(1)} collective-permute-done((bf16[896,512]{1,0:T(8,128)(2,1)S(1)}, bf16[896,512]{1,0:T(8,128)(2,1)S(1)}, u32[]{:S(2)}, u32[]{:S(2)}) %collective-permute-start) | collective-permute-done | bytes 917536 | tf_op jit(solution)/shard_map/ppermute | solution.py:180
  122.1 6.5 %fusion.8 = bf16[1,896,896]{2,1,0:T(8,128)(2,1)S(1)} fusion(f32[896,896]{1,0:T(8,128)S(1)} %fusion.27, bf16[896,1792]{1,0:T(8,128)(2,1)} %collective-permute-done.3, bf16[896,1792]{1,0:T(8,128)(2,1)} %collective-permute-done.2), kind=kOutput, calls=%fused_computation.16 | convolution fusion | flops 2878898176 | bytes 11239424 | tf_op jit(solution)/shard_map/dot_general | solution.py:20
  128.5 6.5 %fusion.9 = bf16[1,896,896]{2,1,0:T(8,128)(2,1)S(1)} fusion(f32[896,896]{1,0:T(8,128)S(1)} %fusion.28, bf16[896,1792]{1,0:T(8,128)(2,1)} %collective-permute-done.2, bf16[896,1792]{1,0:T(8,128)(2,1)} %collective-permute-done.3), kind=kOutput, calls=%fused_computation.17 | convolution fusion | flops 2878898176 | bytes 11239424 | tf_op jit(solution)/shard_map/dot_general | solution.py:20
  135.0 5.5 %fusion.10 = bf16[1,896,896]{2,1,0:T(8,128)(2,1)S(1)} fusion(f32[896,896]{0,1:T(8,128)S(1)} %fusion.19, bf16[896,1792]{1,0:T(8,128)(2,1)} %collective-permute-done.2, bf16[896,2304]{1,0:T(8,128)(2,1)S(1)} %copy-done.6), kind=kOutput, calls=%fused_computation.18 | convolution fusion | flops 2878898176 | bytes 11239424 | tf_op jit(solution)/shard_map/dot_general | solution.py:20
  140.4 5.7 %fusion.11 = bf16[1,896,896]{2,1,0:T(8,128)(2,1)S(1)} fusion(f32[896,896]{0,1:T(8,128)S(1)} %fusion.17, bf16[896,1792]{1,0:T(8,128)(2,1)} %collective-permute-done.3, bf16[896,2304]{1,0:T(8,128)(2,1)S(1)} %copy-done.6), kind=kOutput, calls=%fused_computation.19 | convolution fusion | flops 2878898176 | bytes 11239424 | tf_op jit(solution)/shard_map/dot_general | solution.py:20
  146.1 3.4 pad_maximum_fusion
  149.6 2.4 collective-permute-start.6
  155.3 60.7 %reduce-scatter.5.cloned.1.call-done = bf16[4,112,896]{2,1,0:T(8,128)(2,1)} async-done(((bf16[4,896,896]{2,1,0:T(8,128)(2,1)}), bf16[4,112,896]{2,1,0:T(8,128)(2,1)}) %reduce-scatter.5.cloned.1.call-update) | async-done | bytes 802832 | tf_op jit(solution)/shard_map/reduce_scatter | solution.py:187
  218.7 33.6 %collective-permute-done.4 = bf16[112,896]{1,0:T(8,128)(2,1)S(1)} collective-permute-done((bf16[112,896]{1,0:T(8,128)(2,1)S(1)}, bf16[112,896]{1,0:T(8,128)(2,1)S(1)}, u32[]{:S(2)}, u32[]{:S(2)}) %collective-permute-start.4) | collective-permute-done | bytes 200736 | tf_op jit(solution)/shard_map/ppermute | solution.py:197
  253.0 1.9 pad_maximum_fusion.1.own
  255.1 7.8 %collective-permute-start.10 = (bf16[4,112,896]{2,1,0:T(8,128)(2,1)}, bf16[4,112,896]{2,1,0:T(8,128)(2,1)S(1)}, u32[]{:S(2)}, u32[]{:S(2)}) collective-permute-start(bf16[4,112,896]{2,1,0:T(8,128)(2,1)} %pad_maximum_fusion.1.own), channel_id=1, source_target_pairs={{0,8},{8,16},{16,24},{1,9},{9,17},{17,25},{2,10},{10,18},{18,26},{... | collective-permute-start | bytes 2408456 | tf_op jit(solution)/shard_map/ppermute | solution.py:207
  264.2 7.4 %fusion.2 = f32[896,896]{1,0:T(8,128)S(1)} fusion(bf16[896,1792]{1,0:T(8,128)(2,1)} %collective-permute-done.8, bf16[896,1792]{1,0:T(8,128)(2,1)} %collective-permute-done.6, bf16[896,1792]{1,0:T(8,128)(2,1)} %collective-permute-done.3, bf16[896,1792]{1,0:T(8,128)(2,1)} %collective-permute-done.2, pred[]{:T(512)S(6)} %eq.8), kind=kOutput, calls=%fused_computation.6 | convolution fusion | flops 2880503808 | bytes 16056321 | tf_op jit(solution)/shard_map/dot_general | solution.py:20
  271.6 2.4 add_convert_fusion
  274.0 3.3 collective-permute-done.10.r1
  277.3 4.5 collective-permute-done.11.l1
  281.9 2.4 collective-permute-done.12
  284.3 1.8 fusion.6
  288.2 19.5 %collective-permute-done.13 = bf16[2,112,896]{2,1,0:T(8,128)(2,1)} collective-permute-done((bf16[2,112,896]{2,1,0:T(8,128)(2,1)}, bf16[2,112,896]{2,1,0:T(8,128)(2,1)}, u32[]{:S(2)}, u32[]{:S(2)}) %collective-permute-start.13) | collective-permute-done | bytes 401440 | tf_op jit(solution)/shard_map/ppermute | solution.py:167
  310.9 2.3 collective-permute-start.16
  317.9 72.2 %collective-permute-done.15.end = bf16[112,896]{1,0:T(8,128)(2,1)S(1)} collective-permute-done((bf16[112,896]{1,0:T(8,128)(2,1)S(1)}, bf16[112,896]{1,0:T(8,128)(2,1)S(1)}, u32[]{:S(2)}, u32[]{:S(2)}) %collective-permute-start.15) | collective-permute-done | bytes 200736 | tf_op jit(solution)/shard_map/ppermute | solution.py:216
  395.3 17.0 %collective-permute-done.20.l2 = bf16[4,112,896]{2,1,0:T(8,128)(2,1)} collective-permute-done((bf16[4,112,896]{2,1,0:T(8,128)(2,1)S(1)}, bf16[4,112,896]{2,1,0:T(8,128)(2,1)}, u32[]{:S(2)}, u32[]{:S(2)}) %collective-permute-start.20) | collective-permute-done | bytes 802848 | tf_op jit(solution)/shard_map/ppermute | solution.py:210
  415.6 18.0 %collective-permute-done.21.l3 = bf16[4,112,896]{2,1,0:T(8,128)(2,1)} collective-permute-done((bf16[4,112,896]{2,1,0:T(8,128)(2,1)}, bf16[4,112,896]{2,1,0:T(8,128)(2,1)}, u32[]{:S(2)}, u32[]{:S(2)}) %collective-permute-start.21) | collective-permute-done | bytes 802848 | tf_op jit(solution)/shard_map/ppermute | solution.py:212
  433.6 2.0 collective-permute-done.23.last
  436.5 10.0 %shard_map.17 = bf16[896,448]{1,0:T(8,128)(2,1)} custom-call(s32[1]{0:T(128)} %bitcast.z_ref, bf16[4,896,896]{2,1,0:T(8,128)(2,1)} %all-gather.5.cloned.1.call-done.panel, bf16[896,896]{1,0:T(8,128)(2,1)} %all-gather.7.cloned.1.call-done.far_panel, bf16[4,112,896]{2,1,0:T(8,128)(2,1)S(1)} %copy-done, bf16[4,112,896]{2,1,0:T(8,128)(2,1)S(1)} %collective-permute-done.11.l1, ...), custom_call_target="tpu_custom_call" | custom-call | flops 2877292544 | bytes 8028160 | tf_op jit(solution)/shard_map/pallas_call | solution.py:89
  448.6 19.4 %collective-permute-done.25 = bf16[896,512]{1,0:T(8,128)(2,1)S(1)} collective-permute-done((bf16[896,512]{1,0:T(8,128)(2,1)}, bf16[896,512]{1,0:T(8,128)(2,1)S(1)}, u32[]{:S(2)}, u32[]{:S(2)}) %collective-permute-start.25) | collective-permute-done | bytes 917536 | tf_op jit(solution)/shard_map/ppermute | solution.py:180
  468.0 25.9 %all-gather.9.cloned.1.call-done = bf16[7168,448]{1,0:T(8,128)(2,1)} async-done(((bf16[896,448]{1,0:T(8,128)(2,1)}), bf16[7168,448]{1,0:T(8,128)(2,1)}) %all-gather.9.cloned.1.call-update) | async-done | bytes 6422544 | tf_op jit(solution)/shard_map/all_gather | solution.py:224
  493.9 26.6 %shard_map.18 = bf16[896,2304]{1,0:T(8,128)(2,1)} custom-call(bf16[8,896,448]{2,1,0:T(8,128)(2,1)} %bitcast.81, bf16[8,112,2304]{2,1,0:T(8,128)(2,1)} %bitcast.75, bf16[8,112,1792]{2,1,0:T(8,128)(2,1)} %bitcast.20.rest_0_, bf16[8,112,512]{2,1,0:T(8,128)(2,1)} %bitcast.74, bf16[8,112,1792]{2,1,0:T(8,128)(2,1)} %bitcast.22.rest_2_, ...), custom_call_target="tpu_custom_call" | custom-call | flops 14797504512 | bytes 49545216 | tf_op jit(solution)/shard_map/pallas_call | solution.py:140
  (85 shorter events, 39.2 us)
Async XLA Ops:
  6.5 109.9 %reduce-scatter.3.cloned.1.call-start = ((), (), s32[]{:S(2)}) async-start(), calls=%async_computation.2 | async-start | bytes 1806336 | tf_op jit(solution)/shard_map/reduce_scatter | solution.py:187
  17.1 199.0 %reduce-scatter.5.cloned.1.call-start = ((), (), s32[]{:S(2)}) async-start(), calls=%async_computation.3 | async-start | bytes 7225344 | tf_op jit(solution)/shard_map/reduce_scatter | solution.py:187
  20.9 101.1 %collective-permute-start.2 = (bf16[896,1792]{1,0:T(8,128)(2,1)}, bf16[896,1792]{1,0:T(8,128)(2,1)}, u32[]{:S(2)}, u32[]{:S(2)}) collective-permute-start(bf16[896,1792]{1,0:T(8,128)(2,1)} %slice.18), channel_id=1, source_target_pairs={{24,16},{16,8},{8,0},{25,17},{17,9},{9,1},{26,18},{18,10},{10,2},{... | collective-permute-start | bytes 9633800 | tf_op jit(solution)/shard_map/ppermute | solution.py:180
  22.2 99.8 %collective-permute-start.3 = (bf16[896,1792]{1,0:T(8,128)(2,1)}, bf16[896,1792]{1,0:T(8,128)(2,1)}, u32[]{:S(2)}, u32[]{:S(2)}) collective-permute-start(bf16[896,1792]{1,0:T(8,128)(2,1)} %slice.18), channel_id=1, source_target_pairs={{0,8},{8,16},{16,24},{1,9},{9,17},{17,25},{2,10},{10,18},{18,26},{... | collective-permute-start | bytes 9633800 | tf_op jit(solution)/shard_map/ppermute | solution.py:180
  30.7 85.7 %collective-permute-start = (bf16[896,512]{1,0:T(8,128)(2,1)S(1)}, bf16[896,512]{1,0:T(8,128)(2,1)S(1)}, u32[]{:S(2)}, u32[]{:S(2)}) collective-permute-start(bf16[896,512]{1,0:T(8,128)(2,1)S(1)} %slice.19), channel_id=1, source_target_pairs={{0,8},{8,16},{16,24},{1,9},{9,17},{17,25},{2,10},{10,18},{18,26},{... | collective-permute-start | bytes 2752520 | tf_op jit(solution)/shard_map/ppermute | solution.py:180
  33.1 83.3 %collective-permute-start.1 = (bf16[896,512]{1,0:T(8,128)(2,1)S(1)}, bf16[896,512]{1,0:T(8,128)(2,1)S(1)}, u32[]{:S(2)}, u32[]{:S(2)}) collective-permute-start(bf16[896,512]{1,0:T(8,128)(2,1)S(1)} %slice.19), channel_id=1, source_target_pairs={{24,16},{16,8},{8,0},{25,17},{17,9},{9,1},{26,18},{18,10},{10,2},{... | collective-permute-start | bytes 2752520 | tf_op jit(solution)/shard_map/ppermute | solution.py:180
  116.4 155.2 %copy-start.3 = (bf16[896,512]{1,0:T(8,128)(2,1)}, bf16[896,512]{1,0:T(8,128)(2,1)S(1)}, u32[]{:S(2)}) copy-start(bf16[896,512]{1,0:T(8,128)(2,1)S(1)} %collective-permute-done) | copy-start | bytes 2752516
  149.6 240.5 %all-gather.5.cloned.1.call-start = ((), (), s32[]{:S(2)}) async-start(), calls=%async_computation.4 | async-start | bytes 7225344 | tf_op jit(solution)/shard_map/all_gather | solution.py:200
  149.6 105.3 %collective-permute-start.6 = (bf16[896,1792]{1,0:T(8,128)(2,1)}, bf16[896,1792]{1,0:T(8,128)(2,1)}, u32[]{:S(2)}, u32[]{:S(2)}) collective-permute-start(bf16[896,1792]{1,0:T(8,128)(2,1)} %collective-permute-done.3), channel_id=1, source_target_pairs={{8,16},{16,24},{9,17},{17,25},{10,18},{18,26},{11,19},{19,27},{12,... | collective-permute-start | bytes 9633800 | tf_op jit(solution)/shard_map/ppermute | solution.py:180
  152.0 103.0 %collective-permute-start.8 = (bf16[896,1792]{1,0:T(8,128)(2,1)}, bf16[896,1792]{1,0:T(8,128)(2,1)}, u32[]{:S(2)}, u32[]{:S(2)}) collective-permute-start(bf16[896,1792]{1,0:T(8,128)(2,1)} %collective-permute-done.2), channel_id=1, source_target_pairs={{16,8},{8,0},{17,9},{9,1},{18,10},{10,2},{19,11},{11,3},{20,12},{1... | collective-permute-start | bytes 9633800 | tf_op jit(solution)/shard_map/ppermute | solution.py:180
  153.3 101.6 %collective-permute-start.7 = (bf16[896,512]{1,0:T(8,128)(2,1)S(1)}, bf16[896,512]{1,0:T(8,128)(2,1)S(1)}, u32[]{:S(2)}, u32[]{:S(2)}) collective-permute-start(bf16[896,512]{1,0:T(8,128)(2,1)S(1)} %collective-permute-done), channel_id=1, source_target_pairs={{8,16},{16,24},{9,17},{17,25},{10,18},{18,26},{11,19},{19,27},{12,... | collective-permute-start | bytes 2752520 | tf_op jit(solution)/shard_map/ppermute | solution.py:180
  154.0 100.9 %collective-permute-start.9 = (bf16[896,512]{1,0:T(8,128)(2,1)S(1)}, bf16[896,512]{1,0:T(8,128)(2,1)}, u32[]{:S(2)}, u32[]{:S(2)}) collective-permute-start(bf16[896,512]{1,0:T(8,128)(2,1)S(1)} %collective-permute-done.1), channel_id=1, source_target_pairs={{16,8},{8,0},{17,9},{9,1},{18,10},{10,2},{19,11},{11,3},{20,12},{1... | collective-permute-start | bytes 2752520 | tf_op jit(solution)/shard_map/ppermute | solution.py:180
  217.4 34.9 %collective-permute-start.4 = (bf16[112,896]{1,0:T(8,128)(2,1)S(1)}, bf16[112,896]{1,0:T(8,128)(2,1)S(1)}, u32[]{:S(2)}, u32[]{:S(2)}) collective-permute-start(bf16[112,896]{1,0:T(8,128)(2,1)S(1)} %get-tuple-element.40), channel_id=1, source_target_pairs={{16,8},{8,0},{17,9},{9,1},{18,10},{10,2},{19,11},{11,3},{20,12},{1... | collective-permute-start | bytes 602120 | tf_op jit(solution)/shard_map/ppermute | solution.py:197
  252.3 0.7 collective-permute-start.5
  255.0 160.6 %all-gather.7.cloned.1.call-start = ((), (), s32[]{:S(2)}) async-start(), calls=%async_computation.5 | async-start | bytes 1806336 | tf_op jit(solution)/shard_map/all_gather | solution.py:220
  255.1 22.2 %collective-permute-start.10 = (bf16[4,112,896]{2,1,0:T(8,128)(2,1)}, bf16[4,112,896]{2,1,0:T(8,128)(2,1)S(1)}, u32[]{:S(2)}, u32[]{:S(2)}) collective-permute-start(bf16[4,112,896]{2,1,0:T(8,128)(2,1)} %pad_maximum_fusion.1.own), channel_id=1, source_target_pairs={{0,8},{8,16},{16,24},{1,9},{9,17},{17,25},{2,10},{10,18},{18,26},{... | collective-permute-start | bytes 2408456 | tf_op jit(solution)/shard_map/ppermute | solution.py:207
  262.9 18.8 %collective-permute-start.11 = (bf16[4,112,896]{2,1,0:T(8,128)(2,1)}, bf16[4,112,896]{2,1,0:T(8,128)(2,1)S(1)}, u32[]{:S(2)}, u32[]{:S(2)}) collective-permute-start(bf16[4,112,896]{2,1,0:T(8,128)(2,1)} %pad_maximum_fusion.1.own), channel_id=1, source_target_pairs={{24,16},{16,8},{8,0},{25,17},{17,9},{9,1},{26,18},{18,10},{10,2},{... | collective-permute-start | bytes 2408456 | tf_op jit(solution)/shard_map/ppermute | solution.py:208
  281.8 2.5 collective-permute-start.12
  286.9 20.7 %collective-permute-start.13 = (bf16[2,112,896]{2,1,0:T(8,128)(2,1)}, bf16[2,112,896]{2,1,0:T(8,128)(2,1)}, u32[]{:S(2)}, u32[]{:S(2)}) collective-permute-start(bf16[2,112,896]{2,1,0:T(8,128)(2,1)} %dynamic-slice_bitcast_fusion.1), channel_id=1, source_target_pairs={{0,2},{1,3},{2,0},{3,1},{4,6},{5,7},{6,4},{7,5},{8,10},{9,11},{10,... | collective-permute-start | bytes 1204232 | tf_op jit(solution)/shard_map/ppermute | solution.py:167
  309.5 6.1 %collective-permute-start.14 = (bf16[1,112,896]{2,1,0:T(8,128)(2,1)S(1)}, bf16[1,112,896]{2,1,0:T(8,128)(2,1)S(1)}, u32[]{:S(2)}, u32[]{:S(2)}) collective-permute-start(bf16[1,112,896]{2,1,0:T(8,128)(2,1)S(1)} %constant_dynamic-slice_fusion), channel_id=1, source_target_pairs={{0,4},{1,5},{2,6},{3,7},{4,0},{5,1},{6,2},{7,3},{8,12},{9,13},{10,... | collective-permute-start | bytes 602120 | tf_op jit(solution)/shard_map/ppermute | solution.py:167
  310.9 104.6 %collective-permute-start.16 = (bf16[896,1792]{1,0:T(8,128)(2,1)}, bf16[896,1792]{1,0:T(8,128)(2,1)}, u32[]{:S(2)}, u32[]{:S(2)}) collective-permute-start(bf16[896,1792]{1,0:T(8,128)(2,1)} %collective-permute-done.6), channel_id=1, source_target_pairs={{16,24},{17,25},{18,26},{19,27},{20,28},{21,29},{22,30},{23,31}} | collective-permute-start | bytes 9633800 | tf_op jit(solution)/shard_map/ppermute | solution.py:180
  313.2 102.3 %collective-permute-start.17 = (bf16[896,1792]{1,0:T(8,128)(2,1)}, bf16[896,1792]{1,0:T(8,128)(2,1)}, u32[]{:S(2)}, u32[]{:S(2)}) collective-permute-start(bf16[896,1792]{1,0:T(8,128)(2,1)} %collective-permute-done.8), channel_id=1, source_target_pairs={{8,0},{9,1},{10,2},{11,3},{12,4},{13,5},{14,6},{15,7}} | collective-permute-start | bytes 9633800 | tf_op jit(solution)/shard_map/ppermute | solution.py:180
  316.6 73.5 %collective-permute-start.15 = (bf16[112,896]{1,0:T(8,128)(2,1)S(1)}, bf16[112,896]{1,0:T(8,128)(2,1)S(1)}, u32[]{:S(2)}, u32[]{:S(2)}) collective-permute-start(bf16[112,896]{1,0:T(8,128)(2,1)S(1)} %fusion.16.corner), channel_id=1, source_target_pairs={{8,0},{16,24},{9,1},{17,25},{10,2},{18,26},{11,3},{19,27},{12,4},{... | collective-permute-start | bytes 602120 | tf_op jit(solution)/shard_map/ppermute | solution.py:216
  390.8 103.2 %all-gather.9.cloned.1.call-start = ((), (), s32[]{:S(2)}) async-start(), calls=%async_computation.6 | async-start | bytes 8257536 | tf_op jit(solution)/shard_map/all_gather | solution.py:224
  390.8 2.9 collective-permute-start.18
  392.4 19.9 %collective-permute-start.20 = (bf16[4,112,896]{2,1,0:T(8,128)(2,1)S(1)}, bf16[4,112,896]{2,1,0:T(8,128)(2,1)}, u32[]{:S(2)}, u32[]{:S(2)}) collective-permute-start(bf16[4,112,896]{2,1,0:T(8,128)(2,1)S(1)} %collective-permute-done.11.l1), channel_id=1, source_target_pairs={{16,8},{8,0},{17,9},{9,1},{18,10},{10,2},{19,11},{11,3},{20,12},{1... | collective-permute-start | bytes 2408456 | tf_op jit(solution)/shard_map/ppermute | solution.py:210
  393.7 21.9 %collective-permute-start.19 = (bf16[4,112,896]{2,1,0:T(8,128)(2,1)}, bf16[4,112,896]{2,1,0:T(8,128)(2,1)}, u32[]{:S(2)}, u32[]{:S(2)}) collective-permute-start(bf16[4,112,896]{2,1,0:T(8,128)(2,1)} %collective-permute-done.18.r2), channel_id=1, source_target_pairs={{16,24},{17,25},{18,26},{19,27},{20,28},{21,29},{22,30},{23,31}} | collective-permute-start | bytes 2408456 | tf_op jit(solution)/shard_map/ppermute | solution.py:211
  412.2 21.3 %collective-permute-start.21 = (bf16[4,112,896]{2,1,0:T(8,128)(2,1)}, bf16[4,112,896]{2,1,0:T(8,128)(2,1)}, u32[]{:S(2)}, u32[]{:S(2)}) collective-permute-start(bf16[4,112,896]{2,1,0:T(8,128)(2,1)} %collective-permute-done.20.l2), channel_id=1, source_target_pairs={{8,0},{9,1},{10,2},{11,3},{12,4},{13,5},{14,6},{15,7}} | collective-permute-start | bytes 2408456 | tf_op jit(solution)/shard_map/ppermute | solution.py:212
  413.5 0.7 collective-permute-start.22
  414.2 21.4 %collective-permute-start.23 = (bf16[112,896]{1,0:T(8,128)(2,1)S(1)}, bf16[112,896]{1,0:T(8,128)(2,1)S(1)}, u32[]{:S(2)}, u32[]{:S(2)}) collective-permute-start(bf16[112,896]{1,0:T(8,128)(2,1)S(1)} %collective-permute-done.22.pair), channel_id=1, source_target_pairs={{8,0},{16,24},{9,1},{17,25},{10,2},{18,26},{11,3},{19,27},{12,4},{... | collective-permute-start | bytes 602120 | tf_op jit(solution)/shard_map/ppermute | solution.py:218
  446.6 2.0 collective-permute-start.24
  447.3 20.7 %collective-permute-start.25 = (bf16[896,512]{1,0:T(8,128)(2,1)}, bf16[896,512]{1,0:T(8,128)(2,1)S(1)}, u32[]{:S(2)}, u32[]{:S(2)}) collective-permute-start(bf16[896,512]{1,0:T(8,128)(2,1)} %collective-permute-done.9), channel_id=1, source_target_pairs={{8,0},{9,1},{10,2},{11,3},{12,4},{13,5},{14,6},{15,7}} | collective-permute-start | bytes 2752520 | tf_op jit(solution)/shard_map/ppermute | solution.py:180
  (11 other events, 308.1 us)
Sparse Core Ops, SparseCore 0:
  17.2 41.4 reduce-scatter.2
  149.7 66.3 reduce-scatter.4
  255.1 59.6 all-gather.4
  390.9 23.0 all-gather.6
  446.7 47.1 all-gather.8

commit v3 on v2

--- a/solution.py
+++ b/solution.py
@@ -98,21 +98,20 @@
     )(z.reshape(1).astype(jnp.int32), panel, *others)
 
 
-def product_kernel(starts, f, x, *rest):
+def product_kernel(starts, f, x, l1, l2, r2, r1, *rest):
     n_piece = len(starts) - 1
-    groups = [rest[g * n_piece : (g + 1) * n_piece] for g in range(6)]
-    l1, r3, l2, r2, r1, l3 = groups
-    out, wide = rest[6 * n_piece :]
+    r3, l3 = rest[:n_piece], rest[n_piece : 2 * n_piece]
+    out, wide = rest[-2:]
     n_col, part, width = x.shape
     step = pl.program_id(0)
     wide[:, :part, :] = x[...]
+    wide[:, 2 * part : 3 * part, :] = l2[...] + r2[...]
     for p in range(n_piece):
 
         @pl.when(jnp.logical_and(step >= starts[p], step < starts[p + 1]))
         def _(p=p):
-            wide[:, part : 2 * part, :] = l1[p][...] + r3[p][...]
-            wide[:, 2 * part : 3 * part, :] = l2[p][...] + r2[p][...]
-            wide[:, 3 * part :, :] = r1[p][...] + l3[p][...]
+            wide[:, part : 2 * part, :] = l1[...] + r3[p][...]
+            wide[:, 3 * part :, :] = r1[...] + l3[p][...]
 
     total = coef_a * x[...].reshape(n_col * part, width).astype(jnp.float32)
     for c in range(n_col):
@@ -120,7 +119,7 @@
     out[...] = (math.sqrt(N) * total).astype(out.dtype)
 
 
-def product(f, x, groups, tile):
+def product(f, x, l1, l2, r2, r1, r3, l3, tile, first, before):
     n_col, rows, depth = f.shape
     part = rows // n_col
     columns = x.shape[1]
@@ -129,37 +128,48 @@
         return value.reshape(n_col, part, value.shape[1])
 
     starts = [0]
-    for piece in groups[0]:
+    for piece in r3:
         starts.append(starts[-1] + piece.shape[1] // tile)
 
     def piece_spec(p):
-        first, count = starts[p], starts[p + 1] - starts[p]
-        return pl.BlockSpec((n_col, part, tile), lambda i: (0, 0, jnp.clip(i - first, 0, count - 1)))
-
-    pieces = [piece_spec(p) for p in range(len(groups[0]))]
+        begin, count = starts[p], starts[p + 1] - starts[p]
+        return pl.BlockSpec((n_col, part, tile), lambda i: (0, 0, jnp.clip(i - begin, 0, count - 1)))
+
+    plain = pl.BlockSpec((n_col, part, tile), lambda i: (0, 0, i + first))
+    pieces = [piece_spec(p) for p in range(len(r3))]
+    operands = [f, *(split(value) for value in (x, l1, l2, r2, r1, *r3, *l3))]
+    in_specs = [
+        pl.BlockSpec((n_col, rows, depth), lambda i: (0, 0, 0), pipeline_mode=pl.Buffered(1))
+    ]
+    in_specs += [plain] * 5 + pieces * 2
+    aliases = {}
+    if before is not None:
+        aliases = {len(operands): 0}
+        operands.append(before)
+        in_specs.append(pl.BlockSpec(memory_space=pl.ANY))
+    share = tile * starts[-1]
     return pl.pallas_call(
         functools.partial(product_kernel, tuple(starts)),
-        grid=(columns // tile,),
+        grid=(starts[-1],),
         out_shape=jax.ShapeDtypeStruct((rows, columns), jnp.bfloat16),
-        in_specs=[
-            pl.BlockSpec((n_col, rows, depth), lambda i: (0, 0, 0), pipeline_mode=pl.Buffered(1)),
-            pl.BlockSpec((n_col, part, tile), lambda i: (0, 0, i)),
-        ]
-        + pieces * 6,
-        out_specs=pl.BlockSpec((rows, tile), lambda i: (0, i)),
+        in_specs=in_specs,
+        out_specs=pl.BlockSpec((rows, tile), lambda i: (0, i + first)),
         scratch_shapes=[pltpu.VMEM((n_col, depth, tile), jnp.bfloat16)],
+        input_output_aliases=aliases,
         compiler_params=pltpu.CompilerParams(vmem_limit_bytes=56 * 2**20),
         cost_estimate=pl.CostEstimate(
-            flops=2 * rows * n_col * depth * columns, bytes_accessed=2 * 12 * rows * columns, transcendentals=0
+            flops=2 * rows * n_col * depth * share, bytes_accessed=2 * 12 * rows * share, transcendentals=0
         ),
-    )(f, *(split(value) for value in (x, *(piece for group in groups for piece in group))))
-
-
-def sum_scatter(value, n_col):
+    )(*operands)
+
+
+def sum_scatter(value, n_col, fence):
     c = lax.axis_index("col")
     value = value.reshape(n_col, value.shape[0] // n_col, value.shape[1])
     bit = 1
     while bit < n_col:
+        if 2 * bit == n_col:
+            value, *fence = lax.optimization_barrier((value, *fence))
         here = (c // bit) % 2
         value = value.reshape(-1, 2, *value.shape[1:])
         keep = lax.dynamic_index_in_dim(value, here, axis=1, keepdims=False)
@@ -167,62 +177,66 @@
         other = lax.ppermute(send, "col", [(i, i ^ bit) for i in range(n_col)])
         value = (keep.astype(jnp.float32) + other.astype(jnp.float32)).astype(jnp.bfloat16)
         bit *= 2
-    return value[0]
+    return value[0], fence
 
 
 def per_device_line(n_col, x):
     z = lax.axis_index("row")
     right, left = [(0, 1), (1, 2), (2, 3)], [(3, 2), (2, 1), (1, 0)]
-    unit = 256
-    marks = [0, x.shape[1] - 2 * unit, x.shape[1]]
-
-    def send(pieces, pairs):
-        return [lax.ppermute(piece, "row", pairs) for piece in pieces]
 
     def gram_block(one, other):
-        total = sum(dot_rows(a, b) for a, b in zip(one, other))
-        return total.astype(jnp.bfloat16)
+        return dot_rows(one, other).astype(jnp.bfloat16)
 
     def scatter(blocks):
         return lax.psum_scatter(jnp.stack(blocks), "col", scatter_dimension=1, tiled=True)
 
-    xs = [x[:, a:b] for a, b in zip(marks, marks[1:])]
-    r1, l1 = send(xs, right), send(xs, left)
-    r2, l2 = send(r1, right[1:]), send(l1, left[1:])
-    r1, l1 = list(r1), list(l1)
-
-    own = scatter([gram_block(xs, xs)])
-    own, r1[1], l1[1] = lax.optimization_barrier((own, r1[1], l1[1]))
-    first = scatter([gram_block(xs, l1), gram_block(xs, r1), gram_block(r1, l1), gram_block(l1, r1)])
+    r1 = lax.ppermute(x, "row", right)
+    l1 = lax.ppermute(x, "row", left)
+    r2 = lax.ppermute(r1, "row", right[1:])
+    l2 = lax.ppermute(l1, "row", left[1:])
+
+    own = scatter([gram_block(x, x)])
+    own, near_r, near_l = lax.optimization_barrier((own, r1, l1))
+    first = scatter(
+        [
+            gram_block(x, near_l),
+            gram_block(x, near_r),
+            gram_block(near_r, near_l),
+            gram_block(near_l, near_r),
+        ]
+    )
     second = lax.ppermute(first[2], "row", left[1:]) + lax.ppermute(first[3], "row", right[1:])
     tile = jnp.stack([own[0], first[0], second, first[1]])
-    tile, r2, l2 = lax.optimization_barrier((tile, r2, l2))
+
+    corner = gram_block(jnp.where(z == 1, r1, l1), l2 + r2)
+    corner, tile = lax.optimization_barrier((corner, tile))
+
     panel = lax.all_gather(tile, "col", axis=1, tiled=True)
-    r3, l3 = send(r2, right[2:]), send(l2, left[2:])
-
-    corner = gram_block(
-        [jnp.where(z == 1, a, b) for a, b in zip(r1, l1)], [a + b for a, b in zip(l2, r2)]
-    )
-
     tr1 = lax.ppermute(tile, "row", right)
     tl1 = lax.ppermute(tile, "row", left)
+    corner, (tr1, tl1) = sum_scatter(corner, n_col, [tr1, tl1])
     tr2 = lax.ppermute(tr1, "row", right[1:])
     tl2 = lax.ppermute(tl1, "row", left[1:])
+    end = lax.ppermute(corner, "row", [(1, 0), (2, 3)])
+    pair = lax.ppermute(corner, "row", [(1, 2), (2, 1)])
+    end, pair, tr2, tl2, last_r, last_l = lax.optimization_barrier((end, pair, tr2, tl2, r2, l2))
+    last = lax.ppermute(pair, "row", [(1, 0), (2, 3)])
     tr3 = lax.ppermute(tr2, "row", right[2:])
     tl3 = lax.ppermute(tl2, "row", left[2:])
-
-    corner, tr1, tl1 = lax.optimization_barrier((corner, tr1, tl1))
-    corner = sum_scatter(corner, n_col)
-    end = lax.ppermute(corner, "row", [(1, 0), (2, 3)])
-    pair = lax.ppermute(corner, "row", [(1, 2), (2, 1)])
-    last = lax.ppermute(pair, "row", [(1, 0), (2, 3)])
-    panel, end = lax.optimization_barrier((panel, end))
+    end, panel = lax.optimization_barrier((end, panel))
     far_panel = lax.all_gather(end, "col", axis=0, tiled=True)
+
+    unit = 256
+    marks = [0, 2 * unit, 5 * unit, x.shape[1]]
+    pieces = [slice(a, b) for a, b in zip(marks, marks[1:])]
+    r3 = [lax.ppermute(last_r[:, piece], "row", right[2:]) for piece in pieces]
+    l3 = [lax.ppermute(last_l[:, piece], "row", left[2:]) for piece in pieces]
     far_panel, r3[0], l3[0] = lax.optimization_barrier((far_panel, r3[0], l3[0]))
 
     factor = square(z, panel, far_panel, tile, tl1, tr3, tl2, tr2, tr1, tl3, corner, pair, end, last)
     factor = lax.all_gather(factor, "col", axis=0, tiled=False)
-    return product(factor, x, [l1, r3, l2, r2, r1, l3], unit)
+    out = product(factor, x, l1, l2, r2, r1, r3[:2], l3[:2], unit, 0, None)
+    return product(factor, x, l1, l2, r2, r1, r3[2:], l3[2:], unit, marks[2] // unit, out)
 
 
 def solution(mesh):

time: 528 us -> 456 us (0.86)
  waiting for transfers between devices: 361 us -> 282 us
    ppermute x1, waiting for transfers between devices: 72.2 us -> 16.1 us  [per_device_line(): end = lax.ppermute(corner, 'row', [(1, 0), (2, 3)])]
    reduce_scatter x2, waiting for transfers between devices: 60.8 us -> 102 us  [scatter(): lax.psum_scatter(jnp.stack(blocks), 'col', scatter_dimension=1, tiled=True)]
    ppermute x1, waiting for transfers between devices: 33.6 us -> 0.01 us  [per_device_line(): lax.ppermute(first[2], 'row', left[1:])]
    ppermute x1, waiting for transfers between devices: 18 us -> 0.01 us  [per_device_line(): tl3 = lax.ppermute(tl2, 'row', left[2:])]
    ppermute x1, waiting for transfers between devices: 17 us -> 0.01 us  [per_device_line(): tl2 = lax.ppermute(tl1, 'row', left[1:])]
    ppermute x1, waiting for transfers between devices: 2.04 us -> 16 us  [per_device_line(): last = lax.ppermute(pair, 'row', [(1, 0), (2, 3)])]
    all_gather x1, waiting for transfers between devices: 25.9 us -> 12.3 us  [per_device_line(): factor = lax.all_gather(factor, 'col', axis=0, tiled=False)]
    ppermute x12 -> x10, waiting for transfers between devices: 101 us -> 109 us  [the longest x3 46.3 us: per_device_line(): l3 = [lax.ppermute(last_l[:, piece], 'row', left[2:]) for piece in pieces]]
  transfers between devices with their start and end apart: 31 -> 29, of which waited for: 14 -> 13; matrix products, arithmetic and copies ran while one was open for 5% -> 8% of each run, Pallas kernels for 0% -> 4%
where the time goes in v3:
time: 456 us; the launch traced here: 455 us
  waiting for transfers between devices  282 us (62%)
  matrix products  47.2 us (10%)
  starting transfers between devices  46 us (10%)
  Pallas kernels  41.8 us (9%)
  local copies, waits for them, and re-layouts  15.8 us (3%)
  between operations  13.6 us (3%)
  other arithmetic  9.05 us (2%)
    reduce_scatter x2, waiting for transfers between devices, scatter(): lax.psum_scatter(jnp.stack(blocks), 'col', scatter_dimension=1, tiled=True)  102 us
    dot_general x6, matrix products, dot_rows(): lax.dot_general(left, right, (((1,), (1,)), ((), ())), preferred_element_...  47.2 us
    ppermute x3, waiting for transfers between devices, per_device_line(): l3 = [lax.ppermute(last_l[:, piece], 'row', left[2:]) for piece in pieces]  46.3 us
    ppermute x1, waiting for transfers between devices, per_device_line(): l1 = lax.ppermute(x, 'row', left)  36.9 us
    pallas_call x2, Pallas kernels, product(): pl.pallas_call(functools.partial(product_kernel, tuple(starts)), grid=(st...  31.8 us
    ppermute x3, waiting for transfers between devices, sum_scatter(): other = lax.ppermute(send, 'col', [(i, i ^ bit) for i in range(n_col)])  26.2 us
    ppermute x1, waiting for transfers between devices, per_device_line(): l2 = lax.ppermute(l1, 'row', left[1:])  24.3 us
    ppermute x1, waiting for transfers between devices, per_device_line(): end = lax.ppermute(corner, 'row', [(1, 0), (2, 3)])  16.1 us
  transfers between devices with their start and end apart: 29, of which 13 were waited for; matrix products, arithmetic and copies ran while one was open for 8% of the time, Pallas kernels for 4%

profile of v3, /device:TPU:0, one launch (start us, length us, event | category | flops | bytes accessed | tf_op | source)
XLA Modules:
  0.0 455.3 jit_solution(9629911105978008505)
XLA Ops:
  7.8 7.5 %collective-permute-start = (bf16[896,2304]{1,0:T(8,128)(2,1)}, bf16[896,2304]{1,0:T(8,128)(2,1)}, u32[]{:S(2)}, u32[]{:S(2)}) collective-permute-start(bf16[896,2304]{1,0:T(8,128)(2,1)} %param.1), channel_id=1, source_target_pairs={{0,8},{8,16},{16,24},{1,9},{9,17},{17,25},{2,10},{10,18},{18,26},{... | collective-permute-start | bytes 12386312 | tf_op jit(solution)/shard_map/ppermute | solution.py:193
  15.3 9.0 %fusion.10 = bf16[1,896,896]{2,1,0:T(8,128)(2,1)} fusion(bf16[896,2304]{1,0:T(8,128)(2,1)} %param.1), kind=kOutput, calls=%fused_computation.13 | convolution fusion | flops 3700178944 | bytes 5734400 | tf_op jit(solution)/shard_map/dot_general | solution.py:20
  24.6 39.4 %reduce-scatter.3.cloned.1.call-done = bf16[1,112,896]{2,1,0:T(8,128)(2,1)} async-done(((bf16[1,896,896]{2,1,0:T(8,128)(2,1)}), bf16[1,112,896]{2,1,0:T(8,128)(2,1)}) %reduce-scatter.3.cloned.1.call-update) | async-done | bytes 200720 | tf_op jit(solution)/shard_map/reduce_scatter | solution.py:191
  64.0 36.9 %collective-permute-done.1 = bf16[896,2304]{1,0:T(8,128)(2,1)} collective-permute-done((bf16[896,2304]{1,0:T(8,128)(2,1)}, bf16[896,2304]{1,0:T(8,128)(2,1)}, u32[]{:S(2)}, u32[]{:S(2)}) %collective-permute-start.1) | collective-permute-done | bytes 4128800 | tf_op jit(solution)/shard_map/ppermute | solution.py:194
  102.1 7.9 %fusion.14 = bf16[1,896,896]{2,1,0:T(8,128)(2,1)S(1)} fusion(bf16[896,2304]{1,0:T(8,128)(2,1)} %collective-permute-done.1, bf16[896,2304]{1,0:T(8,128)(2,1)} %collective-permute-done), kind=kOutput, calls=%fused_computation.17 | convolution fusion | flops 3700178944 | bytes 9863168 | tf_op jit(solution)/shard_map/dot_general | solution.py:20
  110.0 8.0 %fusion.13 = bf16[1,896,896]{2,1,0:T(8,128)(2,1)S(1)} fusion(bf16[896,2304]{1,0:T(8,128)(2,1)} %collective-permute-done, bf16[896,2304]{1,0:T(8,128)(2,1)} %collective-permute-done.1), kind=kOutput, calls=%fused_computation.16 | convolution fusion | flops 3700178944 | bytes 9863168 | tf_op jit(solution)/shard_map/dot_general | solution.py:20
  118.0 6.6 %fusion.11 = bf16[1,896,896]{2,1,0:T(8,128)(2,1)S(1)} fusion(bf16[896,2304]{1,0:T(8,128)(2,1)} %collective-permute-done.1, bf16[896,2304]{1,0:T(8,128)(2,1)S(1)} %copy-done.3), kind=kOutput, calls=%fused_computation.14 | convolution fusion | flops 3700178944 | bytes 9863168 | tf_op jit(solution)/shard_map/dot_general | solution.py:20
  124.6 6.6 %fusion.12 = bf16[1,896,896]{2,1,0:T(8,128)(2,1)S(1)} fusion(bf16[896,2304]{1,0:T(8,128)(2,1)} %collective-permute-done, bf16[896,2304]{1,0:T(8,128)(2,1)S(1)} %copy-done.3), kind=kOutput, calls=%fused_computation.15 | convolution fusion | flops 3700178944 | bytes 9863168 | tf_op jit(solution)/shard_map/dot_general | solution.py:20
  131.3 3.4 pad_maximum_fusion
  136.1 2.6 collective-permute-start.3
  138.7 62.9 %reduce-scatter.5.cloned.1.call-done = bf16[4,112,896]{2,1,0:T(8,128)(2,1)} async-done(((bf16[4,896,896]{2,1,0:T(8,128)(2,1)}), bf16[4,112,896]{2,1,0:T(8,128)(2,1)}) %reduce-scatter.5.cloned.1.call-update) | async-done | bytes 802832 | tf_op jit(solution)/shard_map/reduce_scatter | solution.py:191
  203.6 1.6 collective-permute-start.4
  205.2 24.3 %collective-permute-done.2 = bf16[896,2304]{1,0:T(8,128)(2,1)} collective-permute-done((bf16[896,2304]{1,0:T(8,128)(2,1)}, bf16[896,2304]{1,0:T(8,128)(2,1)}, u32[]{:S(2)}, u32[]{:S(2)}) %collective-permute-start.2) | collective-permute-done | bytes 4128800 | tf_op jit(solution)/shard_map/ppermute | solution.py:196
  229.6 9.1 %fusion.4 = bf16[896,896]{1,0:T(8,128)(2,1)S(1)} fusion(bf16[896,2304]{1,0:T(8,128)(2,1)} %collective-permute-done.2, bf16[896,2304]{1,0:T(8,128)(2,1)} %collective-permute-done.3, bf16[896,2304]{1,0:T(8,128)(2,1)} %collective-permute-done, bf16[896,2304]{1,0:T(8,128)(2,1)} %collective-permute-done.1, pred[]{:T(512)S(6)} %eq.7), kind=kOutput, calls=%fused_computation.5 | convolution fusion | flops 3704307712 | bytes 18120704 | tf_op jit(solution)/shard_map/dot_general | solution.py:20
  241.6 7.9 %collective-permute-start.8 = (bf16[4,112,896]{2,1,0:T(8,128)(2,1)}, bf16[4,112,896]{2,1,0:T(8,128)(2,1)S(1)}, u32[]{:S(2)}, u32[]{:S(2)}) collective-permute-start(bf16[4,112,896]{2,1,0:T(8,128)(2,1)} %pad_maximum_fusion.1.own), channel_id=1, source_target_pairs={{0,8},{8,16},{16,24},{1,9},{9,17},{17,25},{2,10},{10,18},{18,26},{... | collective-permute-start | bytes 2408456 | tf_op jit(solution)/shard_map/ppermute | solution.py:215
  253.4 17.9 %collective-permute-done.7 = bf16[2,112,896]{2,1,0:T(8,128)(2,1)} collective-permute-done((bf16[2,112,896]{2,1,0:T(8,128)(2,1)}, bf16[2,112,896]{2,1,0:T(8,128)(2,1)}, u32[]{:S(2)}, u32[]{:S(2)}) %collective-permute-start.7) | collective-permute-done | bytes 401440 | tf_op jit(solution)/shard_map/ppermute | solution.py:177
  271.4 1.8 fusion.15
  277.0 1.6 collective-permute-start.10
  278.7 8.3 %collective-permute-done.10 = bf16[1,112,896]{2,1,0:T(8,128)(2,1)S(1)} collective-permute-done((bf16[1,112,896]{2,1,0:T(8,128)(2,1)S(1)}, bf16[1,112,896]{2,1,0:T(8,128)(2,1)S(1)}, u32[]{:S(2)}, u32[]{:S(2)}) %collective-permute-start.10) | collective-permute-done | bytes 200736 | tf_op jit(solution)/shard_map/ppermute | solution.py:177
  289.9 16.1 %collective-permute-done.11.end = bf16[112,896]{1,0:T(8,128)(2,1)S(1)} collective-permute-done((bf16[112,896]{1,0:T(8,128)(2,1)S(1)}, bf16[112,896]{1,0:T(8,128)(2,1)S(1)}, u32[]{:S(2)}, u32[]{:S(2)}) %collective-permute-start.11) | collective-permute-done | bytes 200736 | tf_op jit(solution)/shard_map/ppermute | solution.py:220
  316.4 18.1 %collective-permute-done.16 = bf16[896,512]{1,0:T(8,128)(2,1)S(1)} collective-permute-done((bf16[896,512]{1,0:T(8,128)(2,1)S(1)}, bf16[896,512]{1,0:T(8,128)(2,1)S(1)}, u32[]{:S(2)}, u32[]{:S(2)}) %collective-permute-start.16) | collective-permute-done | bytes 917536 | tf_op jit(solution)/shard_map/ppermute | solution.py:233
  335.4 16.0 %collective-permute-done.19.last = bf16[112,896]{1,0:T(8,128)(2,1)S(1)} collective-permute-done((bf16[112,896]{1,0:T(8,128)(2,1)S(1)}, bf16[112,896]{1,0:T(8,128)(2,1)S(1)}, u32[]{:S(2)}, u32[]{:S(2)}) %collective-permute-start.19) | collective-permute-done | bytes 200736 | tf_op jit(solution)/shard_map/ppermute | solution.py:223
  352.4 10.0 %shard_map.17 = bf16[896,448]{1,0:T(8,128)(2,1)} custom-call(s32[1]{0:T(128)} %bitcast.z_ref, bf16[4,896,896]{2,1,0:T(8,128)(2,1)} %all-gather.5.cloned.1.call-done.panel, bf16[896,896]{1,0:T(8,128)(2,1)} %all-gather.7.cloned.1.call-done.far_panel, bf16[4,112,896]{2,1,0:T(8,128)(2,1)S(1)} %copy-done, bf16[4,112,896]{2,1,0:T(8,128)(2,1)S(1)} %collective-permute-done.9.l1, ...), custom_call_target="tpu_custom_call" | custom-call | flops 2877292544 | bytes 8028160 | tf_op jit(solution)/shard_map/pallas_call | solution.py:89
  366.6 1.7 collective-permute-start.22
  368.3 1.8 slice.36
  370.2 3.0 slice.37
  374.5 2.0 collective-permute-start.20
  376.5 23.8 %collective-permute-done.23 = bf16[896,768]{1,0:T(8,128)(2,1)S(1)} collective-permute-done((bf16[896,768]{1,0:T(8,128)(2,1)S(1)}, bf16[896,768]{1,0:T(8,128)(2,1)S(1)}, u32[]{:S(2)}, u32[]{:S(2)}) %collective-permute-start.23) | collective-permute-done | bytes 1376288 | tf_op jit(solution)/shard_map/ppermute | solution.py:233
  400.3 12.3 %all-gather.9.cloned.1.call-done = bf16[7168,448]{1,0:T(8,128)(2,1)} async-done(((bf16[896,448]{1,0:T(8,128)(2,1)}), bf16[7168,448]{1,0:T(8,128)(2,1)}) %all-gather.9.cloned.1.call-update) | async-done | bytes 6422544 | tf_op jit(solution)/shard_map/all_gather | solution.py:237
  412.6 17.4 %shard_map.18.rest_2_ = bf16[896,2304]{1,0:T(8,128)(2,1)} custom-call(bf16[8,896,448]{2,1,0:T(8,128)(2,1)} %bitcast.61, bf16[8,112,2304]{2,1,0:T(8,128)(2,1)} %bitcast.63, bf16[8,112,2304]{2,1,0:T(8,128)(2,1)} %bitcast.20.l1, bf16[8,112,2304]{2,1,0:T(8,128)(2,1)} %bitcast.21.l2, bf16[8,112,2304]{2,1,0:T(8,128)(2,1)} %bitcast.22.r2, ...), custom_call_target="tpu_custom_call" | custom-call | flops 8220835840 | bytes 27525120 | tf_op jit(solution)/shard_map/pallas_call | solution.py:151
  430.0 4.4 collective-permute-done.21
  434.4 14.4 %shard_map.19 = bf16[896,2304]{1,0:T(8,128)(2,1)} custom-call(bf16[8,896,448]{2,1,0:T(8,128)(2,1)} %bitcast.62, bf16[8,112,2304]{2,1,0:T(8,128)(2,1)} %bitcast.64, bf16[8,112,2304]{2,1,0:T(8,128)(2,1)} %bitcast.20.l1, bf16[8,112,2304]{2,1,0:T(8,128)(2,1)} %bitcast.21.l2, bf16[8,112,2304]{2,1,0:T(8,128)(2,1)} %bitcast.22.r2, ...), custom_call_target="tpu_custom_call", output_to_operand_aliasing={{}: (8, {})} | custom-call | flops 6576668672 | bytes 22020096 | tf_op jit(solution)/shard_map/pallas_call | solution.py:151
  (72 shorter events, 37.1 us)
Async XLA Ops:
  6.5 57.5 %reduce-scatter.3.cloned.1.call-start = ((), (), s32[]{:S(2)}) async-start(), calls=%async_computation.2 | async-start | bytes 1806336 | tf_op jit(solution)/shard_map/reduce_scatter | solution.py:191
  6.5 94.4 %collective-permute-start.1 = (bf16[896,2304]{1,0:T(8,128)(2,1)}, bf16[896,2304]{1,0:T(8,128)(2,1)}, u32[]{:S(2)}, u32[]{:S(2)}) collective-permute-start(bf16[896,2304]{1,0:T(8,128)(2,1)} %param.1), channel_id=1, source_target_pairs={{24,16},{16,8},{8,0},{25,17},{17,9},{9,1},{26,18},{18,10},{10,2},{... | collective-permute-start | bytes 12386312 | tf_op jit(solution)/shard_map/ppermute | solution.py:194
  7.8 94.3 %collective-permute-start = (bf16[896,2304]{1,0:T(8,128)(2,1)}, bf16[896,2304]{1,0:T(8,128)(2,1)}, u32[]{:S(2)}, u32[]{:S(2)}) collective-permute-start(bf16[896,2304]{1,0:T(8,128)(2,1)} %param.1), channel_id=1, source_target_pairs={{0,8},{8,16},{16,24},{1,9},{9,17},{17,25},{2,10},{10,18},{18,26},{... | collective-permute-start | bytes 12386312 | tf_op jit(solution)/shard_map/ppermute | solution.py:193
  24.4 177.2 %reduce-scatter.5.cloned.1.call-start = ((), (), s32[]{:S(2)}) async-start(), calls=%async_computation.3 | async-start | bytes 7225344 | tf_op jit(solution)/shard_map/reduce_scatter | solution.py:191
  134.7 171.4 %all-gather.5.cloned.1.call-start = ((), (), s32[]{:S(2)}) async-start(), calls=%async_computation.4 | async-start | bytes 7225344 | tf_op jit(solution)/shard_map/all_gather | solution.py:214
  134.8 94.8 %collective-permute-start.2 = (bf16[896,2304]{1,0:T(8,128)(2,1)}, bf16[896,2304]{1,0:T(8,128)(2,1)}, u32[]{:S(2)}, u32[]{:S(2)}) collective-permute-start(bf16[896,2304]{1,0:T(8,128)(2,1)} %collective-permute-done.1), channel_id=1, source_target_pairs={{16,8},{8,0},{17,9},{9,1},{18,10},{10,2},{19,11},{11,3},{20,12},{1... | collective-permute-start | bytes 12386312 | tf_op jit(solution)/shard_map/ppermute | solution.py:196
  136.1 93.5 %collective-permute-start.3 = (bf16[896,2304]{1,0:T(8,128)(2,1)}, bf16[896,2304]{1,0:T(8,128)(2,1)}, u32[]{:S(2)}, u32[]{:S(2)}) collective-permute-start(bf16[896,2304]{1,0:T(8,128)(2,1)} %collective-permute-done), channel_id=1, source_target_pairs={{8,16},{16,24},{9,17},{17,25},{10,18},{18,26},{11,19},{19,27},{12,... | collective-permute-start | bytes 12386312 | tf_op jit(solution)/shard_map/ppermute | solution.py:195
  202.9 35.8 %collective-permute-start.5 = (bf16[112,896]{1,0:T(8,128)(2,1)S(1)}, bf16[112,896]{1,0:T(8,128)(2,1)S(1)}, u32[]{:S(2)}, u32[]{:S(2)}) collective-permute-start(bf16[112,896]{1,0:T(8,128)(2,1)S(1)} %get-tuple-element.45), channel_id=1, source_target_pairs={{8,16},{16,24},{9,17},{17,25},{10,18},{18,26},{11,19},{19,27},{12,... | collective-permute-start | bytes 602120 | tf_op jit(solution)/shard_map/ppermute | solution.py:208
  203.6 35.1 %copy-start.7 = (bf16[1,112,896]{2,1,0:T(8,128)(2,1)S(1)}, bf16[1,112,896]{2,1,0:T(8,128)(2,1)}, u32[]{:S(2)}) copy-start(bf16[1,112,896]{2,1,0:T(8,128)(2,1)} %reduce-scatter.3.cloned.1.call-done) | copy-start | bytes 602116
  203.6 35.1 %collective-permute-start.4 = (bf16[112,896]{1,0:T(8,128)(2,1)S(1)}, bf16[112,896]{1,0:T(8,128)(2,1)S(1)}, u32[]{:S(2)}, u32[]{:S(2)}) collective-permute-start(bf16[112,896]{1,0:T(8,128)(2,1)S(1)} %get-tuple-element.46), channel_id=1, source_target_pairs={{16,8},{8,0},{17,9},{9,1},{18,10},{10,2},{19,11},{11,3},{20,12},{1... | collective-permute-start | bytes 602120 | tf_op jit(solution)/shard_map/ppermute | solution.py:208
  239.9 95.5 %all-gather.7.cloned.1.call-start = ((), (), s32[]{:S(2)}) async-start(), calls=%async_computation.5 | async-start | bytes 1806336 | tf_op jit(solution)/shard_map/all_gather | solution.py:227
  240.1 9.5 %collective-permute-start.6 = (bf16[4,112,896]{2,1,0:T(8,128)(2,1)S(1)}, bf16[4,112,896]{2,1,0:T(8,128)(2,1)}, u32[]{:S(2)}, u32[]{:S(2)}) collective-permute-start(bf16[4,112,896]{2,1,0:T(8,128)(2,1)S(1)} %dynamic-slice_bitcast_fusion), channel_id=1, source_target_pairs={{0,1},{1,0},{2,3},{3,2},{4,5},{5,4},{6,7},{7,6},{8,9},{9,8},{10,11... | collective-permute-start | bytes 2408456 | tf_op jit(solution)/shard_map/ppermute | solution.py:177
  240.2 111.2 %copy-start = (bf16[4,112,896]{2,1,0:T(8,128)(2,1)S(1)}, bf16[4,112,896]{2,1,0:T(8,128)(2,1)}, u32[]{:S(2)}) copy-start(bf16[4,112,896]{2,1,0:T(8,128)(2,1)} %pad_maximum_fusion.1.own) | copy-start | bytes 2408452
  240.2 33.0 %collective-permute-start.9 = (bf16[4,112,896]{2,1,0:T(8,128)(2,1)}, bf16[4,112,896]{2,1,0:T(8,128)(2,1)S(1)}, u32[]{:S(2)}, u32[]{:S(2)}) collective-permute-start(bf16[4,112,896]{2,1,0:T(8,128)(2,1)} %pad_maximum_fusion.1.own), channel_id=1, source_target_pairs={{24,16},{16,8},{8,0},{25,17},{17,9},{9,1},{26,18},{18,10},{10,2},{... | collective-permute-start | bytes 2408456 | tf_op jit(solution)/shard_map/ppermute | solution.py:216
  241.6 31.6 %collective-permute-start.8 = (bf16[4,112,896]{2,1,0:T(8,128)(2,1)}, bf16[4,112,896]{2,1,0:T(8,128)(2,1)S(1)}, u32[]{:S(2)}, u32[]{:S(2)}) collective-permute-start(bf16[4,112,896]{2,1,0:T(8,128)(2,1)} %pad_maximum_fusion.1.own), channel_id=1, source_target_pairs={{0,8},{8,16},{16,24},{1,9},{9,17},{17,25},{2,10},{10,18},{18,26},{... | collective-permute-start | bytes 2408456 | tf_op jit(solution)/shard_map/ppermute | solution.py:215
  251.9 19.4 %collective-permute-start.7 = (bf16[2,112,896]{2,1,0:T(8,128)(2,1)}, bf16[2,112,896]{2,1,0:T(8,128)(2,1)}, u32[]{:S(2)}, u32[]{:S(2)}) collective-permute-start(bf16[2,112,896]{2,1,0:T(8,128)(2,1)} %dynamic-slice_bitcast_fusion.1), channel_id=1, source_target_pairs={{0,2},{1,3},{2,0},{3,1},{4,6},{5,7},{6,4},{7,5},{8,10},{9,11},{10,... | collective-permute-start | bytes 1204232 | tf_op jit(solution)/shard_map/ppermute | solution.py:177
  273.2 32.9 %collective-permute-start.13 = (bf16[4,112,896]{2,1,0:T(8,128)(2,1)S(1)}, bf16[4,112,896]{2,1,0:T(8,128)(2,1)}, u32[]{:S(2)}, u32[]{:S(2)}) collective-permute-start(bf16[4,112,896]{2,1,0:T(8,128)(2,1)S(1)} %collective-permute-done.8.r1), channel_id=1, source_target_pairs={{8,16},{16,24},{9,17},{17,25},{10,18},{18,26},{11,19},{19,27},{12,... | collective-permute-start | bytes 2408456 | tf_op jit(solution)/shard_map/ppermute | solution.py:218
  274.8 31.3 %collective-permute-start.14 = (bf16[4,112,896]{2,1,0:T(8,128)(2,1)S(1)}, bf16[4,112,896]{2,1,0:T(8,128)(2,1)}, u32[]{:S(2)}, u32[]{:S(2)}) collective-permute-start(bf16[4,112,896]{2,1,0:T(8,128)(2,1)S(1)} %collective-permute-done.9.l1), channel_id=1, source_target_pairs={{16,8},{8,0},{17,9},{9,1},{18,10},{10,2},{19,11},{11,3},{20,12},{1... | collective-permute-start | bytes 2408456 | tf_op jit(solution)/shard_map/ppermute | solution.py:219
  277.0 9.9 %collective-permute-start.10 = (bf16[1,112,896]{2,1,0:T(8,128)(2,1)S(1)}, bf16[1,112,896]{2,1,0:T(8,128)(2,1)S(1)}, u32[]{:S(2)}, u32[]{:S(2)}) collective-permute-start(bf16[1,112,896]{2,1,0:T(8,128)(2,1)S(1)} %constant_dynamic-slice_fusion), channel_id=1, source_target_pairs={{0,4},{1,5},{2,6},{3,7},{4,0},{5,1},{6,2},{7,3},{8,12},{9,13},{10,... | collective-permute-start | bytes 602120 | tf_op jit(solution)/shard_map/ppermute | solution.py:177
  287.9 2.0 collective-permute-start.12
  288.6 17.4 %collective-permute-start.11 = (bf16[112,896]{1,0:T(8,128)(2,1)S(1)}, bf16[112,896]{1,0:T(8,128)(2,1)S(1)}, u32[]{:S(2)}, u32[]{:S(2)}) collective-permute-start(bf16[112,896]{1,0:T(8,128)(2,1)S(1)} %fusion.16.corner), channel_id=1, source_target_pairs={{8,0},{16,24},{9,1},{17,25},{10,2},{18,26},{11,3},{19,27},{12,4},{... | collective-permute-start | bytes 602120 | tf_op jit(solution)/shard_map/ppermute | solution.py:220
  306.8 105.8 %all-gather.9.cloned.1.call-start = ((), (), s32[]{:S(2)}) async-start(), calls=%async_computation.6 | async-start | bytes 8257536 | tf_op jit(solution)/shard_map/all_gather | solution.py:237
  309.3 25.2 %collective-permute-start.16 = (bf16[896,512]{1,0:T(8,128)(2,1)S(1)}, bf16[896,512]{1,0:T(8,128)(2,1)S(1)}, u32[]{:S(2)}, u32[]{:S(2)}) collective-permute-start(bf16[896,512]{1,0:T(8,128)(2,1)S(1)} %slice.35), channel_id=1, source_target_pairs={{8,0},{9,1},{10,2},{11,3},{12,4},{13,5},{14,6},{15,7}} | collective-permute-start | bytes 2752520 | tf_op jit(solution)/shard_map/ppermute | solution.py:233
  310.6 24.8 %collective-permute-start.15 = (bf16[896,512]{1,0:T(8,128)(2,1)S(1)}, bf16[896,512]{1,0:T(8,128)(2,1)}, u32[]{:S(2)}, u32[]{:S(2)}) collective-permute-start(bf16[896,512]{1,0:T(8,128)(2,1)S(1)} %slice.34), channel_id=1, source_target_pairs={{16,24},{17,25},{18,26},{19,27},{20,28},{21,29},{22,30},{23,31}} | collective-permute-start | bytes 2752520 | tf_op jit(solution)/shard_map/ppermute | solution.py:232
  312.2 39.2 %collective-permute-start.17 = (bf16[4,112,896]{2,1,0:T(8,128)(2,1)}, bf16[4,112,896]{2,1,0:T(8,128)(2,1)}, u32[]{:S(2)}, u32[]{:S(2)}) collective-permute-start(bf16[4,112,896]{2,1,0:T(8,128)(2,1)} %collective-permute-done.13.r2), channel_id=1, source_target_pairs={{16,24},{17,25},{18,26},{19,27},{20,28},{21,29},{22,30},{23,31}} | collective-permute-start | bytes 2408456 | tf_op jit(solution)/shard_map/ppermute | solution.py:224
  313.8 37.7 %collective-permute-start.18 = (bf16[4,112,896]{2,1,0:T(8,128)(2,1)}, bf16[4,112,896]{2,1,0:T(8,128)(2,1)}, u32[]{:S(2)}, u32[]{:S(2)}) collective-permute-start(bf16[4,112,896]{2,1,0:T(8,128)(2,1)} %collective-permute-done.14.l2), channel_id=1, source_target_pairs={{8,0},{9,1},{10,2},{11,3},{12,4},{13,5},{14,6},{15,7}} | collective-permute-start | bytes 2408456 | tf_op jit(solution)/shard_map/ppermute | solution.py:225
  315.1 36.4 %collective-permute-start.19 = (bf16[112,896]{1,0:T(8,128)(2,1)S(1)}, bf16[112,896]{1,0:T(8,128)(2,1)S(1)}, u32[]{:S(2)}, u32[]{:S(2)}) collective-permute-start(bf16[112,896]{1,0:T(8,128)(2,1)S(1)} %collective-permute-done.12.pair), channel_id=1, source_target_pairs={{8,0},{16,24},{9,1},{17,25},{10,2},{18,26},{11,3},{19,27},{12,4},{... | collective-permute-start | bytes 602120 | tf_op jit(solution)/shard_map/ppermute | solution.py:223
  365.3 35.0 %collective-permute-start.23 = (bf16[896,768]{1,0:T(8,128)(2,1)S(1)}, bf16[896,768]{1,0:T(8,128)(2,1)S(1)}, u32[]{:S(2)}, u32[]{:S(2)}) collective-permute-start(bf16[896,768]{1,0:T(8,128)(2,1)S(1)} %slice.39), channel_id=1, source_target_pairs={{8,0},{9,1},{10,2},{11,3},{12,4},{13,5},{14,6},{15,7}} | collective-permute-start | bytes 4128776 | tf_op jit(solution)/shard_map/ppermute | solution.py:233
  366.6 33.7 %collective-permute-start.22 = (bf16[896,768]{1,0:T(8,128)(2,1)S(1)}, bf16[896,768]{1,0:T(8,128)(2,1)}, u32[]{:S(2)}, u32[]{:S(2)}) collective-permute-start(bf16[896,768]{1,0:T(8,128)(2,1)S(1)} %slice.38), channel_id=1, source_target_pairs={{16,24},{17,25},{18,26},{19,27},{20,28},{21,29},{22,30},{23,31}} | collective-permute-start | bytes 4128776 | tf_op jit(solution)/shard_map/ppermute | solution.py:232
  373.2 61.2 %collective-permute-start.21 = (bf16[896,1024]{1,0:T(8,128)(2,1)}, bf16[896,1024]{1,0:T(8,128)(2,1)}, u32[]{:S(2)}, u32[]{:S(2)}) collective-permute-start(bf16[896,1024]{1,0:T(8,128)(2,1)} %slice.37), channel_id=1, source_target_pairs={{8,0},{9,1},{10,2},{11,3},{12,4},{13,5},{14,6},{15,7}} | collective-permute-start | bytes 5505032 | tf_op jit(solution)/shard_map/ppermute | solution.py:233
  374.5 59.9 %collective-permute-start.20 = (bf16[896,1024]{1,0:T(8,128)(2,1)S(1)}, bf16[896,1024]{1,0:T(8,128)(2,1)}, u32[]{:S(2)}, u32[]{:S(2)}) collective-permute-start(bf16[896,1024]{1,0:T(8,128)(2,1)S(1)} %slice.36), channel_id=1, source_target_pairs={{16,24},{17,25},{18,26},{19,27},{20,28},{21,29},{22,30},{23,31}} | collective-permute-start | bytes 5505032 | tf_op jit(solution)/shard_map/ppermute | solution.py:232
  400.3 12.3 %copy-start.5 = (bf16[896,768]{1,0:T(8,128)(2,1)}, bf16[896,768]{1,0:T(8,128)(2,1)S(1)}, u32[]{:S(2)}) copy-start(bf16[896,768]{1,0:T(8,128)(2,1)S(1)} %collective-permute-done.23) | copy-start | bytes 4128772
  (5 other events, 12.1 us)
Sparse Core Ops, SparseCore 0:
  24.5 39.4 reduce-scatter.2
  134.8 66.6 reduce-scatter.4
  240.0 61.6 all-gather.4
  306.9 24.0 all-gather.6
  362.5 50.0 all-gather.8

commit v4 on v3

v4 whole, which is shorter than its diff:
```python
import functools
import math

import jax
import jax.numpy as jnp
from jax import lax
from jax.experimental import pallas as pl
from jax.experimental.pallas import tpu as pltpu
from jax.sharding import PartitionSpec as P

N = 18432


coef_a = 3.4445
coef_b = -4.775
coef_c = 2.0315


def dot_rows(left, right):
    return lax.dot_general(
        left, right, (((1,), (1,)), ((), ())), preferred_element_type=jnp.float32
    )


def per_device(iterate):
    contract = (((1,), (1,)), ((), ()))
    gathered = lax.all_gather(iterate, "row", axis=0, tiled=True)
    partial_value = lax.dot_general(
        iterate, gathered, contract, preferred_element_type=jnp.float32
    )
    partial_value = partial_value.astype(jnp.bfloat16)
    gram_tile = lax.psum_scatter(partial_value, "col", scatter_dimension=1, tiled=True)
    gram_panel = lax.all_gather(gram_tile, "col", axis=1, tiled=True)
    squared = jnp.dot(
        gram_panel,
        lax.all_gather(gram_tile, "row", axis=0, tiled=True),
        preferred_element_type=jnp.float32,
    )
    factor = (coef_b * gram_tile.astype(jnp.float32) + coef_c * squared).astype(jnp.bfloat16)
    factor_panel = lax.all_gather(factor, "col", axis=1, tiled=True)
    product = jnp.dot(factor_panel, gathered, preferred_element_type=jnp.float32)
    result = coef_a * iterate.astype(jnp.float32) + product
    return (math.sqrt(N) * result).astype(jnp.bfloat16)


def whole():
    return pl.BlockSpec(memory_space=pltpu.VMEM)


def scalars():
    return pl.BlockSpec(memory_space=pltpu.SMEM)


def store_rows(out, block, left, right):
    half = right.shape[0] // 2
    for part in (slice(0, half), slice(half, 2 * half)):
        out[block, :, part] = dot_rows(left[...], right[part, :]).astype(out.dtype)


def near_kernel(x, l1, r1, out):
    store_rows(out, 0, x, l1)
    store_rows(out, 1, x, r1)
    store_rows(out, 2, r1, l1)
    store_rows(out, 3, l1, r1)


def corner_kernel(place, l1, r1, early, out):
    on_one = jnp.logical_and(place[0] == 1, place[1] == 0)
    on_two = jnp.logical_and(place[0] == 2, place[1] == 1)

    @pl.when(on_one)
    def _():
        store_rows(out, 0, r1, early)
        store_rows(out, 1, early, r1)

    @pl.when(on_two)
    def _():
        store_rows(out, 0, early, l1)
        store_rows(out, 1, l1, early)

    @pl.when(jnp.logical_not(jnp.logical_or(on_one, on_two)))
    def _():
        out[...] = jnp.zeros_like(out)


def gram_call(kernel, count, operands, scalar):
    rows, depth = operands[0].shape
    first = [] if scalar is None else [scalar]
    return pl.pallas_call(
        kernel,
        out_shape=jax.ShapeDtypeStruct((count, rows, rows), jnp.bfloat16),
        in_specs=[scalars()] * len(first) + [whole()] * len(operands),
        out_specs=whole(),
        compiler_params=pltpu.CompilerParams(vmem_limit_bytes=48 * 2**20),
        cost_estimate=pl.CostEstimate(
            flops=2 * count * rows * rows * depth, bytes_accessed=6 * rows * depth, transcendentals=0
        ),
    )(*first, *operands)


def square_kernel(place, panel, own, l1, r3, l2, r2, r1, l3, corner, out):
    z = place[0]
    part = own.shape[1]
    rows = panel.shape[1]
    low, high = corner[0], corner[1]
    zero = jnp.zeros_like(low)

    def strip(e, block):
        if e == 0:
            value = own[block]
        else:
            one, other = {1: (l1, r3), 2: (l2, r2), 3: (r1, l3)}[e]
            value = one[block] + other[block]
        if block == 3:
            value = value + jnp.where((z + e) % 4 == 0, low, zero)
        if block == 1:
            value = value + jnp.where((z + e) % 4 == 3, high, zero)
        return value

    total = jnp.zeros((rows, 4 * part), jnp.float32)
    for d in range(4):
        right = jnp.concatenate([strip(e, (d - e) % 4) for e in range(4)], axis=0)
        total = total + dot_rows(panel[d], right)
    index = lax.broadcasted_iota(jnp.int32, (rows, rows), 0)
    other = lax.broadcasted_iota(jnp.int32, (rows, rows), 1)
    unit = jnp.where(index == other, 1.0, 0.0).astype(jnp.bfloat16)
    linear = dot_rows(unit, jnp.concatenate([strip(e, (-e) % 4) for e in range(4)], axis=0))
    out[...] = (coef_b * linear + coef_c * total).astype(out.dtype)


def square(place, panel, *others):
    rows = panel.shape[1]
    part = others[0].shape[1]
    return pl.pallas_call(
        square_kernel,
        out_shape=jax.ShapeDtypeStruct((rows, 4 * part), jnp.bfloat16),
        in_specs=[scalars()] + [whole()] * (1 + len(others)),
        out_specs=whole(),
        compiler_params=pltpu.CompilerParams(vmem_limit_bytes=48 * 2**20),
        cost_estimate=pl.CostEstimate(
            flops=2 * rows * rows * 4 * 4 * part, bytes_accessed=2 * 5 * rows * rows, transcendentals=0
        ),
    )(place, panel, *others)


def product_kernel(starts, place, f, x, l1, r1, early, late, *rest):
    n_piece = len(starts) - 1
    far = [rest[p : 2 * n_piece : n_piece] for p in range(n_piece)]
    out, wide = rest[-2:]
    n_col, part, width = x.shape
    step = pl.program_id(0)
    wide[:, :part, :] = x[...]
    wide[:, 2 * part : 3 * part, :] = early[...] + late[...]
    for p in range(n_piece):

        @pl.when(jnp.logical_and(step >= starts[p], step < starts[p + 1]))
        def _(p=p):
            value = far[p][0][...] + far[p][1][...]
            zero = jnp.zeros_like(value)
            wide[:, part : 2 * part, :] = l1[...] + jnp.where(place[0] == 3, value, zero)
            wide[:, 3 * part :, :] = r1[...] + jnp.where(place[0] == 0, value, zero)

    total = coef_a * x[...].reshape(n_col * part, width).astype(jnp.float32)
    for c in range(n_col):
        total = total + jnp.dot(f[c], wide[c], preferred_element_type=jnp.float32)
    out[...] = (math.sqrt(N) * total).astype(out.dtype)


def product(place, f, near, far, tile, first, before):
    n_col, rows, depth = f.shape
    part = rows // n_col
    columns = near[0].shape[1]

    def split(value):
        return value.reshape(n_col, part, value.shape[1])

    starts = [0]
    for piece in far[0]:
        starts.append(starts[-1] + piece.shape[1] // tile)

    def piece_spec(p):
        begin, count = starts[p], starts[p + 1] - starts[p]
        return pl.BlockSpec((n_col, part, tile), lambda i: (0, 0, jnp.clip(i - begin, 0, count - 1)))

    plain = pl.BlockSpec((n_col, part, tile), lambda i: (0, 0, i + first))
    pieces = [piece_spec(p) for p in range(len(far[0]))]
    operands = [place, f, *(split(value) for value in (*near, *far[0], *far[1]))]
    in_specs = [
        scalars(),
        pl.BlockSpec((n_col, rows, depth), lambda i: (0, 0, 0), pipeline_mode=pl.Buffered(1)),
    ]
    in_specs += [plain] * len(near) + pieces * 2
    aliases = {}
    if before is not None:
        aliases = {len(operands): 0}
        operands.append(before)
        in_specs.append(pl.BlockSpec(memory_space=pl.ANY))
    share = tile * starts[-1]
    return pl.pallas_call(
        functools.partial(product_kernel, tuple(starts)),
        grid=(starts[-1],),
        out_shape=jax.ShapeDtypeStruct((rows, columns), jnp.bfloat16),
        in_specs=in_specs,
        out_specs=pl.BlockSpec((rows, tile), lambda i: (0, i + first)),
        scratch_shapes=[pltpu.VMEM((n_col, depth, tile), jnp.bfloat16)],
        input_output_aliases=aliases,
        compiler_params=pltpu.CompilerParams(vmem_limit_bytes=56 * 2**20),
        cost_estimate=pl.CostEstimate(
            flops=2 * rows * n_col * depth * share, bytes_accessed=2 * 12 * rows * share, transcendentals=0
        ),
    )(*operands)


def per_device_line(n_col, x):
    z, c = lax.axis_index("row"), lax.axis_index("col")
    place = jnp.stack([z, c % 2]).astype(jnp.int32)
    right, left = [(0, 1), (1, 2), (2, 3)], [(3, 2), (2, 1), (1, 0)]

    def send(value, pairs):
        return lax.ppermute(value, "row", pairs)

    def send_cores(value, even, odd):
        pairs = [
            (a * n_col + i, b * n_col + i)
            for i in range(n_col)
            for a, b in (odd if i % 2 else even)
        ]
        return lax.ppermute(value, ("row", "col"), pairs)

    def scatter(blocks):
        return lax.psum_scatter(blocks, "col", scatter_dimension=1, tiled=True)

    r1 = send(x, right)
    l1 = send(x, left)
    early = send_cores(jnp.where(c % 2 == 0, l1, r1), left[1:], right[1:])
    late = send_cores(jnp.where(c % 2 == 0, r1, l1), right[1:], left[1:])

    own = scatter(dot_rows(x, x).astype(jnp.bfloat16)[None])
    own, near_l, near_r = lax.optimization_barrier((own, l1, r1))
    blocks = gram_call(near_kernel, 4, [x, near_l, near_r], None)
    first = scatter(blocks)
    blocks, early_now = lax.optimization_barrier((blocks, early))
    corner = gram_call(corner_kernel, 2, [l1, r1, early_now], place)
    corner, first = lax.optimization_barrier((corner, first))
    corner = scatter(corner)

    first, late = lax.optimization_barrier((first, late))
    second = send(first[2], left[1:]) + send(first[3], right[1:])
    tile = jnp.stack([own[0], first[0], second, first[1]])
    tr1, tl1 = send(tile, right), send(tile, left)

    corner, tr1, tl1 = lax.optimization_barrier((corner, tr1, tl1))
    corner = corner + send(corner, [(1, 2), (2, 1)])
    corner = corner + send(corner, [(1, 0), (2, 3)])
    zero = jnp.zeros_like(corner[0])
    added = jnp.stack(
        [zero, jnp.where(z == 3, corner[1], zero), zero, jnp.where(z == 0, corner[0], zero)]
    )
    panel = lax.all_gather(tile + added, "col", axis=1, tiled=True)

    tr2, tl2 = send(tr1, right[1:]), send(tl1, left[1:])
    tr3, tl3 = send(tr2, right[2:]), send(tl2, left[2:])
    unit = 256
    marks = [0, 2 * unit, 5 * unit, x.shape[1]]
    pieces = [slice(a, b) for a, b in zip(marks, marks[1:])]
    tr3, tl3, early_on, late_on = lax.optimization_barrier((tr3, tl3, early, late))
    far = [
        [send_cores(early_on[:, piece], left[2:], right[2:]) for piece in pieces],
        [send_cores(late_on[:, piece], right[2:], left[2:]) for piece in pieces],
    ]
    panel, far[0][0], far[1][0] = lax.optimization_barrier((panel, far[0][0], far[1][0]))

    factor = square(place, panel, tile, tl1, tr3, tl2, tr2, tr1, tl3, corner)
    factor = lax.all_gather(factor, "col", axis=0, tiled=False)
    near = [x, l1, r1, early, late]
    out = product(place, factor, near, [part[:2] for part in far], unit, 0, None)
    return product(place, factor, near, [part[2:] for part in far], unit, marks[2] // unit, out)


def solution(mesh):
    n_row, n_col = mesh.shape["row"], mesh.shape["col"]

    def body(iterate):
        if (n_row, n_col) == (4, 8) and iterate.shape == (896, 2304):
            return per_device_line(n_col, iterate)
        return per_device(iterate)

    return jax.shard_map(
        body,
        mesh=mesh,
        in_specs=(P("row", "col"),),
        out_specs=P("row", "col"),
        check_vma=False,
    )
```

time: 456 us -> 492 us (1.079)
  waiting for transfers between devices: 282 us -> 331 us
  matrix products: 47.2 us -> 9.03 us
  Pallas kernels: 41.8 us -> 70.8 us
  starting transfers between devices: 46 us -> 33.8 us
  local copies, waits for them, and re-layouts: 15.8 us -> 22.8 us
    ppermute x24 -> x20, waiting for transfers between devices: 167 us -> 258 us  [the longest x8 137 us: send_cores(): return lax.ppermute(value, ('row', 'col'), pairs)]
    reduce_scatter x2 -> x3, waiting for transfers between devices: 102 us -> 60.2 us  [scatter(): return lax.psum_scatter(blocks, 'col', scatter_dimension=1, tiled=True)]
    dot_general x6 -> x1, matrix products: 47.2 us -> 9.03 us  [dot_rows(): lax.dot_general(left, right, (((1,), (1,)), ((), ())), preferred_element_...]
    pallas_call x0 -> x2, Pallas kernels: none -> 30 us  [gram_call(): pl.pallas_call(kernel, out_shape=jax.ShapeDtypeStruct((count, rows, rows)...]
    ppermute x24 -> x20, starting transfers between devices: 45.7 us -> 33.6 us  [the longest x12 22.2 us: send(): return lax.ppermute(value, 'row', pairs)]
    unnamed x16 -> x28, local copies, waits for them, and re-layouts: 2.51 us -> 11.3 us
    select_n x0 -> x2, other arithmetic: none -> 6.16 us  [the longest x1 6.11 us: per_device_line(): late = send_cores(jnp.where(c % 2 == 0, r1, l1), right[1:], left[1:])]
  transfers between devices with their start and end apart: 29 -> 25, of which waited for: 13 -> 15; matrix products, arithmetic and copies ran while one was open for 8% -> 5% of each run, Pallas kernels for 4% -> 5%
where the time goes in v4:
time: 492 us; the launch traced here: 491 us
  waiting for transfers between devices  331 us (67%)
  Pallas kernels  70.8 us (14%)
  starting transfers between devices  33.8 us (7%)
  local copies, waits for them, and re-layouts  22.8 us (5%)
  between operations  13.5 us (3%)
  other arithmetic  10.7 us (2%)
  matrix products  9.03 us (2%)
    ppermute x8, waiting for transfers between devices, send_cores(): return lax.ppermute(value, ('row', 'col'), pairs)  137 us
    ppermute x12, waiting for transfers between devices, send(): return lax.ppermute(value, 'row', pairs)  121 us
    reduce_scatter x3, waiting for transfers between devices, scatter(): return lax.psum_scatter(blocks, 'col', scatter_dimension=1, tiled=True)  60.2 us
    pallas_call x2, Pallas kernels, product(): pl.pallas_call(functools.partial(product_kernel, tuple(starts)), grid=(st...  32.1 us
    pallas_call x2, Pallas kernels, gram_call(): pl.pallas_call(kernel, out_shape=jax.ShapeDtypeStruct((count, rows, rows)...  30 us
    ppermute x12, starting transfers between devices, send(): return lax.ppermute(value, 'row', pairs)  22.2 us
    all_gather x1, waiting for transfers between devices, per_device_line(): factor = lax.all_gather(factor, 'col', axis=0, tiled=False)  12 us
    ppermute x8, starting transfers between devices, send_cores(): return lax.ppermute(value, ('row', 'col'), pairs)  11.4 us
  transfers between devices with their start and end apart: 25, of which 15 were waited for; matrix products, arithmetic and copies ran while one was open for 5% of the time, Pallas kernels for 5%

profile of v4, /device:TPU:0, one launch (start us, length us, event | category | flops | bytes accessed | tf_op | source)
XLA Modules:
  0.0 491.2 jit_solution(2443929306218610905)
XLA Ops:
  6.5 6.8 %collective-permute-start.1 = (bf16[896,2304]{1,0:T(8,128)(2,1)}, bf16[896,2304]{1,0:T(8,128)(2,1)}, u32[]{:S(2)}, u32[]{:S(2)}) collective-permute-start(bf16[896,2304]{1,0:T(8,128)(2,1)} %x.1), channel_id=1, source_target_pairs={{0,8},{8,16},{16,24},{1,9},{9,17},{17,25},{2,10},{10,18},{18,26},{... | collective-permute-start | bytes 12386312 | tf_op jit(solution)/shard_map/ppermute | solution.py:220
  14.7 9.0 %fusion = bf16[1,896,896]{2,1,0:T(8,128)(2,1)} fusion(bf16[896,2304]{1,0:T(8,128)(2,1)} %x.1), kind=kOutput, calls=%fused_computation.3 | convolution fusion | flops 3700178944 | bytes 5734400 | tf_op jit(solution)/shard_map/dot_general | solution.py:20
  23.8 41.3 %reduce-scatter.4.cloned.1.call-done = bf16[1,112,896]{2,1,0:T(8,128)(2,1)} async-done(((bf16[1,896,896]{2,1,0:T(8,128)(2,1)}), bf16[1,112,896]{2,1,0:T(8,128)(2,1)}) %reduce-scatter.4.cloned.1.call-update) | async-done | bytes 200720 | tf_op jit(solution)/shard_map/reduce_scatter | solution.py:231
  65.1 35.1 %collective-permute-done.1.r1 = bf16[896,2304]{1,0:T(8,128)(2,1)} collective-permute-done((bf16[896,2304]{1,0:T(8,128)(2,1)}, bf16[896,2304]{1,0:T(8,128)(2,1)}, u32[]{:S(2)}, u32[]{:S(2)}) %collective-permute-start.1) | collective-permute-done | bytes 4128800 | tf_op jit(solution)/shard_map/ppermute | solution.py:220
  100.2 6.0 %collective-permute-done.l1 = bf16[896,2304]{1,0:T(8,128)(2,1)} collective-permute-done((bf16[896,2304]{1,0:T(8,128)(2,1)}, bf16[896,2304]{1,0:T(8,128)(2,1)}, u32[]{:S(2)}, u32[]{:S(2)}) %collective-permute-start) | collective-permute-done | bytes 4128800 | tf_op jit(solution)/shard_map/ppermute | solution.py:220
  106.2 2.2 copy-done
  108.4 23.4 %shard_map.17 = bf16[4,896,896]{2,1,0:T(8,128)(2,1)} custom-call(bf16[896,2304]{1,0:T(8,128)(2,1)S(1)} %copy-done, bf16[896,2304]{1,0:T(8,128)(2,1)} %collective-permute-done.l1, bf16[896,2304]{1,0:T(8,128)(2,1)} %collective-permute-done.1.r1), custom_call_target="tpu_custom_call" | custom-call | flops 14797504512 | bytes 12386304 | tf_op jit(solution)/shard_map/pallas_call | solution.py:89
  131.9 6.1 %broadcast_select_fusion = (bf16[896,2304]{1,0:T(8,128)(2,1)}, bf16[896,2304]{1,0:T(8,128)(2,1)}) fusion(bf16[896,2304]{1,0:T(8,128)(2,1)} %collective-permute-done.1.r1, bf16[896,2304]{1,0:T(8,128)(2,1)} %collective-permute-done.l1, pred[]{:T(512)S(6)} %eq.14), kind=kLoop, calls=%fused_computation | loop fusion | flops 4128768 | bytes 16515073 | tf_op jit(solution)/shard_map/jit(_where)/select_n | solution.py:236
  138.0 1.5 collective-permute-start.2
  139.5 2.7 collective-permute-start.3
  142.3 89.2 %collective-permute-done.2.early = bf16[896,2304]{1,0:T(8,128)(2,1)} collective-permute-done((bf16[896,2304]{1,0:T(8,128)(2,1)}, bf16[896,2304]{1,0:T(8,128)(2,1)}, u32[]{:S(2)}, u32[]{:S(2)}) %collective-permute-start.2) | collective-permute-done | bytes 4128800 | tf_op jit(solution)/shard_map/ppermute | solution.py:228
  231.5 6.6 %shard_map.18 = bf16[2,896,896]{2,1,0:T(8,128)(2,1)} custom-call(s32[2]{0:T(128)S(1)} %pad_add_fusion.place, bf16[896,2304]{1,0:T(8,128)(2,1)} %collective-permute-done.l1, bf16[896,2304]{1,0:T(8,128)(2,1)} %collective-permute-done.1.r1, bf16[896,2304]{1,0:T(8,128)(2,1)} %collective-permute-done.2.early), custom_call_target="tpu_custom_call" | custom-call | flops 7398752256 | bytes 12386304 | tf_op jit(solution)/shard_map/pallas_call | solution.py:89
  241.5 15.1 %collective-permute-done.4 = bf16[112,896]{1,0:T(8,128)(2,1)S(1)} collective-permute-done((bf16[112,896]{1,0:T(8,128)(2,1)S(1)}, bf16[112,896]{1,0:T(8,128)(2,1)S(1)}, u32[]{:S(2)}, u32[]{:S(2)}) %collective-permute-start.4) | collective-permute-done | bytes 200736 | tf_op jit(solution)/shard_map/ppermute | solution.py:220
  258.1 4.6 collective-permute-start.6
  262.7 8.2 %collective-permute-done.7.l1 = bf16[4,112,896]{2,1,0:T(8,128)(2,1)S(1)} collective-permute-done((bf16[4,112,896]{2,1,0:T(8,128)(2,1)S(1)}, bf16[4,112,896]{2,1,0:T(8,128)(2,1)S(1)}, u32[]{:S(2)}, u32[]{:S(2)}) %collective-permute-start.7) | collective-permute-done | bytes 802848 | tf_op jit(solution)/shard_map/ppermute | solution.py:220
  270.9 1.5 collective-permute-done.6.r1
  272.4 19.0 %reduce-scatter.8.cloned.1.call-done = bf16[2,112,896]{2,1,0:T(8,128)(2,1)} async-done(((bf16[2,896,896]{2,1,0:T(8,128)(2,1)}), bf16[2,112,896]{2,1,0:T(8,128)(2,1)}) %reduce-scatter.8.cloned.1.call-update) | async-done | bytes 401424 | tf_op jit(solution)/shard_map/reduce_scatter | solution.py:231
  294.4 22.4 %collective-permute-done.9 = bf16[2,112,896]{2,1,0:T(8,128)(2,1)} collective-permute-done((bf16[2,112,896]{2,1,0:T(8,128)(2,1)S(1)}, bf16[2,112,896]{2,1,0:T(8,128)(2,1)}, u32[]{:S(2)}, u32[]{:S(2)}) %collective-permute-start.9) | collective-permute-done | bytes 401440 | tf_op jit(solution)/shard_map/ppermute | solution.py:220
  318.1 2.0 maximum_add_fusion
  324.0 17.2 %collective-permute-done.12.l2 = bf16[4,112,896]{2,1,0:T(8,128)(2,1)S(1)} collective-permute-done((bf16[4,112,896]{2,1,0:T(8,128)(2,1)S(1)}, bf16[4,112,896]{2,1,0:T(8,128)(2,1)S(1)}, u32[]{:S(2)}, u32[]{:S(2)}) %collective-permute-start.12) | collective-permute-done | bytes 802848 | tf_op jit(solution)/shard_map/ppermute | solution.py:220
  341.1 1.5 collective-permute-start.13
  344.4 15.9 %collective-permute-done.13.l3 = bf16[4,112,896]{2,1,0:T(8,128)(2,1)S(1)} collective-permute-done((bf16[4,112,896]{2,1,0:T(8,128)(2,1)S(1)}, bf16[4,112,896]{2,1,0:T(8,128)(2,1)S(1)}, u32[]{:S(2)}, u32[]{:S(2)}) %collective-permute-start.13) | collective-permute-done | bytes 802848 | tf_op jit(solution)/shard_map/ppermute | solution.py:220
  366.6 18.0 %collective-permute-done.14 = bf16[896,512]{1,0:T(8,128)(2,1)} collective-permute-done((bf16[896,512]{1,0:T(8,128)(2,1)S(1)}, bf16[896,512]{1,0:T(8,128)(2,1)}, u32[]{:S(2)}, u32[]{:S(2)}) %collective-permute-start.14) | collective-permute-done | bytes 917536 | tf_op jit(solution)/shard_map/ppermute | solution.py:228
  389.2 8.7 %shard_map.19 = bf16[896,448]{1,0:T(8,128)(2,1)} custom-call(s32[2]{0:T(128)S(1)} %pad_add_fusion.place, bf16[4,896,896]{2,1,0:T(8,128)(2,1)} %all-gather.4.cloned.1.call-done.panel, bf16[4,112,896]{2,1,0:T(8,128)(2,1)S(1)} %pad_maximum_fusion.own, bf16[4,112,896]{2,1,0:T(8,128)(2,1)S(1)} %collective-permute-done.7.l1, bf16[4,112,896]{2,1,0:T(8,128)(2,1)S(1)} %copy-done.6, ...), custom_call_target="tpu_custom_call" | custom-call | flops 2877292544 | bytes 8028160 | tf_op jit(solution)/shard_map/pallas_call | solution.py:134
  402.8 1.6 slice.44
  404.5 3.1 slice.45
  407.6 1.9 collective-permute-start.17
  410.8 25.8 %collective-permute-done.18 = bf16[896,768]{1,0:T(8,128)(2,1)} collective-permute-done((bf16[896,768]{1,0:T(8,128)(2,1)S(1)}, bf16[896,768]{1,0:T(8,128)(2,1)}, u32[]{:S(2)}, u32[]{:S(2)}) %collective-permute-start.18) | collective-permute-done | bytes 1376288 | tf_op jit(solution)/shard_map/ppermute | solution.py:228
  436.7 12.0 %all-gather.6.cloned.1.call-done = bf16[7168,448]{1,0:T(8,128)(2,1)} async-done(((bf16[896,448]{1,0:T(8,128)(2,1)}), bf16[7168,448]{1,0:T(8,128)(2,1)}) %all-gather.6.cloned.1.call-update) | async-done | bytes 6422544 | tf_op jit(solution)/shard_map/all_gather | solution.py:274
  448.7 17.5 %shard_map.20.rest_2_ = bf16[896,2304]{1,0:T(8,128)(2,1)} custom-call(s32[2]{0:T(128)} %copy-done.9, bf16[8,896,448]{2,1,0:T(8,128)(2,1)} %bitcast.26, bf16[8,112,2304]{2,1,0:T(8,128)(2,1)} %bitcast.24, bf16[8,112,2304]{2,1,0:T(8,128)(2,1)} %bitcast.8.l1, bf16[8,112,2304]{2,1,0:T(8,128)(2,1)} %bitcast.9.r1, bf16[8,112,2304]{2,1,0:T(8,128)(2,1)} %bitcast.10.early, ...), custom_call_target="tpu_custom_call" | custom-call | flops 8220835840 | bytes 27525120 | tf_op jit(solution)/shard_map/pallas_call | solution.py:199
  466.2 4.0 collective-permute-done.16
  470.2 14.6 %shard_map.21 = bf16[896,2304]{1,0:T(8,128)(2,1)} custom-call(s32[2]{0:T(128)} %copy-done.9, bf16[8,896,448]{2,1,0:T(8,128)(2,1)} %bitcast.27, bf16[8,112,2304]{2,1,0:T(8,128)(2,1)} %bitcast.25, bf16[8,112,2304]{2,1,0:T(8,128)(2,1)} %bitcast.8.l1, bf16[8,112,2304]{2,1,0:T(8,128)(2,1)} %bitcast.9.r1, ...), custom_call_target="tpu_custom_call", output_to_operand_aliasing={{}: (9, {})} | custom-call | flops 6576668672 | bytes 22020096 | tf_op jit(solution)/shard_map/pallas_call | solution.py:199
  (73 shorter events, 33.2 us)
Async XLA Ops:
  6.5 58.5 %reduce-scatter.4.cloned.1.call-start = ((), (), s32[]{:S(2)}) async-start(), calls=%async_computation.3 | async-start | bytes 1806336 | tf_op jit(solution)/shard_map/reduce_scatter | solution.py:231
  6.5 93.7 %collective-permute-start.1 = (bf16[896,2304]{1,0:T(8,128)(2,1)}, bf16[896,2304]{1,0:T(8,128)(2,1)}, u32[]{:S(2)}, u32[]{:S(2)}) collective-permute-start(bf16[896,2304]{1,0:T(8,128)(2,1)} %x.1), channel_id=1, source_target_pairs={{0,8},{8,16},{16,24},{1,9},{9,17},{17,25},{2,10},{10,18},{18,26},{... | collective-permute-start | bytes 12386312 | tf_op jit(solution)/shard_map/ppermute | solution.py:220
  13.4 92.8 %collective-permute-start = (bf16[896,2304]{1,0:T(8,128)(2,1)}, bf16[896,2304]{1,0:T(8,128)(2,1)}, u32[]{:S(2)}, u32[]{:S(2)}) collective-permute-start(bf16[896,2304]{1,0:T(8,128)(2,1)} %x.1), channel_id=1, source_target_pairs={{24,16},{16,8},{8,0},{25,17},{17,9},{9,1},{26,18},{18,10},{10,2},{... | collective-permute-start | bytes 12386312 | tf_op jit(solution)/shard_map/ppermute | solution.py:220
  23.7 214.4 %reduce-scatter.6.cloned.1.call-start = ((), (), s32[]{:S(2)}) async-start(), calls=%async_computation.4 | async-start | bytes 7225344 | tf_op jit(solution)/shard_map/reduce_scatter | solution.py:231
  106.2 2.2 copy-start
  131.8 159.5 %reduce-scatter.8.cloned.1.call-start = ((), (), s32[]{:S(2)}) async-start(), calls=%async_computation.5 | async-start | bytes 3612672 | tf_op jit(solution)/shard_map/reduce_scatter | solution.py:231
  138.0 93.5 %collective-permute-start.2 = (bf16[896,2304]{1,0:T(8,128)(2,1)}, bf16[896,2304]{1,0:T(8,128)(2,1)}, u32[]{:S(2)}, u32[]{:S(2)}) collective-permute-start(bf16[896,2304]{1,0:T(8,128)(2,1)} %get-tuple-element.42), channel_id=1, source_target_pairs={{16,8},{8,0},{9,17},{17,25},{18,10},{10,2},{11,19},{19,27},{20,12}... | collective-permute-start | bytes 12386312 | tf_op jit(solution)/shard_map/ppermute | solution.py:228
  139.5 98.7 %collective-permute-start.3 = (bf16[896,2304]{1,0:T(8,128)(2,1)}, bf16[896,2304]{1,0:T(8,128)(2,1)}, u32[]{:S(2)}, u32[]{:S(2)}) collective-permute-start(bf16[896,2304]{1,0:T(8,128)(2,1)} %get-tuple-element.41), channel_id=1, source_target_pairs={{8,16},{16,24},{17,9},{9,1},{10,18},{18,26},{19,11},{11,3},{12,20}... | collective-permute-start | bytes 12386312 | tf_op jit(solution)/shard_map/ppermute | solution.py:228
  142.3 242.4 %copy-start.9 = (s32[2]{0:T(128)}, s32[2]{0:T(128)S(1)}, u32[]{:S(2)}) copy-start(s32[2]{0:T(128)S(1)} %pad_add_fusion.place) | copy-start | bytes 28
  238.1 18.5 %copy-start.13 = (bf16[1,112,896]{2,1,0:T(8,128)(2,1)S(1)}, bf16[1,112,896]{2,1,0:T(8,128)(2,1)}, u32[]{:S(2)}) copy-start(bf16[1,112,896]{2,1,0:T(8,128)(2,1)} %reduce-scatter.4.cloned.1.call-done) | copy-start | bytes 602116
  238.2 146.5 %all-gather.4.cloned.1.call-start = ((), (), s32[]{:S(2)}) async-start(), calls=%async_computation.6 | async-start | bytes 7225344 | tf_op jit(solution)/shard_map/all_gather | solution.py:259
  239.5 2.0 collective-permute-start.5
  240.2 16.4 %collective-permute-start.4 = (bf16[112,896]{1,0:T(8,128)(2,1)S(1)}, bf16[112,896]{1,0:T(8,128)(2,1)S(1)}, u32[]{:S(2)}, u32[]{:S(2)}) collective-permute-start(bf16[112,896]{1,0:T(8,128)(2,1)S(1)} %get-tuple-element.46), channel_id=1, source_target_pairs={{16,8},{8,0},{17,9},{9,1},{18,10},{10,2},{19,11},{11,3},{20,12},{1... | collective-permute-start | bytes 602120 | tf_op jit(solution)/shard_map/ppermute | solution.py:220
  256.8 14.1 %collective-permute-start.7 = (bf16[4,112,896]{2,1,0:T(8,128)(2,1)S(1)}, bf16[4,112,896]{2,1,0:T(8,128)(2,1)S(1)}, u32[]{:S(2)}, u32[]{:S(2)}) collective-permute-start(bf16[4,112,896]{2,1,0:T(8,128)(2,1)S(1)} %pad_maximum_fusion.own), channel_id=1, source_target_pairs={{24,16},{16,8},{8,0},{25,17},{17,9},{9,1},{26,18},{18,10},{10,2},{... | collective-permute-start | bytes 2408456 | tf_op jit(solution)/shard_map/ppermute | solution.py:220
  258.1 14.3 %collective-permute-start.6 = (bf16[4,112,896]{2,1,0:T(8,128)(2,1)S(1)}, bf16[4,112,896]{2,1,0:T(8,128)(2,1)S(1)}, u32[]{:S(2)}, u32[]{:S(2)}) collective-permute-start(bf16[4,112,896]{2,1,0:T(8,128)(2,1)S(1)} %pad_maximum_fusion.own), channel_id=1, source_target_pairs={{0,8},{8,16},{16,24},{1,9},{9,17},{17,25},{2,10},{10,18},{18,26},{... | collective-permute-start | bytes 2408456 | tf_op jit(solution)/shard_map/ppermute | solution.py:220
  291.3 0.7 collective-permute-start.8
  293.1 1.3 copy-start.10
  293.1 23.7 %collective-permute-start.9 = (bf16[2,112,896]{2,1,0:T(8,128)(2,1)S(1)}, bf16[2,112,896]{2,1,0:T(8,128)(2,1)}, u32[]{:S(2)}, u32[]{:S(2)}) collective-permute-start(bf16[2,112,896]{2,1,0:T(8,128)(2,1)S(1)} %add.26), channel_id=1, source_target_pairs={{8,0},{16,24},{9,1},{17,25},{10,2},{18,26},{11,3},{19,27},{12,4},{... | collective-permute-start | bytes 1204232 | tf_op jit(solution)/shard_map/ppermute | solution.py:220
  320.2 128.5 %all-gather.6.cloned.1.call-start = ((), (), s32[]{:S(2)}) async-start(), calls=%async_computation.7 | async-start | bytes 8257536 | tf_op jit(solution)/shard_map/all_gather | solution.py:274
  320.2 2.0 collective-permute-start.10
  321.0 20.2 %collective-permute-start.12 = (bf16[4,112,896]{2,1,0:T(8,128)(2,1)S(1)}, bf16[4,112,896]{2,1,0:T(8,128)(2,1)S(1)}, u32[]{:S(2)}, u32[]{:S(2)}) collective-permute-start(bf16[4,112,896]{2,1,0:T(8,128)(2,1)S(1)} %collective-permute-done.7.l1), channel_id=1, source_target_pairs={{16,8},{8,0},{17,9},{9,1},{18,10},{10,2},{19,11},{11,3},{20,12},{1... | collective-permute-start | bytes 2408456 | tf_op jit(solution)/shard_map/ppermute | solution.py:220
  322.3 21.3 %collective-permute-start.11 = (bf16[4,112,896]{2,1,0:T(8,128)(2,1)S(1)}, bf16[4,112,896]{2,1,0:T(8,128)(2,1)S(1)}, u32[]{:S(2)}, u32[]{:S(2)}) collective-permute-start(bf16[4,112,896]{2,1,0:T(8,128)(2,1)S(1)} %collective-permute-done.10.r2), channel_id=1, source_target_pairs={{16,24},{17,25},{18,26},{19,27},{20,28},{21,29},{22,30},{23,31}} | collective-permute-start | bytes 2408456 | tf_op jit(solution)/shard_map/ppermute | solution.py:220
  341.1 19.2 %collective-permute-start.13 = (bf16[4,112,896]{2,1,0:T(8,128)(2,1)S(1)}, bf16[4,112,896]{2,1,0:T(8,128)(2,1)S(1)}, u32[]{:S(2)}, u32[]{:S(2)}) collective-permute-start(bf16[4,112,896]{2,1,0:T(8,128)(2,1)S(1)} %collective-permute-done.12.l2), channel_id=1, source_target_pairs={{8,0},{9,1},{10,2},{11,3},{12,4},{13,5},{14,6},{15,7}} | collective-permute-start | bytes 2408456 | tf_op jit(solution)/shard_map/ppermute | solution.py:220
  363.7 2.0 collective-permute-start.15
  364.4 20.2 %collective-permute-start.14 = (bf16[896,512]{1,0:T(8,128)(2,1)S(1)}, bf16[896,512]{1,0:T(8,128)(2,1)}, u32[]{:S(2)}, u32[]{:S(2)}) collective-permute-start(bf16[896,512]{1,0:T(8,128)(2,1)S(1)} %slice.42), channel_id=1, source_target_pairs={{8,0},{17,25},{10,2},{19,27},{12,4},{21,29},{14,6},{23,31}} | collective-permute-start | bytes 2752520 | tf_op jit(solution)/shard_map/ppermute | solution.py:228
  384.6 1.1 copy-start.2
  385.8 1.1 copy-start.4
  400.8 10.0 %collective-permute-start.19 = (bf16[896,768]{1,0:T(8,128)(2,1)S(1)}, bf16[896,768]{1,0:T(8,128)(2,1)S(1)}, u32[]{:S(2)}, u32[]{:S(2)}) collective-permute-start(bf16[896,768]{1,0:T(8,128)(2,1)S(1)} %slice.47), channel_id=1, source_target_pairs={{16,24},{9,1},{18,26},{11,3},{20,28},{13,5},{22,30},{15,7}} | collective-permute-start | bytes 4128776 | tf_op jit(solution)/shard_map/ppermute | solution.py:228
  401.5 35.1 %collective-permute-start.18 = (bf16[896,768]{1,0:T(8,128)(2,1)S(1)}, bf16[896,768]{1,0:T(8,128)(2,1)}, u32[]{:S(2)}, u32[]{:S(2)}) collective-permute-start(bf16[896,768]{1,0:T(8,128)(2,1)S(1)} %slice.46), channel_id=1, source_target_pairs={{8,0},{17,25},{10,2},{19,27},{12,4},{21,29},{14,6},{23,31}} | collective-permute-start | bytes 4128776 | tf_op jit(solution)/shard_map/ppermute | solution.py:228
  407.6 58.5 %collective-permute-start.17 = (bf16[896,1024]{1,0:T(8,128)(2,1)}, bf16[896,1024]{1,0:T(8,128)(2,1)}, u32[]{:S(2)}, u32[]{:S(2)}) collective-permute-start(bf16[896,1024]{1,0:T(8,128)(2,1)} %slice.45), channel_id=1, source_target_pairs={{16,24},{9,1},{18,26},{11,3},{20,28},{13,5},{22,30},{15,7}} | collective-permute-start | bytes 5505032 | tf_op jit(solution)/shard_map/ppermute | solution.py:228
  409.5 60.6 %collective-permute-start.16 = (bf16[896,1024]{1,0:T(8,128)(2,1)S(1)}, bf16[896,1024]{1,0:T(8,128)(2,1)}, u32[]{:S(2)}, u32[]{:S(2)}) collective-permute-start(bf16[896,1024]{1,0:T(8,128)(2,1)S(1)} %slice.44), channel_id=1, source_target_pairs={{8,0},{17,25},{10,2},{19,27},{12,4},{21,29},{14,6},{23,31}} | collective-permute-start | bytes 5505032 | tf_op jit(solution)/shard_map/ppermute | solution.py:228
  410.8 37.8 %copy-start.11 = (bf16[896,768]{1,0:T(8,128)(2,1)}, bf16[896,768]{1,0:T(8,128)(2,1)S(1)}, u32[]{:S(2)}) copy-start(bf16[896,768]{1,0:T(8,128)(2,1)S(1)} %collective-permute-done.19) | copy-start | bytes 4128772
  (7 other events, 6.9 us)
Sparse Core Ops, SparseCore 0:
  23.9 41.1 reduce-scatter.3
  131.9 60.7 reduce-scatter.5
  238.3 52.9 reduce-scatter.7
  320.3 45.0 all-gather.3
  398.0 50.5 all-gather.5

commit v5 on v4

--- a/solution.py
+++ b/solution.py
@@ -51,58 +51,66 @@
     return pl.BlockSpec(memory_space=pltpu.SMEM)
 
 
-def store_rows(out, block, left, right):
-    half = right.shape[0] // 2
-    for part in (slice(0, half), slice(half, 2 * half)):
-        out[block, :, part] = dot_rows(left[...], right[part, :]).astype(out.dtype)
-
-
-def near_kernel(x, l1, r1, out):
-    store_rows(out, 0, x, l1)
-    store_rows(out, 1, x, r1)
-    store_rows(out, 2, r1, l1)
-    store_rows(out, 3, l1, r1)
-
-
-def corner_kernel(place, l1, r1, early, out):
-    on_one = jnp.logical_and(place[0] == 1, place[1] == 0)
-    on_two = jnp.logical_and(place[0] == 2, place[1] == 1)
-
-    @pl.when(on_one)
-    def _():
-        store_rows(out, 0, r1, early)
-        store_rows(out, 1, early, r1)
-
-    @pl.when(on_two)
-    def _():
-        store_rows(out, 0, early, l1)
-        store_rows(out, 1, l1, early)
-
-    @pl.when(jnp.logical_not(jnp.logical_or(on_one, on_two)))
-    def _():
-        out[...] = jnp.zeros_like(out)
-
-
-def gram_call(kernel, count, operands, scalar):
-    rows, depth = operands[0].shape
-    first = [] if scalar is None else [scalar]
-    return pl.pallas_call(
-        kernel,
-        out_shape=jax.ShapeDtypeStruct((count, rows, rows), jnp.bfloat16),
-        in_specs=[scalars()] * len(first) + [whole()] * len(operands),
+def near_kernel(x, l1, r1, out, both):
+    rows = x.shape[0]
+    both[:rows, :] = x[...]
+    for place, one, other in ((0, l1, r1), (1, r1, l1)):
+        both[rows:, :] = other[...]
+        for part in (slice(0, rows // 2), slice(rows // 2, rows)):
+            value = dot_rows(both[...], one[part, :]).astype(out.dtype)
+            out[place, :, part] = value[:rows]
+            out[place + 2, :, part] = value[rows:]
+
+
+def near_blocks(x, l1, r1):
+    rows, depth = x.shape
+    return pl.pallas_call(
+        near_kernel,
+        out_shape=jax.ShapeDtypeStruct((4, rows, rows), jnp.bfloat16),
+        in_specs=[whole()] * 3,
+        out_specs=whole(),
+        scratch_shapes=[pltpu.VMEM((2 * rows, depth), jnp.bfloat16)],
+        compiler_params=pltpu.CompilerParams(vmem_limit_bytes=52 * 2**20),
+        cost_estimate=pl.CostEstimate(
+            flops=8 * rows * rows * depth, bytes_accessed=6 * rows * depth, transcendentals=0
+        ),
+    )(x, l1, r1)
+
+
+def corner_kernel(place, l1, r1, l2, r2, out):
+    rows = l1.shape[0]
+    out[...] = jnp.zeros_like(out)
+    for plane, one, other in ((1, r1, l2), (2, l1, r2)):
+
+        @pl.when(place[0] == plane)
+        def _(one=one, other=other):
+            for part in (slice(0, rows // 2), slice(rows // 2, rows)):
+                out[0, :, part] = dot_rows(one[...], other[part, :]).astype(out.dtype)
+
+
+def corner_block(place, l1, r1, l2, r2):
+    rows, depth = l1.shape
+    return pl.pallas_call(
+        corner_kernel,
+        out_shape=jax.ShapeDtypeStruct((1, rows, rows), jnp.bfloat16),
+        in_specs=[scalars()] + [whole()] * 4,
         out_specs=whole(),
         compiler_params=pltpu.CompilerParams(vmem_limit_bytes=48 * 2**20),
         cost_estimate=pl.CostEstimate(
-            flops=2 * count * rows * rows * depth, bytes_accessed=6 * rows * depth, transcendentals=0
-        ),
-    )(*first, *operands)
-
-
-def square_kernel(place, panel, own, l1, r3, l2, r2, r1, l3, corner, out):
+            flops=128 * rows * rows * depth, bytes_accessed=8 * rows * depth, transcendentals=0
+        ),
+    )(place, l1, r1, l2, r2)
+
+
+def square_kernel(place, panel, own, l1, r3, l2, r2, r1, l3, corner, pair, end, last, out):
     z = place[0]
     part = own.shape[1]
     rows = panel.shape[1]
-    low, high = corner[0], corner[1]
+    at_end = jnp.logical_or(z == 0, z == 3)
+    near = jnp.where(at_end, end[0], corner[0])
+    far = jnp.where(at_end, last[0], pair[0])
+    low = jnp.where(z < 2, near, far)
+    high = jnp.where(z < 2, far, near)
     zero = jnp.zeros_like(low)
 
     def strip(e, block):
@@ -143,14 +151,14 @@
     )(place, panel, *others)
 
 
-def product_kernel(starts, place, f, x, l1, r1, early, late, *rest):
+def product_kernel(starts, place, f, x, l1, r1, l2, r2, *rest):
     n_piece = len(starts) - 1
     far = [rest[p : 2 * n_piece : n_piece] for p in range(n_piece)]
     out, wide = rest[-2:]
     n_col, part, width = x.shape
     step = pl.program_id(0)
     wide[:, :part, :] = x[...]
-    wide[:, 2 * part : 3 * part, :] = early[...] + late[...]
+    wide[:, 2 * part : 3 * part, :] = l2[...] + r2[...]
     for p in range(n_piece):
 
         @pl.when(jnp.logical_and(step >= starts[p], step < starts[p + 1]))
@@ -212,67 +220,54 @@
 
 
 def per_device_line(n_col, x):
-    z, c = lax.axis_index("row"), lax.axis_index("col")
-    place = jnp.stack([z, c % 2]).astype(jnp.int32)
+    z = lax.axis_index("row")
+    place = z.reshape(1).astype(jnp.int32)
     right, left = [(0, 1), (1, 2), (2, 3)], [(3, 2), (2, 1), (1, 0)]
 
     def send(value, pairs):
         return lax.ppermute(value, "row", pairs)
 
-    def send_cores(value, even, odd):
-        pairs = [
-            (a * n_col + i, b * n_col + i)
-            for i in range(n_col)
-            for a, b in (odd if i % 2 else even)
-        ]
-        return lax.ppermute(value, ("row", "col"), pairs)
-
     def scatter(blocks):
         return lax.psum_scatter(blocks, "col", scatter_dimension=1, tiled=True)
 
-    r1 = send(x, right)
-    l1 = send(x, left)
-    early = send_cores(jnp.where(c % 2 == 0, l1, r1), left[1:], right[1:])
-    late = send_cores(jnp.where(c % 2 == 0, r1, l1), right[1:], left[1:])
-
+    r1, l1 = send(x, right), send(x, left)
     own = scatter(dot_rows(x, x).astype(jnp.bfloat16)[None])
-    own, near_l, near_r = lax.optimization_barrier((own, l1, r1))
-    blocks = gram_call(near_kernel, 4, [x, near_l, near_r], None)
-    first = scatter(blocks)
-    blocks, early_now = lax.optimization_barrier((blocks, early))
-    corner = gram_call(corner_kernel, 2, [l1, r1, early_now], place)
+    own, r1, l1 = lax.optimization_barrier((own, r1, l1))
+    r2, l2 = send(r1, right[1:]), send(l1, left[1:])
+
+    first = scatter(near_blocks(x, l1, r1))
+    corner = corner_block(place, l1, r1, l2, r2)
     corner, first = lax.optimization_barrier((corner, first))
     corner = scatter(corner)
 
-    first, late = lax.optimization_barrier((first, late))
     second = send(first[2], left[1:]) + send(first[3], right[1:])
     tile = jnp.stack([own[0], first[0], second, first[1]])
     tr1, tl1 = send(tile, right), send(tile, left)
 
     corner, tr1, tl1 = lax.optimization_barrier((corner, tr1, tl1))
-    corner = corner + send(corner, [(1, 2), (2, 1)])
-    corner = corner + send(corner, [(1, 0), (2, 3)])
-    zero = jnp.zeros_like(corner[0])
-    added = jnp.stack(
-        [zero, jnp.where(z == 3, corner[1], zero), zero, jnp.where(z == 0, corner[0], zero)]
-    )
-    panel = lax.all_gather(tile + added, "col", axis=1, tiled=True)
-
+    end = send(corner, [(1, 0), (2, 3)])
+    pair = send(corner, [(1, 2), (2, 1)])
+    zero = jnp.zeros_like(end)
+    added = [zero, jnp.where(z == 3, end, zero), zero, jnp.where(z == 0, end, zero)]
+    panel = lax.all_gather(tile + jnp.concatenate(added), "col", axis=1, tiled=True)
+
+    end, pair, tr1, tl1 = lax.optimization_barrier((end, pair, tr1, tl1))
+    last = send(pair, [(1, 0), (2, 3)])
     tr2, tl2 = send(tr1, right[1:]), send(tl1, left[1:])
     tr3, tl3 = send(tr2, right[2:]), send(tl2, left[2:])
     unit = 256
     marks = [0, 2 * unit, 5 * unit, x.shape[1]]
     pieces = [slice(a, b) for a, b in zip(marks, marks[1:])]
-    tr3, tl3, early_on, late_on = lax.optimization_barrier((tr3, tl3, early, late))
+    tr3, tl3, last, on_r, on_l = lax.optimization_barrier((tr3, tl3, last, r2, l2))
     far = [
-        [send_cores(early_on[:, piece], left[2:], right[2:]) for piece in pieces],
-        [send_cores(late_on[:, piece], right[2:], left[2:]) for piece in pieces],
+        [send(on_r[:, piece], right[2:]) for piece in pieces],
+        [send(on_l[:, piece], left[2:]) for piece in pieces],
     ]
     panel, far[0][0], far[1][0] = lax.optimization_barrier((panel, far[0][0], far[1][0]))
 
-    factor = square(place, panel, tile, tl1, tr3, tl2, tr2, tr1, tl3, corner)
+    factor = square(place, panel, tile, tl1, tr3, tl2, tr2, tr1, tl3, corner, pair, end, last)
     factor = lax.all_gather(factor, "col", axis=0, tiled=False)
-    near = [x, l1, r1, early, late]
+    near = [x, l1, r1, l2, r2]
     out = product(place, factor, near, [part[:2] for part in far], unit, 0, None)
     return product(place, factor, near, [part[2:] for part in far], unit, marks[2] // unit, out)
 

time: 492 us -> 446 us (0.907)
  waiting for transfers between devices: 331 us -> 291 us
  other arithmetic: 10.7 us -> 1.31 us
    ppermute x8 -> x0, waiting for transfers between devices: 137 us -> none  [send_cores(): return lax.ppermute(value, ('row', 'col'), pairs)]
    ppermute x12 -> x21, waiting for transfers between devices: 121 us -> 234 us  [send(): return lax.ppermute(value, 'row', pairs)]
    ppermute x12 -> x21, starting transfers between devices: 22.2 us -> 37 us  [send(): return lax.ppermute(value, 'row', pairs)]
    reduce_scatter x3, waiting for transfers between devices: 60.2 us -> 47.1 us  [scatter(): return lax.psum_scatter(blocks, 'col', scatter_dimension=1, tiled=True)]
    ppermute x8 -> x0, starting transfers between devices: 11.4 us -> none  [send_cores(): return lax.ppermute(value, ('row', 'col'), pairs)]
    select_n x2 -> x1, other arithmetic: 6.16 us -> 0.04 us  [per_device_line(): jnp.where(z == 3, end, zero)]
    unnamed x28 -> x24, local copies, waits for them, and re-layouts: 11.3 us -> 9.25 us
  transfers between devices with their start and end apart: 25 -> 26, of which waited for: 15 -> 15; matrix products, arithmetic and copies ran while one was open for 5% -> 5% of each run, Pallas kernels for 5% -> 11%
where the time goes in v5:
time: 446 us; the launch traced here: 445 us
  waiting for transfers between devices  291 us (65%)
  Pallas kernels  73.1 us (16%)
  starting transfers between devices  37.2 us (8%)
  local copies, waits for them, and re-layouts  20.7 us (5%)
  between operations  13.4 us (3%)
  matrix products  9.03 us (2%)
    ppermute x21, waiting for transfers between devices, send(): return lax.ppermute(value, 'row', pairs)  234 us
    reduce_scatter x3, waiting for transfers between devices, scatter(): return lax.psum_scatter(blocks, 'col', scatter_dimension=1, tiled=True)  47.1 us
    ppermute x21, starting transfers between devices, send(): return lax.ppermute(value, 'row', pairs)  37 us
    pallas_call x2, Pallas kernels, product(): pl.pallas_call(functools.partial(product_kernel, tuple(starts)), grid=(st...  32 us
    pallas_call x1, Pallas kernels, near_blocks(): pl.pallas_call(near_kernel, out_shape=jax.ShapeDtypeStruct((4, rows, rows...  25 us
    all_gather x1, waiting for transfers between devices, per_device_line(): factor = lax.all_gather(factor, 'col', axis=0, tiled=False)  9.64 us
    unnamed x24, local copies, waits for them, and re-layouts  9.25 us
    dot_general x1, matrix products, dot_rows(): lax.dot_general(left, right, (((1,), (1,)), ((), ())), preferred_element_...  9.03 us
  transfers between devices with their start and end apart: 26, of which 15 were waited for; matrix products, arithmetic and copies ran while one was open for 5% of the time, Pallas kernels for 11%

profile of v5, /device:TPU:0, one launch (start us, length us, event | category | flops | bytes accessed | tf_op | source)
XLA Modules:
  0.0 445.3 jit_solution(14260183629381142643)
XLA Ops:
  7.8 7.5 %collective-permute-start = (bf16[896,2304]{1,0:T(8,128)(2,1)}, bf16[896,2304]{1,0:T(8,128)(2,1)}, u32[]{:S(2)}, u32[]{:S(2)}) collective-permute-start(bf16[896,2304]{1,0:T(8,128)(2,1)} %x.1), channel_id=1, source_target_pairs={{0,8},{8,16},{16,24},{1,9},{9,17},{17,25},{2,10},{10,18},{18,26},{... | collective-permute-start | bytes 12386312 | tf_op jit(solution)/shard_map/ppermute | solution.py:228
  15.3 9.0 %fusion = bf16[1,896,896]{2,1,0:T(8,128)(2,1)} fusion(bf16[896,2304]{1,0:T(8,128)(2,1)} %x.1), kind=kOutput, calls=%fused_computation.1 | convolution fusion | flops 3700178944 | bytes 5734400 | tf_op jit(solution)/shard_map/dot_general | solution.py:20
  24.4 39.6 %reduce-scatter.4.cloned.1.call-done = bf16[1,112,896]{2,1,0:T(8,128)(2,1)} async-done(((bf16[1,896,896]{2,1,0:T(8,128)(2,1)}), bf16[1,112,896]{2,1,0:T(8,128)(2,1)}) %reduce-scatter.4.cloned.1.call-update) | async-done | bytes 200720 | tf_op jit(solution)/shard_map/reduce_scatter | solution.py:231
  64.0 36.9 %collective-permute-done.1.l1 = bf16[896,2304]{1,0:T(8,128)(2,1)} collective-permute-done((bf16[896,2304]{1,0:T(8,128)(2,1)}, bf16[896,2304]{1,0:T(8,128)(2,1)}, u32[]{:S(2)}, u32[]{:S(2)}) %collective-permute-start.1) | collective-permute-done | bytes 4128800 | tf_op jit(solution)/shard_map/ppermute | solution.py:228
  103.4 2.6 collective-permute-start.3
  106.0 25.0 %shard_map.18 = bf16[4,896,896]{2,1,0:T(8,128)(2,1)} custom-call(bf16[896,2304]{1,0:T(8,128)(2,1)} %x.1, bf16[896,2304]{1,0:T(8,128)(2,1)} %collective-permute-done.1.l1, bf16[896,2304]{1,0:T(8,128)(2,1)} %collective-permute-done.r1), custom_call_target="tpu_custom_call" | custom-call | flops 14797504512 | bytes 12386304 | tf_op jit(solution)/shard_map/pallas_call | solution.py:67
  131.1 64.0 %collective-permute-done.2.l2 = bf16[896,2304]{1,0:T(8,128)(2,1)} collective-permute-done((bf16[896,2304]{1,0:T(8,128)(2,1)}, bf16[896,2304]{1,0:T(8,128)(2,1)}, u32[]{:S(2)}, u32[]{:S(2)}) %collective-permute-start.2) | collective-permute-done | bytes 4128800 | tf_op jit(solution)/shard_map/ppermute | solution.py:228
  195.1 7.2 %shard_map.17 = bf16[1,896,896]{2,1,0:T(8,128)(2,1)} custom-call(s32[1]{0:T(128)} %bitcast.place, bf16[896,2304]{1,0:T(8,128)(2,1)} %collective-permute-done.1.l1, bf16[896,2304]{1,0:T(8,128)(2,1)} %collective-permute-done.r1, bf16[896,2304]{1,0:T(8,128)(2,1)} %collective-permute-done.2.l2, bf16[896,2304]{1,0:T(8,128)(2,1)} %collective-permute-done.3.r2), custom_call_target="tpu_custom_call" | custom-call | flops 236760072192 | bytes 16515072 | tf_op jit(solution)/shard_map/pallas_call | solution.py:93
  202.4 1.3 fusion.1
  204.4 1.3 collective-permute-start.4
  205.7 17.3 %collective-permute-done.4 = bf16[112,896]{1,0:T(8,128)(2,1)S(1)} collective-permute-done((bf16[112,896]{1,0:T(8,128)(2,1)S(1)}, bf16[112,896]{1,0:T(8,128)(2,1)S(1)}, u32[]{:S(2)}, u32[]{:S(2)}) %collective-permute-start.4) | collective-permute-done | bytes 200736 | tf_op jit(solution)/shard_map/ppermute | solution.py:228
  224.5 4.6 %collective-permute-start.6 = (bf16[4,112,896]{2,1,0:T(8,128)(2,1)S(1)}, bf16[4,112,896]{2,1,0:T(8,128)(2,1)S(1)}, u32[]{:S(2)}, u32[]{:S(2)}) collective-permute-start(bf16[4,112,896]{2,1,0:T(8,128)(2,1)S(1)} %pad_maximum_fusion.own), channel_id=1, source_target_pairs={{0,8},{8,16},{16,24},{1,9},{9,17},{17,25},{2,10},{10,18},{18,26},{... | collective-permute-start | bytes 2408456 | tf_op jit(solution)/shard_map/ppermute | solution.py:228
  229.1 12.4 %collective-permute-done.7.l1 = bf16[4,112,896]{2,1,0:T(8,128)(2,1)S(1)} collective-permute-done((bf16[4,112,896]{2,1,0:T(8,128)(2,1)S(1)}, bf16[4,112,896]{2,1,0:T(8,128)(2,1)S(1)}, u32[]{:S(2)}, u32[]{:S(2)}) %collective-permute-start.7) | collective-permute-done | bytes 802848 | tf_op jit(solution)/shard_map/ppermute | solution.py:228
  242.7 7.5 %reduce-scatter.8.cloned.1.call-done.corner = bf16[1,112,896]{2,1,0:T(8,128)(2,1)} async-done(((bf16[1,896,896]{2,1,0:T(8,128)(2,1)}), bf16[1,112,896]{2,1,0:T(8,128)(2,1)}) %reduce-scatter.8.cloned.1.call-update) | async-done | bytes 200720 | tf_op jit(solution)/shard_map/reduce_scatter | solution.py:231
  251.5 7.5 %collective-permute-done.8.end = bf16[1,112,896]{2,1,0:T(8,128)(2,1)S(1)} collective-permute-done((bf16[1,112,896]{2,1,0:T(8,128)(2,1)}, bf16[1,112,896]{2,1,0:T(8,128)(2,1)S(1)}, u32[]{:S(2)}, u32[]{:S(2)}) %collective-permute-start.8) | collective-permute-done | bytes 200736 | tf_op jit(solution)/shard_map/ppermute | solution.py:228
  263.7 26.3 %collective-permute-done.12.l2 = bf16[4,112,896]{2,1,0:T(8,128)(2,1)S(1)} collective-permute-done((bf16[4,112,896]{2,1,0:T(8,128)(2,1)S(1)}, bf16[4,112,896]{2,1,0:T(8,128)(2,1)S(1)}, u32[]{:S(2)}, u32[]{:S(2)}) %collective-permute-start.12) | collective-permute-done | bytes 802848 | tf_op jit(solution)/shard_map/ppermute | solution.py:228
  294.2 18.9 %collective-permute-done.14.last = bf16[1,112,896]{2,1,0:T(8,128)(2,1)S(1)} collective-permute-done((bf16[1,112,896]{2,1,0:T(8,128)(2,1)S(1)}, bf16[1,112,896]{2,1,0:T(8,128)(2,1)S(1)}, u32[]{:S(2)}, u32[]{:S(2)}) %collective-permute-start.14) | collective-permute-done | bytes 200736 | tf_op jit(solution)/shard_map/ppermute | solution.py:228
  317.2 1.3 collective-permute-start.16
  318.5 1.6 collective-permute-start.15
  320.1 17.5 %collective-permute-done.16 = bf16[896,512]{1,0:T(8,128)(2,1)S(1)} collective-permute-done((bf16[896,512]{1,0:T(8,128)(2,1)S(1)}, bf16[896,512]{1,0:T(8,128)(2,1)S(1)}, u32[]{:S(2)}, u32[]{:S(2)}) %collective-permute-start.16) | collective-permute-done | bytes 917536 | tf_op jit(solution)/shard_map/ppermute | solution.py:228
  343.7 8.9 %shard_map.19 = bf16[896,448]{1,0:T(8,128)(2,1)} custom-call(s32[1]{0:T(128)} %bitcast.place, bf16[4,896,896]{2,1,0:T(8,128)(2,1)} %all-gather.4.cloned.1.call-done.panel, bf16[4,112,896]{2,1,0:T(8,128)(2,1)S(1)} %pad_maximum_fusion.own, bf16[4,112,896]{2,1,0:T(8,128)(2,1)S(1)} %collective-permute-done.7.l1, bf16[4,112,896]{2,1,0:T(8,128)(2,1)S(1)} %copy-done.3, ...), custom_call_target="tpu_custom_call" | custom-call | flops 2877292544 | bytes 8028160 | tf_op jit(solution)/shard_map/pallas_call | solution.py:142
  352.6 1.4 slice.38
  354.0 1.4 slice.39
  356.7 1.7 collective-permute-start.19
  358.5 1.9 slice.36
  360.4 2.9 slice.37
  364.6 2.0 collective-permute-start.17
  366.6 23.9 %collective-permute-done.20 = bf16[896,768]{1,0:T(8,128)(2,1)S(1)} collective-permute-done((bf16[896,768]{1,0:T(8,128)(2,1)S(1)}, bf16[896,768]{1,0:T(8,128)(2,1)S(1)}, u32[]{:S(2)}, u32[]{:S(2)}) %collective-permute-start.20) | collective-permute-done | bytes 1376288 | tf_op jit(solution)/shard_map/ppermute | solution.py:228
  390.4 9.6 %all-gather.6.cloned.1.call-done = bf16[7168,448]{1,0:T(8,128)(2,1)} async-done(((bf16[896,448]{1,0:T(8,128)(2,1)}), bf16[7168,448]{1,0:T(8,128)(2,1)}) %all-gather.6.cloned.1.call-update) | async-done | bytes 6422544 | tf_op jit(solution)/shard_map/all_gather | solution.py:269
  400.1 17.5 %shard_map.20.rest_2_ = bf16[896,2304]{1,0:T(8,128)(2,1)} custom-call(s32[1]{0:T(128)} %bitcast.place, bf16[8,896,448]{2,1,0:T(8,128)(2,1)} %bitcast.23, bf16[8,112,2304]{2,1,0:T(8,128)(2,1)} %bitcast.25, bf16[8,112,2304]{2,1,0:T(8,128)(2,1)} %bitcast.7.l1, bf16[8,112,2304]{2,1,0:T(8,128)(2,1)} %bitcast.8.r1, bf16[8,112,2304]{2,1,0:T(8,128)(2,1)} %bitcast.9.l2, ...), custom_call_target="tpu_custom_call" | custom-call | flops 8220835840 | bytes 27525120 | tf_op jit(solution)/shard_map/pallas_call | solution.py:207
  417.5 6.7 %collective-permute-done.18 = bf16[896,1024]{1,0:T(8,128)(2,1)} collective-permute-done((bf16[896,1024]{1,0:T(8,128)(2,1)}, bf16[896,1024]{1,0:T(8,128)(2,1)}, u32[]{:S(2)}, u32[]{:S(2)}) %collective-permute-start.18) | collective-permute-done | bytes 1835040 | tf_op jit(solution)/shard_map/ppermute | solution.py:228
  424.2 14.5 %shard_map.21 = bf16[896,2304]{1,0:T(8,128)(2,1)} custom-call(s32[1]{0:T(128)} %bitcast.place, bf16[8,896,448]{2,1,0:T(8,128)(2,1)} %bitcast.24, bf16[8,112,2304]{2,1,0:T(8,128)(2,1)} %bitcast.26, bf16[8,112,2304]{2,1,0:T(8,128)(2,1)} %bitcast.7.l1, bf16[8,112,2304]{2,1,0:T(8,128)(2,1)} %bitcast.8.r1, ...), custom_call_target="tpu_custom_call", output_to_operand_aliasing={{}: (9, {})} | custom-call | flops 6576668672 | bytes 22020096 | tf_op jit(solution)/shard_map/pallas_call | solution.py:207
  (67 shorter events, 30.0 us)
Async XLA Ops:
  6.5 57.5 %reduce-scatter.4.cloned.1.call-start = ((), (), s32[]{:S(2)}) async-start(), calls=%async_computation.3 | async-start | bytes 1806336 | tf_op jit(solution)/shard_map/reduce_scatter | solution.py:231
  6.5 94.4 %collective-permute-start.1 = (bf16[896,2304]{1,0:T(8,128)(2,1)}, bf16[896,2304]{1,0:T(8,128)(2,1)}, u32[]{:S(2)}, u32[]{:S(2)}) collective-permute-start(bf16[896,2304]{1,0:T(8,128)(2,1)} %x.1), channel_id=1, source_target_pairs={{24,16},{16,8},{8,0},{25,17},{17,9},{9,1},{26,18},{18,10},{10,2},{... | collective-permute-start | bytes 12386312 | tf_op jit(solution)/shard_map/ppermute | solution.py:228
  7.8 94.3 %collective-permute-start = (bf16[896,2304]{1,0:T(8,128)(2,1)}, bf16[896,2304]{1,0:T(8,128)(2,1)}, u32[]{:S(2)}, u32[]{:S(2)}) collective-permute-start(bf16[896,2304]{1,0:T(8,128)(2,1)} %x.1), channel_id=1, source_target_pairs={{0,8},{8,16},{16,24},{1,9},{9,17},{17,25},{2,10},{10,18},{18,26},{... | collective-permute-start | bytes 12386312 | tf_op jit(solution)/shard_map/ppermute | solution.py:228
  24.4 178.0 %reduce-scatter.6.cloned.1.call-start = ((), (), s32[]{:S(2)}) async-start(), calls=%async_computation.4 | async-start | bytes 7225344 | tf_op jit(solution)/shard_map/reduce_scatter | solution.py:231
  102.1 93.0 %collective-permute-start.2 = (bf16[896,2304]{1,0:T(8,128)(2,1)}, bf16[896,2304]{1,0:T(8,128)(2,1)}, u32[]{:S(2)}, u32[]{:S(2)}) collective-permute-start(bf16[896,2304]{1,0:T(8,128)(2,1)} %collective-permute-done.1.l1), channel_id=1, source_target_pairs={{16,8},{8,0},{17,9},{9,1},{18,10},{10,2},{19,11},{11,3},{20,12},{1... | collective-permute-start | bytes 12386312 | tf_op jit(solution)/shard_map/ppermute | solution.py:228
  103.4 91.7 %collective-permute-start.3 = (bf16[896,2304]{1,0:T(8,128)(2,1)}, bf16[896,2304]{1,0:T(8,128)(2,1)}, u32[]{:S(2)}, u32[]{:S(2)}) collective-permute-start(bf16[896,2304]{1,0:T(8,128)(2,1)} %collective-permute-done.r1), channel_id=1, source_target_pairs={{8,16},{16,24},{9,17},{17,25},{10,18},{18,26},{11,19},{19,27},{12,... | collective-permute-start | bytes 12386312 | tf_op jit(solution)/shard_map/ppermute | solution.py:228
  131.0 119.1 %reduce-scatter.8.cloned.1.call-start = ((), (), s32[]{:S(2)}) async-start(), calls=%async_computation.5 | async-start | bytes 1806336 | tf_op jit(solution)/shard_map/reduce_scatter | solution.py:231
  195.1 28.0 %copy-start.11 = (bf16[1,112,896]{2,1,0:T(8,128)(2,1)S(1)}, bf16[1,112,896]{2,1,0:T(8,128)(2,1)}, u32[]{:S(2)}) copy-start(bf16[1,112,896]{2,1,0:T(8,128)(2,1)} %reduce-scatter.4.cloned.1.call-done) | copy-start | bytes 602116
  202.4 136.2 %all-gather.4.cloned.1.call-start = ((), (), s32[]{:S(2)}) async-start(), calls=%async_computation.6 | async-start | bytes 7225344 | tf_op jit(solution)/shard_map/all_gather | solution.py:252
  203.7 2.0 collective-permute-start.5
  204.4 18.6 %collective-permute-start.4 = (bf16[112,896]{1,0:T(8,128)(2,1)S(1)}, bf16[112,896]{1,0:T(8,128)(2,1)S(1)}, u32[]{:S(2)}, u32[]{:S(2)}) collective-permute-start(bf16[112,896]{1,0:T(8,128)(2,1)S(1)} %get-tuple-element.48), channel_id=1, source_target_pairs={{16,8},{8,0},{17,9},{9,1},{18,10},{10,2},{19,11},{11,3},{20,12},{1... | collective-permute-start | bytes 602120 | tf_op jit(solution)/shard_map/ppermute | solution.py:228
  223.2 18.3 %collective-permute-start.7 = (bf16[4,112,896]{2,1,0:T(8,128)(2,1)S(1)}, bf16[4,112,896]{2,1,0:T(8,128)(2,1)S(1)}, u32[]{:S(2)}, u32[]{:S(2)}) collective-permute-start(bf16[4,112,896]{2,1,0:T(8,128)(2,1)S(1)} %pad_maximum_fusion.own), channel_id=1, source_target_pairs={{24,16},{16,8},{8,0},{25,17},{17,9},{9,1},{26,18},{18,10},{10,2},{... | collective-permute-start | bytes 2408456 | tf_op jit(solution)/shard_map/ppermute | solution.py:228
  224.5 18.2 %collective-permute-start.6 = (bf16[4,112,896]{2,1,0:T(8,128)(2,1)S(1)}, bf16[4,112,896]{2,1,0:T(8,128)(2,1)S(1)}, u32[]{:S(2)}, u32[]{:S(2)}) collective-permute-start(bf16[4,112,896]{2,1,0:T(8,128)(2,1)S(1)} %pad_maximum_fusion.own), channel_id=1, source_target_pairs={{0,8},{8,16},{16,24},{1,9},{9,17},{17,25},{2,10},{10,18},{18,26},{... | collective-permute-start | bytes 2408456 | tf_op jit(solution)/shard_map/ppermute | solution.py:228
  250.2 8.8 %collective-permute-start.8 = (bf16[1,112,896]{2,1,0:T(8,128)(2,1)}, bf16[1,112,896]{2,1,0:T(8,128)(2,1)S(1)}, u32[]{:S(2)}, u32[]{:S(2)}) collective-permute-start(bf16[1,112,896]{2,1,0:T(8,128)(2,1)} %reduce-scatter.8.cloned.1.call-done.corner), channel_id=1, source_target_pairs={{8,0},{16,24},{9,1},{17,25},{10,2},{18,26},{11,3},{19,27},{12,4},{... | collective-permute-start | bytes 602120 | tf_op jit(solution)/shard_map/ppermute | solution.py:228
  260.2 139.9 %all-gather.6.cloned.1.call-start = ((), (), s32[]{:S(2)}) async-start(), calls=%async_computation.7 | async-start | bytes 8257536 | tf_op jit(solution)/shard_map/all_gather | solution.py:269
  260.3 0.7 collective-permute-start.9
  260.9 2.0 collective-permute-start.10
  261.7 28.3 %collective-permute-start.12 = (bf16[4,112,896]{2,1,0:T(8,128)(2,1)S(1)}, bf16[4,112,896]{2,1,0:T(8,128)(2,1)S(1)}, u32[]{:S(2)}, u32[]{:S(2)}) collective-permute-start(bf16[4,112,896]{2,1,0:T(8,128)(2,1)S(1)} %collective-permute-done.7.l1), channel_id=1, source_target_pairs={{16,8},{8,0},{17,9},{9,1},{18,10},{10,2},{19,11},{11,3},{20,12},{1... | collective-permute-start | bytes 2408456 | tf_op jit(solution)/shard_map/ppermute | solution.py:228
  263.0 50.8 %collective-permute-start.11 = (bf16[4,112,896]{2,1,0:T(8,128)(2,1)S(1)}, bf16[4,112,896]{2,1,0:T(8,128)(2,1)S(1)}, u32[]{:S(2)}, u32[]{:S(2)}) collective-permute-start(bf16[4,112,896]{2,1,0:T(8,128)(2,1)S(1)} %collective-permute-done.10.r2), channel_id=1, source_target_pairs={{16,24},{17,25},{18,26},{19,27},{20,28},{21,29},{22,30},{23,31}} | collective-permute-start | bytes 2408456 | tf_op jit(solution)/shard_map/ppermute | solution.py:228
  290.0 24.8 %collective-permute-start.13 = (bf16[4,112,896]{2,1,0:T(8,128)(2,1)S(1)}, bf16[4,112,896]{2,1,0:T(8,128)(2,1)}, u32[]{:S(2)}, u32[]{:S(2)}) collective-permute-start(bf16[4,112,896]{2,1,0:T(8,128)(2,1)S(1)} %collective-permute-done.12.l2), channel_id=1, source_target_pairs={{8,0},{9,1},{10,2},{11,3},{12,4},{13,5},{14,6},{15,7}} | collective-permute-start | bytes 2408456 | tf_op jit(solution)/shard_map/ppermute | solution.py:228
  291.3 0.9 copy-start
  292.2 20.9 %collective-permute-start.14 = (bf16[1,112,896]{2,1,0:T(8,128)(2,1)S(1)}, bf16[1,112,896]{2,1,0:T(8,128)(2,1)S(1)}, u32[]{:S(2)}, u32[]{:S(2)}) collective-permute-start(bf16[1,112,896]{2,1,0:T(8,128)(2,1)S(1)} %collective-permute-done.9.pair), channel_id=1, source_target_pairs={{8,0},{16,24},{9,1},{17,25},{10,2},{18,26},{11,3},{19,27},{12,4},{... | collective-permute-start | bytes 602120 | tf_op jit(solution)/shard_map/ppermute | solution.py:228
  313.8 1.0 copy-start.2
  317.2 20.5 %collective-permute-start.16 = (bf16[896,512]{1,0:T(8,128)(2,1)S(1)}, bf16[896,512]{1,0:T(8,128)(2,1)S(1)}, u32[]{:S(2)}, u32[]{:S(2)}) collective-permute-start(bf16[896,512]{1,0:T(8,128)(2,1)S(1)} %slice.35), channel_id=1, source_target_pairs={{8,0},{9,1},{10,2},{11,3},{12,4},{13,5},{14,6},{15,7}} | collective-permute-start | bytes 2752520 | tf_op jit(solution)/shard_map/ppermute | solution.py:228
  318.5 20.1 %collective-permute-start.15 = (bf16[896,512]{1,0:T(8,128)(2,1)S(1)}, bf16[896,512]{1,0:T(8,128)(2,1)}, u32[]{:S(2)}, u32[]{:S(2)}) collective-permute-start(bf16[896,512]{1,0:T(8,128)(2,1)S(1)} %slice.34), channel_id=1, source_target_pairs={{16,24},{17,25},{18,26},{19,27},{20,28},{21,29},{22,30},{23,31}} | collective-permute-start | bytes 2752520 | tf_op jit(solution)/shard_map/ppermute | solution.py:228
  338.6 1.1 copy-start.1
  339.7 1.1 copy-start.3
  355.4 35.0 %collective-permute-start.20 = (bf16[896,768]{1,0:T(8,128)(2,1)S(1)}, bf16[896,768]{1,0:T(8,128)(2,1)S(1)}, u32[]{:S(2)}, u32[]{:S(2)}) collective-permute-start(bf16[896,768]{1,0:T(8,128)(2,1)S(1)} %slice.39), channel_id=1, source_target_pairs={{8,0},{9,1},{10,2},{11,3},{12,4},{13,5},{14,6},{15,7}} | collective-permute-start | bytes 4128776 | tf_op jit(solution)/shard_map/ppermute | solution.py:228
  356.7 33.7 %collective-permute-start.19 = (bf16[896,768]{1,0:T(8,128)(2,1)S(1)}, bf16[896,768]{1,0:T(8,128)(2,1)}, u32[]{:S(2)}, u32[]{:S(2)}) collective-permute-start(bf16[896,768]{1,0:T(8,128)(2,1)S(1)} %slice.38), channel_id=1, source_target_pairs={{16,24},{17,25},{18,26},{19,27},{20,28},{21,29},{22,30},{23,31}} | collective-permute-start | bytes 4128776 | tf_op jit(solution)/shard_map/ppermute | solution.py:228
  363.3 60.9 %collective-permute-start.18 = (bf16[896,1024]{1,0:T(8,128)(2,1)}, bf16[896,1024]{1,0:T(8,128)(2,1)}, u32[]{:S(2)}, u32[]{:S(2)}) collective-permute-start(bf16[896,1024]{1,0:T(8,128)(2,1)} %slice.37), channel_id=1, source_target_pairs={{8,0},{9,1},{10,2},{11,3},{12,4},{13,5},{14,6},{15,7}} | collective-permute-start | bytes 5505032 | tf_op jit(solution)/shard_map/ppermute | solution.py:228
  364.6 59.6 %collective-permute-start.17 = (bf16[896,1024]{1,0:T(8,128)(2,1)S(1)}, bf16[896,1024]{1,0:T(8,128)(2,1)}, u32[]{:S(2)}, u32[]{:S(2)}) collective-permute-start(bf16[896,1024]{1,0:T(8,128)(2,1)S(1)} %slice.36), channel_id=1, source_target_pairs={{16,24},{17,25},{18,26},{19,27},{20,28},{21,29},{22,30},{23,31}} | collective-permute-start | bytes 5505032 | tf_op jit(solution)/shard_map/ppermute | solution.py:228
  390.4 9.6 %copy-start.9 = (bf16[896,768]{1,0:T(8,128)(2,1)}, bf16[896,768]{1,0:T(8,128)(2,1)S(1)}, u32[]{:S(2)}) copy-start(bf16[896,768]{1,0:T(8,128)(2,1)S(1)} %collective-permute-done.20) | copy-start | bytes 4128772
  (6 other events, 5.1 us)
Sparse Core Ops, SparseCore 0:
  24.5 39.4 reduce-scatter.3
  131.2 68.5 reduce-scatter.5
  203.5 46.5 reduce-scatter.7
  260.3 46.0 all-gather.3
  352.7 47.3 all-gather.5

commit v6 on v5

--- a/solution.py
+++ b/solution.py
@@ -77,15 +77,28 @@
     )(x, l1, r1)
 
 
-def corner_kernel(place, l1, r1, l2, r2, out):
+def corner_kernel(place, l1, r1, l2, r2, out, held, sems):
     rows = l1.shape[0]
-    out[...] = jnp.zeros_like(out)
+    half = rows // 2
     for plane, one, other in ((1, r1, l2), (2, l1, r2)):
 
         @pl.when(place[0] == plane)
         def _(one=one, other=other):
-            for part in (slice(0, rows // 2), slice(rows // 2, rows)):
-                out[0, :, part] = dot_rows(one[...], other[part, :]).astype(out.dtype)
+            copies = [
+                pltpu.make_async_copy(one, held.at[0], sems.at[0]),
+                pltpu.make_async_copy(other.at[:half, :], held.at[1, :half, :], sems.at[1]),
+                pltpu.make_async_copy(other.at[half:, :], held.at[1, half:, :], sems.at[2]),
+            ]
+            for copy in copies:
+                copy.start()
+            copies[0].wait()
+            for part, copy in ((slice(0, half), copies[1]), (slice(half, rows), copies[2])):
+                copy.wait()
+                out[0, :, part] = dot_rows(held[0], held[1, part, :]).astype(out.dtype)
+
+    @pl.when(jnp.logical_or(place[0] == 0, place[0] == 3))
+    def _():
+        out[...] = jnp.zeros_like(out)
 
 
 def corner_block(place, l1, r1, l2, r2):
@@ -93,9 +106,10 @@
     return pl.pallas_call(
         corner_kernel,
         out_shape=jax.ShapeDtypeStruct((1, rows, rows), jnp.bfloat16),
-        in_specs=[scalars()] + [whole()] * 4,
+        in_specs=[scalars()] + [pl.BlockSpec(memory_space=pl.ANY)] * 4,
         out_specs=whole(),
-        compiler_params=pltpu.CompilerParams(vmem_limit_bytes=48 * 2**20),
+        scratch_shapes=[pltpu.VMEM((2, rows, depth), jnp.bfloat16), pltpu.SemaphoreType.DMA((3,))],
+        compiler_params=pltpu.CompilerParams(vmem_limit_bytes=32 * 2**20),
         cost_estimate=pl.CostEstimate(
             flops=128 * rows * rows * depth, bytes_accessed=8 * rows * depth, transcendentals=0
         ),
@@ -151,27 +165,67 @@
     )(place, panel, *others)
 
 
-def product_kernel(starts, place, f, x, l1, r1, l2, r2, *rest):
+def product_kernel(starts, first, place, f, x, l1, r1, l2, r2, *rest):
     n_piece = len(starts) - 1
-    far = [rest[p : 2 * n_piece : n_piece] for p in range(n_piece)]
-    out, wide = rest[-2:]
-    n_col, part, width = x.shape
+    from_r, from_l = rest[:n_piece], rest[n_piece : 2 * n_piece]
+    out, whole_f, wide, sems = rest[-4:]
+    z = place[0]
+    n_col, rows, depth = f.shape
+    part = depth // 4
+    width = out.shape[1]
     step = pl.program_id(0)
-    wide[:, :part, :] = x[...]
-    wide[:, 2 * part : 3 * part, :] = l2[...] + r2[...]
-    for p in range(n_piece):
-
-        @pl.when(jnp.logical_and(step >= starts[p], step < starts[p + 1]))
-        def _(p=p):
-            value = far[p][0][...] + far[p][1][...]
-            zero = jnp.zeros_like(value)
-            wide[:, part : 2 * part, :] = l1[...] + jnp.where(place[0] == 3, value, zero)
-            wide[:, 3 * part :, :] = r1[...] + jnp.where(place[0] == 0, value, zero)
-
-    total = coef_a * x[...].reshape(n_col * part, width).astype(jnp.float32)
-    for c in range(n_col):
-        total = total + jnp.dot(f[c], wide[c], preferred_element_type=jnp.float32)
-    out[...] = (math.sqrt(N) * total).astype(out.dtype)
+
+    def copy(source, tile, slot, d):
+        return pltpu.make_async_copy(
+            source.at[:, :, pl.ds(pl.multiple_of(tile * width, width), width)],
+            wide.at[slot, :, pl.ds(d * part, part), :],
+            sems.at[slot, d],
+        )
+
+    def fetch(tile, slot):
+        copy(x, first + tile, slot, 0).start()
+        for d, usual, edge, pieces in ((1, l1, 3, from_r), (3, r1, 0, from_l)):
+
+            @pl.when(z != edge)
+            def _(d=d, usual=usual):
+                copy(usual, first + tile, slot, d).start()
+
+            for p in range(n_piece):
+                inside = jnp.logical_and(tile >= starts[p], tile < starts[p + 1])
+
+                @pl.when(jnp.logical_and(z == edge, inside))
+                def _(d=d, piece=pieces[p], begin=starts[p]):
+                    copy(piece, tile - begin, slot, d).start()
+
+        @pl.when(z < 2)
+        def _():
+            copy(l2, first + tile, slot, 2).start()
+
+        @pl.when(z >= 2)
+        def _():
+            copy(r2, first + tile, slot, 2).start()
+
+    slot = lax.rem(step, 2)
+
+    @pl.when(step == 0)
+    def _():
+        fetch(0, 0)
+        for c in range(n_col):
+            whole_f[:, c * depth : (c + 1) * depth] = f[c]
+
+    @pl.when(step + 1 < starts[-1])
+    def _():
+        fetch(step + 1, 1 - slot)
+
+    for d in range(4):
+        copy(x, first + step, slot, d).wait()
+    total = jnp.dot(
+        whole_f[...],
+        wide[slot].reshape(n_col * depth, width),
+        preferred_element_type=jnp.float32,
+    )
+    own = wide[slot, :, :part, :].reshape(rows, width).astype(jnp.float32)
+    out[...] = (math.sqrt(N) * (coef_a * own + total)).astype(out.dtype)
 
 
 def product(place, f, near, far, tile, first, before):
@@ -186,35 +240,32 @@
     for piece in far[0]:
         starts.append(starts[-1] + piece.shape[1] // tile)
 
-    def piece_spec(p):
-        begin, count = starts[p], starts[p + 1] - starts[p]
-        return pl.BlockSpec((n_col, part, tile), lambda i: (0, 0, jnp.clip(i - begin, 0, count - 1)))
-
-    plain = pl.BlockSpec((n_col, part, tile), lambda i: (0, 0, i + first))
-    pieces = [piece_spec(p) for p in range(len(far[0]))]
+    outside = pl.BlockSpec(memory_space=pl.ANY)
     operands = [place, f, *(split(value) for value in (*near, *far[0], *far[1]))]
-    in_specs = [
-        scalars(),
-        pl.BlockSpec((n_col, rows, depth), lambda i: (0, 0, 0), pipeline_mode=pl.Buffered(1)),
-    ]
-    in_specs += [plain] * len(near) + pieces * 2
     aliases = {}
     if before is not None:
         aliases = {len(operands): 0}
         operands.append(before)
-        in_specs.append(pl.BlockSpec(memory_space=pl.ANY))
     share = tile * starts[-1]
     return pl.pallas_call(
-        functools.partial(product_kernel, tuple(starts)),
+        functools.partial(product_kernel, tuple(starts), first),
         grid=(starts[-1],),
         out_shape=jax.ShapeDtypeStruct((rows, columns), jnp.bfloat16),
-        in_specs=in_specs,
+        in_specs=[
+            scalars(),
+            pl.BlockSpec((n_col, rows, depth), lambda i: (0, 0, 0), pipeline_mode=pl.Buffered(1)),
+        ]
+        + [outside] * (len(operands) - 2),
         out_specs=pl.BlockSpec((rows, tile), lambda i: (0, i + first)),
-        scratch_shapes=[pltpu.VMEM((n_col, depth, tile), jnp.bfloat16)],
+        scratch_shapes=[
+            pltpu.VMEM((rows, n_col * depth), jnp.bfloat16),
+            pltpu.VMEM((2, n_col, depth, tile), jnp.bfloat16),
+            pltpu.SemaphoreType.DMA((2, 4)),
+        ],
         input_output_aliases=aliases,
-        compiler_params=pltpu.CompilerParams(vmem_limit_bytes=56 * 2**20),
+        compiler_params=pltpu.CompilerParams(vmem_limit_bytes=48 * 2**20),
         cost_estimate=pl.CostEstimate(
-            flops=2 * rows * n_col * depth * share, bytes_accessed=2 * 12 * rows * share, transcendentals=0
+            flops=2 * rows * n_col * depth * share, bytes_accessed=2 * 6 * rows * share, transcendentals=0
         ),
     )(*operands)
 
@@ -251,19 +302,23 @@
     added = [zero, jnp.where(z == 3, end, zero), zero, jnp.where(z == 0, end, zero)]
     panel = lax.all_gather(tile + jnp.concatenate(added), "col", axis=1, tiled=True)
 
-    end, pair, tr1, tl1 = lax.optimization_barrier((end, pair, tr1, tl1))
+    end, tr1, tl1 = lax.optimization_barrier((end, tr1, tl1))
     last = send(pair, [(1, 0), (2, 3)])
     tr2, tl2 = send(tr1, right[1:]), send(tl1, left[1:])
     tr3, tl3 = send(tr2, right[2:]), send(tl2, left[2:])
     unit = 256
-    marks = [0, 2 * unit, 5 * unit, x.shape[1]]
+    marks = [0, unit, 4 * unit, x.shape[1]]
     pieces = [slice(a, b) for a, b in zip(marks, marks[1:])]
-    tr3, tl3, last, on_r, on_l = lax.optimization_barrier((tr3, tl3, last, r2, l2))
-    far = [
-        [send(on_r[:, piece], right[2:]) for piece in pieces],
-        [send(on_l[:, piece], left[2:]) for piece in pieces],
-    ]
-    panel, far[0][0], far[1][0] = lax.optimization_barrier((panel, far[0][0], far[1][0]))
+    tr3, tl3, on_r, on_l = lax.optimization_barrier((tr3, tl3, r2, l2))
+    from_r, from_l = [], []
+    for piece in pieces:
+        from_r.append(send(on_r[:, piece], right[2:]))
+        from_l.append(send(on_l[:, piece], left[2:]))
+        from_r[-1], from_l[-1], on_r, on_l = lax.optimization_barrier(
+            (from_r[-1], from_l[-1], on_r, on_l)
+        )
+    panel, from_r[0], from_l[0] = lax.optimization_barrier((panel, from_r[0], from_l[0]))
+    far = [from_r, from_l]
 
     factor = square(place, panel, tile, tl1, tr3, tl2, tr2, tr1, tl3, corner, pair, end, last)
     factor = lax.all_gather(factor, "col", axis=0, tiled=False)

time: 446 us -> 458 us (1.027)
  waiting for transfers between devices: 291 us -> 313 us
  Pallas kernels: 73.1 us -> 63 us
    ppermute x21, waiting for transfers between devices: 234 us -> 262 us  [send(): return lax.ppermute(value, 'row', pairs)]
    all_gather x1, waiting for transfers between devices: 9.64 us -> 0.01 us  [per_device_line(): factor = lax.all_gather(factor, 'col', axis=0, tiled=False)]
    pallas_call x1, Pallas kernels: 7.25 us -> 1.3 us  [corner_block(): pl.pallas_call(corner_kernel, out_shape=jax.ShapeDtypeStruct((1, rows, ro...]
    unnamed x24 -> x32, local copies, waits for them, and re-layouts: 9.25 us -> 13 us
  transfers between devices with their start and end apart: 26 -> 26, of which waited for: 15 -> 16; matrix products, arithmetic and copies ran while one was open for 5% -> 4% of each run, Pallas kernels for 11% -> 6%
where the time goes in v6:
time: 458 us; the launch traced here: 457 us
  waiting for transfers between devices  313 us (68%)
  Pallas kernels  63 us (14%)
  starting transfers between devices  35.1 us (8%)
  local copies, waits for them, and re-layouts  22.9 us (5%)
  between operations  13.4 us (3%)
  matrix products  9.03 us (2%)
    ppermute x21, waiting for transfers between devices, send(): return lax.ppermute(value, 'row', pairs)  262 us
    reduce_scatter x3, waiting for transfers between devices, scatter(): return lax.psum_scatter(blocks, 'col', scatter_dimension=1, tiled=True)  50.3 us
    ppermute x21, starting transfers between devices, send(): return lax.ppermute(value, 'row', pairs)  35 us
    pallas_call x2, Pallas kernels, product(): pl.pallas_call(functools.partial(product_kernel, tuple(starts), first), g...  27.8 us
    pallas_call x1, Pallas kernels, near_blocks(): pl.pallas_call(near_kernel, out_shape=jax.ShapeDtypeStruct((4, rows, rows...  25 us
    unnamed x32, local copies, waits for them, and re-layouts  13 us
  transfers between devices with their start and end apart: 26, of which 16 were waited for; matrix products, arithmetic and copies ran while one was open for 4% of the time, Pallas kernels for 6%

profile of v6, /device:TPU:0, one launch (start us, length us, event | category | flops | bytes accessed | tf_op | source)
XLA Modules:
  0.0 457.4 jit_solution(136542286570555303)
XLA Ops:
  7.8 7.5 %collective-permute-start = (bf16[896,2304]{1,0:T(8,128)(2,1)}, bf16[896,2304]{1,0:T(8,128)(2,1)}, u32[]{:S(2)}, u32[]{:S(2)}) collective-permute-start(bf16[896,2304]{1,0:T(8,128)(2,1)} %x.1), channel_id=1, source_target_pairs={{0,8},{8,16},{16,24},{1,9},{9,17},{17,25},{2,10},{10,18},{18,26},{... | collective-permute-start | bytes 12386312 | tf_op jit(solution)/shard_map/ppermute | solution.py:279
  15.3 9.0 %fusion = bf16[1,896,896]{2,1,0:T(8,128)(2,1)} fusion(bf16[896,2304]{1,0:T(8,128)(2,1)} %x.1), kind=kOutput, calls=%fused_computation.1 | convolution fusion | flops 3700178944 | bytes 5734400 | tf_op jit(solution)/shard_map/dot_general | solution.py:20
  24.4 39.6 %reduce-scatter.4.cloned.1.call-done = bf16[1,112,896]{2,1,0:T(8,128)(2,1)} async-done(((bf16[1,896,896]{2,1,0:T(8,128)(2,1)}), bf16[1,112,896]{2,1,0:T(8,128)(2,1)}) %reduce-scatter.4.cloned.1.call-update) | async-done | bytes 200720 | tf_op jit(solution)/shard_map/reduce_scatter | solution.py:282
  64.0 36.9 %collective-permute-done.1.l1 = bf16[896,2304]{1,0:T(8,128)(2,1)} collective-permute-done((bf16[896,2304]{1,0:T(8,128)(2,1)}, bf16[896,2304]{1,0:T(8,128)(2,1)}, u32[]{:S(2)}, u32[]{:S(2)}) %collective-permute-start.1) | collective-permute-done | bytes 4128800 | tf_op jit(solution)/shard_map/ppermute | solution.py:279
  103.4 2.6 collective-permute-start.3
  106.0 25.0 %shard_map.18 = bf16[4,896,896]{2,1,0:T(8,128)(2,1)} custom-call(bf16[896,2304]{1,0:T(8,128)(2,1)} %x.1, bf16[896,2304]{1,0:T(8,128)(2,1)} %collective-permute-done.1.l1, bf16[896,2304]{1,0:T(8,128)(2,1)} %collective-permute-done.r1), custom_call_target="tpu_custom_call" | custom-call | flops 14797504512 | bytes 12386304 | tf_op jit(solution)/shard_map/pallas_call | solution.py:67
  131.1 64.0 %collective-permute-done.2.l2 = bf16[896,2304]{1,0:T(8,128)(2,1)} collective-permute-done((bf16[896,2304]{1,0:T(8,128)(2,1)}, bf16[896,2304]{1,0:T(8,128)(2,1)}, u32[]{:S(2)}, u32[]{:S(2)}) %collective-permute-start.2) | collective-permute-done | bytes 4128800 | tf_op jit(solution)/shard_map/ppermute | solution.py:279
  196.4 3.3 reduce-scatter.6.cloned.1.call-done
  203.0 17.2 %collective-permute-done.4 = bf16[112,896]{1,0:T(8,128)(2,1)S(1)} collective-permute-done((bf16[112,896]{1,0:T(8,128)(2,1)S(1)}, bf16[112,896]{1,0:T(8,128)(2,1)S(1)}, u32[]{:S(2)}, u32[]{:S(2)}) %collective-permute-start.4) | collective-permute-done | bytes 200736 | tf_op jit(solution)/shard_map/ppermute | solution.py:279
  221.7 4.6 %collective-permute-start.6 = (bf16[4,112,896]{2,1,0:T(8,128)(2,1)S(1)}, bf16[4,112,896]{2,1,0:T(8,128)(2,1)S(1)}, u32[]{:S(2)}, u32[]{:S(2)}) collective-permute-start(bf16[4,112,896]{2,1,0:T(8,128)(2,1)S(1)} %pad_maximum_fusion.own), channel_id=1, source_target_pairs={{0,8},{8,16},{16,24},{1,9},{9,17},{17,25},{2,10},{10,18},{18,26},{... | collective-permute-start | bytes 2408456 | tf_op jit(solution)/shard_map/ppermute | solution.py:279
  226.3 12.4 %collective-permute-done.7.l1 = bf16[4,112,896]{2,1,0:T(8,128)(2,1)S(1)} collective-permute-done((bf16[4,112,896]{2,1,0:T(8,128)(2,1)S(1)}, bf16[4,112,896]{2,1,0:T(8,128)(2,1)S(1)}, u32[]{:S(2)}, u32[]{:S(2)}) %collective-permute-start.7) | collective-permute-done | bytes 802848 | tf_op jit(solution)/shard_map/ppermute | solution.py:279
  239.9 7.5 %reduce-scatter.8.cloned.1.call-done.corner = bf16[1,112,896]{2,1,0:T(8,128)(2,1)} async-done(((bf16[1,896,896]{2,1,0:T(8,128)(2,1)}), bf16[1,112,896]{2,1,0:T(8,128)(2,1)}) %reduce-scatter.8.cloned.1.call-update) | async-done | bytes 200720 | tf_op jit(solution)/shard_map/reduce_scatter | solution.py:282
  248.6 7.5 %collective-permute-done.8.end = bf16[1,112,896]{2,1,0:T(8,128)(2,1)S(1)} collective-permute-done((bf16[1,112,896]{2,1,0:T(8,128)(2,1)}, bf16[1,112,896]{2,1,0:T(8,128)(2,1)S(1)}, u32[]{:S(2)}, u32[]{:S(2)}) %collective-permute-start.8) | collective-permute-done | bytes 200736 | tf_op jit(solution)/shard_map/ppermute | solution.py:279
  260.2 19.9 %collective-permute-done.11.l2 = bf16[4,112,896]{2,1,0:T(8,128)(2,1)S(1)} collective-permute-done((bf16[4,112,896]{2,1,0:T(8,128)(2,1)S(1)}, bf16[4,112,896]{2,1,0:T(8,128)(2,1)S(1)}, u32[]{:S(2)}, u32[]{:S(2)}) %collective-permute-start.11) | collective-permute-done | bytes 802848 | tf_op jit(solution)/shard_map/ppermute | solution.py:279
  283.3 16.6 %collective-permute-done.12.l3 = bf16[4,112,896]{2,1,0:T(8,128)(2,1)} collective-permute-done((bf16[4,112,896]{2,1,0:T(8,128)(2,1)S(1)}, bf16[4,112,896]{2,1,0:T(8,128)(2,1)}, u32[]{:S(2)}, u32[]{:S(2)}) %collective-permute-start.12) | collective-permute-done | bytes 802848 | tf_op jit(solution)/shard_map/ppermute | solution.py:279
  304.1 1.3 collective-permute-start.15
  305.4 1.5 collective-permute-start.16
  307.0 7.3 %collective-permute-done.14 = bf16[896,256]{1,0:T(8,128)(2,1)S(1)} collective-permute-done((bf16[896,256]{1,0:T(8,128)(2,1)S(1)}, bf16[896,256]{1,0:T(8,128)(2,1)S(1)}, u32[]{:S(2)}, u32[]{:S(2)}) %collective-permute-start.14) | collective-permute-done | bytes 458784 | tf_op jit(solution)/shard_map/ppermute | solution.py:279
  315.9 4.1 collective-permute-done.16.last
  323.1 9.0 %shard_map.19 = bf16[896,448]{1,0:T(8,128)(2,1)} custom-call(s32[1]{0:T(128)} %bitcast.place, bf16[4,896,896]{2,1,0:T(8,128)(2,1)} %all-gather.4.cloned.1.call-done.panel, bf16[4,112,896]{2,1,0:T(8,128)(2,1)S(1)} %pad_maximum_fusion.own, bf16[4,112,896]{2,1,0:T(8,128)(2,1)S(1)} %collective-permute-done.7.l1, bf16[4,112,896]{2,1,0:T(8,128)(2,1)S(1)} %copy-done.9, ...), custom_call_target="tpu_custom_call" | custom-call | flops 2877292544 | bytes 8028160 | tf_op jit(solution)/shard_map/pallas_call | solution.py:156
  332.1 1.4 slice.36
  333.5 1.4 slice.37
  335.0 1.4 collective-permute-start.18
  337.2 27.6 %collective-permute-done.18 = bf16[896,768]{1,0:T(8,128)(2,1)S(1)} collective-permute-done((bf16[896,768]{1,0:T(8,128)(2,1)S(1)}, bf16[896,768]{1,0:T(8,128)(2,1)S(1)}, u32[]{:S(2)}, u32[]{:S(2)}) %collective-permute-start.18) | collective-permute-done | bytes 1376288 | tf_op jit(solution)/shard_map/ppermute | solution.py:279
  366.9 1.8 slice.38
  368.8 1.8 slice.39
  372.7 46.3 %collective-permute-done.20 = bf16[896,1280]{1,0:T(8,128)(2,1)S(1)} collective-permute-done((bf16[896,1280]{1,0:T(8,128)(2,1)S(1)}, bf16[896,1280]{1,0:T(8,128)(2,1)S(1)}, u32[]{:S(2)}, u32[]{:S(2)}) %collective-permute-start.20) | collective-permute-done | bytes 2293792 | tf_op jit(solution)/shard_map/ppermute | solution.py:279
  419.0 1.4 copy-done
  420.4 1.3 copy-done.3
  421.7 1.3 copy-done.5
  423.1 13.0 %shard_map.20.rest_2_ = bf16[896,2304]{1,0:T(8,128)(2,1)} custom-call(s32[1]{0:T(128)} %bitcast.place, bf16[8,896,448]{2,1,0:T(8,128)(2,1)} %bitcast.29, bf16[8,112,2304]{2,1,0:T(8,128)(2,1)} %bitcast.31, bf16[8,112,2304]{2,1,0:T(8,128)(2,1)} %bitcast.7.l1, bf16[8,112,2304]{2,1,0:T(8,128)(2,1)} %bitcast.8.r1, bf16[8,112,2304]{2,1,0:T(8,128)(2,1)} %bitcast.9.l2, ...), custom_call_target="tpu_custom_call" | custom-call | flops 6576668672 | bytes 11010048 | tf_op jit(solution)/shard_map/pallas_call | solution.py:250
  436.1 14.8 %shard_map.21 = bf16[896,2304]{1,0:T(8,128)(2,1)} custom-call(s32[1]{0:T(128)} %bitcast.place, bf16[8,896,448]{2,1,0:T(8,128)(2,1)} %bitcast.30, bf16[8,112,2304]{2,1,0:T(8,128)(2,1)} %bitcast.32, bf16[8,112,2304]{2,1,0:T(8,128)(2,1)} %bitcast.7.l1, bf16[8,112,2304]{2,1,0:T(8,128)(2,1)} %bitcast.8.r1, ...), custom_call_target="tpu_custom_call", output_to_operand_aliasing={{}: (9, {})} | custom-call | flops 8220835840 | bytes 13762560 | tf_op jit(solution)/shard_map/pallas_call | solution.py:250
  (75 shorter events, 33.4 us)
Async XLA Ops:
  6.5 57.5 %reduce-scatter.4.cloned.1.call-start = ((), (), s32[]{:S(2)}) async-start(), calls=%async_computation.3 | async-start | bytes 1806336 | tf_op jit(solution)/shard_map/reduce_scatter | solution.py:282
  6.5 94.4 %collective-permute-start.1 = (bf16[896,2304]{1,0:T(8,128)(2,1)}, bf16[896,2304]{1,0:T(8,128)(2,1)}, u32[]{:S(2)}, u32[]{:S(2)}) collective-permute-start(bf16[896,2304]{1,0:T(8,128)(2,1)} %x.1), channel_id=1, source_target_pairs={{24,16},{16,8},{8,0},{25,17},{17,9},{9,1},{26,18},{18,10},{10,2},{... | collective-permute-start | bytes 12386312 | tf_op jit(solution)/shard_map/ppermute | solution.py:279
  7.8 94.3 %collective-permute-start = (bf16[896,2304]{1,0:T(8,128)(2,1)}, bf16[896,2304]{1,0:T(8,128)(2,1)}, u32[]{:S(2)}, u32[]{:S(2)}) collective-permute-start(bf16[896,2304]{1,0:T(8,128)(2,1)} %x.1), channel_id=1, source_target_pairs={{0,8},{8,16},{16,24},{1,9},{9,17},{17,25},{2,10},{10,18},{18,26},{... | collective-permute-start | bytes 12386312 | tf_op jit(solution)/shard_map/ppermute | solution.py:279
  24.4 175.3 %reduce-scatter.6.cloned.1.call-start = ((), (), s32[]{:S(2)}) async-start(), calls=%async_computation.4 | async-start | bytes 7225344 | tf_op jit(solution)/shard_map/reduce_scatter | solution.py:282
  102.1 93.0 %collective-permute-start.2 = (bf16[896,2304]{1,0:T(8,128)(2,1)}, bf16[896,2304]{1,0:T(8,128)(2,1)}, u32[]{:S(2)}, u32[]{:S(2)}) collective-permute-start(bf16[896,2304]{1,0:T(8,128)(2,1)} %collective-permute-done.1.l1), channel_id=1, source_target_pairs={{16,8},{8,0},{17,9},{9,1},{18,10},{10,2},{19,11},{11,3},{20,12},{1... | collective-permute-start | bytes 12386312 | tf_op jit(solution)/shard_map/ppermute | solution.py:279
  103.4 91.7 %collective-permute-start.3 = (bf16[896,2304]{1,0:T(8,128)(2,1)}, bf16[896,2304]{1,0:T(8,128)(2,1)}, u32[]{:S(2)}, u32[]{:S(2)}) collective-permute-start(bf16[896,2304]{1,0:T(8,128)(2,1)} %collective-permute-done.r1), channel_id=1, source_target_pairs={{8,16},{16,24},{9,17},{17,25},{10,18},{18,26},{11,19},{19,27},{12,... | collective-permute-start | bytes 12386312 | tf_op jit(solution)/shard_map/ppermute | solution.py:279
  131.0 116.3 %reduce-scatter.8.cloned.1.call-start = ((), (), s32[]{:S(2)}) async-start(), calls=%async_computation.5 | async-start | bytes 1806336 | tf_op jit(solution)/shard_map/reduce_scatter | solution.py:282
  195.1 25.1 %copy-start.15 = (bf16[1,112,896]{2,1,0:T(8,128)(2,1)S(1)}, bf16[1,112,896]{2,1,0:T(8,128)(2,1)}, u32[]{:S(2)}) copy-start(bf16[1,112,896]{2,1,0:T(8,128)(2,1)} %reduce-scatter.4.cloned.1.call-done) | copy-start | bytes 602116
  199.7 116.2 %all-gather.4.cloned.1.call-start = ((), (), s32[]{:S(2)}) async-start(), calls=%async_computation.6 | async-start | bytes 7225344 | tf_op jit(solution)/shard_map/all_gather | solution.py:303
  201.1 2.0 collective-permute-start.5
  201.7 18.5 %collective-permute-start.4 = (bf16[112,896]{1,0:T(8,128)(2,1)S(1)}, bf16[112,896]{1,0:T(8,128)(2,1)S(1)}, u32[]{:S(2)}, u32[]{:S(2)}) collective-permute-start(bf16[112,896]{1,0:T(8,128)(2,1)S(1)} %get-tuple-element.64), channel_id=1, source_target_pairs={{16,8},{8,0},{17,9},{9,1},{18,10},{10,2},{19,11},{11,3},{20,12},{1... | collective-permute-start | bytes 602120 | tf_op jit(solution)/shard_map/ppermute | solution.py:279
  220.4 18.3 %collective-permute-start.7 = (bf16[4,112,896]{2,1,0:T(8,128)(2,1)S(1)}, bf16[4,112,896]{2,1,0:T(8,128)(2,1)S(1)}, u32[]{:S(2)}, u32[]{:S(2)}) collective-permute-start(bf16[4,112,896]{2,1,0:T(8,128)(2,1)S(1)} %pad_maximum_fusion.own), channel_id=1, source_target_pairs={{24,16},{16,8},{8,0},{25,17},{17,9},{9,1},{26,18},{18,10},{10,2},{... | collective-permute-start | bytes 2408456 | tf_op jit(solution)/shard_map/ppermute | solution.py:279
  221.7 18.2 %collective-permute-start.6 = (bf16[4,112,896]{2,1,0:T(8,128)(2,1)S(1)}, bf16[4,112,896]{2,1,0:T(8,128)(2,1)S(1)}, u32[]{:S(2)}, u32[]{:S(2)}) collective-permute-start(bf16[4,112,896]{2,1,0:T(8,128)(2,1)S(1)} %pad_maximum_fusion.own), channel_id=1, source_target_pairs={{0,8},{8,16},{16,24},{1,9},{9,17},{17,25},{2,10},{10,18},{18,26},{... | collective-permute-start | bytes 2408456 | tf_op jit(solution)/shard_map/ppermute | solution.py:279
  247.3 8.8 %collective-permute-start.8 = (bf16[1,112,896]{2,1,0:T(8,128)(2,1)}, bf16[1,112,896]{2,1,0:T(8,128)(2,1)S(1)}, u32[]{:S(2)}, u32[]{:S(2)}) collective-permute-start(bf16[1,112,896]{2,1,0:T(8,128)(2,1)} %reduce-scatter.8.cloned.1.call-done.corner), channel_id=1, source_target_pairs={{8,0},{16,24},{9,1},{17,25},{10,2},{18,26},{11,3},{19,27},{12,4},{... | collective-permute-start | bytes 602120 | tf_op jit(solution)/shard_map/ppermute | solution.py:279
  257.4 163.0 %all-gather.6.cloned.1.call-start = ((), (), s32[]{:S(2)}) async-start(), calls=%async_computation.7 | async-start | bytes 8257536 | tf_op jit(solution)/shard_map/all_gather | solution.py:324
  257.4 2.0 collective-permute-start.9
  258.2 22.0 %collective-permute-start.11 = (bf16[4,112,896]{2,1,0:T(8,128)(2,1)S(1)}, bf16[4,112,896]{2,1,0:T(8,128)(2,1)S(1)}, u32[]{:S(2)}, u32[]{:S(2)}) collective-permute-start(bf16[4,112,896]{2,1,0:T(8,128)(2,1)S(1)} %collective-permute-done.7.l1), channel_id=1, source_target_pairs={{16,8},{8,0},{17,9},{9,1},{18,10},{10,2},{19,11},{11,3},{20,12},{1... | collective-permute-start | bytes 2408456 | tf_op jit(solution)/shard_map/ppermute | solution.py:279
  259.5 22.9 %collective-permute-start.10 = (bf16[4,112,896]{2,1,0:T(8,128)(2,1)S(1)}, bf16[4,112,896]{2,1,0:T(8,128)(2,1)S(1)}, u32[]{:S(2)}, u32[]{:S(2)}) collective-permute-start(bf16[4,112,896]{2,1,0:T(8,128)(2,1)S(1)} %collective-permute-done.9.r2), channel_id=1, source_target_pairs={{16,24},{17,25},{18,26},{19,27},{20,28},{21,29},{22,30},{23,31}} | collective-permute-start | bytes 2408456 | tf_op jit(solution)/shard_map/ppermute | solution.py:279
  280.1 19.8 %collective-permute-start.12 = (bf16[4,112,896]{2,1,0:T(8,128)(2,1)S(1)}, bf16[4,112,896]{2,1,0:T(8,128)(2,1)}, u32[]{:S(2)}, u32[]{:S(2)}) collective-permute-start(bf16[4,112,896]{2,1,0:T(8,128)(2,1)S(1)} %collective-permute-done.11.l2), channel_id=1, source_target_pairs={{8,0},{9,1},{10,2},{11,3},{12,4},{13,5},{14,6},{15,7}} | collective-permute-start | bytes 2408456 | tf_op jit(solution)/shard_map/ppermute | solution.py:279
  302.1 12.2 %collective-permute-start.14 = (bf16[896,256]{1,0:T(8,128)(2,1)S(1)}, bf16[896,256]{1,0:T(8,128)(2,1)S(1)}, u32[]{:S(2)}, u32[]{:S(2)}) collective-permute-start(bf16[896,256]{1,0:T(8,128)(2,1)S(1)} %slice.35), channel_id=1, source_target_pairs={{8,0},{9,1},{10,2},{11,3},{12,4},{13,5},{14,6},{15,7}} | collective-permute-start | bytes 1376264 | tf_op jit(solution)/shard_map/ppermute | solution.py:279
  303.4 11.7 %collective-permute-start.13 = (bf16[896,256]{1,0:T(8,128)(2,1)S(1)}, bf16[896,256]{1,0:T(8,128)(2,1)S(1)}, u32[]{:S(2)}, u32[]{:S(2)}) collective-permute-start(bf16[896,256]{1,0:T(8,128)(2,1)S(1)} %slice.34), channel_id=1, source_target_pairs={{16,24},{17,25},{18,26},{19,27},{20,28},{21,29},{22,30},{23,31}} | collective-permute-start | bytes 1376264 | tf_op jit(solution)/shard_map/ppermute | solution.py:279
  304.1 1.3 collective-permute-start.15
  305.4 14.5 %collective-permute-start.16 = (bf16[1,112,896]{2,1,0:T(8,128)(2,1)}, bf16[1,112,896]{2,1,0:T(8,128)(2,1)}, u32[]{:S(2)}, u32[]{:S(2)}) collective-permute-start(bf16[1,112,896]{2,1,0:T(8,128)(2,1)} %collective-permute-done.15.pair), channel_id=1, source_target_pairs={{8,0},{16,24},{9,1},{17,25},{10,2},{18,26},{11,3},{19,27},{12,4},{... | collective-permute-start | bytes 602120 | tf_op jit(solution)/shard_map/ppermute | solution.py:279
  335.0 85.4 %copy-start.11 = (bf16[896,256]{1,0:T(8,128)(2,1)S(1)}, bf16[896,256]{1,0:T(8,128)(2,1)}, u32[]{:S(2)}) copy-start(bf16[896,256]{1,0:T(8,128)(2,1)} %copy-done.10) | copy-start | bytes 1376260
  335.0 85.4 %copy-start.13 = (bf16[896,256]{1,0:T(8,128)(2,1)S(1)}, bf16[896,256]{1,0:T(8,128)(2,1)}, u32[]{:S(2)}) copy-start(bf16[896,256]{1,0:T(8,128)(2,1)} %copy-done.12) | copy-start | bytes 1376260
  335.0 29.8 %collective-permute-start.18 = (bf16[896,768]{1,0:T(8,128)(2,1)S(1)}, bf16[896,768]{1,0:T(8,128)(2,1)S(1)}, u32[]{:S(2)}, u32[]{:S(2)}) collective-permute-start(bf16[896,768]{1,0:T(8,128)(2,1)S(1)} %slice.37), channel_id=1, source_target_pairs={{8,0},{9,1},{10,2},{11,3},{12,4},{13,5},{14,6},{15,7}} | collective-permute-start | bytes 4128776 | tf_op jit(solution)/shard_map/ppermute | solution.py:279
  336.4 29.4 %collective-permute-start.17 = (bf16[896,768]{1,0:T(8,128)(2,1)S(1)}, bf16[896,768]{1,0:T(8,128)(2,1)S(1)}, u32[]{:S(2)}, u32[]{:S(2)}) collective-permute-start(bf16[896,768]{1,0:T(8,128)(2,1)S(1)} %slice.36), channel_id=1, source_target_pairs={{16,24},{17,25},{18,26},{19,27},{20,28},{21,29},{22,30},{23,31}} | collective-permute-start | bytes 4128776 | tf_op jit(solution)/shard_map/ppermute | solution.py:279
  370.6 48.4 %collective-permute-start.20 = (bf16[896,1280]{1,0:T(8,128)(2,1)S(1)}, bf16[896,1280]{1,0:T(8,128)(2,1)S(1)}, u32[]{:S(2)}, u32[]{:S(2)}) collective-permute-start(bf16[896,1280]{1,0:T(8,128)(2,1)S(1)} %slice.39), channel_id=1, source_target_pairs={{8,0},{9,1},{10,2},{11,3},{12,4},{13,5},{14,6},{15,7}} | collective-permute-start | bytes 6881288 | tf_op jit(solution)/shard_map/ppermute | solution.py:279
  371.9 47.1 %collective-permute-start.19 = (bf16[896,1280]{1,0:T(8,128)(2,1)S(1)}, bf16[896,1280]{1,0:T(8,128)(2,1)S(1)}, u32[]{:S(2)}, u32[]{:S(2)}) collective-permute-start(bf16[896,1280]{1,0:T(8,128)(2,1)S(1)} %slice.38), channel_id=1, source_target_pairs={{16,24},{17,25},{18,26},{19,27},{20,28},{21,29},{22,30},{23,31}} | collective-permute-start | bytes 6881288 | tf_op jit(solution)/shard_map/ppermute | solution.py:279
  419.0 1.4 copy-start
  420.4 1.3 copy-start.3
  423.1 13.0 %copy-start.1 = (bf16[896,1280]{1,0:T(8,128)(2,1)S(1)}, bf16[896,1280]{1,0:T(8,128)(2,1)}, u32[]{:S(2)}) copy-start(bf16[896,1280]{1,0:T(8,128)(2,1)} %copy-done) | copy-start | bytes 6881284
  (10 other events, 10.2 us)
Sparse Core Ops, SparseCore 0:
  24.5 39.4 reduce-scatter.3
  131.2 68.4 reduce-scatter.5
  203.5 43.7 reduce-scatter.7
  257.5 46.0 all-gather.3
  332.2 48.8 all-gather.5

commit v7 on v6

--- a/solution.py
+++ b/solution.py
@@ -116,13 +116,26 @@
     )(place, l1, r1, l2, r2)
 
 
-def square_kernel(place, panel, own, l1, r3, l2, r2, r1, l3, corner, pair, end, last, out):
+def square_kernel(place, panel, own, l1, r3, l2, r2, r1, l3, corner, pair, end, out, last):
     z = place[0]
     part = own.shape[1]
     rows = panel.shape[1]
     at_end = jnp.logical_or(z == 0, z == 3)
+    for plane, block in ((0, 3), (3, 1)):
+
+        @pl.when(z == plane)
+        def _(block=block):
+            index = lax.broadcasted_iota(jnp.int32, (part, rows), 0) + place[1] * part
+            other = lax.broadcasted_iota(jnp.int32, (part, rows), 1)
+            pick = jnp.where(index == other, 1.0, 0.0).astype(jnp.bfloat16)
+            last[...] = dot_rows(pick, panel[block]).astype(last.dtype)
+
+    @pl.when(jnp.logical_not(at_end))
+    def _():
+        last[...] = pair[0]
+
     near = jnp.where(at_end, end[0], corner[0])
-    far = jnp.where(at_end, last[0], pair[0])
+    far = last[...]
     low = jnp.where(z < 2, near, far)
     high = jnp.where(z < 2, far, near)
     zero = jnp.zeros_like(low)
@@ -158,6 +171,7 @@
         out_shape=jax.ShapeDtypeStruct((rows, 4 * part), jnp.bfloat16),
         in_specs=[scalars()] + [whole()] * (1 + len(others)),
         out_specs=whole(),
+        scratch_shapes=[pltpu.VMEM((part, rows), jnp.bfloat16)],
         compiler_params=pltpu.CompilerParams(vmem_limit_bytes=48 * 2**20),
         cost_estimate=pl.CostEstimate(
             flops=2 * rows * rows * 4 * 4 * part, bytes_accessed=2 * 5 * rows * rows, transcendentals=0
@@ -165,9 +179,9 @@
     )(place, panel, *others)
 
 
-def product_kernel(starts, first, place, f, x, l1, r1, l2, r2, *rest):
+def product_kernel(starts, first, place, f, x, l1, r1, across, *rest):
     n_piece = len(starts) - 1
-    from_r, from_l = rest[:n_piece], rest[n_piece : 2 * n_piece]
+    far = rest[:n_piece]
     out, whole_f, wide, sems = rest[-4:]
     z = place[0]
     n_col, rows, depth = f.shape
@@ -184,7 +198,8 @@
 
     def fetch(tile, slot):
         copy(x, first + tile, slot, 0).start()
-        for d, usual, edge, pieces in ((1, l1, 3, from_r), (3, r1, 0, from_l)):
+        copy(across, first + tile, slot, 2).start()
+        for d, usual, edge in ((1, l1, 3), (3, r1, 0)):
 
             @pl.when(z != edge)
             def _(d=d, usual=usual):
@@ -194,16 +209,8 @@
                 inside = jnp.logical_and(tile >= starts[p], tile < starts[p + 1])
 
                 @pl.when(jnp.logical_and(z == edge, inside))
-                def _(d=d, piece=pieces[p], begin=starts[p]):
+                def _(d=d, piece=far[p], begin=starts[p]):
                     copy(piece, tile - begin, slot, d).start()
-
-        @pl.when(z < 2)
-        def _():
-            copy(l2, first + tile, slot, 2).start()
-
-        @pl.when(z >= 2)
-        def _():
-            copy(r2, first + tile, slot, 2).start()
 
     slot = lax.rem(step, 2)
 
@@ -237,11 +244,11 @@
         return value.reshape(n_col, part, value.shape[1])
 
     starts = [0]
-    for piece in far[0]:
+    for piece in far:
         starts.append(starts[-1] + piece.shape[1] // tile)
 
     outside = pl.BlockSpec(memory_space=pl.ANY)
-    operands = [place, f, *(split(value) for value in (*near, *far[0], *far[1]))]
+    operands = [place, f, *(split(value) for value in (*near, *far))]
     aliases = {}
     if before is not None:
         aliases = {len(operands): 0}
@@ -270,9 +277,25 @@
     )(*operands)
 
 
+def arrived_kernel(value, out):
+    pass
+
+
+def arrived(value):
+    outside = pl.BlockSpec(memory_space=pl.ANY)
+    return pl.pallas_call(
+        arrived_kernel,
+        out_shape=jax.ShapeDtypeStruct(value.shape, value.dtype),
+        in_specs=[outside],
+        out_specs=outside,
+        input_output_aliases={0: 0},
+        cost_estimate=pl.CostEstimate(flops=2 * 10**11, bytes_accessed=0, transcendentals=0),
+    )(value)
+
+
 def per_device_line(n_col, x):
     z = lax.axis_index("row")
-    place = z.reshape(1).astype(jnp.int32)
+    place = jnp.stack([z, lax.axis_index("col")]).astype(jnp.int32)
     right, left = [(0, 1), (1, 2), (2, 3)], [(3, 2), (2, 1), (1, 0)]
 
     def send(value, pairs):
@@ -303,28 +326,20 @@
     panel = lax.all_gather(tile + jnp.concatenate(added), "col", axis=1, tiled=True)
 
     end, tr1, tl1 = lax.optimization_barrier((end, tr1, tl1))
-    last = send(pair, [(1, 0), (2, 3)])
     tr2, tl2 = send(tr1, right[1:]), send(tl1, left[1:])
     tr3, tl3 = send(tr2, right[2:]), send(tl2, left[2:])
     unit = 256
-    marks = [0, unit, 4 * unit, x.shape[1]]
-    pieces = [slice(a, b) for a, b in zip(marks, marks[1:])]
-    tr3, tl3, on_r, on_l = lax.optimization_barrier((tr3, tl3, r2, l2))
-    from_r, from_l = [], []
-    for piece in pieces:
-        from_r.append(send(on_r[:, piece], right[2:]))
-        from_l.append(send(on_l[:, piece], left[2:]))
-        from_r[-1], from_l[-1], on_r, on_l = lax.optimization_barrier(
-            (from_r[-1], from_l[-1], on_r, on_l)
-        )
-    panel, from_r[0], from_l[0] = lax.optimization_barrier((panel, from_r[0], from_l[0]))
-    far = [from_r, from_l]
-
-    factor = square(place, panel, tile, tl1, tr3, tl2, tr2, tr1, tl3, corner, pair, end, last)
+    marks = [0, x.shape[1] - 2 * unit, x.shape[1]]
+    across = l2 + r2
+    tr3, tl3, onward = lax.optimization_barrier((tr3, tl3, across))
+    far = [send(onward[:, a:b], [(1, 0), (2, 3)]) for a, b in zip(marks, marks[1:])]
+    far[0] = arrived(far[0])
+
+    factor = square(place, panel, tile, tl1, tr3, tl2, tr2, tr1, tl3, corner, pair, end)
     factor = lax.all_gather(factor, "col", axis=0, tiled=False)
-    near = [x, l1, r1, l2, r2]
-    out = product(place, factor, near, [part[:2] for part in far], unit, 0, None)
-    return product(place, factor, near, [part[2:] for part in far], unit, marks[2] // unit, out)
+    near = [x, l1, r1, across]
+    out = product(place, factor, near, far[:1], unit, 0, None)
+    return product(place, factor, near, far[1:], unit, marks[1] // unit, out)
 
 
 def solution(mesh):

time: 458 us -> 414 us (0.904)
  waiting for transfers between devices: 313 us -> 279 us
  local copies, waits for them, and re-layouts: 22.9 us -> 12 us
  starting transfers between devices: 35.1 us -> 29.3 us
  other arithmetic: 1.31 us -> 6.69 us
    ppermute x21 -> x16, waiting for transfers between devices: 262 us -> 226 us  [send(): return lax.ppermute(value, 'row', pairs)]
    ppermute x21 -> x16, starting transfers between devices: 35 us -> 29.1 us  [send(): return lax.ppermute(value, 'row', pairs)]
    slice x6 -> x2, local copies, waits for them, and re-layouts: 8.59 us -> 2.93 us  [per_device_line(): onward[:, a:b]]
    add x0 -> x1, other arithmetic: none -> 5.31 us  [per_device_line(): across = l2 + r2]
    unnamed x32 -> x26, local copies, waits for them, and re-layouts: 13 us -> 7.77 us
  transfers between devices with their start and end apart: 26 -> 21, of which waited for: 16 -> 14; matrix products, arithmetic and copies ran while one was open for 4% -> 5% of each run, Pallas kernels for 6% -> 13%
where the time goes in v7:
time: 414 us; the launch traced here: 413 us
  waiting for transfers between devices  279 us (67%)
  Pallas kernels  64.3 us (16%)
  starting transfers between devices  29.3 us (7%)
  between operations  13.4 us (3%)
  local copies, waits for them, and re-layouts  12 us (3%)
  matrix products  9.03 us (2%)
  other arithmetic  6.69 us (2%)
    ppermute x16, waiting for transfers between devices, send(): return lax.ppermute(value, 'row', pairs)  226 us
    reduce_scatter x3, waiting for transfers between devices, scatter(): return lax.psum_scatter(blocks, 'col', scatter_dimension=1, tiled=True)  49.9 us
    ppermute x16, starting transfers between devices, send(): return lax.ppermute(value, 'row', pairs)  29.1 us
    pallas_call x2, Pallas kernels, product(): pl.pallas_call(functools.partial(product_kernel, tuple(starts), first), g...  27.9 us
    pallas_call x1, Pallas kernels, near_blocks(): pl.pallas_call(near_kernel, out_shape=jax.ShapeDtypeStruct((4, rows, rows...  25 us
    pallas_call x1, Pallas kernels, square(): pl.pallas_call(square_kernel, out_shape=jax.ShapeDtypeStruct((rows, 4 * p...  9.64 us
    dot_general x1, matrix products, dot_rows(): lax.dot_general(left, right, (((1,), (1,)), ((), ())), preferred_element_...  9.03 us
  transfers between devices with their start and end apart: 21, of which 14 were waited for; matrix products, arithmetic and copies ran while one was open for 5% of the time, Pallas kernels for 13%

profile of v7, /device:TPU:0, one launch (start us, length us, event | category | flops | bytes accessed | tf_op | source)
XLA Modules:
  0.0 413.3 jit_solution(9487601517309559409)
XLA Ops:
  6.5 1.3 collective-permute-start.1
  7.8 7.5 %collective-permute-start = (bf16[896,2304]{1,0:T(8,128)(2,1)}, bf16[896,2304]{1,0:T(8,128)(2,1)}, u32[]{:S(2)}, u32[]{:S(2)}) collective-permute-start(bf16[896,2304]{1,0:T(8,128)(2,1)} %x.1), channel_id=1, source_target_pairs={{0,8},{8,16},{16,24},{1,9},{9,17},{17,25},{2,10},{10,18},{18,26},{... | collective-permute-start | bytes 12386312 | tf_op jit(solution)/shard_map/ppermute | solution.py:302
  15.3 9.0 %fusion = bf16[1,896,896]{2,1,0:T(8,128)(2,1)} fusion(bf16[896,2304]{1,0:T(8,128)(2,1)} %x.1), kind=kOutput, calls=%fused_computation.1 | convolution fusion | flops 3700178944 | bytes 5734400 | tf_op jit(solution)/shard_map/dot_general | solution.py:20
  24.4 39.6 %reduce-scatter.4.cloned.1.call-done = bf16[1,112,896]{2,1,0:T(8,128)(2,1)} async-done(((bf16[1,896,896]{2,1,0:T(8,128)(2,1)}), bf16[1,112,896]{2,1,0:T(8,128)(2,1)}) %reduce-scatter.4.cloned.1.call-update) | async-done | bytes 200720 | tf_op jit(solution)/shard_map/reduce_scatter | solution.py:305
  64.0 36.9 %collective-permute-done.1.l1 = bf16[896,2304]{1,0:T(8,128)(2,1)} collective-permute-done((bf16[896,2304]{1,0:T(8,128)(2,1)}, bf16[896,2304]{1,0:T(8,128)(2,1)}, u32[]{:S(2)}, u32[]{:S(2)}) %collective-permute-start.1) | collective-permute-done | bytes 4128800 | tf_op jit(solution)/shard_map/ppermute | solution.py:302
  102.1 1.3 collective-permute-start.2
  103.4 2.7 collective-permute-start.3
  106.1 25.0 %shard_map.18 = bf16[4,896,896]{2,1,0:T(8,128)(2,1)} custom-call(bf16[896,2304]{1,0:T(8,128)(2,1)} %x.1, bf16[896,2304]{1,0:T(8,128)(2,1)} %collective-permute-done.1.l1, bf16[896,2304]{1,0:T(8,128)(2,1)} %collective-permute-done.r1), custom_call_target="tpu_custom_call" | custom-call | flops 14797504512 | bytes 12386304 | tf_op jit(solution)/shard_map/pallas_call | solution.py:67
  131.2 63.9 %collective-permute-done.2.l2 = bf16[896,2304]{1,0:T(8,128)(2,1)} collective-permute-done((bf16[896,2304]{1,0:T(8,128)(2,1)}, bf16[896,2304]{1,0:T(8,128)(2,1)}, u32[]{:S(2)}, u32[]{:S(2)}) %collective-permute-start.2) | collective-permute-done | bytes 4128800 | tf_op jit(solution)/shard_map/ppermute | solution.py:302
  195.1 1.9 shard_map.17
  197.0 2.9 reduce-scatter.6.cloned.1.call-done
  199.9 1.3 fusion.1
  201.9 1.3 collective-permute-start.4
  203.2 17.6 %collective-permute-done.4 = bf16[112,896]{1,0:T(8,128)(2,1)S(1)} collective-permute-done((bf16[112,896]{1,0:T(8,128)(2,1)S(1)}, bf16[112,896]{1,0:T(8,128)(2,1)S(1)}, u32[]{:S(2)}, u32[]{:S(2)}) %collective-permute-start.4) | collective-permute-done | bytes 200736 | tf_op jit(solution)/shard_map/ppermute | solution.py:302
  220.9 1.3 collective-permute-start.7
  222.2 4.6 %collective-permute-start.6 = (bf16[4,112,896]{2,1,0:T(8,128)(2,1)S(1)}, bf16[4,112,896]{2,1,0:T(8,128)(2,1)S(1)}, u32[]{:S(2)}, u32[]{:S(2)}) collective-permute-start(bf16[4,112,896]{2,1,0:T(8,128)(2,1)S(1)} %pad_maximum_fusion.own), channel_id=1, source_target_pairs={{0,8},{8,16},{16,24},{1,9},{9,17},{17,25},{2,10},{10,18},{18,26},{... | collective-permute-start | bytes 2408456 | tf_op jit(solution)/shard_map/ppermute | solution.py:302
  226.8 12.4 %collective-permute-done.7.l1 = bf16[4,112,896]{2,1,0:T(8,128)(2,1)S(1)} collective-permute-done((bf16[4,112,896]{2,1,0:T(8,128)(2,1)S(1)}, bf16[4,112,896]{2,1,0:T(8,128)(2,1)S(1)}, u32[]{:S(2)}, u32[]{:S(2)}) %collective-permute-start.7) | collective-permute-done | bytes 802848 | tf_op jit(solution)/shard_map/ppermute | solution.py:302
  240.4 7.5 %reduce-scatter.8.cloned.1.call-done.corner = bf16[1,112,896]{2,1,0:T(8,128)(2,1)} async-done(((bf16[1,896,896]{2,1,0:T(8,128)(2,1)}), bf16[1,112,896]{2,1,0:T(8,128)(2,1)}) %reduce-scatter.8.cloned.1.call-update) | async-done | bytes 200720 | tf_op jit(solution)/shard_map/reduce_scatter | solution.py:305
  247.9 1.3 collective-permute-start.8
  249.2 7.5 %collective-permute-done.8.end = bf16[1,112,896]{2,1,0:T(8,128)(2,1)S(1)} collective-permute-done((bf16[1,112,896]{2,1,0:T(8,128)(2,1)}, bf16[1,112,896]{2,1,0:T(8,128)(2,1)S(1)}, u32[]{:S(2)}, u32[]{:S(2)}) %collective-permute-start.8) | collective-permute-done | bytes 200736 | tf_op jit(solution)/shard_map/ppermute | solution.py:302
  258.0 1.3 collective-permute-start.11
  260.0 18.6 %collective-permute-done.11.l2 = bf16[4,112,896]{2,1,0:T(8,128)(2,1)S(1)} collective-permute-done((bf16[4,112,896]{2,1,0:T(8,128)(2,1)S(1)}, bf16[4,112,896]{2,1,0:T(8,128)(2,1)S(1)}, u32[]{:S(2)}, u32[]{:S(2)}) %collective-permute-start.11) | collective-permute-done | bytes 802848 | tf_op jit(solution)/shard_map/ppermute | solution.py:302
  278.6 1.3 collective-permute-start.12
  280.6 5.3 %add.17 = bf16[896,2304]{1,0:T(8,128)(2,1)S(1)} add(bf16[896,2304]{1,0:T(8,128)(2,1)} %collective-permute-done.2.l2, bf16[896,2304]{1,0:T(8,128)(2,1)} %collective-permute-done.3.r2) | non-fusion elementwise | flops 2064384 | bytes 12386304 | tf_op jit(solution)/shard_map/add | solution.py:333
  286.0 12.4 %collective-permute-done.12.l3 = bf16[4,112,896]{2,1,0:T(8,128)(2,1)S(1)} collective-permute-done((bf16[4,112,896]{2,1,0:T(8,128)(2,1)S(1)}, bf16[4,112,896]{2,1,0:T(8,128)(2,1)S(1)}, u32[]{:S(2)}, u32[]{:S(2)}) %collective-permute-start.12) | collective-permute-done | bytes 802848 | tf_op jit(solution)/shard_map/ppermute | solution.py:302
  300.3 1.9 slice.23
  305.2 1.3 collective-permute-start.14
  312.4 9.6 %shard_map.19 = bf16[896,448]{1,0:T(8,128)(2,1)} custom-call(s32[2]{0:T(128)S(1)} %pad_add_fusion.place, bf16[4,896,896]{2,1,0:T(8,128)(2,1)} %all-gather.4.cloned.1.call-done.panel, bf16[4,112,896]{2,1,0:T(8,128)(2,1)S(1)} %pad_maximum_fusion.own, bf16[4,112,896]{2,1,0:T(8,128)(2,1)S(1)} %collective-permute-done.7.l1, bf16[4,112,896]{2,1,0:T(8,128)(2,1)S(1)} %copy-done.6, ...), custom_call_target="tpu_custom_call" | custom-call | flops 2877292544 | bytes 8028160 | tf_op jit(solution)/shard_map/pallas_call | solution.py:169
  322.1 54.7 %collective-permute-done.15.value = bf16[896,1792]{1,0:T(8,128)(2,1)} collective-permute-done((bf16[896,1792]{1,0:T(8,128)(2,1)}, bf16[896,1792]{1,0:T(8,128)(2,1)}, u32[]{:S(2)}, u32[]{:S(2)}) %collective-permute-start.15) | collective-permute-done | bytes 3211296 | tf_op jit(solution)/shard_map/ppermute | solution.py:302
  376.8 2.0 all-gather.6.cloned.1.call-done
  378.8 18.8 %shard_map.21.rest_1_ = bf16[896,2304]{1,0:T(8,128)(2,1)} custom-call(s32[2]{0:T(128)S(1)} %pad_add_fusion.place, bf16[8,896,448]{2,1,0:T(8,128)(2,1)} %bitcast.23, bf16[8,112,2304]{2,1,0:T(8,128)(2,1)} %bitcast.19, bf16[8,112,2304]{2,1,0:T(8,128)(2,1)} %bitcast.8.l1, bf16[8,112,2304]{2,1,0:T(8,128)(2,1)} %bitcast.9.r1, bf16[8,112,2304]{2,1,0:T(8,128)(2,1)} %bitcast.21, ...), custom_call_target="tpu_custom_call" | custom-call | flops 11509170176 | bytes 19267584 | tf_op jit(solution)/shard_map/pallas_call | solution.py:257
  397.7 9.0 %shard_map.22 = bf16[896,2304]{1,0:T(8,128)(2,1)} custom-call(s32[2]{0:T(128)S(1)} %pad_add_fusion.place, bf16[8,896,448]{2,1,0:T(8,128)(2,1)} %bitcast.24, bf16[8,112,2304]{2,1,0:T(8,128)(2,1)S(1)} %bitcast.20, bf16[8,112,2304]{2,1,0:T(8,128)(2,1)} %bitcast.8.l1, bf16[8,112,2304]{2,1,0:T(8,128)(2,1)} %bitcast.9.r1, ...), custom_call_target="tpu_custom_call", output_to_operand_aliasing={{}: (7, {})} | custom-call | flops 3288334336 | bytes 5505024 | tf_op jit(solution)/shard_map/pallas_call | solution.py:257
  (58 shorter events, 16.9 us)
Async XLA Ops:
  6.5 57.5 %reduce-scatter.4.cloned.1.call-start = ((), (), s32[]{:S(2)}) async-start(), calls=%async_computation.3 | async-start | bytes 1806336 | tf_op jit(solution)/shard_map/reduce_scatter | solution.py:305
  6.5 94.4 %collective-permute-start.1 = (bf16[896,2304]{1,0:T(8,128)(2,1)}, bf16[896,2304]{1,0:T(8,128)(2,1)}, u32[]{:S(2)}, u32[]{:S(2)}) collective-permute-start(bf16[896,2304]{1,0:T(8,128)(2,1)} %x.1), channel_id=1, source_target_pairs={{24,16},{16,8},{8,0},{25,17},{17,9},{9,1},{26,18},{18,10},{10,2},{... | collective-permute-start | bytes 12386312 | tf_op jit(solution)/shard_map/ppermute | solution.py:302
  7.8 94.3 %collective-permute-start = (bf16[896,2304]{1,0:T(8,128)(2,1)}, bf16[896,2304]{1,0:T(8,128)(2,1)}, u32[]{:S(2)}, u32[]{:S(2)}) collective-permute-start(bf16[896,2304]{1,0:T(8,128)(2,1)} %x.1), channel_id=1, source_target_pairs={{0,8},{8,16},{16,24},{1,9},{9,17},{17,25},{2,10},{10,18},{18,26},{... | collective-permute-start | bytes 12386312 | tf_op jit(solution)/shard_map/ppermute | solution.py:302
  24.4 175.4 %reduce-scatter.6.cloned.1.call-start = ((), (), s32[]{:S(2)}) async-start(), calls=%async_computation.4 | async-start | bytes 7225344 | tf_op jit(solution)/shard_map/reduce_scatter | solution.py:305
  102.1 93.0 %collective-permute-start.2 = (bf16[896,2304]{1,0:T(8,128)(2,1)}, bf16[896,2304]{1,0:T(8,128)(2,1)}, u32[]{:S(2)}, u32[]{:S(2)}) collective-permute-start(bf16[896,2304]{1,0:T(8,128)(2,1)} %collective-permute-done.1.l1), channel_id=1, source_target_pairs={{16,8},{8,0},{17,9},{9,1},{18,10},{10,2},{19,11},{11,3},{20,12},{1... | collective-permute-start | bytes 12386312 | tf_op jit(solution)/shard_map/ppermute | solution.py:302
  103.4 91.7 %collective-permute-start.3 = (bf16[896,2304]{1,0:T(8,128)(2,1)}, bf16[896,2304]{1,0:T(8,128)(2,1)}, u32[]{:S(2)}, u32[]{:S(2)}) collective-permute-start(bf16[896,2304]{1,0:T(8,128)(2,1)} %collective-permute-done.r1), channel_id=1, source_target_pairs={{8,16},{16,24},{9,17},{17,25},{10,18},{18,26},{11,19},{19,27},{12,... | collective-permute-start | bytes 12386312 | tf_op jit(solution)/shard_map/ppermute | solution.py:302
  131.1 116.8 %reduce-scatter.8.cloned.1.call-start = ((), (), s32[]{:S(2)}) async-start(), calls=%async_computation.5 | async-start | bytes 1806336 | tf_op jit(solution)/shard_map/reduce_scatter | solution.py:305
  195.1 25.7 %copy-start.12 = (bf16[1,112,896]{2,1,0:T(8,128)(2,1)S(1)}, bf16[1,112,896]{2,1,0:T(8,128)(2,1)}, u32[]{:S(2)}) copy-start(bf16[1,112,896]{2,1,0:T(8,128)(2,1)} %reduce-scatter.4.cloned.1.call-done) | copy-start | bytes 602116
  199.9 107.3 %all-gather.4.cloned.1.call-start = ((), (), s32[]{:S(2)}) async-start(), calls=%async_computation.6 | async-start | bytes 7225344 | tf_op jit(solution)/shard_map/all_gather | solution.py:326
  201.2 2.0 collective-permute-start.5
  201.9 18.9 %collective-permute-start.4 = (bf16[112,896]{1,0:T(8,128)(2,1)S(1)}, bf16[112,896]{1,0:T(8,128)(2,1)S(1)}, u32[]{:S(2)}, u32[]{:S(2)}) collective-permute-start(bf16[112,896]{1,0:T(8,128)(2,1)S(1)} %get-tuple-element.36), channel_id=1, source_target_pairs={{16,8},{8,0},{17,9},{9,1},{18,10},{10,2},{19,11},{11,3},{20,12},{1... | collective-permute-start | bytes 602120 | tf_op jit(solution)/shard_map/ppermute | solution.py:302
  220.9 18.3 %collective-permute-start.7 = (bf16[4,112,896]{2,1,0:T(8,128)(2,1)S(1)}, bf16[4,112,896]{2,1,0:T(8,128)(2,1)S(1)}, u32[]{:S(2)}, u32[]{:S(2)}) collective-permute-start(bf16[4,112,896]{2,1,0:T(8,128)(2,1)S(1)} %pad_maximum_fusion.own), channel_id=1, source_target_pairs={{24,16},{16,8},{8,0},{25,17},{17,9},{9,1},{26,18},{18,10},{10,2},{... | collective-permute-start | bytes 2408456 | tf_op jit(solution)/shard_map/ppermute | solution.py:302
  222.2 18.2 %collective-permute-start.6 = (bf16[4,112,896]{2,1,0:T(8,128)(2,1)S(1)}, bf16[4,112,896]{2,1,0:T(8,128)(2,1)S(1)}, u32[]{:S(2)}, u32[]{:S(2)}) collective-permute-start(bf16[4,112,896]{2,1,0:T(8,128)(2,1)S(1)} %pad_maximum_fusion.own), channel_id=1, source_target_pairs={{0,8},{8,16},{16,24},{1,9},{9,17},{17,25},{2,10},{10,18},{18,26},{... | collective-permute-start | bytes 2408456 | tf_op jit(solution)/shard_map/ppermute | solution.py:302
  247.9 8.8 %collective-permute-start.8 = (bf16[1,112,896]{2,1,0:T(8,128)(2,1)}, bf16[1,112,896]{2,1,0:T(8,128)(2,1)S(1)}, u32[]{:S(2)}, u32[]{:S(2)}) collective-permute-start(bf16[1,112,896]{2,1,0:T(8,128)(2,1)} %reduce-scatter.8.cloned.1.call-done.corner), channel_id=1, source_target_pairs={{8,0},{16,24},{9,1},{17,25},{10,2},{18,26},{11,3},{19,27},{12,4},{... | collective-permute-start | bytes 602120 | tf_op jit(solution)/shard_map/ppermute | solution.py:302
  257.9 120.9 %all-gather.6.cloned.1.call-start = ((), (), s32[]{:S(2)}) async-start(), calls=%async_computation.7 | async-start | bytes 8257536 | tf_op jit(solution)/shard_map/all_gather | solution.py:339
  258.0 20.6 %collective-permute-start.11 = (bf16[4,112,896]{2,1,0:T(8,128)(2,1)S(1)}, bf16[4,112,896]{2,1,0:T(8,128)(2,1)S(1)}, u32[]{:S(2)}, u32[]{:S(2)}) collective-permute-start(bf16[4,112,896]{2,1,0:T(8,128)(2,1)S(1)} %collective-permute-done.7.l1), channel_id=1, source_target_pairs={{16,8},{8,0},{17,9},{9,1},{18,10},{10,2},{19,11},{11,3},{20,12},{1... | collective-permute-start | bytes 2408456 | tf_op jit(solution)/shard_map/ppermute | solution.py:302
  259.3 20.6 %collective-permute-start.9 = (bf16[4,112,896]{2,1,0:T(8,128)(2,1)S(1)}, bf16[4,112,896]{2,1,0:T(8,128)(2,1)S(1)}, u32[]{:S(2)}, u32[]{:S(2)}) collective-permute-start(bf16[4,112,896]{2,1,0:T(8,128)(2,1)S(1)} %collective-permute-done.6.r1), channel_id=1, source_target_pairs={{8,16},{16,24},{9,17},{17,25},{10,18},{18,26},{11,19},{19,27},{12,... | collective-permute-start | bytes 2408456 | tf_op jit(solution)/shard_map/ppermute | solution.py:302
  278.6 19.8 %collective-permute-start.12 = (bf16[4,112,896]{2,1,0:T(8,128)(2,1)S(1)}, bf16[4,112,896]{2,1,0:T(8,128)(2,1)S(1)}, u32[]{:S(2)}, u32[]{:S(2)}) collective-permute-start(bf16[4,112,896]{2,1,0:T(8,128)(2,1)S(1)} %collective-permute-done.11.l2), channel_id=1, source_target_pairs={{8,0},{9,1},{10,2},{11,3},{12,4},{13,5},{14,6},{15,7}} | collective-permute-start | bytes 2408456 | tf_op jit(solution)/shard_map/ppermute | solution.py:302
  279.9 6.0 %copy-start.1 = (bf16[4,112,896]{2,1,0:T(8,128)(2,1)}, bf16[4,112,896]{2,1,0:T(8,128)(2,1)S(1)}, u32[]{:S(2)}) copy-start(bf16[4,112,896]{2,1,0:T(8,128)(2,1)S(1)} %collective-permute-done.9.r2) | copy-start | bytes 2408452
  279.9 19.4 %collective-permute-start.10 = (bf16[4,112,896]{2,1,0:T(8,128)(2,1)S(1)}, bf16[4,112,896]{2,1,0:T(8,128)(2,1)S(1)}, u32[]{:S(2)}, u32[]{:S(2)}) collective-permute-start(bf16[4,112,896]{2,1,0:T(8,128)(2,1)S(1)} %collective-permute-done.9.r2), channel_id=1, source_target_pairs={{16,24},{17,25},{18,26},{19,27},{20,28},{21,29},{22,30},{23,31}} | collective-permute-start | bytes 2408456 | tf_op jit(solution)/shard_map/ppermute | solution.py:302
  286.0 19.2 %copy-start.11 = (bf16[896,2304]{1,0:T(8,128)(2,1)}, bf16[896,2304]{1,0:T(8,128)(2,1)S(1)}, u32[]{:S(2)}) copy-start(bf16[896,2304]{1,0:T(8,128)(2,1)S(1)} %add.17) | copy-start | bytes 12386308
  286.0 17.5 %copy-start.7 = (bf16[1,112,896]{2,1,0:T(8,128)(2,1)S(1)}, bf16[1,112,896]{2,1,0:T(8,128)(2,1)}, u32[]{:S(2)}) copy-start(bf16[1,112,896]{2,1,0:T(8,128)(2,1)} %reduce-scatter.8.cloned.1.call-done.corner) | copy-start | bytes 602116
  298.4 0.9 copy-start.3
  302.1 74.6 %collective-permute-start.15 = (bf16[896,1792]{1,0:T(8,128)(2,1)}, bf16[896,1792]{1,0:T(8,128)(2,1)}, u32[]{:S(2)}, u32[]{:S(2)}) collective-permute-start(bf16[896,1792]{1,0:T(8,128)(2,1)} %slice.23), channel_id=1, source_target_pairs={{8,0},{16,24},{9,1},{17,25},{10,2},{18,26},{11,3},{19,27},{12,4},{... | collective-permute-start | bytes 9633800 | tf_op jit(solution)/shard_map/ppermute | solution.py:302
  303.4 3.0 collective-permute-start.13
  305.2 92.5 %collective-permute-start.14 = (bf16[896,512]{1,0:T(8,128)(2,1)}, bf16[896,512]{1,0:T(8,128)(2,1)}, u32[]{:S(2)}, u32[]{:S(2)}) collective-permute-start(bf16[896,512]{1,0:T(8,128)(2,1)} %slice.22), channel_id=1, source_target_pairs={{8,0},{16,24},{9,1},{17,25},{10,2},{18,26},{11,3},{19,27},{12,4},{... | collective-permute-start | bytes 2752520 | tf_op jit(solution)/shard_map/ppermute | solution.py:302
  307.1 1.1 copy-start.2
  308.3 1.1 copy-start.4
  309.4 1.1 copy-start.6
  310.6 0.9 copy-start.8
  311.5 0.9 copy-start.10
  378.8 18.9 %copy-start = (bf16[896,2304]{1,0:T(8,128)(2,1)S(1)}, bf16[896,2304]{1,0:T(8,128)(2,1)}, u32[]{:S(2)}) copy-start(bf16[896,2304]{1,0:T(8,128)(2,1)} %x.1) | copy-start | bytes 12386308
  (2 other events, 1.6 us)
Sparse Core Ops, SparseCore 0:
  24.5 39.4 reduce-scatter.3
  131.2 68.5 reduce-scatter.5
  203.6 44.2 reduce-scatter.7
  258.0 46.0 all-gather.3
  322.2 56.5 all-gather.5

commit v8 on v7

--- a/solution.py
+++ b/solution.py
@@ -116,67 +116,90 @@
     )(place, l1, r1, l2, r2)
 
 
-def square_kernel(place, panel, own, l1, r3, l2, r2, r1, l3, corner, pair, end, out, last):
+def strips_kernel(place, own, l1, r3, l2, r2, r1, l3, corner, pair, end, out):
     z = place[0]
     part = own.shape[1]
-    rows = panel.shape[1]
     at_end = jnp.logical_or(z == 0, z == 3)
-    for plane, block in ((0, 3), (3, 1)):
+    zero = jnp.zeros_like(end[0])
+    near = jnp.where(at_end, end[0], corner[0])
+    far = jnp.where(at_end, zero, pair[0])
+    low = jnp.where(z < 2, near, far)
+    high = jnp.where(z < 2, far, near)
+    for e in range(4):
+        for block in range(4):
+            if e == 0:
+                value = own[block]
+            else:
+                one, other = {1: (l1, r3), 2: (l2, r2), 3: (r1, l3)}[e]
+                value = one[block] + other[block]
+            if block == 3:
+                value = value + jnp.where((z + e) % 4 == 0, low, zero)
+            if block == 1:
+                value = value + jnp.where((z + e) % 4 == 3, high, zero)
+            out[(block + e) % 4, e * part : (e + 1) * part, :] = value
+
+
+def strips(place, *others):
+    _, part, rows = others[0].shape
+    return pl.pallas_call(
+        strips_kernel,
+        out_shape=jax.ShapeDtypeStruct((4, 4 * part, rows), jnp.bfloat16),
+        in_specs=[scalars()] + [whole()] * len(others),
+        out_specs=whole(),
+        compiler_params=pltpu.CompilerParams(vmem_limit_bytes=24 * 2**20),
+        cost_estimate=pl.CostEstimate(
+            flops=16 * part * rows, bytes_accessed=2 * 44 * part * rows, transcendentals=0
+        ),
+    )(place, *others)
+
+
+def square_kernel(place, panel, right, out, held, first, sems):
+    z = place[0]
+    rows, part = panel.shape[1], right.shape[1] // 4
+    order = (3, 1, 2, 0)
+    copies = {d: pltpu.make_async_copy(panel.at[d], held.at[d], sems.at[d]) for d in order}
+    for d in order:
+        copies[d].start()
+    first[...] = right[0]
+    total = jnp.zeros(out.shape, jnp.float32)
+    for d in order[:3]:
+        copies[d].wait()
+        total = total + dot_rows(held[d], right[d])
+    for plane, block, e in ((0, 3, 3), (3, 1, 1)):
 
         @pl.when(z == plane)
-        def _(block=block):
+        def _(block=block, e=e):
             index = lax.broadcasted_iota(jnp.int32, (part, rows), 0) + place[1] * part
             other = lax.broadcasted_iota(jnp.int32, (part, rows), 1)
             pick = jnp.where(index == other, 1.0, 0.0).astype(jnp.bfloat16)
-            last[...] = dot_rows(pick, panel[block]).astype(last.dtype)
-
-    @pl.when(jnp.logical_not(at_end))
-    def _():
-        last[...] = pair[0]
-
-    near = jnp.where(at_end, end[0], corner[0])
-    far = last[...]
-    low = jnp.where(z < 2, near, far)
-    high = jnp.where(z < 2, far, near)
-    zero = jnp.zeros_like(low)
-
-    def strip(e, block):
-        if e == 0:
-            value = own[block]
-        else:
-            one, other = {1: (l1, r3), 2: (l2, r2), 3: (r1, l3)}[e]
-            value = one[block] + other[block]
-        if block == 3:
-            value = value + jnp.where((z + e) % 4 == 0, low, zero)
-        if block == 1:
-            value = value + jnp.where((z + e) % 4 == 3, high, zero)
-        return value
-
-    total = jnp.zeros((rows, 4 * part), jnp.float32)
-    for d in range(4):
-        right = jnp.concatenate([strip(e, (d - e) % 4) for e in range(4)], axis=0)
-        total = total + dot_rows(panel[d], right)
+            far = dot_rows(pick, held[block]).astype(first.dtype)
+            first[e * part : (e + 1) * part, :] = right[0, e * part : (e + 1) * part, :] + far
+
+    copies[0].wait()
+    total = total + dot_rows(held[0], first[...])
     index = lax.broadcasted_iota(jnp.int32, (rows, rows), 0)
     other = lax.broadcasted_iota(jnp.int32, (rows, rows), 1)
     unit = jnp.where(index == other, 1.0, 0.0).astype(jnp.bfloat16)
-    linear = dot_rows(unit, jnp.concatenate([strip(e, (-e) % 4) for e in range(4)], axis=0))
-    out[...] = (coef_b * linear + coef_c * total).astype(out.dtype)
-
-
-def square(place, panel, *others):
-    rows = panel.shape[1]
-    part = others[0].shape[1]
+    out[...] = (coef_b * dot_rows(unit, first[...]) + coef_c * total).astype(out.dtype)
+
+
+def square(place, panel, right):
+    rows, depth = panel.shape[1], right.shape[1]
     return pl.pallas_call(
         square_kernel,
-        out_shape=jax.ShapeDtypeStruct((rows, 4 * part), jnp.bfloat16),
-        in_specs=[scalars()] + [whole()] * (1 + len(others)),
+        out_shape=jax.ShapeDtypeStruct((rows, depth), jnp.bfloat16),
+        in_specs=[scalars(), pl.BlockSpec(memory_space=pl.ANY), whole()],
         out_specs=whole(),
-        scratch_shapes=[pltpu.VMEM((part, rows), jnp.bfloat16)],
-        compiler_params=pltpu.CompilerParams(vmem_limit_bytes=48 * 2**20),
-        cost_estimate=pl.CostEstimate(
-            flops=2 * rows * rows * 4 * 4 * part, bytes_accessed=2 * 5 * rows * rows, transcendentals=0
-        ),
-    )(place, panel, *others)
+        scratch_shapes=[
+            pltpu.VMEM(panel.shape, jnp.bfloat16),
+            pltpu.VMEM((depth, rows), jnp.bfloat16),
+            pltpu.SemaphoreType.DMA((4,)),
+        ],
+        compiler_params=pltpu.CompilerParams(vmem_limit_bytes=40 * 2**20),
+        cost_estimate=pl.CostEstimate(
+            flops=2 * rows * rows * 4 * depth, bytes_accessed=2 * 5 * rows * rows, transcendentals=0
+        ),
+    )(place, panel, right)
 
 
 def product_kernel(starts, first, place, f, x, l1, r1, across, *rest):
@@ -318,7 +341,16 @@
     tile = jnp.stack([own[0], first[0], second, first[1]])
     tr1, tl1 = send(tile, right), send(tile, left)
 
-    corner, tr1, tl1 = lax.optimization_barrier((corner, tr1, tl1))
+    unit = 256
+    marks = [0, unit, x.shape[1] - 2 * unit, x.shape[1]]
+    across = l2 + r2
+
+    def send_on(p, *after):
+        value = lax.optimization_barrier((across, *after))[0]
+        return send(value[:, marks[p] : marks[p + 1]], [(1, 0), (2, 3)])
+
+    far = [send_on(0, tile)]
+    corner, tr1, tl1, far[0] = lax.optimization_barrier((corner, tr1, tl1, far[0]))
     end = send(corner, [(1, 0), (2, 3)])
     pair = send(corner, [(1, 2), (2, 1)])
     zero = jnp.zeros_like(end)
@@ -328,18 +360,15 @@
     end, tr1, tl1 = lax.optimization_barrier((end, tr1, tl1))
     tr2, tl2 = send(tr1, right[1:]), send(tl1, left[1:])
     tr3, tl3 = send(tr2, right[2:]), send(tl2, left[2:])
-    unit = 256
-    marks = [0, x.shape[1] - 2 * unit, x.shape[1]]
-    across = l2 + r2
-    tr3, tl3, onward = lax.optimization_barrier((tr3, tl3, across))
-    far = [send(onward[:, a:b], [(1, 0), (2, 3)]) for a, b in zip(marks, marks[1:])]
-    far[0] = arrived(far[0])
-
-    factor = square(place, panel, tile, tl1, tr3, tl2, tr2, tr1, tl3, corner, pair, end)
+    far.append(arrived(send_on(1, tr3, tl3, pair)))
+
+    rights = strips(place, tile, tl1, tr3, tl2, tr2, tr1, tl3, corner, pair, end)
+    factor = square(place, panel, rights)
+    far.append(send_on(2, factor))
     factor = lax.all_gather(factor, "col", axis=0, tiled=False)
     near = [x, l1, r1, across]
-    out = product(place, factor, near, far[:1], unit, 0, None)
-    return product(place, factor, near, far[1:], unit, marks[1] // unit, out)
+    out = product(place, factor, near, far[:2], unit, 0, None)
+    return product(place, factor, near, far[2:], unit, marks[2] // unit, out)
 
 
 def solution(mesh):

time: 414 us -> 404 us (0.976)
  waiting for transfers between devices: 279 us -> 264 us
    ppermute x16 -> x17, waiting for transfers between devices: 226 us -> 213 us  [send(): return lax.ppermute(value, 'row', pairs)]
    reduce_scatter x3, waiting for transfers between devices: 49.9 us -> 42.5 us  [scatter(): return lax.psum_scatter(blocks, 'col', scatter_dimension=1, tiled=True)]
    all_gather x1, waiting for transfers between devices: 2.02 us -> 7.27 us  [per_device_line(): factor = lax.all_gather(factor, 'col', axis=0, tiled=False)]
    ppermute x16 -> x17, starting transfers between devices: 29.1 us -> 30.8 us  [send(): return lax.ppermute(value, 'row', pairs)]
    pallas_call x1 -> x2, Pallas kernels: 9.64 us -> 8.27 us  [the longest x1 7.3 us: square(): pl.pallas_call(square_kernel, out_shape=jax.ShapeDtypeStruct((rows, depth...]
  transfers between devices with their start and end apart: 21 -> 22, of which waited for: 14 -> 13; matrix products, arithmetic and copies ran while one was open for 5% -> 6% of each run, Pallas kernels for 13% -> 13%
where the time goes in v8:
time: 404 us; the launch traced here: 403 us
  waiting for transfers between devices  264 us (65%)
  Pallas kernels  62.8 us (16%)
  starting transfers between devices  30.9 us (8%)
  local copies, waits for them, and re-layouts  15.3 us (4%)
  between operations  13.5 us (3%)
  matrix products  9.03 us (2%)
  other arithmetic  7.99 us (2%)
    ppermute x17, waiting for transfers between devices, send(): return lax.ppermute(value, 'row', pairs)  213 us
    reduce_scatter x3, waiting for transfers between devices, scatter(): return lax.psum_scatter(blocks, 'col', scatter_dimension=1, tiled=True)  42.5 us
    ppermute x17, starting transfers between devices, send(): return lax.ppermute(value, 'row', pairs)  30.8 us
    pallas_call x2, Pallas kernels, product(): pl.pallas_call(functools.partial(product_kernel, tuple(starts), first), g...  27.7 us
    pallas_call x1, Pallas kernels, near_blocks(): pl.pallas_call(near_kernel, out_shape=jax.ShapeDtypeStruct((4, rows, rows...  25 us
    dot_general x1, matrix products, dot_rows(): lax.dot_general(left, right, (((1,), (1,)), ((), ())), preferred_element_...  9.03 us
    unnamed x26, local copies, waits for them, and re-layouts  8.12 us
  transfers between devices with their start and end apart: 22, of which 13 were waited for; matrix products, arithmetic and copies ran while one was open for 6% of the time, Pallas kernels for 13%

profile of v8, /device:TPU:0, one launch (start us, length us, event | category | flops | bytes accessed | tf_op | source)
XLA Modules:
  0.0 403.1 jit_solution(11468786986103502544)
XLA Ops:
  7.8 7.5 %collective-permute-start = (bf16[896,2304]{1,0:T(8,128)(2,1)}, bf16[896,2304]{1,0:T(8,128)(2,1)}, u32[]{:S(2)}, u32[]{:S(2)}) collective-permute-start(bf16[896,2304]{1,0:T(8,128)(2,1)} %x.1), channel_id=1, source_target_pairs={{0,8},{8,16},{16,24},{1,9},{9,17},{17,25},{2,10},{10,18},{18,26},{... | collective-permute-start | bytes 12386312 | tf_op jit(solution)/shard_map/ppermute | solution.py:325
  15.4 9.0 %fusion = bf16[1,896,896]{2,1,0:T(8,128)(2,1)} fusion(bf16[896,2304]{1,0:T(8,128)(2,1)} %x.1), kind=kOutput, calls=%fused_computation.1 | convolution fusion | flops 3700178944 | bytes 5734400 | tf_op jit(solution)/shard_map/dot_general | solution.py:20
  24.5 39.6 %reduce-scatter.4.cloned.1.call-done = bf16[1,112,896]{2,1,0:T(8,128)(2,1)} async-done(((bf16[1,896,896]{2,1,0:T(8,128)(2,1)}), bf16[1,112,896]{2,1,0:T(8,128)(2,1)}) %reduce-scatter.4.cloned.1.call-update) | async-done | bytes 200720 | tf_op jit(solution)/shard_map/reduce_scatter | solution.py:328
  64.0 36.9 %collective-permute-done.1.l1 = bf16[896,2304]{1,0:T(8,128)(2,1)} collective-permute-done((bf16[896,2304]{1,0:T(8,128)(2,1)}, bf16[896,2304]{1,0:T(8,128)(2,1)}, u32[]{:S(2)}, u32[]{:S(2)}) %collective-permute-start.1) | collective-permute-done | bytes 4128800 | tf_op jit(solution)/shard_map/ppermute | solution.py:325
  103.4 2.7 collective-permute-start.3
  106.2 25.0 %shard_map.18 = bf16[4,896,896]{2,1,0:T(8,128)(2,1)} custom-call(bf16[896,2304]{1,0:T(8,128)(2,1)} %x.1, bf16[896,2304]{1,0:T(8,128)(2,1)} %collective-permute-done.1.l1, bf16[896,2304]{1,0:T(8,128)(2,1)} %collective-permute-done.r1), custom_call_target="tpu_custom_call" | custom-call | flops 14797504512 | bytes 12386304 | tf_op jit(solution)/shard_map/pallas_call | solution.py:67
  131.2 63.9 %collective-permute-done.2.l2 = bf16[896,2304]{1,0:T(8,128)(2,1)} collective-permute-done((bf16[896,2304]{1,0:T(8,128)(2,1)}, bf16[896,2304]{1,0:T(8,128)(2,1)}, u32[]{:S(2)}, u32[]{:S(2)}) %collective-permute-start.2) | collective-permute-done | bytes 4128800 | tf_op jit(solution)/shard_map/ppermute | solution.py:325
  195.1 1.9 shard_map.17
  197.0 3.0 reduce-scatter.6.cloned.1.call-done
  200.0 1.3 fusion.1
  202.0 1.3 collective-permute-start.4
  203.3 17.5 %collective-permute-done.4 = bf16[112,896]{1,0:T(8,128)(2,1)S(1)} collective-permute-done((bf16[112,896]{1,0:T(8,128)(2,1)S(1)}, bf16[112,896]{1,0:T(8,128)(2,1)S(1)}, u32[]{:S(2)}, u32[]{:S(2)}) %collective-permute-start.4) | collective-permute-done | bytes 200736 | tf_op jit(solution)/shard_map/ppermute | solution.py:325
  221.0 1.3 collective-permute-start.7
  222.3 4.6 %collective-permute-start.6 = (bf16[4,112,896]{2,1,0:T(8,128)(2,1)S(1)}, bf16[4,112,896]{2,1,0:T(8,128)(2,1)S(1)}, u32[]{:S(2)}, u32[]{:S(2)}) collective-permute-start(bf16[4,112,896]{2,1,0:T(8,128)(2,1)S(1)} %pad_maximum_fusion.own), channel_id=1, source_target_pairs={{0,8},{8,16},{16,24},{1,9},{9,17},{17,25},{2,10},{10,18},{18,26},{... | collective-permute-start | bytes 2408456 | tf_op jit(solution)/shard_map/ppermute | solution.py:325
  226.9 6.6 %add.16 = bf16[896,2304]{1,0:T(8,128)(2,1)} add(bf16[896,2304]{1,0:T(8,128)(2,1)} %collective-permute-done.2.l2, bf16[896,2304]{1,0:T(8,128)(2,1)} %collective-permute-done.3.r2) | non-fusion elementwise | flops 2064384 | bytes 12386304 | tf_op jit(solution)/shard_map/add | solution.py:346
  234.6 1.3 collective-permute-start.8
  235.9 13.3 %collective-permute-done.8 = bf16[896,256]{1,0:T(8,128)(2,1)S(1)} collective-permute-done((bf16[896,256]{1,0:T(8,128)(2,1)S(1)}, bf16[896,256]{1,0:T(8,128)(2,1)S(1)}, u32[]{:S(2)}, u32[]{:S(2)}) %collective-permute-start.8) | collective-permute-done | bytes 458784 | tf_op jit(solution)/shard_map/ppermute | solution.py:325
  249.2 1.3 collective-permute-start.9
  250.5 6.5 %collective-permute-done.9.end = bf16[1,112,896]{2,1,0:T(8,128)(2,1)S(1)} collective-permute-done((bf16[1,112,896]{2,1,0:T(8,128)(2,1)}, bf16[1,112,896]{2,1,0:T(8,128)(2,1)S(1)}, u32[]{:S(2)}, u32[]{:S(2)}) %collective-permute-start.9) | collective-permute-done | bytes 200736 | tf_op jit(solution)/shard_map/ppermute | solution.py:325
  258.3 1.3 collective-permute-start.12
  260.3 17.1 %collective-permute-done.12.l2 = bf16[4,112,896]{2,1,0:T(8,128)(2,1)S(1)} collective-permute-done((bf16[4,112,896]{2,1,0:T(8,128)(2,1)S(1)}, bf16[4,112,896]{2,1,0:T(8,128)(2,1)S(1)}, u32[]{:S(2)}, u32[]{:S(2)}) %collective-permute-start.12) | collective-permute-done | bytes 802848 | tf_op jit(solution)/shard_map/ppermute | solution.py:325
  280.1 15.6 %collective-permute-done.13.l3 = bf16[4,112,896]{2,1,0:T(8,128)(2,1)S(1)} collective-permute-done((bf16[4,112,896]{2,1,0:T(8,128)(2,1)S(1)}, bf16[4,112,896]{2,1,0:T(8,128)(2,1)S(1)}, u32[]{:S(2)}, u32[]{:S(2)}) %collective-permute-start.13) | collective-permute-done | bytes 802848 | tf_op jit(solution)/shard_map/ppermute | solution.py:325
  295.7 3.5 slice.27
  299.2 1.6 collective-permute-start.16
  306.7 2.8 copy-done.9
  309.5 7.3 %shard_map.20 = bf16[896,448]{1,0:T(8,128)(2,1)S(1)} custom-call(s32[2]{0:T(128)S(1)} %pad_add_fusion.place, bf16[4,896,896]{2,1,0:T(8,128)(2,1)S(1)} %copy-done.9, bf16[4,448,896]{2,1,0:T(8,128)(2,1)S(1)} %shard_map.19.right), custom_call_target="tpu_custom_call" | custom-call | flops 2877292544 | bytes 8028160 | tf_op jit(solution)/shard_map/pallas_call | solution.py:188
  317.8 41.2 %collective-permute-done.16.value = bf16[896,1536]{1,0:T(8,128)(2,1)} collective-permute-done((bf16[896,1536]{1,0:T(8,128)(2,1)}, bf16[896,1536]{1,0:T(8,128)(2,1)}, u32[]{:S(2)}, u32[]{:S(2)}) %collective-permute-start.16) | collective-permute-done | bytes 2752544 | tf_op jit(solution)/shard_map/ppermute | solution.py:325
  358.9 1.3 slice.26
  360.2 1.3 collective-permute-start.15
  361.5 7.3 %all-gather.6.cloned.1.call-done = bf16[7168,448]{1,0:T(8,128)(2,1)} async-done(((bf16[896,448]{1,0:T(8,128)(2,1)}), bf16[7168,448]{1,0:T(8,128)(2,1)}) %all-gather.6.cloned.1.call-update) | async-done | bytes 6422544 | tf_op jit(solution)/shard_map/all_gather | solution.py:368
  368.8 18.8 %shard_map.22.rest_1_ = bf16[896,2304]{1,0:T(8,128)(2,1)} custom-call(s32[2]{0:T(128)S(1)} %pad_add_fusion.place, bf16[8,896,448]{2,1,0:T(8,128)(2,1)} %bitcast.24, bf16[8,112,2304]{2,1,0:T(8,128)(2,1)} %bitcast.20, bf16[8,112,2304]{2,1,0:T(8,128)(2,1)} %bitcast.8.l1, bf16[8,112,2304]{2,1,0:T(8,128)(2,1)} %bitcast.9.r1, ...), custom_call_target="tpu_custom_call" | custom-call | flops 11509170176 | bytes 19267584 | tf_op jit(solution)/shard_map/pallas_call | solution.py:280
  387.6 8.9 %shard_map.23 = bf16[896,2304]{1,0:T(8,128)(2,1)} custom-call(s32[2]{0:T(128)S(1)} %pad_add_fusion.place, bf16[8,896,448]{2,1,0:T(8,128)(2,1)} %bitcast.25, bf16[8,112,2304]{2,1,0:T(8,128)(2,1)S(1)} %bitcast.21, bf16[8,112,2304]{2,1,0:T(8,128)(2,1)} %bitcast.8.l1, bf16[8,112,2304]{2,1,0:T(8,128)(2,1)} %bitcast.9.r1, ...), custom_call_target="tpu_custom_call", output_to_operand_aliasing={{}: (7, {})} | custom-call | flops 3288334336 | bytes 5505024 | tf_op jit(solution)/shard_map/pallas_call | solution.py:280
  (62 shorter events, 17.4 us)
Async XLA Ops:
  6.5 57.5 %reduce-scatter.4.cloned.1.call-start = ((), (), s32[]{:S(2)}) async-start(), calls=%async_computation.3 | async-start | bytes 1806336 | tf_op jit(solution)/shard_map/reduce_scatter | solution.py:328
  6.5 94.4 %collective-permute-start.1 = (bf16[896,2304]{1,0:T(8,128)(2,1)}, bf16[896,2304]{1,0:T(8,128)(2,1)}, u32[]{:S(2)}, u32[]{:S(2)}) collective-permute-start(bf16[896,2304]{1,0:T(8,128)(2,1)} %x.1), channel_id=1, source_target_pairs={{24,16},{16,8},{8,0},{25,17},{17,9},{9,1},{26,18},{18,10},{10,2},{... | collective-permute-start | bytes 12386312 | tf_op jit(solution)/shard_map/ppermute | solution.py:325
  7.8 94.3 %collective-permute-start = (bf16[896,2304]{1,0:T(8,128)(2,1)}, bf16[896,2304]{1,0:T(8,128)(2,1)}, u32[]{:S(2)}, u32[]{:S(2)}) collective-permute-start(bf16[896,2304]{1,0:T(8,128)(2,1)} %x.1), channel_id=1, source_target_pairs={{0,8},{8,16},{16,24},{1,9},{9,17},{17,25},{2,10},{10,18},{18,26},{... | collective-permute-start | bytes 12386312 | tf_op jit(solution)/shard_map/ppermute | solution.py:325
  24.4 175.5 %reduce-scatter.6.cloned.1.call-start = ((), (), s32[]{:S(2)}) async-start(), calls=%async_computation.4 | async-start | bytes 7225344 | tf_op jit(solution)/shard_map/reduce_scatter | solution.py:328
  102.1 93.0 %collective-permute-start.2 = (bf16[896,2304]{1,0:T(8,128)(2,1)}, bf16[896,2304]{1,0:T(8,128)(2,1)}, u32[]{:S(2)}, u32[]{:S(2)}) collective-permute-start(bf16[896,2304]{1,0:T(8,128)(2,1)} %collective-permute-done.1.l1), channel_id=1, source_target_pairs={{16,8},{8,0},{17,9},{9,1},{18,10},{10,2},{19,11},{11,3},{20,12},{1... | collective-permute-start | bytes 12386312 | tf_op jit(solution)/shard_map/ppermute | solution.py:325
  103.4 91.7 %collective-permute-start.3 = (bf16[896,2304]{1,0:T(8,128)(2,1)}, bf16[896,2304]{1,0:T(8,128)(2,1)}, u32[]{:S(2)}, u32[]{:S(2)}) collective-permute-start(bf16[896,2304]{1,0:T(8,128)(2,1)} %collective-permute-done.r1), channel_id=1, source_target_pairs={{8,16},{16,24},{9,17},{17,25},{10,18},{18,26},{11,19},{19,27},{12,... | collective-permute-start | bytes 12386312 | tf_op jit(solution)/shard_map/ppermute | solution.py:325
  131.2 118.0 %reduce-scatter.8.cloned.1.call-start = ((), (), s32[]{:S(2)}) async-start(), calls=%async_computation.5 | async-start | bytes 1806336 | tf_op jit(solution)/shard_map/reduce_scatter | solution.py:328
  195.1 25.7 %copy-start.12 = (bf16[1,112,896]{2,1,0:T(8,128)(2,1)S(1)}, bf16[1,112,896]{2,1,0:T(8,128)(2,1)}, u32[]{:S(2)}) copy-start(bf16[1,112,896]{2,1,0:T(8,128)(2,1)} %reduce-scatter.4.cloned.1.call-done) | copy-start | bytes 602116
  200.0 106.7 %all-gather.4.cloned.1.call-start = ((), (), s32[]{:S(2)}) async-start(), calls=%async_computation.6 | async-start | bytes 7225344 | tf_op jit(solution)/shard_map/all_gather | solution.py:358
  201.3 2.0 collective-permute-start.5
  202.0 18.8 %collective-permute-start.4 = (bf16[112,896]{1,0:T(8,128)(2,1)S(1)}, bf16[112,896]{1,0:T(8,128)(2,1)S(1)}, u32[]{:S(2)}, u32[]{:S(2)}) collective-permute-start(bf16[112,896]{1,0:T(8,128)(2,1)S(1)} %get-tuple-element.38), channel_id=1, source_target_pairs={{16,8},{8,0},{17,9},{9,1},{18,10},{10,2},{19,11},{11,3},{20,12},{1... | collective-permute-start | bytes 602120 | tf_op jit(solution)/shard_map/ppermute | solution.py:325
  221.0 12.5 %copy-start.1 = (bf16[4,112,896]{2,1,0:T(8,128)(2,1)}, bf16[4,112,896]{2,1,0:T(8,128)(2,1)S(1)}, u32[]{:S(2)}) copy-start(bf16[4,112,896]{2,1,0:T(8,128)(2,1)S(1)} %pad_maximum_fusion.own) | copy-start | bytes 2408452
  221.0 28.2 %collective-permute-start.7 = (bf16[4,112,896]{2,1,0:T(8,128)(2,1)S(1)}, bf16[4,112,896]{2,1,0:T(8,128)(2,1)S(1)}, u32[]{:S(2)}, u32[]{:S(2)}) collective-permute-start(bf16[4,112,896]{2,1,0:T(8,128)(2,1)S(1)} %pad_maximum_fusion.own), channel_id=1, source_target_pairs={{24,16},{16,8},{8,0},{25,17},{17,9},{9,1},{26,18},{18,10},{10,2},{... | collective-permute-start | bytes 2408456 | tf_op jit(solution)/shard_map/ppermute | solution.py:325
  222.3 26.9 %collective-permute-start.6 = (bf16[4,112,896]{2,1,0:T(8,128)(2,1)S(1)}, bf16[4,112,896]{2,1,0:T(8,128)(2,1)S(1)}, u32[]{:S(2)}, u32[]{:S(2)}) collective-permute-start(bf16[4,112,896]{2,1,0:T(8,128)(2,1)S(1)} %pad_maximum_fusion.own), channel_id=1, source_target_pairs={{0,8},{8,16},{16,24},{1,9},{9,17},{17,25},{2,10},{10,18},{18,26},{... | collective-permute-start | bytes 2408456 | tf_op jit(solution)/shard_map/ppermute | solution.py:325
  234.6 14.6 %collective-permute-start.8 = (bf16[896,256]{1,0:T(8,128)(2,1)S(1)}, bf16[896,256]{1,0:T(8,128)(2,1)S(1)}, u32[]{:S(2)}, u32[]{:S(2)}) collective-permute-start(bf16[896,256]{1,0:T(8,128)(2,1)S(1)} %slice.25), channel_id=1, source_target_pairs={{8,0},{16,24},{9,1},{17,25},{10,2},{18,26},{11,3},{19,27},{12,4},{... | collective-permute-start | bytes 1376264 | tf_op jit(solution)/shard_map/ppermute | solution.py:325
  249.1 50.1 %copy-start.10 = (bf16[896,256]{1,0:T(8,128)(2,1)}, bf16[896,256]{1,0:T(8,128)(2,1)S(1)}, u32[]{:S(2)}) copy-start(bf16[896,256]{1,0:T(8,128)(2,1)S(1)} %collective-permute-done.8) | copy-start | bytes 1376260
  249.2 50.1 %copy-start.4 = (bf16[4,112,896]{2,1,0:T(8,128)(2,1)}, bf16[4,112,896]{2,1,0:T(8,128)(2,1)S(1)}, u32[]{:S(2)}) copy-start(bf16[4,112,896]{2,1,0:T(8,128)(2,1)S(1)} %collective-permute-done.7.l1) | copy-start | bytes 2408452
  249.2 50.0 %copy-start.6 = (bf16[4,112,896]{2,1,0:T(8,128)(2,1)}, bf16[4,112,896]{2,1,0:T(8,128)(2,1)S(1)}, u32[]{:S(2)}) copy-start(bf16[4,112,896]{2,1,0:T(8,128)(2,1)S(1)} %collective-permute-done.6.r1) | copy-start | bytes 2408452
  249.2 7.8 %collective-permute-start.9 = (bf16[1,112,896]{2,1,0:T(8,128)(2,1)}, bf16[1,112,896]{2,1,0:T(8,128)(2,1)S(1)}, u32[]{:S(2)}, u32[]{:S(2)}) collective-permute-start(bf16[1,112,896]{2,1,0:T(8,128)(2,1)} %reduce-scatter.8.cloned.1.call-done.corner), channel_id=1, source_target_pairs={{8,0},{16,24},{9,1},{17,25},{10,2},{18,26},{11,3},{19,27},{12,4},{... | collective-permute-start | bytes 602120 | tf_op jit(solution)/shard_map/ppermute | solution.py:325
  258.2 110.5 %all-gather.6.cloned.1.call-start = ((), (), s32[]{:S(2)}) async-start(), calls=%async_computation.7 | async-start | bytes 8257536 | tf_op jit(solution)/shard_map/all_gather | solution.py:368
  258.3 19.1 %collective-permute-start.12 = (bf16[4,112,896]{2,1,0:T(8,128)(2,1)S(1)}, bf16[4,112,896]{2,1,0:T(8,128)(2,1)S(1)}, u32[]{:S(2)}, u32[]{:S(2)}) collective-permute-start(bf16[4,112,896]{2,1,0:T(8,128)(2,1)S(1)} %collective-permute-done.7.l1), channel_id=1, source_target_pairs={{16,8},{8,0},{17,9},{9,1},{18,10},{10,2},{19,11},{11,3},{20,12},{1... | collective-permute-start | bytes 2408456 | tf_op jit(solution)/shard_map/ppermute | solution.py:325
  259.6 19.1 %collective-permute-start.10 = (bf16[4,112,896]{2,1,0:T(8,128)(2,1)S(1)}, bf16[4,112,896]{2,1,0:T(8,128)(2,1)S(1)}, u32[]{:S(2)}, u32[]{:S(2)}) collective-permute-start(bf16[4,112,896]{2,1,0:T(8,128)(2,1)S(1)} %collective-permute-done.6.r1), channel_id=1, source_target_pairs={{8,16},{16,24},{9,17},{17,25},{10,18},{18,26},{11,19},{19,27},{12,... | collective-permute-start | bytes 2408456 | tf_op jit(solution)/shard_map/ppermute | solution.py:325
  277.4 18.3 %collective-permute-start.13 = (bf16[4,112,896]{2,1,0:T(8,128)(2,1)S(1)}, bf16[4,112,896]{2,1,0:T(8,128)(2,1)S(1)}, u32[]{:S(2)}, u32[]{:S(2)}) collective-permute-start(bf16[4,112,896]{2,1,0:T(8,128)(2,1)S(1)} %collective-permute-done.12.l2), channel_id=1, source_target_pairs={{8,0},{9,1},{10,2},{11,3},{12,4},{13,5},{14,6},{15,7}} | collective-permute-start | bytes 2408456 | tf_op jit(solution)/shard_map/ppermute | solution.py:325
  278.7 17.0 %collective-permute-start.11 = (bf16[4,112,896]{2,1,0:T(8,128)(2,1)S(1)}, bf16[4,112,896]{2,1,0:T(8,128)(2,1)S(1)}, u32[]{:S(2)}, u32[]{:S(2)}) collective-permute-start(bf16[4,112,896]{2,1,0:T(8,128)(2,1)S(1)} %collective-permute-done.10.r2), channel_id=1, source_target_pairs={{16,24},{17,25},{18,26},{19,27},{20,28},{21,29},{22,30},{23,31}} | collective-permute-start | bytes 2408456 | tf_op jit(solution)/shard_map/ppermute | solution.py:325
  279.4 0.7 collective-permute-start.14
  299.2 59.7 %collective-permute-start.16 = (bf16[896,1536]{1,0:T(8,128)(2,1)}, bf16[896,1536]{1,0:T(8,128)(2,1)}, u32[]{:S(2)}, u32[]{:S(2)}) collective-permute-start(bf16[896,1536]{1,0:T(8,128)(2,1)} %slice.27), channel_id=1, source_target_pairs={{8,0},{16,24},{9,1},{17,25},{10,2},{18,26},{11,3},{19,27},{12,4},{... | collective-permute-start | bytes 8257544 | tf_op jit(solution)/shard_map/ppermute | solution.py:325
  300.8 1.1 copy-start.2
  301.9 1.1 copy-start.5
  306.7 2.8 copy-start.9
  358.9 9.9 %copy-start.11 = (bf16[896,256]{1,0:T(8,128)(2,1)S(1)}, bf16[896,256]{1,0:T(8,128)(2,1)}, u32[]{:S(2)}) copy-start(bf16[896,256]{1,0:T(8,128)(2,1)} %copy-done.10) | copy-start | bytes 1376260
  360.2 27.4 %collective-permute-start.15 = (bf16[896,512]{1,0:T(8,128)(2,1)S(1)}, bf16[896,512]{1,0:T(8,128)(2,1)S(1)}, u32[]{:S(2)}, u32[]{:S(2)}) collective-permute-start(bf16[896,512]{1,0:T(8,128)(2,1)S(1)} %slice.26), channel_id=1, source_target_pairs={{8,0},{16,24},{9,1},{17,25},{10,2},{18,26},{11,3},{19,27},{12,4},{... | collective-permute-start | bytes 2752520 | tf_op jit(solution)/shard_map/ppermute | solution.py:325
  368.8 18.8 %copy-start = (bf16[896,2304]{1,0:T(8,128)(2,1)S(1)}, bf16[896,2304]{1,0:T(8,128)(2,1)}, u32[]{:S(2)}) copy-start(bf16[896,2304]{1,0:T(8,128)(2,1)} %x.1) | copy-start | bytes 12386308
  (3 other events, 3.0 us)
Sparse Core Ops, SparseCore 0:
  24.5 39.4 reduce-scatter.3
  131.3 68.5 reduce-scatter.5
  203.7 44.1 reduce-scatter.7
  258.3 48.2 all-gather.3
  317.9 50.8 all-gather.5

commit v9 on v8

--- a/solution.py
+++ b/solution.py
@@ -79,20 +79,21 @@
 
 def corner_kernel(place, l1, r1, l2, r2, out, held, sems):
     rows = l1.shape[0]
-    half = rows // 2
+    marks = [*range(0, rows, 256), rows]
+    parts = [slice(a, b) for a, b in zip(marks, marks[1:])]
     for plane, one, other in ((1, r1, l2), (2, l1, r2)):
 
         @pl.when(place[0] == plane)
         def _(one=one, other=other):
-            copies = [
-                pltpu.make_async_copy(one, held.at[0], sems.at[0]),
-                pltpu.make_async_copy(other.at[:half, :], held.at[1, :half, :], sems.at[1]),
-                pltpu.make_async_copy(other.at[half:, :], held.at[1, half:, :], sems.at[2]),
-            ]
+            copies = [pltpu.make_async_copy(one, held.at[0], sems.at[len(parts)])]
+            for p, part in enumerate(parts):
+                copies.append(
+                    pltpu.make_async_copy(other.at[part, :], held.at[1, part, :], sems.at[p])
+                )
             for copy in copies:
                 copy.start()
             copies[0].wait()
-            for part, copy in ((slice(0, half), copies[1]), (slice(half, rows), copies[2])):
+            for part, copy in zip(parts, copies[1:]):
                 copy.wait()
                 out[0, :, part] = dot_rows(held[0], held[1, part, :]).astype(out.dtype)
 
@@ -108,8 +109,11 @@
         out_shape=jax.ShapeDtypeStruct((1, rows, rows), jnp.bfloat16),
         in_specs=[scalars()] + [pl.BlockSpec(memory_space=pl.ANY)] * 4,
         out_specs=whole(),
-        scratch_shapes=[pltpu.VMEM((2, rows, depth), jnp.bfloat16), pltpu.SemaphoreType.DMA((3,))],
-        compiler_params=pltpu.CompilerParams(vmem_limit_bytes=32 * 2**20),
+        scratch_shapes=[
+            pltpu.VMEM((2, rows, depth), jnp.bfloat16),
+            pltpu.SemaphoreType.DMA((pl.cdiv(rows, 256) + 1,)),
+        ],
+        compiler_params=pltpu.CompilerParams(vmem_limit_bytes=56 * 2**20),
         cost_estimate=pl.CostEstimate(
             flops=128 * rows * rows * depth, bytes_accessed=8 * rows * depth, transcendentals=0
         ),
@@ -195,7 +199,7 @@
             pltpu.VMEM((depth, rows), jnp.bfloat16),
             pltpu.SemaphoreType.DMA((4,)),
         ],
-        compiler_params=pltpu.CompilerParams(vmem_limit_bytes=40 * 2**20),
+        compiler_params=pltpu.CompilerParams(vmem_limit_bytes=56 * 2**20),
         cost_estimate=pl.CostEstimate(
             flops=2 * rows * rows * 4 * depth, bytes_accessed=2 * 5 * rows * rows, transcendentals=0
         ),
@@ -205,7 +209,7 @@
 def product_kernel(starts, first, place, f, x, l1, r1, across, *rest):
     n_piece = len(starts) - 1
     far = rest[:n_piece]
-    out, whole_f, wide, sems = rest[-4:]
+    out, held_f, whole_f, wide, sems, f_sems = rest[-6:]
     z = place[0]
     n_col, rows, depth = f.shape
     part = depth // 4
@@ -239,9 +243,13 @@
 
     @pl.when(step == 0)
     def _():
+        copies = [pltpu.make_async_copy(f.at[c], held_f.at[c], f_sems.at[c]) for c in range(n_col)]
+        for one in copies:
+            one.start()
         fetch(0, 0)
         for c in range(n_col):
-            whole_f[:, c * depth : (c + 1) * depth] = f[c]
+            copies[c].wait()
+            whole_f[:, c * depth : (c + 1) * depth] = held_f[c]
 
     @pl.when(step + 1 < starts[-1])
     def _():
@@ -281,21 +289,21 @@
         functools.partial(product_kernel, tuple(starts), first),
         grid=(starts[-1],),
         out_shape=jax.ShapeDtypeStruct((rows, columns), jnp.bfloat16),
-        in_specs=[
-            scalars(),
-            pl.BlockSpec((n_col, rows, depth), lambda i: (0, 0, 0), pipeline_mode=pl.Buffered(1)),
-        ]
-        + [outside] * (len(operands) - 2),
+        in_specs=[scalars()] + [outside] * (len(operands) - 1),
         out_specs=pl.BlockSpec((rows, tile), lambda i: (0, i + first)),
         scratch_shapes=[
+            pltpu.VMEM(f.shape, jnp.bfloat16),
             pltpu.VMEM((rows, n_col * depth), jnp.bfloat16),
             pltpu.VMEM((2, n_col, depth, tile), jnp.bfloat16),
             pltpu.SemaphoreType.DMA((2, 4)),
+            pltpu.SemaphoreType.DMA((n_col,)),
         ],
         input_output_aliases=aliases,
-        compiler_params=pltpu.CompilerParams(vmem_limit_bytes=48 * 2**20),
-        cost_estimate=pl.CostEstimate(
-            flops=2 * rows * n_col * depth * share, bytes_accessed=2 * 6 * rows * share, transcendentals=0
+        compiler_params=pltpu.CompilerParams(vmem_limit_bytes=56 * 2**20),
+        cost_estimate=pl.CostEstimate(
+            flops=2 * rows * n_col * depth * share if first else 0,
+            bytes_accessed=2 * 6 * rows * share if first else 0,
+            transcendentals=0,
         ),
     )(*operands)
 

time: 404 us -> 411 us (1.017)
  waiting for transfers between devices: 264 us -> 271 us
  local copies, waits for them, and re-layouts: 15.3 us -> 9.54 us
    unnamed x26 -> x12, local copies, waits for them, and re-layouts: 8.12 us -> 2.45 us
    ppermute x17, waiting for transfers between devices: 213 us -> 219 us  [send(): return lax.ppermute(value, 'row', pairs)]
    all_gather x1, waiting for transfers between devices: 0.56 us -> 4.76 us  [per_device_line(): lax.all_gather(tile + jnp.concatenate(added), 'col', axis=1, tiled=True)]
  transfers between devices with their start and end apart: 22 -> 22, of which waited for: 13 -> 13; matrix products, arithmetic and copies ran while one was open for 6% -> 5% of each run, Pallas kernels for 13% -> 14%
where the time goes in v9:
time: 411 us; the launch traced here: 408 us
  waiting for transfers between devices  271 us (66%)
  Pallas kernels  66.1 us (16%)
  starting transfers between devices  31 us (8%)
  between operations  13.9 us (3%)
  local copies, waits for them, and re-layouts  9.54 us (2%)
  matrix products  9.03 us (2%)
  other arithmetic  7.52 us (2%)
    ppermute x17, waiting for transfers between devices, send(): return lax.ppermute(value, 'row', pairs)  219 us
    reduce_scatter x3, waiting for transfers between devices, scatter(): return lax.psum_scatter(blocks, 'col', scatter_dimension=1, tiled=True)  42.7 us
    ppermute x17, starting transfers between devices, send(): return lax.ppermute(value, 'row', pairs)  30.8 us
    pallas_call x2, Pallas kernels, product(): pl.pallas_call(functools.partial(product_kernel, tuple(starts), first), g...  27.4 us
    pallas_call x1, Pallas kernels, near_blocks(): pl.pallas_call(near_kernel, out_shape=jax.ShapeDtypeStruct((4, rows, rows...  24.9 us
    pallas_call x1, Pallas kernels, square(): pl.pallas_call(square_kernel, out_shape=jax.ShapeDtypeStruct((rows, depth...  10.7 us
    dot_general x1, matrix products, dot_rows(): lax.dot_general(left, right, (((1,), (1,)), ((), ())), preferred_element_...  9.03 us
  transfers between devices with their start and end apart: 22, of which 13 were waited for; matrix products, arithmetic and copies ran while one was open for 5% of the time, Pallas kernels for 14%

profile of v9, /device:TPU:0, one launch (start us, length us, event | category | flops | bytes accessed | tf_op | source)
XLA Modules:
  0.0 408.0 jit_solution(10760658902496134820)
XLA Ops:
  7.8 7.5 %collective-permute-start = (bf16[896,2304]{1,0:T(8,128)(2,1)}, bf16[896,2304]{1,0:T(8,128)(2,1)}, u32[]{:S(2)}, u32[]{:S(2)}) collective-permute-start(bf16[896,2304]{1,0:T(8,128)(2,1)} %x.1), channel_id=1, source_target_pairs={{0,8},{8,16},{16,24},{1,9},{9,17},{17,25},{2,10},{10,18},{18,26},{... | collective-permute-start | bytes 12386312 | tf_op jit(solution)/shard_map/ppermute | solution.py:333
  15.4 9.0 %fusion = bf16[1,896,896]{2,1,0:T(8,128)(2,1)} fusion(bf16[896,2304]{1,0:T(8,128)(2,1)} %x.1), kind=kOutput, calls=%fused_computation.1 | convolution fusion | flops 3700178944 | bytes 5734400 | tf_op jit(solution)/shard_map/dot_general | solution.py:20
  24.5 39.6 %reduce-scatter.4.cloned.1.call-done = bf16[1,112,896]{2,1,0:T(8,128)(2,1)} async-done(((bf16[1,896,896]{2,1,0:T(8,128)(2,1)}), bf16[1,112,896]{2,1,0:T(8,128)(2,1)}) %reduce-scatter.4.cloned.1.call-update) | async-done | bytes 200720 | tf_op jit(solution)/shard_map/reduce_scatter | solution.py:336
  64.0 36.9 %collective-permute-done.1.l1 = bf16[896,2304]{1,0:T(8,128)(2,1)} collective-permute-done((bf16[896,2304]{1,0:T(8,128)(2,1)}, bf16[896,2304]{1,0:T(8,128)(2,1)}, u32[]{:S(2)}, u32[]{:S(2)}) %collective-permute-start.1) | collective-permute-done | bytes 4128800 | tf_op jit(solution)/shard_map/ppermute | solution.py:333
  103.4 2.8 collective-permute-start.3
  106.8 24.9 %shard_map.18 = bf16[4,896,896]{2,1,0:T(8,128)(2,1)} custom-call(bf16[896,2304]{1,0:T(8,128)(2,1)} %x.1, bf16[896,2304]{1,0:T(8,128)(2,1)} %collective-permute-done.1.l1, bf16[896,2304]{1,0:T(8,128)(2,1)} %collective-permute-done.r1), custom_call_target="tpu_custom_call" | custom-call | flops 14797504512 | bytes 12386304 | tf_op jit(solution)/shard_map/pallas_call | solution.py:67
  131.8 63.3 %collective-permute-done.2.l2 = bf16[896,2304]{1,0:T(8,128)(2,1)} collective-permute-done((bf16[896,2304]{1,0:T(8,128)(2,1)}, bf16[896,2304]{1,0:T(8,128)(2,1)}, u32[]{:S(2)}, u32[]{:S(2)}) %collective-permute-start.2) | collective-permute-done | bytes 4128800 | tf_op jit(solution)/shard_map/ppermute | solution.py:333
  195.1 2.1 shard_map.17
  197.2 3.1 reduce-scatter.6.cloned.1.call-done
  200.5 1.3 fusion.1
  202.4 1.3 collective-permute-start.4
  203.8 21.5 %collective-permute-done.4 = bf16[112,896]{1,0:T(8,128)(2,1)S(1)} collective-permute-done((bf16[112,896]{1,0:T(8,128)(2,1)S(1)}, bf16[112,896]{1,0:T(8,128)(2,1)S(1)}, u32[]{:S(2)}, u32[]{:S(2)}) %collective-permute-start.4) | collective-permute-done | bytes 200736 | tf_op jit(solution)/shard_map/ppermute | solution.py:333
  225.4 1.3 collective-permute-start.7
  226.7 4.6 %collective-permute-start.6 = (bf16[4,112,896]{2,1,0:T(8,128)(2,1)S(1)}, bf16[4,112,896]{2,1,0:T(8,128)(2,1)S(1)}, u32[]{:S(2)}, u32[]{:S(2)}) collective-permute-start(bf16[4,112,896]{2,1,0:T(8,128)(2,1)S(1)} %pad_maximum_fusion.own), channel_id=1, source_target_pairs={{0,8},{8,16},{16,24},{1,9},{9,17},{17,25},{2,10},{10,18},{18,26},{... | collective-permute-start | bytes 2408456 | tf_op jit(solution)/shard_map/ppermute | solution.py:333
  231.3 4.7 %add.16 = bf16[896,2304]{1,0:T(8,128)(2,1)S(1)} add(bf16[896,2304]{1,0:T(8,128)(2,1)} %collective-permute-done.2.l2, bf16[896,2304]{1,0:T(8,128)(2,1)} %collective-permute-done.3.r2) | non-fusion elementwise | flops 2064384 | bytes 12386304 | tf_op jit(solution)/shard_map/add | solution.py:354
  236.0 1.3 collective-permute-start.8
  237.3 16.2 %collective-permute-done.8 = bf16[896,256]{1,0:T(8,128)(2,1)S(1)} collective-permute-done((bf16[896,256]{1,0:T(8,128)(2,1)S(1)}, bf16[896,256]{1,0:T(8,128)(2,1)S(1)}, u32[]{:S(2)}, u32[]{:S(2)}) %collective-permute-start.8) | collective-permute-done | bytes 458784 | tf_op jit(solution)/shard_map/ppermute | solution.py:333
  254.3 1.3 collective-permute-start.9
  255.6 6.5 %collective-permute-done.9.end = bf16[1,112,896]{2,1,0:T(8,128)(2,1)S(1)} collective-permute-done((bf16[1,112,896]{2,1,0:T(8,128)(2,1)}, bf16[1,112,896]{2,1,0:T(8,128)(2,1)S(1)}, u32[]{:S(2)}, u32[]{:S(2)}) %collective-permute-start.9) | collective-permute-done | bytes 200736 | tf_op jit(solution)/shard_map/ppermute | solution.py:333
  262.2 2.1 maximum_add_fusion
  264.3 1.3 collective-permute-start.12
  266.4 16.4 %collective-permute-done.12.l2 = bf16[4,112,896]{2,1,0:T(8,128)(2,1)S(1)} collective-permute-done((bf16[4,112,896]{2,1,0:T(8,128)(2,1)S(1)}, bf16[4,112,896]{2,1,0:T(8,128)(2,1)S(1)}, u32[]{:S(2)}, u32[]{:S(2)}) %collective-permute-start.12) | collective-permute-done | bytes 802848 | tf_op jit(solution)/shard_map/ppermute | solution.py:333
  285.8 14.7 %collective-permute-done.13.l3 = bf16[4,112,896]{2,1,0:T(8,128)(2,1)S(1)} collective-permute-done((bf16[4,112,896]{2,1,0:T(8,128)(2,1)S(1)}, bf16[4,112,896]{2,1,0:T(8,128)(2,1)S(1)}, u32[]{:S(2)}, u32[]{:S(2)}) %collective-permute-start.13) | collective-permute-done | bytes 802848 | tf_op jit(solution)/shard_map/ppermute | solution.py:333
  300.4 3.6 slice.27
  306.3 1.7 copy-done
  308.0 4.8 %all-gather.4.cloned.1.call-done.panel = bf16[4,896,896]{2,1,0:T(8,128)(2,1)} async-done(((bf16[4,112,896]{2,1,0:T(8,128)(2,1)}), bf16[4,896,896]{2,1,0:T(8,128)(2,1)}) %all-gather.4.cloned.1.call-update) | async-done | bytes 6422544 | tf_op jit(solution)/shard_map/all_gather | solution.py:366
  312.8 10.7 %shard_map.20 = bf16[896,448]{1,0:T(8,128)(2,1)} custom-call(s32[2]{0:T(128)} %pad_add_fusion.place, bf16[4,896,896]{2,1,0:T(8,128)(2,1)} %all-gather.4.cloned.1.call-done.panel, bf16[4,448,896]{2,1,0:T(8,128)(2,1)} %copy-done), custom_call_target="tpu_custom_call" | custom-call | flops 2877292544 | bytes 8028160 | tf_op jit(solution)/shard_map/pallas_call | solution.py:192
  323.5 2.2 slice.26
  326.9 41.9 %collective-permute-done.16.value = bf16[896,1536]{1,0:T(8,128)(2,1)} collective-permute-done((bf16[896,1536]{1,0:T(8,128)(2,1)}, bf16[896,1536]{1,0:T(8,128)(2,1)}, u32[]{:S(2)}, u32[]{:S(2)}) %collective-permute-start.16) | collective-permute-done | bytes 2752544 | tf_op jit(solution)/shard_map/ppermute | solution.py:333
  368.8 4.8 %all-gather.6.cloned.1.call-done = bf16[7168,448]{1,0:T(8,128)(2,1)} async-done(((bf16[896,448]{1,0:T(8,128)(2,1)}), bf16[7168,448]{1,0:T(8,128)(2,1)}) %all-gather.6.cloned.1.call-update) | async-done | bytes 6422544 | tf_op jit(solution)/shard_map/all_gather | solution.py:376
  373.6 18.4 %shard_map.22.rest_1_ = bf16[896,2304]{1,0:T(8,128)(2,1)} custom-call(s32[2]{0:T(128)} %pad_add_fusion.place, bf16[8,896,448]{2,1,0:T(8,128)(2,1)} %bitcast.22, bf16[8,112,2304]{2,1,0:T(8,128)(2,1)} %bitcast.24, bf16[8,112,2304]{2,1,0:T(8,128)(2,1)} %bitcast.8.l1, bf16[8,112,2304]{2,1,0:T(8,128)(2,1)} %bitcast.9.r1, bf16[8,112,2304]{2,1,0:T(8,128)(2,1)} %bitcast.20, ...), custom_call_target="tpu_custom_call" | custom-call | tf_op jit(solution)/shard_map/pallas_call | solution.py:288
  392.0 8.9 %shard_map.23 = bf16[896,2304]{1,0:T(8,128)(2,1)} custom-call(s32[2]{0:T(128)} %pad_add_fusion.place, bf16[8,896,448]{2,1,0:T(8,128)(2,1)} %bitcast.23, bf16[8,112,2304]{2,1,0:T(8,128)(2,1)} %bitcast.25, bf16[8,112,2304]{2,1,0:T(8,128)(2,1)} %bitcast.8.l1, bf16[8,112,2304]{2,1,0:T(8,128)(2,1)} %bitcast.9.r1, ...), custom_call_target="tpu_custom_call", output_to_operand_aliasing={{}: (7, {})} | custom-call | flops 3288334336 | bytes 5505024 | tf_op jit(solution)/shard_map/pallas_call | solution.py:288
  (48 shorter events, 13.4 us)
Async XLA Ops:
  6.5 57.5 %reduce-scatter.4.cloned.1.call-start = ((), (), s32[]{:S(2)}) async-start(), calls=%async_computation.3 | async-start | bytes 1806336 | tf_op jit(solution)/shard_map/reduce_scatter | solution.py:336
  6.5 94.4 %collective-permute-start.1 = (bf16[896,2304]{1,0:T(8,128)(2,1)}, bf16[896,2304]{1,0:T(8,128)(2,1)}, u32[]{:S(2)}, u32[]{:S(2)}) collective-permute-start(bf16[896,2304]{1,0:T(8,128)(2,1)} %x.1), channel_id=1, source_target_pairs={{24,16},{16,8},{8,0},{25,17},{17,9},{9,1},{26,18},{18,10},{10,2},{... | collective-permute-start | bytes 12386312 | tf_op jit(solution)/shard_map/ppermute | solution.py:333
  7.8 94.3 %collective-permute-start = (bf16[896,2304]{1,0:T(8,128)(2,1)}, bf16[896,2304]{1,0:T(8,128)(2,1)}, u32[]{:S(2)}, u32[]{:S(2)}) collective-permute-start(bf16[896,2304]{1,0:T(8,128)(2,1)} %x.1), channel_id=1, source_target_pairs={{0,8},{8,16},{16,24},{1,9},{9,17},{17,25},{2,10},{10,18},{18,26},{... | collective-permute-start | bytes 12386312 | tf_op jit(solution)/shard_map/ppermute | solution.py:333
  24.4 176.0 %reduce-scatter.6.cloned.1.call-start = ((), (), s32[]{:S(2)}) async-start(), calls=%async_computation.4 | async-start | bytes 7225344 | tf_op jit(solution)/shard_map/reduce_scatter | solution.py:336
  102.1 93.0 %collective-permute-start.2 = (bf16[896,2304]{1,0:T(8,128)(2,1)}, bf16[896,2304]{1,0:T(8,128)(2,1)}, u32[]{:S(2)}, u32[]{:S(2)}) collective-permute-start(bf16[896,2304]{1,0:T(8,128)(2,1)} %collective-permute-done.1.l1), channel_id=1, source_target_pairs={{16,8},{8,0},{17,9},{9,1},{18,10},{10,2},{19,11},{11,3},{20,12},{1... | collective-permute-start | bytes 12386312 | tf_op jit(solution)/shard_map/ppermute | solution.py:333
  103.4 91.7 %collective-permute-start.3 = (bf16[896,2304]{1,0:T(8,128)(2,1)}, bf16[896,2304]{1,0:T(8,128)(2,1)}, u32[]{:S(2)}, u32[]{:S(2)}) collective-permute-start(bf16[896,2304]{1,0:T(8,128)(2,1)} %collective-permute-done.r1), channel_id=1, source_target_pairs={{8,16},{16,24},{9,17},{17,25},{10,18},{18,26},{11,19},{19,27},{12,... | collective-permute-start | bytes 12386312 | tf_op jit(solution)/shard_map/ppermute | solution.py:333
  131.7 122.6 %reduce-scatter.8.cloned.1.call-start = ((), (), s32[]{:S(2)}) async-start(), calls=%async_computation.5 | async-start | bytes 1806336 | tf_op jit(solution)/shard_map/reduce_scatter | solution.py:336
  195.1 30.1 %copy-start.4 = (bf16[1,112,896]{2,1,0:T(8,128)(2,1)S(1)}, bf16[1,112,896]{2,1,0:T(8,128)(2,1)}, u32[]{:S(2)}) copy-start(bf16[1,112,896]{2,1,0:T(8,128)(2,1)} %reduce-scatter.4.cloned.1.call-done) | copy-start | bytes 602116
  200.4 112.3 %all-gather.4.cloned.1.call-start = ((), (), s32[]{:S(2)}) async-start(), calls=%async_computation.6 | async-start | bytes 7225344 | tf_op jit(solution)/shard_map/all_gather | solution.py:366
  201.8 2.0 collective-permute-start.5
  202.4 22.8 %collective-permute-start.4 = (bf16[112,896]{1,0:T(8,128)(2,1)S(1)}, bf16[112,896]{1,0:T(8,128)(2,1)S(1)}, u32[]{:S(2)}, u32[]{:S(2)}) collective-permute-start(bf16[112,896]{1,0:T(8,128)(2,1)S(1)} %get-tuple-element.38), channel_id=1, source_target_pairs={{16,8},{8,0},{17,9},{9,1},{18,10},{10,2},{19,11},{11,3},{20,12},{1... | collective-permute-start | bytes 602120 | tf_op jit(solution)/shard_map/ppermute | solution.py:333
  225.4 28.1 %collective-permute-start.7 = (bf16[4,112,896]{2,1,0:T(8,128)(2,1)S(1)}, bf16[4,112,896]{2,1,0:T(8,128)(2,1)S(1)}, u32[]{:S(2)}, u32[]{:S(2)}) collective-permute-start(bf16[4,112,896]{2,1,0:T(8,128)(2,1)S(1)} %pad_maximum_fusion.own), channel_id=1, source_target_pairs={{24,16},{16,8},{8,0},{25,17},{17,9},{9,1},{26,18},{18,10},{10,2},{... | collective-permute-start | bytes 2408456 | tf_op jit(solution)/shard_map/ppermute | solution.py:333
  226.7 27.6 %collective-permute-start.6 = (bf16[4,112,896]{2,1,0:T(8,128)(2,1)S(1)}, bf16[4,112,896]{2,1,0:T(8,128)(2,1)S(1)}, u32[]{:S(2)}, u32[]{:S(2)}) collective-permute-start(bf16[4,112,896]{2,1,0:T(8,128)(2,1)S(1)} %pad_maximum_fusion.own), channel_id=1, source_target_pairs={{0,8},{8,16},{16,24},{1,9},{9,17},{17,25},{2,10},{10,18},{18,26},{... | collective-permute-start | bytes 2408456 | tf_op jit(solution)/shard_map/ppermute | solution.py:333
  236.0 17.5 %copy-start.3 = (bf16[896,2304]{1,0:T(8,128)(2,1)}, bf16[896,2304]{1,0:T(8,128)(2,1)S(1)}, u32[]{:S(2)}) copy-start(bf16[896,2304]{1,0:T(8,128)(2,1)S(1)} %add.16) | copy-start | bytes 12386308
  236.0 17.5 %collective-permute-start.8 = (bf16[896,256]{1,0:T(8,128)(2,1)S(1)}, bf16[896,256]{1,0:T(8,128)(2,1)S(1)}, u32[]{:S(2)}, u32[]{:S(2)}) collective-permute-start(bf16[896,256]{1,0:T(8,128)(2,1)S(1)} %slice.25), channel_id=1, source_target_pairs={{8,0},{16,24},{9,1},{17,25},{10,2},{18,26},{11,3},{19,27},{12,4},{... | collective-permute-start | bytes 1376264 | tf_op jit(solution)/shard_map/ppermute | solution.py:333
  253.5 0.8 copy-start.5
  254.3 7.8 %collective-permute-start.9 = (bf16[1,112,896]{2,1,0:T(8,128)(2,1)}, bf16[1,112,896]{2,1,0:T(8,128)(2,1)S(1)}, u32[]{:S(2)}, u32[]{:S(2)}) collective-permute-start(bf16[1,112,896]{2,1,0:T(8,128)(2,1)} %reduce-scatter.8.cloned.1.call-done.corner), channel_id=1, source_target_pairs={{8,0},{16,24},{9,1},{17,25},{10,2},{18,26},{11,3},{19,27},{12,4},{... | collective-permute-start | bytes 602120 | tf_op jit(solution)/shard_map/ppermute | solution.py:333
  262.2 43.2 %copy-start.1 = (bf16[1,112,896]{2,1,0:T(8,128)(2,1)S(1)}, bf16[1,112,896]{2,1,0:T(8,128)(2,1)}, u32[]{:S(2)}) copy-start(bf16[1,112,896]{2,1,0:T(8,128)(2,1)} %reduce-scatter.8.cloned.1.call-done.corner) | copy-start | bytes 602116
  262.2 43.2 %copy-start.2 = (s32[2]{0:T(128)S(1)}, s32[2]{0:T(128)}, u32[]{:S(2)}) copy-start(s32[2]{0:T(128)} %pad_add_fusion.place) | copy-start | bytes 28
  264.3 109.3 %all-gather.6.cloned.1.call-start = ((), (), s32[]{:S(2)}) async-start(), calls=%async_computation.7 | async-start | bytes 8257536 | tf_op jit(solution)/shard_map/all_gather | solution.py:376
  264.3 18.5 %collective-permute-start.12 = (bf16[4,112,896]{2,1,0:T(8,128)(2,1)S(1)}, bf16[4,112,896]{2,1,0:T(8,128)(2,1)S(1)}, u32[]{:S(2)}, u32[]{:S(2)}) collective-permute-start(bf16[4,112,896]{2,1,0:T(8,128)(2,1)S(1)} %collective-permute-done.7.l1), channel_id=1, source_target_pairs={{16,8},{8,0},{17,9},{9,1},{18,10},{10,2},{19,11},{11,3},{20,12},{1... | collective-permute-start | bytes 2408456 | tf_op jit(solution)/shard_map/ppermute | solution.py:333
  265.6 18.5 %collective-permute-start.10 = (bf16[4,112,896]{2,1,0:T(8,128)(2,1)S(1)}, bf16[4,112,896]{2,1,0:T(8,128)(2,1)S(1)}, u32[]{:S(2)}, u32[]{:S(2)}) collective-permute-start(bf16[4,112,896]{2,1,0:T(8,128)(2,1)S(1)} %collective-permute-done.6.r1), channel_id=1, source_target_pairs={{8,16},{16,24},{9,17},{17,25},{10,18},{18,26},{11,19},{19,27},{12,... | collective-permute-start | bytes 2408456 | tf_op jit(solution)/shard_map/ppermute | solution.py:333
  282.8 17.6 %collective-permute-start.13 = (bf16[4,112,896]{2,1,0:T(8,128)(2,1)S(1)}, bf16[4,112,896]{2,1,0:T(8,128)(2,1)S(1)}, u32[]{:S(2)}, u32[]{:S(2)}) collective-permute-start(bf16[4,112,896]{2,1,0:T(8,128)(2,1)S(1)} %collective-permute-done.12.l2), channel_id=1, source_target_pairs={{8,0},{9,1},{10,2},{11,3},{12,4},{13,5},{14,6},{15,7}} | collective-permute-start | bytes 2408456 | tf_op jit(solution)/shard_map/ppermute | solution.py:333
  284.1 16.3 %collective-permute-start.11 = (bf16[4,112,896]{2,1,0:T(8,128)(2,1)S(1)}, bf16[4,112,896]{2,1,0:T(8,128)(2,1)S(1)}, u32[]{:S(2)}, u32[]{:S(2)}) collective-permute-start(bf16[4,112,896]{2,1,0:T(8,128)(2,1)S(1)} %collective-permute-done.10.r2), channel_id=1, source_target_pairs={{16,24},{17,25},{18,26},{19,27},{20,28},{21,29},{22,30},{23,31}} | collective-permute-start | bytes 2408456 | tf_op jit(solution)/shard_map/ppermute | solution.py:333
  284.8 0.9 collective-permute-start.14
  304.0 64.8 %collective-permute-start.16 = (bf16[896,1536]{1,0:T(8,128)(2,1)}, bf16[896,1536]{1,0:T(8,128)(2,1)}, u32[]{:S(2)}, u32[]{:S(2)}) collective-permute-start(bf16[896,1536]{1,0:T(8,128)(2,1)} %slice.27), channel_id=1, source_target_pairs={{8,0},{16,24},{9,1},{17,25},{10,2},{18,26},{11,3},{19,27},{12,4},{... | collective-permute-start | bytes 8257544 | tf_op jit(solution)/shard_map/ppermute | solution.py:333
  306.3 1.7 copy-start
  325.6 66.4 %collective-permute-start.15 = (bf16[896,512]{1,0:T(8,128)(2,1)}, bf16[896,512]{1,0:T(8,128)(2,1)}, u32[]{:S(2)}, u32[]{:S(2)}) collective-permute-start(bf16[896,512]{1,0:T(8,128)(2,1)} %slice.26), channel_id=1, source_target_pairs={{8,0},{16,24},{9,1},{17,25},{10,2},{18,26},{11,3},{19,27},{12,4},{... | collective-permute-start | bytes 2752520 | tf_op jit(solution)/shard_map/ppermute | solution.py:333
Sparse Core Ops, SparseCore 0:
  24.5 39.4 reduce-scatter.3
  131.8 68.5 reduce-scatter.5
  204.2 48.1 reduce-scatter.7
  264.4 48.3 all-gather.3
  323.6 49.9 all-gather.5

commit v10 on v9

--- a/solution.py
+++ b/solution.py
@@ -56,10 +56,9 @@
     both[:rows, :] = x[...]
     for place, one, other in ((0, l1, r1), (1, r1, l1)):
         both[rows:, :] = other[...]
-        for part in (slice(0, rows // 2), slice(rows // 2, rows)):
-            value = dot_rows(both[...], one[part, :]).astype(out.dtype)
-            out[place, :, part] = value[:rows]
-            out[place + 2, :, part] = value[rows:]
+        value = dot_rows(both[...], one[...]).astype(out.dtype)
+        out[place] = value[:rows]
+        out[place + 2] = value[rows:]
 
 
 def near_blocks(x, l1, r1):
@@ -78,24 +77,19 @@
 
 
 def corner_kernel(place, l1, r1, l2, r2, out, held, sems):
-    rows = l1.shape[0]
-    marks = [*range(0, rows, 256), rows]
-    parts = [slice(a, b) for a, b in zip(marks, marks[1:])]
     for plane, one, other in ((1, r1, l2), (2, l1, r2)):
 
         @pl.when(place[0] == plane)
         def _(one=one, other=other):
-            copies = [pltpu.make_async_copy(one, held.at[0], sems.at[len(parts)])]
-            for p, part in enumerate(parts):
-                copies.append(
-                    pltpu.make_async_copy(other.at[part, :], held.at[1, part, :], sems.at[p])
-                )
+            copies = [
+                pltpu.make_async_copy(one, held.at[0], sems.at[0]),
+                pltpu.make_async_copy(other, held.at[1], sems.at[1]),
+            ]
             for copy in copies:
                 copy.start()
-            copies[0].wait()
-            for part, copy in zip(parts, copies[1:]):
+            for copy in copies:
                 copy.wait()
-                out[0, :, part] = dot_rows(held[0], held[1, part, :]).astype(out.dtype)
+            out[0] = dot_rows(held[0], held[1]).astype(out.dtype)
 
     @pl.when(jnp.logical_or(place[0] == 0, place[0] == 3))
     def _():
@@ -109,10 +103,7 @@
         out_shape=jax.ShapeDtypeStruct((1, rows, rows), jnp.bfloat16),
         in_specs=[scalars()] + [pl.BlockSpec(memory_space=pl.ANY)] * 4,
         out_specs=whole(),
-        scratch_shapes=[
-            pltpu.VMEM((2, rows, depth), jnp.bfloat16),
-            pltpu.SemaphoreType.DMA((pl.cdiv(rows, 256) + 1,)),
-        ],
+        scratch_shapes=[pltpu.VMEM((2, rows, depth), jnp.bfloat16), pltpu.SemaphoreType.DMA((2,))],
         compiler_params=pltpu.CompilerParams(vmem_limit_bytes=56 * 2**20),
         cost_estimate=pl.CostEstimate(
             flops=128 * rows * rows * depth, bytes_accessed=8 * rows * depth, transcendentals=0
@@ -122,7 +113,7 @@
 
 def strips_kernel(place, own, l1, r3, l2, r2, r1, l3, corner, pair, end, out):
     z = place[0]
-    part = own.shape[1]
+    _, part, rows = own.shape
     at_end = jnp.logical_or(z == 0, z == 3)
     zero = jnp.zeros_like(end[0])
     near = jnp.where(at_end, end[0], corner[0])
@@ -140,14 +131,15 @@
                 value = value + jnp.where((z + e) % 4 == 0, low, zero)
             if block == 1:
                 value = value + jnp.where((z + e) % 4 == 3, high, zero)
-            out[(block + e) % 4, e * part : (e + 1) * part, :] = value
+            place_of = (block + e) % 4 * rows
+            out[e * part : (e + 1) * part, place_of : place_of + rows] = value
 
 
 def strips(place, *others):
     _, part, rows = others[0].shape
     return pl.pallas_call(
         strips_kernel,
-        out_shape=jax.ShapeDtypeStruct((4, 4 * part, rows), jnp.bfloat16),
+        out_shape=jax.ShapeDtypeStruct((4 * part, 4 * rows), jnp.bfloat16),
         in_specs=[scalars()] + [whole()] * len(others),
         out_specs=whole(),
         compiler_params=pltpu.CompilerParams(vmem_limit_bytes=24 * 2**20),
@@ -157,18 +149,17 @@
     )(place, *others)
 
 
-def square_kernel(place, panel, right, out, held, first, sems):
+def square_kernel(place, panel, right, out, held, strip, sems):
     z = place[0]
-    rows, part = panel.shape[1], right.shape[1] // 4
-    order = (3, 1, 2, 0)
-    copies = {d: pltpu.make_async_copy(panel.at[d], held.at[d], sems.at[d]) for d in order}
-    for d in order:
-        copies[d].start()
-    first[...] = right[0]
-    total = jnp.zeros(out.shape, jnp.float32)
-    for d in order[:3]:
-        copies[d].wait()
-        total = total + dot_rows(held[d], right[d])
+    rows, part = panel.shape[1], right.shape[0] // 4
+    copies = [pltpu.make_async_copy(right, strip, sems.at[4])]
+    for d in range(4):
+        columns = held.at[:, d * rows : (d + 1) * rows]
+        copies.append(pltpu.make_async_copy(panel.at[d], columns, sems.at[d]))
+    for copy in copies:
+        copy.start()
+    for copy in copies:
+        copy.wait()
     for plane, block, e in ((0, 3, 3), (3, 1, 1)):
 
         @pl.when(z == plane)
@@ -176,28 +167,28 @@
             index = lax.broadcasted_iota(jnp.int32, (part, rows), 0) + place[1] * part
             other = lax.broadcasted_iota(jnp.int32, (part, rows), 1)
             pick = jnp.where(index == other, 1.0, 0.0).astype(jnp.bfloat16)
-            far = dot_rows(pick, held[block]).astype(first.dtype)
-            first[e * part : (e + 1) * part, :] = right[0, e * part : (e + 1) * part, :] + far
-
-    copies[0].wait()
-    total = total + dot_rows(held[0], first[...])
+            far = dot_rows(pick, held[:, block * rows : (block + 1) * rows]).astype(strip.dtype)
+            strip[e * part : (e + 1) * part, :rows] += far
+
+    total = dot_rows(held[...], strip[...])
     index = lax.broadcasted_iota(jnp.int32, (rows, rows), 0)
     other = lax.broadcasted_iota(jnp.int32, (rows, rows), 1)
     unit = jnp.where(index == other, 1.0, 0.0).astype(jnp.bfloat16)
-    out[...] = (coef_b * dot_rows(unit, first[...]) + coef_c * total).astype(out.dtype)
+    out[...] = (coef_b * dot_rows(unit, strip[:, :rows]) + coef_c * total).astype(out.dtype)
 
 
 def square(place, panel, right):
-    rows, depth = panel.shape[1], right.shape[1]
+    rows, depth = panel.shape[1], right.shape[0]
+    outside = pl.BlockSpec(memory_space=pl.ANY)
     return pl.pallas_call(
         square_kernel,
         out_shape=jax.ShapeDtypeStruct((rows, depth), jnp.bfloat16),
-        in_specs=[scalars(), pl.BlockSpec(memory_space=pl.ANY), whole()],
+        in_specs=[scalars(), outside, outside],
         out_specs=whole(),
         scratch_shapes=[
-            pltpu.VMEM(panel.shape, jnp.bfloat16),
-            pltpu.VMEM((depth, rows), jnp.bfloat16),
-            pltpu.SemaphoreType.DMA((4,)),
+            pltpu.VMEM((rows, 4 * rows), jnp.bfloat16),
+            pltpu.VMEM((depth, 4 * rows), jnp.bfloat16),
+            pltpu.SemaphoreType.DMA((5,)),
         ],
         compiler_params=pltpu.CompilerParams(vmem_limit_bytes=56 * 2**20),
         cost_estimate=pl.CostEstimate(
@@ -206,38 +197,43 @@
     )(place, panel, right)
 
 
-def product_kernel(starts, first, place, f, x, l1, r1, across, *rest):
-    n_piece = len(starts) - 1
-    far = rest[:n_piece]
+def product_kernel(marks, first, place, f, x, l1, r1, across, *rest):
+    far = rest[: len(marks) - 1]
     out, held_f, whole_f, wide, sems, f_sems = rest[-6:]
     z = place[0]
     n_col, rows, depth = f.shape
     part = depth // 4
     width = out.shape[1]
+    n_tile = (marks[-1] - marks[0]) // width
     step = pl.program_id(0)
 
-    def copy(source, tile, slot, d):
+    def copy(source, begin, count, slot, d, offset):
         return pltpu.make_async_copy(
-            source.at[:, :, pl.ds(pl.multiple_of(tile * width, width), width)],
-            wide.at[slot, :, pl.ds(d * part, part), :],
+            source.at[:, :, pl.ds(begin, count)],
+            wide.at[slot, :, pl.ds(d * part, part), pl.ds(offset, count)],
             sems.at[slot, d],
         )
 
     def fetch(tile, slot):
-        copy(x, first + tile, slot, 0).start()
-        copy(across, first + tile, slot, 2).start()
+        begin = pl.multiple_of(first + tile * width, 128)
+        copy(x, begin, width, slot, 0, 0).start()
+        copy(across, begin, width, slot, 2, 0).start()
         for d, usual, edge in ((1, l1, 3), (3, r1, 0)):
 
             @pl.when(z != edge)
             def _(d=d, usual=usual):
-                copy(usual, first + tile, slot, d).start()
-
-            for p in range(n_piece):
-                inside = jnp.logical_and(tile >= starts[p], tile < starts[p + 1])
-
-                @pl.when(jnp.logical_and(z == edge, inside))
-                def _(d=d, piece=far[p], begin=starts[p]):
-                    copy(piece, tile - begin, slot, d).start()
+                copy(usual, begin, width, slot, d, 0).start()
+
+            for t in range(n_tile):
+
+                @pl.when(jnp.logical_and(z == edge, tile == t))
+                def _(d=d, t=t):
+                    for piece, low, high in zip(far, marks, marks[1:]):
+                        left = max(low, first + t * width)
+                        right = min(high, first + (t + 1) * width)
+                        if left < right:
+                            offset = left - first - t * width
+                            copy(piece, left - low, right - left, slot, d, offset).start()
 
     slot = lax.rem(step, 2)
 
@@ -251,12 +247,12 @@
             copies[c].wait()
             whole_f[:, c * depth : (c + 1) * depth] = held_f[c]
 
-    @pl.when(step + 1 < starts[-1])
+    @pl.when(step + 1 < n_tile)
     def _():
         fetch(step + 1, 1 - slot)
 
     for d in range(4):
-        copy(x, first + step, slot, d).wait()
+        copy(x, 0, width, slot, d, 0).wait()
     total = jnp.dot(
         whole_f[...],
         wide[slot].reshape(n_col * depth, width),
@@ -266,17 +262,14 @@
     out[...] = (math.sqrt(N) * (coef_a * own + total)).astype(out.dtype)
 
 
-def product(place, f, near, far, tile, first, before):
+def product(place, f, near, far, tile, marks, before):
     n_col, rows, depth = f.shape
     part = rows // n_col
     columns = near[0].shape[1]
+    share = marks[-1] - marks[0]
 
     def split(value):
         return value.reshape(n_col, part, value.shape[1])
-
-    starts = [0]
-    for piece in far:
-        starts.append(starts[-1] + piece.shape[1] // tile)
 
     outside = pl.BlockSpec(memory_space=pl.ANY)
     operands = [place, f, *(split(value) for value in (*near, *far))]
@@ -284,13 +277,12 @@
     if before is not None:
         aliases = {len(operands): 0}
         operands.append(before)
-    share = tile * starts[-1]
-    return pl.pallas_call(
-        functools.partial(product_kernel, tuple(starts), first),
-        grid=(starts[-1],),
+    return pl.pallas_call(
+        functools.partial(product_kernel, tuple(marks), marks[0]),
+        grid=(share // tile,),
         out_shape=jax.ShapeDtypeStruct((rows, columns), jnp.bfloat16),
         in_specs=[scalars()] + [outside] * (len(operands) - 1),
-        out_specs=pl.BlockSpec((rows, tile), lambda i: (0, i + first)),
+        out_specs=pl.BlockSpec((rows, tile), lambda i: (0, i + marks[0] // tile)),
         scratch_shapes=[
             pltpu.VMEM(f.shape, jnp.bfloat16),
             pltpu.VMEM((rows, n_col * depth), jnp.bfloat16),
@@ -301,8 +293,8 @@
         input_output_aliases=aliases,
         compiler_params=pltpu.CompilerParams(vmem_limit_bytes=56 * 2**20),
         cost_estimate=pl.CostEstimate(
-            flops=2 * rows * n_col * depth * share if first else 0,
-            bytes_accessed=2 * 6 * rows * share if first else 0,
+            flops=2 * rows * n_col * depth * share if before is not None else 0,
+            bytes_accessed=2 * 6 * rows * share if before is not None else 0,
             transcendentals=0,
         ),
     )(*operands)
@@ -349,8 +341,7 @@
     tile = jnp.stack([own[0], first[0], second, first[1]])
     tr1, tl1 = send(tile, right), send(tile, left)
 
-    unit = 256
-    marks = [0, unit, x.shape[1] - 2 * unit, x.shape[1]]
+    marks = [0, 256, x.shape[1] - 768, x.shape[1]]
     across = l2 + r2
 
     def send_on(p, *after):
@@ -375,8 +366,8 @@
     far.append(send_on(2, factor))
     factor = lax.all_gather(factor, "col", axis=0, tiled=False)
     near = [x, l1, r1, across]
-    out = product(place, factor, near, far[:2], unit, 0, None)
-    return product(place, factor, near, far[2:], unit, marks[2] // unit, out)
+    out = product(place, factor, near, far[:2], 512, marks[:3], None)
+    return product(place, factor, near, far[2:], 768, marks[2:], out)
 
 
 def solution(mesh):

time: 411 us -> 405 us (0.985)
    ppermute x17, waiting for transfers between devices: 219 us -> 205 us  [send(): return lax.ppermute(value, 'row', pairs)]
    all_gather x1, waiting for transfers between devices: 4.76 us -> 15.1 us  [per_device_line(): factor = lax.all_gather(factor, 'col', axis=0, tiled=False)]
where the time goes in v10:
time: 405 us
  waiting for transfers between devices  268 us (66%)
  Pallas kernels  67.1 us (17%)
  starting transfers between devices  30.6 us (8%)
  between operations  13.4 us (3%)
  local copies, waits for them, and re-layouts  9.51 us (2%)
  matrix products  9.03 us (2%)
  other arithmetic  7.49 us (2%)
    ppermute x17, waiting for transfers between devices, send(): return lax.ppermute(value, 'row', pairs)  205 us
    reduce_scatter x3, waiting for transfers between devices, scatter(): return lax.psum_scatter(blocks, 'col', scatter_dimension=1, tiled=True)  42.5 us
    ppermute x17, starting transfers between devices, send(): return lax.ppermute(value, 'row', pairs)  30.4 us
    pallas_call x2, Pallas kernels, product(): pl.pallas_call(functools.partial(product_kernel, tuple(marks), marks[0]),...  28.4 us
    pallas_call x1, Pallas kernels, near_blocks(): pl.pallas_call(near_kernel, out_shape=jax.ShapeDtypeStruct((4, rows, rows...  24.8 us
    all_gather x1, waiting for transfers between devices, per_device_line(): factor = lax.all_gather(factor, 'col', axis=0, tiled=False)  15.1 us
    pallas_call x1, Pallas kernels, square(): pl.pallas_call(square_kernel, out_shape=jax.ShapeDtypeStruct((rows, depth...  10.7 us
    dot_general x1, matrix products, dot_rows(): lax.dot_general(left, right, (((1,), (1,)), ((), ())), preferred_element_...  9.03 us
  transfers between devices with their start and end apart: 22, of which 13 were waited for; matrix products, arithmetic and copies ran while one was open for 5% of the time, Pallas kernels for 14%

profile of v10, /device:TPU:0, one launch (start us, length us, event | category | flops | bytes accessed | tf_op | source)
XLA Modules:
  0.0 404.7 jit_solution(14352248769646328613)
XLA Ops:
  7.8 7.5 %collective-permute-start = (bf16[896,2304]{1,0:T(8,128)(2,1)}, bf16[896,2304]{1,0:T(8,128)(2,1)}, u32[]{:S(2)}, u32[]{:S(2)}) collective-permute-start(bf16[896,2304]{1,0:T(8,128)(2,1)} %x.1), channel_id=1, source_target_pairs={{0,8},{8,16},{16,24},{1,9},{9,17},{17,25},{2,10},{10,18},{18,26},{... | collective-permute-start | bytes 12386312 | tf_op jit(solution)/shard_map/ppermute | solution.py:325
  15.4 9.0 %fusion = bf16[1,896,896]{2,1,0:T(8,128)(2,1)} fusion(bf16[896,2304]{1,0:T(8,128)(2,1)} %x.1), kind=kOutput, calls=%fused_computation.1 | convolution fusion | flops 3700178944 | bytes 5734400 | tf_op jit(solution)/shard_map/dot_general | solution.py:20
  24.5 39.6 %reduce-scatter.4.cloned.1.call-done = bf16[1,112,896]{2,1,0:T(8,128)(2,1)} async-done(((bf16[1,896,896]{2,1,0:T(8,128)(2,1)}), bf16[1,112,896]{2,1,0:T(8,128)(2,1)}) %reduce-scatter.4.cloned.1.call-update) | async-done | bytes 200720 | tf_op jit(solution)/shard_map/reduce_scatter | solution.py:328
  64.0 36.9 %collective-permute-done.1.l1 = bf16[896,2304]{1,0:T(8,128)(2,1)} collective-permute-done((bf16[896,2304]{1,0:T(8,128)(2,1)}, bf16[896,2304]{1,0:T(8,128)(2,1)}, u32[]{:S(2)}, u32[]{:S(2)}) %collective-permute-start.1) | collective-permute-done | bytes 4128800 | tf_op jit(solution)/shard_map/ppermute | solution.py:325
  103.4 2.6 collective-permute-start.3
  106.6 24.8 %shard_map.18 = bf16[4,896,896]{2,1,0:T(8,128)(2,1)} custom-call(bf16[896,2304]{1,0:T(8,128)(2,1)} %x.1, bf16[896,2304]{1,0:T(8,128)(2,1)} %collective-permute-done.1.l1, bf16[896,2304]{1,0:T(8,128)(2,1)} %collective-permute-done.r1), custom_call_target="tpu_custom_call" | custom-call | flops 14797504512 | bytes 12386304 | tf_op jit(solution)/shard_map/pallas_call | solution.py:66
  131.5 63.6 %collective-permute-done.2.l2 = bf16[896,2304]{1,0:T(8,128)(2,1)} collective-permute-done((bf16[896,2304]{1,0:T(8,128)(2,1)}, bf16[896,2304]{1,0:T(8,128)(2,1)}, u32[]{:S(2)}, u32[]{:S(2)}) %collective-permute-start.2) | collective-permute-done | bytes 4128800 | tf_op jit(solution)/shard_map/ppermute | solution.py:325
  195.1 2.1 shard_map.17
  197.2 2.9 reduce-scatter.6.cloned.1.call-done
  200.2 1.3 fusion.1
  202.2 1.3 collective-permute-start.4
  203.5 17.8 %collective-permute-done.4 = bf16[112,896]{1,0:T(8,128)(2,1)S(1)} collective-permute-done((bf16[112,896]{1,0:T(8,128)(2,1)S(1)}, bf16[112,896]{1,0:T(8,128)(2,1)S(1)}, u32[]{:S(2)}, u32[]{:S(2)}) %collective-permute-start.4) | collective-permute-done | bytes 200736 | tf_op jit(solution)/shard_map/ppermute | solution.py:325
  221.5 1.3 collective-permute-start.7
  222.8 4.6 %collective-permute-start.6 = (bf16[4,112,896]{2,1,0:T(8,128)(2,1)S(1)}, bf16[4,112,896]{2,1,0:T(8,128)(2,1)S(1)}, u32[]{:S(2)}, u32[]{:S(2)}) collective-permute-start(bf16[4,112,896]{2,1,0:T(8,128)(2,1)S(1)} %pad_maximum_fusion.own), channel_id=1, source_target_pairs={{0,8},{8,16},{16,24},{1,9},{9,17},{17,25},{2,10},{10,18},{18,26},{... | collective-permute-start | bytes 2408456 | tf_op jit(solution)/shard_map/ppermute | solution.py:325
  227.4 4.7 %add.16 = bf16[896,2304]{1,0:T(8,128)(2,1)S(1)} add(bf16[896,2304]{1,0:T(8,128)(2,1)} %collective-permute-done.2.l2, bf16[896,2304]{1,0:T(8,128)(2,1)} %collective-permute-done.3.r2) | non-fusion elementwise | flops 2064384 | bytes 12386304 | tf_op jit(solution)/shard_map/add | solution.py:345
  232.2 1.3 collective-permute-start.8
  233.5 16.2 %collective-permute-done.8 = bf16[896,256]{1,0:T(8,128)(2,1)S(1)} collective-permute-done((bf16[896,256]{1,0:T(8,128)(2,1)S(1)}, bf16[896,256]{1,0:T(8,128)(2,1)S(1)}, u32[]{:S(2)}, u32[]{:S(2)}) %collective-permute-start.8) | collective-permute-done | bytes 458784 | tf_op jit(solution)/shard_map/ppermute | solution.py:325
  250.5 1.3 collective-permute-start.9
  251.8 6.5 %collective-permute-done.9.end = bf16[1,112,896]{2,1,0:T(8,128)(2,1)S(1)} collective-permute-done((bf16[1,112,896]{2,1,0:T(8,128)(2,1)}, bf16[1,112,896]{2,1,0:T(8,128)(2,1)S(1)}, u32[]{:S(2)}, u32[]{:S(2)}) %collective-permute-start.9) | collective-permute-done | bytes 200736 | tf_op jit(solution)/shard_map/ppermute | solution.py:325
  258.3 2.1 maximum_add_fusion
  260.5 1.3 collective-permute-start.12
  262.5 16.4 %collective-permute-done.12.l2 = bf16[4,112,896]{2,1,0:T(8,128)(2,1)S(1)} collective-permute-done((bf16[4,112,896]{2,1,0:T(8,128)(2,1)S(1)}, bf16[4,112,896]{2,1,0:T(8,128)(2,1)S(1)}, u32[]{:S(2)}, u32[]{:S(2)}) %collective-permute-start.12) | collective-permute-done | bytes 802848 | tf_op jit(solution)/shard_map/ppermute | solution.py:325
  281.6 14.9 %collective-permute-done.13.l3 = bf16[4,112,896]{2,1,0:T(8,128)(2,1)S(1)} collective-permute-done((bf16[4,112,896]{2,1,0:T(8,128)(2,1)S(1)}, bf16[4,112,896]{2,1,0:T(8,128)(2,1)S(1)}, u32[]{:S(2)}, u32[]{:S(2)}) %collective-permute-start.13) | collective-permute-done | bytes 802848 | tf_op jit(solution)/shard_map/ppermute | solution.py:325
  296.5 3.2 slice.27
  302.0 1.7 copy-done
  303.7 5.2 %all-gather.4.cloned.1.call-done.panel = bf16[4,896,896]{2,1,0:T(8,128)(2,1)} async-done(((bf16[4,112,896]{2,1,0:T(8,128)(2,1)}), bf16[4,896,896]{2,1,0:T(8,128)(2,1)}) %all-gather.4.cloned.1.call-update) | async-done | bytes 6422544 | tf_op jit(solution)/shard_map/all_gather | solution.py:357
  308.8 10.7 %shard_map.20 = bf16[896,448]{1,0:T(8,128)(2,1)} custom-call(s32[2]{0:T(128)} %pad_add_fusion.place, bf16[4,896,896]{2,1,0:T(8,128)(2,1)} %all-gather.4.cloned.1.call-done.panel, bf16[448,3584]{1,0:T(8,128)(2,1)} %copy-done), custom_call_target="tpu_custom_call" | custom-call | flops 2877292544 | bytes 8028160 | tf_op jit(solution)/shard_map/pallas_call | solution.py:183
  319.6 2.5 slice.26
  323.4 31.3 %collective-permute-done.16.value = bf16[896,1280]{1,0:T(8,128)(2,1)} collective-permute-done((bf16[896,1280]{1,0:T(8,128)(2,1)}, bf16[896,1280]{1,0:T(8,128)(2,1)}, u32[]{:S(2)}, u32[]{:S(2)}) %collective-permute-start.16) | collective-permute-done | bytes 2293792 | tf_op jit(solution)/shard_map/ppermute | solution.py:325
  354.7 15.1 %all-gather.6.cloned.1.call-done = bf16[7168,448]{1,0:T(8,128)(2,1)} async-done(((bf16[896,448]{1,0:T(8,128)(2,1)}), bf16[7168,448]{1,0:T(8,128)(2,1)}) %all-gather.6.cloned.1.call-update) | async-done | bytes 6422544 | tf_op jit(solution)/shard_map/all_gather | solution.py:367
  369.7 16.6 %shard_map.22.rest_1_ = bf16[896,2304]{1,0:T(8,128)(2,1)} custom-call(s32[2]{0:T(128)} %pad_add_fusion.place, bf16[8,896,448]{2,1,0:T(8,128)(2,1)} %bitcast.22, bf16[8,112,2304]{2,1,0:T(8,128)(2,1)} %bitcast.24, bf16[8,112,2304]{2,1,0:T(8,128)(2,1)} %bitcast.8.l1, bf16[8,112,2304]{2,1,0:T(8,128)(2,1)} %bitcast.9.r1, bf16[8,112,2304]{2,1,0:T(8,128)(2,1)} %bitcast.20, ...), custom_call_target="tpu_custom_call" | custom-call | tf_op jit(solution)/shard_map/pallas_call | solution.py:280
  386.4 11.8 %shard_map.23 = bf16[896,2304]{1,0:T(8,128)(2,1)} custom-call(s32[2]{0:T(128)} %pad_add_fusion.place, bf16[8,896,448]{2,1,0:T(8,128)(2,1)} %bitcast.23, bf16[8,112,2304]{2,1,0:T(8,128)(2,1)} %bitcast.25, bf16[8,112,2304]{2,1,0:T(8,128)(2,1)} %bitcast.8.l1, bf16[8,112,2304]{2,1,0:T(8,128)(2,1)} %bitcast.9.r1, ...), custom_call_target="tpu_custom_call", output_to_operand_aliasing={{}: (7, {})} | custom-call | flops 4932501504 | bytes 8257536 | tf_op jit(solution)/shard_map/pallas_call | solution.py:280
  (48 shorter events, 13.2 us)
Async XLA Ops:
  6.5 57.5 %reduce-scatter.4.cloned.1.call-start = ((), (), s32[]{:S(2)}) async-start(), calls=%async_computation.3 | async-start | bytes 1806336 | tf_op jit(solution)/shard_map/reduce_scatter | solution.py:328
  6.5 94.4 %collective-permute-start.1 = (bf16[896,2304]{1,0:T(8,128)(2,1)}, bf16[896,2304]{1,0:T(8,128)(2,1)}, u32[]{:S(2)}, u32[]{:S(2)}) collective-permute-start(bf16[896,2304]{1,0:T(8,128)(2,1)} %x.1), channel_id=1, source_target_pairs={{24,16},{16,8},{8,0},{25,17},{17,9},{9,1},{26,18},{18,10},{10,2},{... | collective-permute-start | bytes 12386312 | tf_op jit(solution)/shard_map/ppermute | solution.py:325
  7.8 94.3 %collective-permute-start = (bf16[896,2304]{1,0:T(8,128)(2,1)}, bf16[896,2304]{1,0:T(8,128)(2,1)}, u32[]{:S(2)}, u32[]{:S(2)}) collective-permute-start(bf16[896,2304]{1,0:T(8,128)(2,1)} %x.1), channel_id=1, source_target_pairs={{0,8},{8,16},{16,24},{1,9},{9,17},{17,25},{2,10},{10,18},{18,26},{... | collective-permute-start | bytes 12386312 | tf_op jit(solution)/shard_map/ppermute | solution.py:325
  24.4 175.7 %reduce-scatter.6.cloned.1.call-start = ((), (), s32[]{:S(2)}) async-start(), calls=%async_computation.4 | async-start | bytes 7225344 | tf_op jit(solution)/shard_map/reduce_scatter | solution.py:328
  102.1 93.0 %collective-permute-start.2 = (bf16[896,2304]{1,0:T(8,128)(2,1)}, bf16[896,2304]{1,0:T(8,128)(2,1)}, u32[]{:S(2)}, u32[]{:S(2)}) collective-permute-start(bf16[896,2304]{1,0:T(8,128)(2,1)} %collective-permute-done.1.l1), channel_id=1, source_target_pairs={{16,8},{8,0},{17,9},{9,1},{18,10},{10,2},{19,11},{11,3},{20,12},{1... | collective-permute-start | bytes 12386312 | tf_op jit(solution)/shard_map/ppermute | solution.py:325
  103.4 91.7 %collective-permute-start.3 = (bf16[896,2304]{1,0:T(8,128)(2,1)}, bf16[896,2304]{1,0:T(8,128)(2,1)}, u32[]{:S(2)}, u32[]{:S(2)}) collective-permute-start(bf16[896,2304]{1,0:T(8,128)(2,1)} %collective-permute-done.r1), channel_id=1, source_target_pairs={{8,16},{16,24},{9,17},{17,25},{10,18},{18,26},{11,19},{19,27},{12,... | collective-permute-start | bytes 12386312 | tf_op jit(solution)/shard_map/ppermute | solution.py:325
  131.5 119.0 %reduce-scatter.8.cloned.1.call-start = ((), (), s32[]{:S(2)}) async-start(), calls=%async_computation.5 | async-start | bytes 1806336 | tf_op jit(solution)/shard_map/reduce_scatter | solution.py:328
  195.1 26.3 %copy-start.4 = (bf16[1,112,896]{2,1,0:T(8,128)(2,1)S(1)}, bf16[1,112,896]{2,1,0:T(8,128)(2,1)}, u32[]{:S(2)}) copy-start(bf16[1,112,896]{2,1,0:T(8,128)(2,1)} %reduce-scatter.4.cloned.1.call-done) | copy-start | bytes 602116
  200.2 108.7 %all-gather.4.cloned.1.call-start = ((), (), s32[]{:S(2)}) async-start(), calls=%async_computation.6 | async-start | bytes 7225344 | tf_op jit(solution)/shard_map/all_gather | solution.py:357
  201.5 2.0 collective-permute-start.5
  202.2 19.2 %collective-permute-start.4 = (bf16[112,896]{1,0:T(8,128)(2,1)S(1)}, bf16[112,896]{1,0:T(8,128)(2,1)S(1)}, u32[]{:S(2)}, u32[]{:S(2)}) collective-permute-start(bf16[112,896]{1,0:T(8,128)(2,1)S(1)} %get-tuple-element.38), channel_id=1, source_target_pairs={{16,8},{8,0},{17,9},{9,1},{18,10},{10,2},{19,11},{11,3},{20,12},{1... | collective-permute-start | bytes 602120 | tf_op jit(solution)/shard_map/ppermute | solution.py:325
  221.5 28.2 %collective-permute-start.7 = (bf16[4,112,896]{2,1,0:T(8,128)(2,1)S(1)}, bf16[4,112,896]{2,1,0:T(8,128)(2,1)S(1)}, u32[]{:S(2)}, u32[]{:S(2)}) collective-permute-start(bf16[4,112,896]{2,1,0:T(8,128)(2,1)S(1)} %pad_maximum_fusion.own), channel_id=1, source_target_pairs={{24,16},{16,8},{8,0},{25,17},{17,9},{9,1},{26,18},{18,10},{10,2},{... | collective-permute-start | bytes 2408456 | tf_op jit(solution)/shard_map/ppermute | solution.py:325
  222.8 27.6 %collective-permute-start.6 = (bf16[4,112,896]{2,1,0:T(8,128)(2,1)S(1)}, bf16[4,112,896]{2,1,0:T(8,128)(2,1)S(1)}, u32[]{:S(2)}, u32[]{:S(2)}) collective-permute-start(bf16[4,112,896]{2,1,0:T(8,128)(2,1)S(1)} %pad_maximum_fusion.own), channel_id=1, source_target_pairs={{0,8},{8,16},{16,24},{1,9},{9,17},{17,25},{2,10},{10,18},{18,26},{... | collective-permute-start | bytes 2408456 | tf_op jit(solution)/shard_map/ppermute | solution.py:325
  232.1 17.6 %copy-start.3 = (bf16[896,2304]{1,0:T(8,128)(2,1)}, bf16[896,2304]{1,0:T(8,128)(2,1)S(1)}, u32[]{:S(2)}) copy-start(bf16[896,2304]{1,0:T(8,128)(2,1)S(1)} %add.16) | copy-start | bytes 12386308
  232.2 17.5 %collective-permute-start.8 = (bf16[896,256]{1,0:T(8,128)(2,1)S(1)}, bf16[896,256]{1,0:T(8,128)(2,1)S(1)}, u32[]{:S(2)}, u32[]{:S(2)}) collective-permute-start(bf16[896,256]{1,0:T(8,128)(2,1)S(1)} %slice.25), channel_id=1, source_target_pairs={{8,0},{16,24},{9,1},{17,25},{10,2},{18,26},{11,3},{19,27},{12,4},{... | collective-permute-start | bytes 1376264 | tf_op jit(solution)/shard_map/ppermute | solution.py:325
  249.7 0.8 copy-start.5
  250.5 7.8 %collective-permute-start.9 = (bf16[1,112,896]{2,1,0:T(8,128)(2,1)}, bf16[1,112,896]{2,1,0:T(8,128)(2,1)S(1)}, u32[]{:S(2)}, u32[]{:S(2)}) collective-permute-start(bf16[1,112,896]{2,1,0:T(8,128)(2,1)} %reduce-scatter.8.cloned.1.call-done.corner), channel_id=1, source_target_pairs={{8,0},{16,24},{9,1},{17,25},{10,2},{18,26},{11,3},{19,27},{12,4},{... | collective-permute-start | bytes 602120 | tf_op jit(solution)/shard_map/ppermute | solution.py:325
  251.7 49.2 %copy-start.1 = (bf16[1,112,896]{2,1,0:T(8,128)(2,1)S(1)}, bf16[1,112,896]{2,1,0:T(8,128)(2,1)}, u32[]{:S(2)}) copy-start(bf16[1,112,896]{2,1,0:T(8,128)(2,1)} %reduce-scatter.8.cloned.1.call-done.corner) | copy-start | bytes 602116
  251.8 49.2 %copy-start.2 = (s32[2]{0:T(128)S(1)}, s32[2]{0:T(128)}, u32[]{:S(2)}) copy-start(s32[2]{0:T(128)} %pad_add_fusion.place) | copy-start | bytes 28
  260.4 109.3 %all-gather.6.cloned.1.call-start = ((), (), s32[]{:S(2)}) async-start(), calls=%async_computation.7 | async-start | bytes 8257536 | tf_op jit(solution)/shard_map/all_gather | solution.py:367
  260.5 18.4 %collective-permute-start.12 = (bf16[4,112,896]{2,1,0:T(8,128)(2,1)S(1)}, bf16[4,112,896]{2,1,0:T(8,128)(2,1)S(1)}, u32[]{:S(2)}, u32[]{:S(2)}) collective-permute-start(bf16[4,112,896]{2,1,0:T(8,128)(2,1)S(1)} %collective-permute-done.7.l1), channel_id=1, source_target_pairs={{16,8},{8,0},{17,9},{9,1},{18,10},{10,2},{19,11},{11,3},{20,12},{1... | collective-permute-start | bytes 2408456 | tf_op jit(solution)/shard_map/ppermute | solution.py:325
  261.8 18.4 %collective-permute-start.10 = (bf16[4,112,896]{2,1,0:T(8,128)(2,1)S(1)}, bf16[4,112,896]{2,1,0:T(8,128)(2,1)S(1)}, u32[]{:S(2)}, u32[]{:S(2)}) collective-permute-start(bf16[4,112,896]{2,1,0:T(8,128)(2,1)S(1)} %collective-permute-done.6.r1), channel_id=1, source_target_pairs={{8,16},{16,24},{9,17},{17,25},{10,18},{18,26},{11,19},{19,27},{12,... | collective-permute-start | bytes 2408456 | tf_op jit(solution)/shard_map/ppermute | solution.py:325
  278.9 17.6 %collective-permute-start.13 = (bf16[4,112,896]{2,1,0:T(8,128)(2,1)S(1)}, bf16[4,112,896]{2,1,0:T(8,128)(2,1)S(1)}, u32[]{:S(2)}, u32[]{:S(2)}) collective-permute-start(bf16[4,112,896]{2,1,0:T(8,128)(2,1)S(1)} %collective-permute-done.12.l2), channel_id=1, source_target_pairs={{8,0},{9,1},{10,2},{11,3},{12,4},{13,5},{14,6},{15,7}} | collective-permute-start | bytes 2408456 | tf_op jit(solution)/shard_map/ppermute | solution.py:325
  280.2 16.3 %collective-permute-start.11 = (bf16[4,112,896]{2,1,0:T(8,128)(2,1)S(1)}, bf16[4,112,896]{2,1,0:T(8,128)(2,1)S(1)}, u32[]{:S(2)}, u32[]{:S(2)}) collective-permute-start(bf16[4,112,896]{2,1,0:T(8,128)(2,1)S(1)} %collective-permute-done.10.r2), channel_id=1, source_target_pairs={{16,24},{17,25},{18,26},{19,27},{20,28},{21,29},{22,30},{23,31}} | collective-permute-start | bytes 2408456 | tf_op jit(solution)/shard_map/ppermute | solution.py:325
  280.9 0.7 collective-permute-start.14
  299.7 55.0 %collective-permute-start.16 = (bf16[896,1280]{1,0:T(8,128)(2,1)}, bf16[896,1280]{1,0:T(8,128)(2,1)}, u32[]{:S(2)}, u32[]{:S(2)}) collective-permute-start(bf16[896,1280]{1,0:T(8,128)(2,1)} %slice.27), channel_id=1, source_target_pairs={{8,0},{16,24},{9,1},{17,25},{10,2},{18,26},{11,3},{19,27},{12,4},{... | collective-permute-start | bytes 6881288 | tf_op jit(solution)/shard_map/ppermute | solution.py:325
  302.0 1.7 copy-start
  322.1 64.2 %collective-permute-start.15 = (bf16[896,768]{1,0:T(8,128)(2,1)}, bf16[896,768]{1,0:T(8,128)(2,1)}, u32[]{:S(2)}, u32[]{:S(2)}) collective-permute-start(bf16[896,768]{1,0:T(8,128)(2,1)} %slice.26), channel_id=1, source_target_pairs={{8,0},{16,24},{9,1},{17,25},{10,2},{18,26},{11,3},{19,27},{12,4},{... | collective-permute-start | bytes 4128776 | tf_op jit(solution)/shard_map/ppermute | solution.py:325
Sparse Core Ops, SparseCore 0:
  24.6 39.4 reduce-scatter.3
  131.6 68.5 reduce-scatter.5
  204.0 44.4 reduce-scatter.7
  260.5 48.2 all-gather.3
  319.7 49.9 all-gather.5

commit v11 on v10

--- a/solution.py
+++ b/solution.py
@@ -51,42 +51,62 @@
     return pl.BlockSpec(memory_space=pltpu.SMEM)
 
 
-def near_kernel(x, l1, r1, out, both):
+def load_pieces(pieces, marks, target, sem):
+    copies = [
+        pltpu.make_async_copy(piece, target.at[:, low:high], sem.at[p])
+        for p, (piece, low, high) in enumerate(zip(pieces, marks, marks[1:]))
+    ]
+    for copy in copies:
+        copy.start()
+    return copies
+
+
+def near_kernel(marks, x, *rest):
+    n = len(marks) - 1
+    l1, r1 = rest[:n], rest[n : 2 * n]
+    out, held, sems = rest[2 * n :]
     rows = x.shape[0]
-    both[:rows, :] = x[...]
-    for place, one, other in ((0, l1, r1), (1, r1, l1)):
-        both[rows:, :] = other[...]
-        value = dot_rows(both[...], one[...]).astype(out.dtype)
-        out[place] = value[:rows]
-        out[place + 2] = value[rows:]
-
-
-def near_blocks(x, l1, r1):
+    copies = load_pieces([x], [0, marks[-1]], held.at[rows : 2 * rows], sems.at[0])
+    copies += load_pieces(l1, marks, held.at[2 * rows :], sems.at[1])
+    copies += load_pieces(r1, marks, held.at[:rows], sems.at[2])
+    for copy in copies:
+        copy.wait()
+    value = dot_rows(held[: 2 * rows], held[2 * rows :]).astype(out.dtype)
+    out[2] = value[:rows]
+    out[0] = value[rows:]
+    value = dot_rows(held[rows:], held[:rows]).astype(out.dtype)
+    out[1] = value[:rows]
+    out[3] = value[rows:]
+
+
+def near_blocks(x, l1, r1, marks):
     rows, depth = x.shape
     return pl.pallas_call(
-        near_kernel,
+        functools.partial(near_kernel, marks),
         out_shape=jax.ShapeDtypeStruct((4, rows, rows), jnp.bfloat16),
-        in_specs=[whole()] * 3,
+        in_specs=[pl.BlockSpec(memory_space=pl.ANY)] * (1 + len(l1) + len(r1)),
         out_specs=whole(),
-        scratch_shapes=[pltpu.VMEM((2 * rows, depth), jnp.bfloat16)],
-        compiler_params=pltpu.CompilerParams(vmem_limit_bytes=52 * 2**20),
+        scratch_shapes=[
+            pltpu.VMEM((3 * rows, depth), jnp.bfloat16),
+            pltpu.SemaphoreType.DMA((3, len(l1))),
+        ],
+        compiler_params=pltpu.CompilerParams(vmem_limit_bytes=56 * 2**20),
         cost_estimate=pl.CostEstimate(
             flops=8 * rows * rows * depth, bytes_accessed=6 * rows * depth, transcendentals=0
         ),
-    )(x, l1, r1)
-
-
-def corner_kernel(place, l1, r1, l2, r2, out, held, sems):
+    )(x, *l1, *r1)
+
+
+def corner_kernel(marks, place, *rest):
+    n = len(marks) - 1
+    l1, r1, l2, r2 = (rest[g * n : (g + 1) * n] for g in range(4))
+    out, held, sems = rest[4 * n :]
     for plane, one, other in ((1, r1, l2), (2, l1, r2)):
 
         @pl.when(place[0] == plane)
         def _(one=one, other=other):
-            copies = [
-                pltpu.make_async_copy(one, held.at[0], sems.at[0]),
-                pltpu.make_async_copy(other, held.at[1], sems.at[1]),
-            ]
-            for copy in copies:
-                copy.start()
+            copies = load_pieces(one, marks, held.at[0], sems.at[0])
+            copies += load_pieces(other, marks, held.at[1], sems.at[1])
             for copy in copies:
                 copy.wait()
             out[0] = dot_rows(held[0], held[1]).astype(out.dtype)
@@ -96,19 +116,22 @@
         out[...] = jnp.zeros_like(out)
 
 
-def corner_block(place, l1, r1, l2, r2):
-    rows, depth = l1.shape
-    return pl.pallas_call(
-        corner_kernel,
+def corner_block(place, l1, r1, l2, r2, marks):
+    rows, depth = l1[0].shape[0], marks[-1]
+    return pl.pallas_call(
+        functools.partial(corner_kernel, marks),
         out_shape=jax.ShapeDtypeStruct((1, rows, rows), jnp.bfloat16),
-        in_specs=[scalars()] + [pl.BlockSpec(memory_space=pl.ANY)] * 4,
+        in_specs=[scalars()] + [pl.BlockSpec(memory_space=pl.ANY)] * (4 * len(l1)),
         out_specs=whole(),
-        scratch_shapes=[pltpu.VMEM((2, rows, depth), jnp.bfloat16), pltpu.SemaphoreType.DMA((2,))],
+        scratch_shapes=[
+            pltpu.VMEM((2, rows, depth), jnp.bfloat16),
+            pltpu.SemaphoreType.DMA((2, len(l1))),
+        ],
         compiler_params=pltpu.CompilerParams(vmem_limit_bytes=56 * 2**20),
         cost_estimate=pl.CostEstimate(
             flops=128 * rows * rows * depth, bytes_accessed=8 * rows * depth, transcendentals=0
         ),
-    )(place, l1, r1, l2, r2)
+    )(place, *l1, *r1, *l2, *r2)
 
 
 def strips_kernel(place, own, l1, r3, l2, r2, r1, l3, corner, pair, end, out):
@@ -197,62 +220,70 @@
     )(place, panel, right)
 
 
-def product_kernel(marks, first, place, f, x, l1, r1, across, *rest):
+def product_kernel(marks, ready, place, f, x, *rest):
+    l1, r1, across, *rest = rest
     far = rest[: len(marks) - 1]
-    out, held_f, whole_f, wide, sems, f_sems = rest[-6:]
+    rest = rest[len(marks) - 1 + ready :]
+    out, whole_f, wide, sems = (rest[0], *rest[-4:-1])
     z = place[0]
-    n_col, rows, depth = f.shape
-    part = depth // 4
+    n_col, part, _ = x.shape
+    rows, depth = n_col * part, 4 * part
     width = out.shape[1]
     n_tile = (marks[-1] - marks[0]) // width
     step = pl.program_id(0)
 
-    def copy(source, begin, count, slot, d, offset):
+    def copy(source, begin, slot, d):
         return pltpu.make_async_copy(
-            source.at[:, :, pl.ds(begin, count)],
-            wide.at[slot, :, pl.ds(d * part, part), pl.ds(offset, count)],
+            source.at[:, :, pl.ds(pl.multiple_of(begin, width), width)],
+            wide.at[slot, :, pl.ds(d * part, part), :],
             sems.at[slot, d],
         )
 
     def fetch(tile, slot):
-        begin = pl.multiple_of(first + tile * width, 128)
-        copy(x, begin, width, slot, 0, 0).start()
-        copy(across, begin, width, slot, 2, 0).start()
+        begin = marks[0] + tile * width
+        copy(x, begin, slot, 0).start()
+        copy(across, tile * width, slot, 2).start()
         for d, usual, edge in ((1, l1, 3), (3, r1, 0)):
 
             @pl.when(z != edge)
             def _(d=d, usual=usual):
-                copy(usual, begin, width, slot, d, 0).start()
-
-            for t in range(n_tile):
-
-                @pl.when(jnp.logical_and(z == edge, tile == t))
-                def _(d=d, t=t):
-                    for piece, low, high in zip(far, marks, marks[1:]):
-                        left = max(low, first + t * width)
-                        right = min(high, first + (t + 1) * width)
-                        if left < right:
-                            offset = left - first - t * width
-                            copy(piece, left - low, right - left, slot, d, offset).start()
+                copy(usual, tile * width, slot, d).start()
+
+            for piece, low, high in zip(far, marks, marks[1:]):
+                inside = jnp.logical_and(begin >= low, begin < high)
+
+                @pl.when(jnp.logical_and(z == edge, inside))
+                def _(d=d, piece=piece, low=low):
+                    copy(piece, begin - low, slot, d).start()
 
     slot = lax.rem(step, 2)
+    if ready:
+        f_sems = rest[-1]
+        loads = [pltpu.make_async_copy(f, whole_f, f_sems.at[0])]
+    else:
+        held_f, f_sems = rest[2], rest[-1]
+        loads = [pltpu.make_async_copy(f.at[c], held_f.at[c], f_sems.at[c]) for c in range(n_col)]
+        save = pltpu.make_async_copy(whole_f, rest[1], f_sems.at[n_col])
 
     @pl.when(step == 0)
     def _():
-        copies = [pltpu.make_async_copy(f.at[c], held_f.at[c], f_sems.at[c]) for c in range(n_col)]
-        for one in copies:
+        for one in loads:
             one.start()
         fetch(0, 0)
-        for c in range(n_col):
-            copies[c].wait()
-            whole_f[:, c * depth : (c + 1) * depth] = held_f[c]
+        if ready:
+            loads[0].wait()
+        else:
+            for c in range(n_col):
+                loads[c].wait()
+                whole_f[:, c * depth : (c + 1) * depth] = held_f[c]
+            save.start()
 
     @pl.when(step + 1 < n_tile)
     def _():
         fetch(step + 1, 1 - slot)
 
     for d in range(4):
-        copy(x, 0, width, slot, d, 0).wait()
+        copy(x, 0, slot, d).wait()
     total = jnp.dot(
         whole_f[...],
         wide[slot].reshape(n_col * depth, width),
@@ -260,41 +291,54 @@
     )
     own = wide[slot, :, :part, :].reshape(rows, width).astype(jnp.float32)
     out[...] = (math.sqrt(N) * (coef_a * own + total)).astype(out.dtype)
-
-
-def product(place, f, near, far, tile, marks, before):
-    n_col, rows, depth = f.shape
+    if not ready:
+
+        @pl.when(step == n_tile - 1)
+        def _():
+            save.wait()
+
+
+def product(place, f, x, near, far, tile, marks, before):
+    rows, columns = x.shape
+    share = marks[-1] - marks[0]
+    ready = before is not None
+    n_col = N // columns
     part = rows // n_col
-    columns = near[0].shape[1]
-    share = marks[-1] - marks[0]
+    depth = 4 * part
 
     def split(value):
         return value.reshape(n_col, part, value.shape[1])
 
     outside = pl.BlockSpec(memory_space=pl.ANY)
-    operands = [place, f, *(split(value) for value in (*near, *far))]
+    operands = [place, f, *(split(value) for value in (x, *near, *far))]
     aliases = {}
-    if before is not None:
+    out_shape = [jax.ShapeDtypeStruct((rows, columns), jnp.bfloat16)]
+    out_specs = [pl.BlockSpec((rows, tile), lambda i: (0, i + marks[0] // tile))]
+    scratch = [
+        pltpu.VMEM((rows, n_col * depth), jnp.bfloat16),
+        pltpu.VMEM((2, n_col, depth, tile), jnp.bfloat16),
+        pltpu.SemaphoreType.DMA((2, 4)),
+        pltpu.SemaphoreType.DMA((n_col + 1,)),
+    ]
+    if ready:
         aliases = {len(operands): 0}
         operands.append(before)
-    return pl.pallas_call(
-        functools.partial(product_kernel, tuple(marks), marks[0]),
+    else:
+        out_shape.append(jax.ShapeDtypeStruct((rows, n_col * depth), jnp.bfloat16))
+        out_specs.append(outside)
+        scratch = [pltpu.VMEM(f.shape, jnp.bfloat16), *scratch]
+    return pl.pallas_call(
+        functools.partial(product_kernel, tuple(marks), ready),
         grid=(share // tile,),
-        out_shape=jax.ShapeDtypeStruct((rows, columns), jnp.bfloat16),
+        out_shape=out_shape,
         in_specs=[scalars()] + [outside] * (len(operands) - 1),
-        out_specs=pl.BlockSpec((rows, tile), lambda i: (0, i + marks[0] // tile)),
-        scratch_shapes=[
-            pltpu.VMEM(f.shape, jnp.bfloat16),
-            pltpu.VMEM((rows, n_col * depth), jnp.bfloat16),
-            pltpu.VMEM((2, n_col, depth, tile), jnp.bfloat16),
-            pltpu.SemaphoreType.DMA((2, 4)),
-            pltpu.SemaphoreType.DMA((n_col,)),
-        ],
+        out_specs=out_specs,
+        scratch_shapes=scratch,
         input_output_aliases=aliases,
         compiler_params=pltpu.CompilerParams(vmem_limit_bytes=56 * 2**20),
         cost_estimate=pl.CostEstimate(
-            flops=2 * rows * n_col * depth * share if before is not None else 0,
-            bytes_accessed=2 * 6 * rows * share if before is not None else 0,
+            flops=2 * rows * n_col * depth * share if ready else 0,
+            bytes_accessed=2 * 6 * rows * share if ready else 0,
             transcendentals=0,
         ),
     )(*operands)
@@ -327,13 +371,17 @@
     def scatter(blocks):
         return lax.psum_scatter(blocks, "col", scatter_dimension=1, tiled=True)
 
-    r1, l1 = send(x, right), send(x, left)
+    marks = [0, x.shape[1] - 768, x.shape[1]]
+    xs = [x[:, low:high] for low, high in zip(marks, marks[1:])]
+    r1 = [send(piece, right) for piece in xs]
+    l1 = [send(piece, left) for piece in xs]
     own = scatter(dot_rows(x, x).astype(jnp.bfloat16)[None])
-    own, r1, l1 = lax.optimization_barrier((own, r1, l1))
-    r2, l2 = send(r1, right[1:]), send(l1, left[1:])
-
-    first = scatter(near_blocks(x, l1, r1))
-    corner = corner_block(place, l1, r1, l2, r2)
+    own, r1[0], l1[0] = lax.optimization_barrier((own, r1[0], l1[0]))
+    r2 = [send(piece, right[1:]) for piece in r1]
+    l2 = [send(piece, left[1:]) for piece in l1]
+
+    first = scatter(near_blocks(x, l1, r1, marks))
+    corner = corner_block(place, l1, r1, l2, r2, marks)
     corner, first = lax.optimization_barrier((corner, first))
     corner = scatter(corner)
 
@@ -341,14 +389,13 @@
     tile = jnp.stack([own[0], first[0], second, first[1]])
     tr1, tl1 = send(tile, right), send(tile, left)
 
-    marks = [0, 256, x.shape[1] - 768, x.shape[1]]
-    across = l2 + r2
-
-    def send_on(p, *after):
-        value = lax.optimization_barrier((across, *after))[0]
-        return send(value[:, marks[p] : marks[p + 1]], [(1, 0), (2, 3)])
-
-    far = [send_on(0, tile)]
+    across = [a + b for a, b in zip(l2, r2)]
+    far_marks = [0, 256, *marks[1:]]
+
+    def send_on(value, *after):
+        return send(lax.optimization_barrier((value, *after))[0], [(1, 0), (2, 3)])
+
+    far = [send_on(across[0][:, :256], tile)]
     corner, tr1, tl1, far[0] = lax.optimization_barrier((corner, tr1, tl1, far[0]))
     end = send(corner, [(1, 0), (2, 3)])
     pair = send(corner, [(1, 2), (2, 1)])
@@ -359,15 +406,18 @@
     end, tr1, tl1 = lax.optimization_barrier((end, tr1, tl1))
     tr2, tl2 = send(tr1, right[1:]), send(tl1, left[1:])
     tr3, tl3 = send(tr2, right[2:]), send(tl2, left[2:])
-    far.append(arrived(send_on(1, tr3, tl3, pair)))
+    far.append(arrived(send_on(across[0][:, 256:], tr3, tl3, pair)))
 
     rights = strips(place, tile, tl1, tr3, tl2, tr2, tr1, tl3, corner, pair, end)
     factor = square(place, panel, rights)
-    far.append(send_on(2, factor))
+    far.append(send_on(across[1], factor))
     factor = lax.all_gather(factor, "col", axis=0, tiled=False)
-    near = [x, l1, r1, across]
-    out = product(place, factor, near, far[:2], 512, marks[:3], None)
-    return product(place, factor, near, far[2:], 768, marks[2:], out)
+    near = [l1, r1, across]
+    out, factor = product(
+        place, factor, x, [group[0] for group in near], far[:2], 256, far_marks[:3], None
+    )
+    (out,) = product(place, factor, x, [group[1] for group in near], far[2:], 256, marks[1:], out)
+    return out
 
 
 def solution(mesh):

time: 405 us -> 402 us (level)
  waiting for transfers between devices: 268 us -> 255 us
  starting transfers between devices: 30.6 us -> 37.9 us
    ppermute x17 -> x21, starting transfers between devices: 30.4 us -> 37.7 us  [send(): return lax.ppermute(value, 'row', pairs)]
    ppermute x17 -> x21, waiting for transfers between devices: 205 us -> 200 us  [send(): return lax.ppermute(value, 'row', pairs)]
    all_gather x1, waiting for transfers between devices: 5.16 us -> 0.97 us  [per_device_line(): lax.all_gather(tile + jnp.concatenate(added), 'col', axis=1, tiled=True)]
    slice x3 -> x4, local copies, waits for them, and re-layouts: 5.75 us -> 9.44 us  [the longest x2 6.16 us: per_device_line(): xs = [x[:, low:high] for low, high in zip(marks, marks[1:])]]
  transfers between devices with their start and end apart: 22 -> 26, of which waited for: 13 -> 14; matrix products, arithmetic and copies ran while one was open for 5% -> 5% of each run, Pallas kernels for 14% -> 14%
where the time goes in v11:
time: 402 us; the launch traced here: 401 us
  waiting for transfers between devices  255 us (63%)
  Pallas kernels  66.5 us (17%)
  starting transfers between devices  37.9 us (9%)
  between operations  13.5 us (3%)
  local copies, waits for them, and re-layouts  13.2 us (3%)
  other arithmetic  9.44 us (2%)
  matrix products  5.56 us (1%)
    ppermute x21, waiting for transfers between devices, send(): return lax.ppermute(value, 'row', pairs)  200 us
    reduce_scatter x3, waiting for transfers between devices, scatter(): return lax.psum_scatter(blocks, 'col', scatter_dimension=1, tiled=True)  39.9 us
    ppermute x21, starting transfers between devices, send(): return lax.ppermute(value, 'row', pairs)  37.7 us
    pallas_call x2, Pallas kernels, product(): pl.pallas_call(functools.partial(product_kernel, tuple(marks), ready), gr...  27.9 us
    pallas_call x1, Pallas kernels, near_blocks(): pl.pallas_call(functools.partial(near_kernel, marks), out_shape=jax.Shape...  24.9 us
    all_gather x1, waiting for transfers between devices, per_device_line(): factor = lax.all_gather(factor, 'col', axis=0, tiled=False)  14.1 us
    pallas_call x1, Pallas kernels, square(): pl.pallas_call(square_kernel, out_shape=jax.ShapeDtypeStruct((rows, depth...  10.8 us
  transfers between devices with their start and end apart: 26, of which 14 were waited for; matrix products, arithmetic and copies ran while one was open for 5% of the time, Pallas kernels for 14%

profile of v11, /device:TPU:0, one launch (start us, length us, event | category | flops | bytes accessed | tf_op | source)
XLA Modules:
  0.0 401.0 jit_solution(11155825703632838188)
XLA Ops:
  6.5 3.6 slice.24
  11.5 7.1 %collective-permute-start = (bf16[896,1536]{1,0:T(8,128)(2,1)}, bf16[896,1536]{1,0:T(8,128)(2,1)}, u32[]{:S(2)}, u32[]{:S(2)}) collective-permute-start(bf16[896,1536]{1,0:T(8,128)(2,1)} %slice.24), channel_id=1, source_target_pairs={{0,8},{8,16},{16,24},{1,9},{9,17},{17,25},{2,10},{10,18},{18,26},{... | collective-permute-start | bytes 8257544 | tf_op jit(solution)/shard_map/ppermute | solution.py:369
  18.5 5.6 %fusion = bf16[1,896,896]{2,1,0:T(8,128)(2,1)} fusion(bf16[896,2304]{1,0:T(8,128)(2,1)S(1)} %copy-done.3), kind=kOutput, calls=%fused_computation.1 | convolution fusion | flops 3700178944 | bytes 5734400 | tf_op jit(solution)/shard_map/dot_general | solution.py:20
  24.2 2.5 slice.25
  26.7 3.5 collective-permute-start.3
  31.5 30.9 %reduce-scatter.4.cloned.1.call-done = bf16[1,112,896]{2,1,0:T(8,128)(2,1)} async-done(((bf16[1,896,896]{2,1,0:T(8,128)(2,1)}), bf16[1,112,896]{2,1,0:T(8,128)(2,1)}) %reduce-scatter.4.cloned.1.call-update) | async-done | bytes 200720 | tf_op jit(solution)/shard_map/reduce_scatter | solution.py:372
  62.4 13.4 %collective-permute-done.1.rest_0_ = bf16[896,1536]{1,0:T(8,128)(2,1)S(1)} collective-permute-done((bf16[896,1536]{1,0:T(8,128)(2,1)}, bf16[896,1536]{1,0:T(8,128)(2,1)S(1)}, u32[]{:S(2)}, u32[]{:S(2)}) %collective-permute-start.1) | collective-permute-done | bytes 2752544 | tf_op jit(solution)/shard_map/ppermute | solution.py:369
  75.8 1.6 collective-permute-done.rest_2_
  78.7 2.2 collective-permute-start.6
  81.5 24.2 %collective-permute-done.3.rest_3_ = bf16[896,768]{1,0:T(8,128)(2,1)} collective-permute-done((bf16[896,768]{1,0:T(8,128)(2,1)}, bf16[896,768]{1,0:T(8,128)(2,1)}, u32[]{:S(2)}, u32[]{:S(2)}) %collective-permute-start.3) | collective-permute-done | bytes 1376288 | tf_op jit(solution)/shard_map/ppermute | solution.py:369
  105.8 1.8 collective-permute-start.7
  107.6 1.5 collective-permute-start.5
  109.0 24.9 %shard_map.18 = bf16[4,896,896]{2,1,0:T(8,128)(2,1)} custom-call(bf16[896,2304]{1,0:T(8,128)(2,1)} %x.1, bf16[896,1536]{1,0:T(8,128)(2,1)} %copy-done.5, bf16[896,768]{1,0:T(8,128)(2,1)} %collective-permute-done.2.rest_1_, bf16[896,1536]{1,0:T(8,128)(2,1)} %collective-permute-done.rest_2_, bf16[896,768]{1,0:T(8,128)(2,1)} %collective-permute-done.3.rest_3_), custom_call_target="tpu_custom_call" | custom-call | flops 14797504512 | bytes 12386304 | tf_op jit(solution)/shard_map/pallas_call | solution.py:84
  134.0 59.0 %collective-permute-done.5.rest_5_ = bf16[896,768]{1,0:T(8,128)(2,1)} collective-permute-done((bf16[896,768]{1,0:T(8,128)(2,1)}, bf16[896,768]{1,0:T(8,128)(2,1)}, u32[]{:S(2)}, u32[]{:S(2)}) %collective-permute-start.5) | collective-permute-done | bytes 1376288 | tf_op jit(solution)/shard_map/ppermute | solution.py:369
  193.1 2.0 shard_map.17
  195.1 9.1 %reduce-scatter.6.cloned.1.call-done = bf16[4,112,896]{2,1,0:T(8,128)(2,1)} async-done(((bf16[4,896,896]{2,1,0:T(8,128)(2,1)}), bf16[4,112,896]{2,1,0:T(8,128)(2,1)}) %reduce-scatter.6.cloned.1.call-update) | async-done | bytes 802832 | tf_op jit(solution)/shard_map/reduce_scatter | solution.py:372
  207.5 9.6 %collective-permute-done.8 = bf16[112,896]{1,0:T(8,128)(2,1)S(1)} collective-permute-done((bf16[112,896]{1,0:T(8,128)(2,1)S(1)}, bf16[112,896]{1,0:T(8,128)(2,1)S(1)}, u32[]{:S(2)}, u32[]{:S(2)}) %collective-permute-start.8) | collective-permute-done | bytes 200736 | tf_op jit(solution)/shard_map/ppermute | solution.py:369
  218.6 4.6 %collective-permute-start.10 = (bf16[4,112,896]{2,1,0:T(8,128)(2,1)S(1)}, bf16[4,112,896]{2,1,0:T(8,128)(2,1)S(1)}, u32[]{:S(2)}, u32[]{:S(2)}) collective-permute-start(bf16[4,112,896]{2,1,0:T(8,128)(2,1)S(1)} %pad_maximum_fusion.own), channel_id=1, source_target_pairs={{0,8},{8,16},{16,24},{1,9},{9,17},{17,25},{2,10},{10,18},{18,26},{... | collective-permute-start | bytes 2408456 | tf_op jit(solution)/shard_map/ppermute | solution.py:369
  223.2 3.3 add.19
  227.9 18.5 %collective-permute-done.12 = bf16[896,256]{1,0:T(8,128)(2,1)S(1)} collective-permute-done((bf16[896,256]{1,0:T(8,128)(2,1)S(1)}, bf16[896,256]{1,0:T(8,128)(2,1)S(1)}, u32[]{:S(2)}, u32[]{:S(2)}) %collective-permute-start.12) | collective-permute-done | bytes 458784 | tf_op jit(solution)/shard_map/ppermute | solution.py:369
  248.6 7.1 %collective-permute-done.13.end = bf16[1,112,896]{2,1,0:T(8,128)(2,1)S(1)} collective-permute-done((bf16[1,112,896]{2,1,0:T(8,128)(2,1)}, bf16[1,112,896]{2,1,0:T(8,128)(2,1)S(1)}, u32[]{:S(2)}, u32[]{:S(2)}) %collective-permute-start.13) | collective-permute-done | bytes 200736 | tf_op jit(solution)/shard_map/ppermute | solution.py:369
  255.8 2.1 maximum_add_fusion
  259.9 18.2 %collective-permute-done.16.l2 = bf16[4,112,896]{2,1,0:T(8,128)(2,1)S(1)} collective-permute-done((bf16[4,112,896]{2,1,0:T(8,128)(2,1)S(1)}, bf16[4,112,896]{2,1,0:T(8,128)(2,1)S(1)}, u32[]{:S(2)}, u32[]{:S(2)}) %collective-permute-start.16) | collective-permute-done | bytes 802848 | tf_op jit(solution)/shard_map/ppermute | solution.py:369
  280.8 3.3 slice.33
  284.1 13.4 %collective-permute-done.17.l3 = bf16[4,112,896]{2,1,0:T(8,128)(2,1)S(1)} collective-permute-done((bf16[4,112,896]{2,1,0:T(8,128)(2,1)S(1)}, bf16[4,112,896]{2,1,0:T(8,128)(2,1)S(1)}, u32[]{:S(2)}, u32[]{:S(2)}) %collective-permute-start.17) | collective-permute-done | bytes 802848 | tf_op jit(solution)/shard_map/ppermute | solution.py:369
  298.8 3.2 add.21
  303.0 1.7 copy-done
  305.6 10.8 %shard_map.20 = bf16[896,448]{1,0:T(8,128)(2,1)} custom-call(s32[2]{0:T(128)} %pad_add_fusion.place, bf16[4,896,896]{2,1,0:T(8,128)(2,1)} %all-gather.4.cloned.1.call-done.panel, bf16[448,3584]{1,0:T(8,128)(2,1)} %copy-done), custom_call_target="tpu_custom_call" | custom-call | flops 2877292544 | bytes 8028160 | tf_op jit(solution)/shard_map/pallas_call | solution.py:206
  317.7 34.8 %collective-permute-done.19.value = bf16[896,1280]{1,0:T(8,128)(2,1)} collective-permute-done((bf16[896,1280]{1,0:T(8,128)(2,1)}, bf16[896,1280]{1,0:T(8,128)(2,1)}, u32[]{:S(2)}, u32[]{:S(2)}) %collective-permute-start.19) | collective-permute-done | bytes 2293792 | tf_op jit(solution)/shard_map/ppermute | solution.py:369
  352.5 14.1 %all-gather.6.cloned.1.call-done = bf16[7168,448]{1,0:T(8,128)(2,1)} async-done(((bf16[896,448]{1,0:T(8,128)(2,1)}), bf16[7168,448]{1,0:T(8,128)(2,1)}) %all-gather.6.cloned.1.call-update) | async-done | bytes 6422544 | tf_op jit(solution)/shard_map/all_gather | solution.py:414
  366.5 17.4 %shard_map.22 = (bf16[896,2304]{1,0:T(8,128)(2,1)}, bf16[896,3584]{1,0:T(8,128)(2,1)}) custom-call(s32[2]{0:T(128)} %pad_add_fusion.place, bf16[8,896,448]{2,1,0:T(8,128)(2,1)} %bitcast.26, bf16[8,112,2304]{2,1,0:T(8,128)(2,1)} %bitcast.23, bf16[8,112,1536]{2,1,0:T(8,128)(2,1)} %bitcast.27, bf16[8,112,1536]{2,1,0:T(8,128)(2,1)} %bitcast.9.rest_1_, ...), custom_call_target="tpu_custom_call" | custom-call | tf_op jit(solution)/shard_map/pallas_call | solution.py:330
  383.9 10.5 %shard_map.23 = bf16[896,2304]{1,0:T(8,128)(2,1)} custom-call(s32[2]{0:T(128)} %pad_add_fusion.place, bf16[896,3584]{1,0:T(8,128)(2,1)} %get-tuple-element.36.f, bf16[8,112,2304]{2,1,0:T(8,128)(2,1)} %bitcast.24, bf16[8,112,768]{2,1,0:T(8,128)(2,1)} %bitcast.13.rest_0_, bf16[8,112,768]{2,1,0:T(8,128)(2,1)} %bitcast.14.rest_1_, ...), custom_call_target="tpu_custom_call", output_to_operand_aliasing={{}: (7, {})} | custom-call | flops 4932501504 | bytes 8257536 | tf_op jit(solution)/shard_map/pallas_call | solution.py:330
  (62 shorter events, 22.2 us)
Async XLA Ops:
  6.5 55.9 %reduce-scatter.4.cloned.1.call-start = ((), (), s32[]{:S(2)}) async-start(), calls=%async_computation.3 | async-start | bytes 1806336 | tf_op jit(solution)/shard_map/reduce_scatter | solution.py:372
  6.5 12.0 %copy-start.3 = (bf16[896,2304]{1,0:T(8,128)(2,1)S(1)}, bf16[896,2304]{1,0:T(8,128)(2,1)}, u32[]{:S(2)}) copy-start(bf16[896,2304]{1,0:T(8,128)(2,1)} %x.1) | copy-start | bytes 12386308
  10.2 65.6 %collective-permute-start.1 = (bf16[896,1536]{1,0:T(8,128)(2,1)}, bf16[896,1536]{1,0:T(8,128)(2,1)S(1)}, u32[]{:S(2)}, u32[]{:S(2)}) collective-permute-start(bf16[896,1536]{1,0:T(8,128)(2,1)} %slice.24), channel_id=1, source_target_pairs={{24,16},{16,8},{8,0},{25,17},{17,9},{9,1},{26,18},{18,10},{10,2},{... | collective-permute-start | bytes 8257544 | tf_op jit(solution)/shard_map/ppermute | solution.py:369
  11.5 65.9 %collective-permute-start = (bf16[896,1536]{1,0:T(8,128)(2,1)}, bf16[896,1536]{1,0:T(8,128)(2,1)}, u32[]{:S(2)}, u32[]{:S(2)}) collective-permute-start(bf16[896,1536]{1,0:T(8,128)(2,1)} %slice.24), channel_id=1, source_target_pairs={{0,8},{8,16},{16,24},{1,9},{9,17},{17,25},{2,10},{10,18},{18,26},{... | collective-permute-start | bytes 8257544 | tf_op jit(solution)/shard_map/ppermute | solution.py:369
  24.1 180.0 %reduce-scatter.6.cloned.1.call-start = ((), (), s32[]{:S(2)}) async-start(), calls=%async_computation.4 | async-start | bytes 7225344 | tf_op jit(solution)/shard_map/reduce_scatter | solution.py:372
  26.7 79.1 %collective-permute-start.3 = (bf16[896,768]{1,0:T(8,128)(2,1)}, bf16[896,768]{1,0:T(8,128)(2,1)}, u32[]{:S(2)}, u32[]{:S(2)}) collective-permute-start(bf16[896,768]{1,0:T(8,128)(2,1)} %slice.25), channel_id=1, source_target_pairs={{0,8},{8,16},{16,24},{1,9},{9,17},{17,25},{2,10},{10,18},{18,26},{... | collective-permute-start | bytes 4128776 | tf_op jit(solution)/shard_map/ppermute | solution.py:369
  30.2 77.3 %collective-permute-start.2 = (bf16[896,768]{1,0:T(8,128)(2,1)}, bf16[896,768]{1,0:T(8,128)(2,1)}, u32[]{:S(2)}, u32[]{:S(2)}) collective-permute-start(bf16[896,768]{1,0:T(8,128)(2,1)} %slice.25), channel_id=1, source_target_pairs={{24,16},{16,8},{8,0},{25,17},{17,9},{9,1},{26,18},{18,10},{10,2},{... | collective-permute-start | bytes 4128776 | tf_op jit(solution)/shard_map/ppermute | solution.py:369
  75.8 33.2 %copy-start.5 = (bf16[896,1536]{1,0:T(8,128)(2,1)}, bf16[896,1536]{1,0:T(8,128)(2,1)S(1)}, u32[]{:S(2)}) copy-start(bf16[896,1536]{1,0:T(8,128)(2,1)S(1)} %collective-permute-done.1.rest_0_) | copy-start | bytes 8257540
  77.4 115.6 %collective-permute-start.4 = (bf16[896,1536]{1,0:T(8,128)(2,1)S(1)}, bf16[896,1536]{1,0:T(8,128)(2,1)}, u32[]{:S(2)}, u32[]{:S(2)}) collective-permute-start(bf16[896,1536]{1,0:T(8,128)(2,1)S(1)} %collective-permute-done.1.rest_0_), channel_id=1, source_target_pairs={{16,8},{8,0},{17,9},{9,1},{18,10},{10,2},{19,11},{11,3},{20,12},{1... | collective-permute-start | bytes 8257544 | tf_op jit(solution)/shard_map/ppermute | solution.py:369
  78.7 114.4 %collective-permute-start.6 = (bf16[896,1536]{1,0:T(8,128)(2,1)}, bf16[896,1536]{1,0:T(8,128)(2,1)}, u32[]{:S(2)}, u32[]{:S(2)}) collective-permute-start(bf16[896,1536]{1,0:T(8,128)(2,1)} %collective-permute-done.rest_2_), channel_id=1, source_target_pairs={{8,16},{16,24},{9,17},{17,25},{10,18},{18,26},{11,19},{19,27},{12,... | collective-permute-start | bytes 8257544 | tf_op jit(solution)/shard_map/ppermute | solution.py:369
  105.8 28.3 %collective-permute-start.7 = (bf16[896,768]{1,0:T(8,128)(2,1)}, bf16[896,768]{1,0:T(8,128)(2,1)}, u32[]{:S(2)}, u32[]{:S(2)}) collective-permute-start(bf16[896,768]{1,0:T(8,128)(2,1)} %collective-permute-done.3.rest_3_), channel_id=1, source_target_pairs={{8,16},{16,24},{9,17},{17,25},{10,18},{18,26},{11,19},{19,27},{12,... | collective-permute-start | bytes 4128776 | tf_op jit(solution)/shard_map/ppermute | solution.py:369
  107.6 85.5 %collective-permute-start.5 = (bf16[896,768]{1,0:T(8,128)(2,1)}, bf16[896,768]{1,0:T(8,128)(2,1)}, u32[]{:S(2)}, u32[]{:S(2)}) collective-permute-start(bf16[896,768]{1,0:T(8,128)(2,1)} %collective-permute-done.2.rest_1_), channel_id=1, source_target_pairs={{16,8},{8,0},{17,9},{9,1},{18,10},{10,2},{19,11},{11,3},{20,12},{1... | collective-permute-start | bytes 4128776 | tf_op jit(solution)/shard_map/ppermute | solution.py:369
  134.0 113.2 %reduce-scatter.8.cloned.1.call-start = ((), (), s32[]{:S(2)}) async-start(), calls=%async_computation.5 | async-start | bytes 1806336 | tf_op jit(solution)/shard_map/reduce_scatter | solution.py:372
  195.1 22.1 %copy-start.6 = (bf16[1,112,896]{2,1,0:T(8,128)(2,1)S(1)}, bf16[1,112,896]{2,1,0:T(8,128)(2,1)}, u32[]{:S(2)}) copy-start(bf16[1,112,896]{2,1,0:T(8,128)(2,1)} %reduce-scatter.4.cloned.1.call-done) | copy-start | bytes 602116
  204.2 101.5 %all-gather.4.cloned.1.call-start = ((), (), s32[]{:S(2)}) async-start(), calls=%async_computation.6 | async-start | bytes 7225344 | tf_op jit(solution)/shard_map/all_gather | solution.py:404
  205.5 2.0 collective-permute-start.9
  206.2 10.9 %collective-permute-start.8 = (bf16[112,896]{1,0:T(8,128)(2,1)S(1)}, bf16[112,896]{1,0:T(8,128)(2,1)S(1)}, u32[]{:S(2)}, u32[]{:S(2)}) collective-permute-start(bf16[112,896]{1,0:T(8,128)(2,1)S(1)} %get-tuple-element.42), channel_id=1, source_target_pairs={{16,8},{8,0},{17,9},{9,1},{18,10},{10,2},{19,11},{11,3},{20,12},{1... | collective-permute-start | bytes 602120 | tf_op jit(solution)/shard_map/ppermute | solution.py:369
  217.3 29.1 %collective-permute-start.11 = (bf16[4,112,896]{2,1,0:T(8,128)(2,1)S(1)}, bf16[4,112,896]{2,1,0:T(8,128)(2,1)S(1)}, u32[]{:S(2)}, u32[]{:S(2)}) collective-permute-start(bf16[4,112,896]{2,1,0:T(8,128)(2,1)S(1)} %pad_maximum_fusion.own), channel_id=1, source_target_pairs={{24,16},{16,8},{8,0},{25,17},{17,9},{9,1},{26,18},{18,10},{10,2},{... | collective-permute-start | bytes 2408456 | tf_op jit(solution)/shard_map/ppermute | solution.py:369
  218.6 28.5 %collective-permute-start.10 = (bf16[4,112,896]{2,1,0:T(8,128)(2,1)S(1)}, bf16[4,112,896]{2,1,0:T(8,128)(2,1)S(1)}, u32[]{:S(2)}, u32[]{:S(2)}) collective-permute-start(bf16[4,112,896]{2,1,0:T(8,128)(2,1)S(1)} %pad_maximum_fusion.own), channel_id=1, source_target_pairs={{0,8},{8,16},{16,24},{1,9},{9,17},{17,25},{2,10},{10,18},{18,26},{... | collective-permute-start | bytes 2408456 | tf_op jit(solution)/shard_map/ppermute | solution.py:369
  226.6 19.8 %copy-start.4 = (bf16[896,1536]{1,0:T(8,128)(2,1)}, bf16[896,1536]{1,0:T(8,128)(2,1)S(1)}, u32[]{:S(2)}) copy-start(bf16[896,1536]{1,0:T(8,128)(2,1)S(1)} %add.19) | copy-start | bytes 8257540
  226.6 19.8 %collective-permute-start.12 = (bf16[896,256]{1,0:T(8,128)(2,1)S(1)}, bf16[896,256]{1,0:T(8,128)(2,1)S(1)}, u32[]{:S(2)}, u32[]{:S(2)}) collective-permute-start(bf16[896,256]{1,0:T(8,128)(2,1)S(1)} %slice.32), channel_id=1, source_target_pairs={{8,0},{16,24},{9,1},{17,25},{10,2},{18,26},{11,3},{19,27},{12,4},{... | collective-permute-start | bytes 1376264 | tf_op jit(solution)/shard_map/ppermute | solution.py:369
  247.1 33.0 %copy-start.1 = (bf16[1,112,896]{2,1,0:T(8,128)(2,1)S(1)}, bf16[1,112,896]{2,1,0:T(8,128)(2,1)}, u32[]{:S(2)}) copy-start(bf16[1,112,896]{2,1,0:T(8,128)(2,1)} %reduce-scatter.8.cloned.1.call-done.corner) | copy-start | bytes 602116
  247.1 8.6 %collective-permute-start.13 = (bf16[1,112,896]{2,1,0:T(8,128)(2,1)}, bf16[1,112,896]{2,1,0:T(8,128)(2,1)S(1)}, u32[]{:S(2)}, u32[]{:S(2)}) collective-permute-start(bf16[1,112,896]{2,1,0:T(8,128)(2,1)} %reduce-scatter.8.cloned.1.call-done.corner), channel_id=1, source_target_pairs={{8,0},{16,24},{9,1},{17,25},{10,2},{18,26},{11,3},{19,27},{12,4},{... | collective-permute-start | bytes 602120 | tf_op jit(solution)/shard_map/ppermute | solution.py:369
  257.9 108.7 %all-gather.6.cloned.1.call-start = ((), (), s32[]{:S(2)}) async-start(), calls=%async_computation.7 | async-start | bytes 8257536 | tf_op jit(solution)/shard_map/all_gather | solution.py:414
  257.9 20.2 %collective-permute-start.16 = (bf16[4,112,896]{2,1,0:T(8,128)(2,1)S(1)}, bf16[4,112,896]{2,1,0:T(8,128)(2,1)S(1)}, u32[]{:S(2)}, u32[]{:S(2)}) collective-permute-start(bf16[4,112,896]{2,1,0:T(8,128)(2,1)S(1)} %collective-permute-done.11.l1), channel_id=1, source_target_pairs={{16,8},{8,0},{17,9},{9,1},{18,10},{10,2},{19,11},{11,3},{20,12},{1... | collective-permute-start | bytes 2408456 | tf_op jit(solution)/shard_map/ppermute | solution.py:369
  259.2 20.2 %collective-permute-start.14 = (bf16[4,112,896]{2,1,0:T(8,128)(2,1)S(1)}, bf16[4,112,896]{2,1,0:T(8,128)(2,1)S(1)}, u32[]{:S(2)}, u32[]{:S(2)}) collective-permute-start(bf16[4,112,896]{2,1,0:T(8,128)(2,1)S(1)} %collective-permute-done.10.r1), channel_id=1, source_target_pairs={{8,16},{16,24},{9,17},{17,25},{10,18},{18,26},{11,19},{19,27},{12,... | collective-permute-start | bytes 2408456 | tf_op jit(solution)/shard_map/ppermute | solution.py:369
  278.1 19.4 %collective-permute-start.17 = (bf16[4,112,896]{2,1,0:T(8,128)(2,1)S(1)}, bf16[4,112,896]{2,1,0:T(8,128)(2,1)S(1)}, u32[]{:S(2)}, u32[]{:S(2)}) collective-permute-start(bf16[4,112,896]{2,1,0:T(8,128)(2,1)S(1)} %collective-permute-done.16.l2), channel_id=1, source_target_pairs={{8,0},{9,1},{10,2},{11,3},{12,4},{13,5},{14,6},{15,7}} | collective-permute-start | bytes 2408456 | tf_op jit(solution)/shard_map/ppermute | solution.py:369
  279.4 18.1 %collective-permute-start.15 = (bf16[4,112,896]{2,1,0:T(8,128)(2,1)S(1)}, bf16[4,112,896]{2,1,0:T(8,128)(2,1)S(1)}, u32[]{:S(2)}, u32[]{:S(2)}) collective-permute-start(bf16[4,112,896]{2,1,0:T(8,128)(2,1)S(1)} %collective-permute-done.14.r2), channel_id=1, source_target_pairs={{16,24},{17,25},{18,26},{19,27},{20,28},{21,29},{22,30},{23,31}} | collective-permute-start | bytes 2408456 | tf_op jit(solution)/shard_map/ppermute | solution.py:369
  280.1 3.9 collective-permute-start.18
  284.1 17.9 %copy-start.2 = (s32[2]{0:T(128)S(1)}, s32[2]{0:T(128)}, u32[]{:S(2)}) copy-start(s32[2]{0:T(128)} %pad_add_fusion.place) | copy-start | bytes 28
  297.5 55.0 %collective-permute-start.19 = (bf16[896,1280]{1,0:T(8,128)(2,1)}, bf16[896,1280]{1,0:T(8,128)(2,1)}, u32[]{:S(2)}, u32[]{:S(2)}) collective-permute-start(bf16[896,1280]{1,0:T(8,128)(2,1)} %slice.33), channel_id=1, source_target_pairs={{8,0},{16,24},{9,1},{17,25},{10,2},{18,26},{11,3},{19,27},{12,4},{... | collective-permute-start | bytes 6881288 | tf_op jit(solution)/shard_map/ppermute | solution.py:369
  316.4 67.5 %collective-permute-start.20 = (bf16[896,768]{1,0:T(8,128)(2,1)}, bf16[896,768]{1,0:T(8,128)(2,1)}, u32[]{:S(2)}, u32[]{:S(2)}) collective-permute-start(bf16[896,768]{1,0:T(8,128)(2,1)} %add.21), channel_id=1, source_target_pairs={{8,0},{16,24},{9,1},{17,25},{10,2},{18,26},{11,3},{19,27},{12,4},{... | collective-permute-start | bytes 4128776 | tf_op jit(solution)/shard_map/ppermute | solution.py:369
  (2 other events, 2.4 us)
Sparse Core Ops, SparseCore 0:
  24.2 38.1 reduce-scatter.3
  134.1 69.9 reduce-scatter.5
  208.0 38.7 reduce-scatter.7
  258.0 47.6 all-gather.3
  316.5 49.9 all-gather.5

commit v12 on v11

--- a/solution.py
+++ b/solution.py
@@ -134,7 +134,7 @@
     )(place, *l1, *r1, *l2, *r2)
 
 
-def strips_kernel(place, own, l1, r3, l2, r2, r1, l3, corner, pair, end, out):
+def strips_kernel(place, own, l1, r3, l2, r2, r1, l3, corner, pair, end, out, linear):
     z = place[0]
     _, part, rows = own.shape
     at_end = jnp.logical_or(z == 0, z == 3)
@@ -156,26 +156,36 @@
                 value = value + jnp.where((z + e) % 4 == 3, high, zero)
             place_of = (block + e) % 4 * rows
             out[e * part : (e + 1) * part, place_of : place_of + rows] = value
+    index = lax.broadcasted_iota(jnp.int32, (rows, rows), 0)
+    other = lax.broadcasted_iota(jnp.int32, (rows, rows), 1)
+    unit = jnp.where(index == other, 1.0, 0.0).astype(jnp.bfloat16)
+    linear[...] = dot_rows(unit, out[:, :rows]).astype(linear.dtype)
 
 
 def strips(place, *others):
     _, part, rows = others[0].shape
     return pl.pallas_call(
         strips_kernel,
-        out_shape=jax.ShapeDtypeStruct((4 * part, 4 * rows), jnp.bfloat16),
+        out_shape=[
+            jax.ShapeDtypeStruct((4 * part, 4 * rows), jnp.bfloat16),
+            jax.ShapeDtypeStruct((rows, 4 * part), jnp.bfloat16),
+        ],
         in_specs=[scalars()] + [whole()] * len(others),
-        out_specs=whole(),
-        compiler_params=pltpu.CompilerParams(vmem_limit_bytes=24 * 2**20),
+        out_specs=[whole(), whole()],
+        compiler_params=pltpu.CompilerParams(vmem_limit_bytes=56 * 2**20),
         cost_estimate=pl.CostEstimate(
             flops=16 * part * rows, bytes_accessed=2 * 44 * part * rows, transcendentals=0
         ),
     )(place, *others)
 
 
-def square_kernel(place, panel, right, out, held, strip, sems):
+def square_kernel(place, panel, right, linear, out, held, strip, line, sems):
     z = place[0]
     rows, part = panel.shape[1], right.shape[0] // 4
-    copies = [pltpu.make_async_copy(right, strip, sems.at[4])]
+    copies = [
+        pltpu.make_async_copy(right, strip, sems.at[4]),
+        pltpu.make_async_copy(linear, line, sems.at[5]),
+    ]
     for d in range(4):
         columns = held.at[:, d * rows : (d + 1) * rows]
         copies.append(pltpu.make_async_copy(panel.at[d], columns, sems.at[d]))
@@ -190,34 +200,34 @@
             index = lax.broadcasted_iota(jnp.int32, (part, rows), 0) + place[1] * part
             other = lax.broadcasted_iota(jnp.int32, (part, rows), 1)
             pick = jnp.where(index == other, 1.0, 0.0).astype(jnp.bfloat16)
-            far = dot_rows(pick, held[:, block * rows : (block + 1) * rows]).astype(strip.dtype)
-            strip[e * part : (e + 1) * part, :rows] += far
+            corner = held[:, block * rows : (block + 1) * rows]
+            here = slice(e * part, (e + 1) * part)
+            strip[here, :rows] += dot_rows(pick, corner).astype(strip.dtype)
+            line[:, here] += dot_rows(corner, pick).astype(line.dtype)
 
     total = dot_rows(held[...], strip[...])
-    index = lax.broadcasted_iota(jnp.int32, (rows, rows), 0)
-    other = lax.broadcasted_iota(jnp.int32, (rows, rows), 1)
-    unit = jnp.where(index == other, 1.0, 0.0).astype(jnp.bfloat16)
-    out[...] = (coef_b * dot_rows(unit, strip[:, :rows]) + coef_c * total).astype(out.dtype)
-
-
-def square(place, panel, right):
+    out[...] = (coef_b * line[...].astype(jnp.float32) + coef_c * total).astype(out.dtype)
+
+
+def square(place, panel, right, linear):
     rows, depth = panel.shape[1], right.shape[0]
     outside = pl.BlockSpec(memory_space=pl.ANY)
     return pl.pallas_call(
         square_kernel,
         out_shape=jax.ShapeDtypeStruct((rows, depth), jnp.bfloat16),
-        in_specs=[scalars(), outside, outside],
+        in_specs=[scalars(), outside, outside, outside],
         out_specs=whole(),
         scratch_shapes=[
             pltpu.VMEM((rows, 4 * rows), jnp.bfloat16),
             pltpu.VMEM((depth, 4 * rows), jnp.bfloat16),
-            pltpu.SemaphoreType.DMA((5,)),
+            pltpu.VMEM((rows, depth), jnp.bfloat16),
+            pltpu.SemaphoreType.DMA((6,)),
         ],
         compiler_params=pltpu.CompilerParams(vmem_limit_bytes=56 * 2**20),
         cost_estimate=pl.CostEstimate(
             flops=2 * rows * rows * 4 * depth, bytes_accessed=2 * 5 * rows * rows, transcendentals=0
         ),
-    )(place, panel, right)
+    )(place, panel, right, linear)
 
 
 def product_kernel(marks, ready, place, f, x, *rest):
@@ -383,7 +393,8 @@
     first = scatter(near_blocks(x, l1, r1, marks))
     corner = corner_block(place, l1, r1, l2, r2, marks)
     corner, first = lax.optimization_barrier((corner, first))
-    corner = scatter(corner)
+    shares = lax.all_to_all(corner.reshape(n_col, -1, corner.shape[2]), "col", 0, 0)
+    corner = shares.astype(jnp.float32).sum(0, keepdims=True).astype(jnp.bfloat16)
 
     second = send(first[2], left[1:]) + send(first[3], right[1:])
     tile = jnp.stack([own[0], first[0], second, first[1]])
@@ -395,21 +406,21 @@
     def send_on(value, *after):
         return send(lax.optimization_barrier((value, *after))[0], [(1, 0), (2, 3)])
 
-    far = [send_on(across[0][:, :256], tile)]
-    corner, tr1, tl1, far[0] = lax.optimization_barrier((corner, tr1, tl1, far[0]))
     end = send(corner, [(1, 0), (2, 3)])
     pair = send(corner, [(1, 2), (2, 1)])
     zero = jnp.zeros_like(end)
     added = [zero, jnp.where(z == 3, end, zero), zero, jnp.where(z == 0, end, zero)]
     panel = lax.all_gather(tile + jnp.concatenate(added), "col", axis=1, tiled=True)
 
+    far = [send_on(across[0][:, :256], end)]
+    pair, far[0] = lax.optimization_barrier((pair, far[0]))
     end, tr1, tl1 = lax.optimization_barrier((end, tr1, tl1))
     tr2, tl2 = send(tr1, right[1:]), send(tl1, left[1:])
     tr3, tl3 = send(tr2, right[2:]), send(tl2, left[2:])
     far.append(arrived(send_on(across[0][:, 256:], tr3, tl3, pair)))
 
-    rights = strips(place, tile, tl1, tr3, tl2, tr2, tr1, tl3, corner, pair, end)
-    factor = square(place, panel, rights)
+    strip, linear = strips(place, tile, tl1, tr3, tl2, tr2, tr1, tl3, corner, pair, end)
+    factor = square(place, panel, strip, linear)
     far.append(send_on(across[1], factor))
     factor = lax.all_gather(factor, "col", axis=0, tiled=False)
     near = [l1, r1, across]

time: 402 us -> 418 us (1.040)
  waiting for transfers between devices: 255 us -> 266 us
  Pallas kernels: 66.5 us -> 71 us
    all_to_all x0 -> x1, waiting for transfers between devices: none -> 18.5 us  [per_device_line(): lax.all_to_all(corner.reshape(n_col, -1, corner.shape[2]), 'col', 0, 0)]
    ppermute x21, waiting for transfers between devices: 200 us -> 184 us  [send(): return lax.ppermute(value, 'row', pairs)]
    all_gather x1, waiting for transfers between devices: 14.1 us -> 23.7 us  [per_device_line(): factor = lax.all_gather(factor, 'col', axis=0, tiled=False)]
    pallas_call x1, Pallas kernels: 0.98 us -> 5.93 us  [strips(): pl.pallas_call(strips_kernel, out_shape=[jax.ShapeDtypeStruct((4 * part,...]
    reduce_scatter x3 -> x2, waiting for transfers between devices: 39.9 us -> 39.7 us  [scatter(): return lax.psum_scatter(blocks, 'col', scatter_dimension=1, tiled=True)]
  transfers between devices with their start and end apart: 26 -> 26, of which waited for: 14 -> 14; matrix products, arithmetic and copies ran while one was open for 5% -> 4% of each run, Pallas kernels for 14% -> 14%
where the time goes in v12:
time: 418 us; the launch traced here: 417 us
  waiting for transfers between devices  266 us (64%)
  Pallas kernels  71 us (17%)
  starting transfers between devices  41.4 us (10%)
  between operations  13.5 us (3%)
  local copies, waits for them, and re-layouts  11 us (3%)
  other arithmetic  8.63 us (2%)
  matrix products  5.52 us (1%)
    ppermute x21, waiting for transfers between devices, send(): return lax.ppermute(value, 'row', pairs)  184 us
    reduce_scatter x2, waiting for transfers between devices, scatter(): return lax.psum_scatter(blocks, 'col', scatter_dimension=1, tiled=True)  39.7 us
    ppermute x21, starting transfers between devices, send(): return lax.ppermute(value, 'row', pairs)  37.6 us
    pallas_call x2, Pallas kernels, product(): pl.pallas_call(functools.partial(product_kernel, tuple(marks), ready), gr...  27.9 us
    pallas_call x1, Pallas kernels, near_blocks(): pl.pallas_call(functools.partial(near_kernel, marks), out_shape=jax.Shape...  24.9 us
    all_gather x1, waiting for transfers between devices, per_device_line(): factor = lax.all_gather(factor, 'col', axis=0, tiled=False)  23.7 us
    all_to_all x1, waiting for transfers between devices, per_device_line(): lax.all_to_all(corner.reshape(n_col, -1, corner.shape[2]), 'col', 0, 0)  18.5 us
    pallas_call x1, Pallas kernels, square(): pl.pallas_call(square_kernel, out_shape=jax.ShapeDtypeStruct((rows, depth...  10.4 us
  transfers between devices with their start and end apart: 26, of which 14 were waited for; matrix products, arithmetic and copies ran while one was open for 4% of the time, Pallas kernels for 14%

profile of v12, /device:TPU:0, one launch (start us, length us, event | category | flops | bytes accessed | tf_op | source)
XLA Modules:
  0.0 417.5 jit_solution(2614530128958016183)
XLA Ops:
  6.5 3.6 slice.24
  11.5 7.1 %collective-permute-start = (bf16[896,1536]{1,0:T(8,128)(2,1)}, bf16[896,1536]{1,0:T(8,128)(2,1)}, u32[]{:S(2)}, u32[]{:S(2)}) collective-permute-start(bf16[896,1536]{1,0:T(8,128)(2,1)} %slice.24), channel_id=1, source_target_pairs={{0,8},{8,16},{16,24},{1,9},{9,17},{17,25},{2,10},{10,18},{18,26},{... | collective-permute-start | bytes 8257544 | tf_op jit(solution)/shard_map/ppermute | solution.py:379
  18.6 5.5 %fusion = bf16[1,896,896]{2,1,0:T(8,128)(2,1)} fusion(bf16[896,2304]{1,0:T(8,128)(2,1)S(1)} %copy-done), kind=kOutput, calls=%fused_computation.1 | convolution fusion | flops 3700178944 | bytes 5734400 | tf_op jit(solution)/shard_map/dot_general | solution.py:20
  24.2 2.6 slice.25
  26.8 3.5 collective-permute-start.3
  31.5 30.8 %reduce-scatter.3.cloned.1.call-done = bf16[1,112,896]{2,1,0:T(8,128)(2,1)} async-done(((bf16[1,896,896]{2,1,0:T(8,128)(2,1)}), bf16[1,112,896]{2,1,0:T(8,128)(2,1)}) %reduce-scatter.3.cloned.1.call-update) | async-done | bytes 200720 | tf_op jit(solution)/shard_map/reduce_scatter | solution.py:382
  62.4 13.4 %collective-permute-done.1.rest_0_ = bf16[896,1536]{1,0:T(8,128)(2,1)S(1)} collective-permute-done((bf16[896,1536]{1,0:T(8,128)(2,1)}, bf16[896,1536]{1,0:T(8,128)(2,1)S(1)}, u32[]{:S(2)}, u32[]{:S(2)}) %collective-permute-start.1) | collective-permute-done | bytes 2752544 | tf_op jit(solution)/shard_map/ppermute | solution.py:379
  75.8 1.6 collective-permute-done.rest_2_
  78.7 2.3 collective-permute-start.6
  81.6 24.2 %collective-permute-done.3.rest_3_ = bf16[896,768]{1,0:T(8,128)(2,1)} collective-permute-done((bf16[896,768]{1,0:T(8,128)(2,1)}, bf16[896,768]{1,0:T(8,128)(2,1)}, u32[]{:S(2)}, u32[]{:S(2)}) %collective-permute-start.3) | collective-permute-done | bytes 1376288 | tf_op jit(solution)/shard_map/ppermute | solution.py:379
  105.8 1.7 collective-permute-start.7
  107.5 1.5 collective-permute-start.5
  109.0 24.9 %shard_map.18 = bf16[4,896,896]{2,1,0:T(8,128)(2,1)} custom-call(bf16[896,2304]{1,0:T(8,128)(2,1)} %x.1, bf16[896,1536]{1,0:T(8,128)(2,1)} %copy-done.3, bf16[896,768]{1,0:T(8,128)(2,1)} %collective-permute-done.2.rest_1_, bf16[896,1536]{1,0:T(8,128)(2,1)} %collective-permute-done.rest_2_, bf16[896,768]{1,0:T(8,128)(2,1)} %collective-permute-done.3.rest_3_), custom_call_target="tpu_custom_call" | custom-call | flops 14797504512 | bytes 12386304 | tf_op jit(solution)/shard_map/pallas_call | solution.py:84
  133.9 59.2 %collective-permute-done.5.rest_5_ = bf16[896,768]{1,0:T(8,128)(2,1)} collective-permute-done((bf16[896,768]{1,0:T(8,128)(2,1)}, bf16[896,768]{1,0:T(8,128)(2,1)}, u32[]{:S(2)}, u32[]{:S(2)}) %collective-permute-start.5) | collective-permute-done | bytes 1376288 | tf_op jit(solution)/shard_map/ppermute | solution.py:379
  193.1 2.0 shard_map.17
  195.1 8.9 %reduce-scatter.5.cloned.1.call-done = bf16[4,112,896]{2,1,0:T(8,128)(2,1)} async-done(((bf16[4,896,896]{2,1,0:T(8,128)(2,1)}), bf16[4,112,896]{2,1,0:T(8,128)(2,1)}) %reduce-scatter.5.cloned.1.call-update) | async-done | bytes 802832 | tf_op jit(solution)/shard_map/reduce_scatter | solution.py:382
  204.0 3.7 all-to-all-start
  210.6 18.5 %all-to-all-done = bf16[8,112,896]{2,1,0:T(8,128)(2,1)S(1)} async-done(((bf16[8,112,896]{2,1,0:T(8,128)(2,1)}), bf16[8,112,896]{2,1,0:T(8,128)(2,1)S(1)}, u32[]{:S(2)}, u32[]{:S(2)}) %all-to-all-start) | async-done | bytes 1605664 | tf_op jit(solution)/shard_map/all_to_all | solution.py:396
  230.6 6.3 %collective-permute-done.10.end = bf16[1,112,896]{2,1,0:T(8,128)(2,1)S(1)} collective-permute-done((bf16[1,112,896]{2,1,0:T(8,128)(2,1)S(1)}, bf16[1,112,896]{2,1,0:T(8,128)(2,1)S(1)}, u32[]{:S(2)}, u32[]{:S(2)}) %collective-permute-start.10) | collective-permute-done | bytes 200736 | tf_op jit(solution)/shard_map/ppermute | solution.py:379
  239.5 4.6 %collective-permute-start.11 = (bf16[4,112,896]{2,1,0:T(8,128)(2,1)S(1)}, bf16[4,112,896]{2,1,0:T(8,128)(2,1)S(1)}, u32[]{:S(2)}, u32[]{:S(2)}) collective-permute-start(bf16[4,112,896]{2,1,0:T(8,128)(2,1)S(1)} %get-tuple-element.39.own), channel_id=1, source_target_pairs={{0,8},{8,16},{16,24},{1,9},{9,17},{17,25},{2,10},{10,18},{18,26},{... | collective-permute-start | bytes 2408456 | tf_op jit(solution)/shard_map/ppermute | solution.py:379
  244.1 11.6 %collective-permute-done.12.l1 = bf16[4,112,896]{2,1,0:T(8,128)(2,1)S(1)} collective-permute-done((bf16[4,112,896]{2,1,0:T(8,128)(2,1)S(1)}, bf16[4,112,896]{2,1,0:T(8,128)(2,1)S(1)}, u32[]{:S(2)}, u32[]{:S(2)}) %collective-permute-start.12) | collective-permute-done | bytes 802848 | tf_op jit(solution)/shard_map/ppermute | solution.py:379
  258.9 16.4 %collective-permute-done.15.l2 = bf16[4,112,896]{2,1,0:T(8,128)(2,1)S(1)} collective-permute-done((bf16[4,112,896]{2,1,0:T(8,128)(2,1)S(1)}, bf16[4,112,896]{2,1,0:T(8,128)(2,1)S(1)}, u32[]{:S(2)}, u32[]{:S(2)}) %collective-permute-start.15) | collective-permute-done | bytes 802848 | tf_op jit(solution)/shard_map/ppermute | solution.py:379
  277.4 3.3 add.18
  282.8 1.6 slice.33
  284.4 17.8 %collective-permute-done.18 = bf16[896,256]{1,0:T(8,128)(2,1)S(1)} collective-permute-done((bf16[896,256]{1,0:T(8,128)(2,1)S(1)}, bf16[896,256]{1,0:T(8,128)(2,1)S(1)}, u32[]{:S(2)}, u32[]{:S(2)}) %collective-permute-start.18) | collective-permute-done | bytes 458784 | tf_op jit(solution)/shard_map/ppermute | solution.py:379
  304.3 3.2 add.19
  307.5 5.9 %shard_map.19 = (bf16[448,3584]{1,0:T(8,128)(2,1)}, bf16[896,448]{1,0:T(8,128)(2,1)}) custom-call(s32[2]{0:T(128)} %pad_add_fusion.place, bf16[4,112,896]{2,1,0:T(8,128)(2,1)} %copy-done.2, bf16[4,112,896]{2,1,0:T(8,128)(2,1)} %copy-done.6, bf16[4,112,896]{2,1,0:T(8,128)(2,1)} %copy-done.11, bf16[4,112,896]{2,1,0:T(8,128)(2,1)} %copy-done.8, ...), custom_call_target="tpu_custom_call" | custom-call | flops 1605632 | bytes 8830976 | tf_op jit(solution)/shard_map/pallas_call | solution.py:167
  313.4 10.4 %shard_map.20 = bf16[896,448]{1,0:T(8,128)(2,1)} custom-call(s32[2]{0:T(128)} %pad_add_fusion.place, bf16[4,896,896]{2,1,0:T(8,128)(2,1)} %all-gather.4.cloned.1.call-done.panel, bf16[448,3584]{1,0:T(8,128)(2,1)} %get-tuple-element.32.right, bf16[896,448]{1,0:T(8,128)(2,1)} %get-tuple-element.33.linear), custom_call_target="tpu_custom_call" | custom-call | flops 2877292544 | bytes 8028160 | tf_op jit(solution)/shard_map/pallas_call | solution.py:215
  325.1 32.7 %collective-permute-done.19.value = bf16[896,1280]{1,0:T(8,128)(2,1)S(1)} collective-permute-done((bf16[896,1280]{1,0:T(8,128)(2,1)}, bf16[896,1280]{1,0:T(8,128)(2,1)S(1)}, u32[]{:S(2)}, u32[]{:S(2)}) %collective-permute-start.19) | collective-permute-done | bytes 2293792 | tf_op jit(solution)/shard_map/ppermute | solution.py:379
  359.3 23.7 %all-gather.6.cloned.1.call-done = bf16[7168,448]{1,0:T(8,128)(2,1)} async-done(((bf16[896,448]{1,0:T(8,128)(2,1)}), bf16[7168,448]{1,0:T(8,128)(2,1)}) %all-gather.6.cloned.1.call-update) | async-done | bytes 6422544 | tf_op jit(solution)/shard_map/all_gather | solution.py:425
  383.0 17.4 %shard_map.22 = (bf16[896,2304]{1,0:T(8,128)(2,1)}, bf16[896,3584]{1,0:T(8,128)(2,1)}) custom-call(s32[2]{0:T(128)} %pad_add_fusion.place, bf16[8,896,448]{2,1,0:T(8,128)(2,1)} %bitcast.28, bf16[8,112,2304]{2,1,0:T(8,128)(2,1)} %bitcast.25, bf16[8,112,1536]{2,1,0:T(8,128)(2,1)} %bitcast.29, bf16[8,112,1536]{2,1,0:T(8,128)(2,1)} %bitcast.11.rest_1_, ...), custom_call_target="tpu_custom_call" | custom-call | tf_op jit(solution)/shard_map/pallas_call | solution.py:340
  400.4 10.5 %shard_map.23 = bf16[896,2304]{1,0:T(8,128)(2,1)} custom-call(s32[2]{0:T(128)} %pad_add_fusion.place, bf16[896,3584]{1,0:T(8,128)(2,1)} %get-tuple-element.36.f, bf16[8,112,2304]{2,1,0:T(8,128)(2,1)} %bitcast.26, bf16[8,112,768]{2,1,0:T(8,128)(2,1)} %bitcast.15.rest_0_, bf16[8,112,768]{2,1,0:T(8,128)(2,1)} %bitcast.16.rest_1_, ...), custom_call_target="tpu_custom_call", output_to_operand_aliasing={{}: (7, {})} | custom-call | flops 4932501504 | bytes 8257536 | tf_op jit(solution)/shard_map/pallas_call | solution.py:340
  (79 shorter events, 23.6 us)
Async XLA Ops:
  6.5 55.8 %reduce-scatter.3.cloned.1.call-start = ((), (), s32[]{:S(2)}) async-start(), calls=%async_computation.3 | async-start | bytes 1806336 | tf_op jit(solution)/shard_map/reduce_scatter | solution.py:382
  10.2 65.6 %collective-permute-start.1 = (bf16[896,1536]{1,0:T(8,128)(2,1)}, bf16[896,1536]{1,0:T(8,128)(2,1)S(1)}, u32[]{:S(2)}, u32[]{:S(2)}) collective-permute-start(bf16[896,1536]{1,0:T(8,128)(2,1)} %slice.24), channel_id=1, source_target_pairs={{24,16},{16,8},{8,0},{25,17},{17,9},{9,1},{26,18},{18,10},{10,2},{... | collective-permute-start | bytes 8257544 | tf_op jit(solution)/shard_map/ppermute | solution.py:379
  11.5 65.9 %collective-permute-start = (bf16[896,1536]{1,0:T(8,128)(2,1)}, bf16[896,1536]{1,0:T(8,128)(2,1)}, u32[]{:S(2)}, u32[]{:S(2)}) collective-permute-start(bf16[896,1536]{1,0:T(8,128)(2,1)} %slice.24), channel_id=1, source_target_pairs={{0,8},{8,16},{16,24},{1,9},{9,17},{17,25},{2,10},{10,18},{18,26},{... | collective-permute-start | bytes 8257544 | tf_op jit(solution)/shard_map/ppermute | solution.py:379
  24.1 179.8 %reduce-scatter.5.cloned.1.call-start = ((), (), s32[]{:S(2)}) async-start(), calls=%async_computation.4 | async-start | bytes 7225344 | tf_op jit(solution)/shard_map/reduce_scatter | solution.py:382
  26.8 79.0 %collective-permute-start.3 = (bf16[896,768]{1,0:T(8,128)(2,1)}, bf16[896,768]{1,0:T(8,128)(2,1)}, u32[]{:S(2)}, u32[]{:S(2)}) collective-permute-start(bf16[896,768]{1,0:T(8,128)(2,1)} %slice.25), channel_id=1, source_target_pairs={{0,8},{8,16},{16,24},{1,9},{9,17},{17,25},{2,10},{10,18},{18,26},{... | collective-permute-start | bytes 4128776 | tf_op jit(solution)/shard_map/ppermute | solution.py:379
  30.3 77.2 %collective-permute-start.2 = (bf16[896,768]{1,0:T(8,128)(2,1)}, bf16[896,768]{1,0:T(8,128)(2,1)}, u32[]{:S(2)}, u32[]{:S(2)}) collective-permute-start(bf16[896,768]{1,0:T(8,128)(2,1)} %slice.25), channel_id=1, source_target_pairs={{24,16},{16,8},{8,0},{25,17},{17,9},{9,1},{26,18},{18,10},{10,2},{... | collective-permute-start | bytes 4128776 | tf_op jit(solution)/shard_map/ppermute | solution.py:379
  75.8 33.2 %copy-start.3 = (bf16[896,1536]{1,0:T(8,128)(2,1)}, bf16[896,1536]{1,0:T(8,128)(2,1)S(1)}, u32[]{:S(2)}) copy-start(bf16[896,1536]{1,0:T(8,128)(2,1)S(1)} %collective-permute-done.1.rest_0_) | copy-start | bytes 8257540
  77.4 115.6 %collective-permute-start.4 = (bf16[896,1536]{1,0:T(8,128)(2,1)S(1)}, bf16[896,1536]{1,0:T(8,128)(2,1)}, u32[]{:S(2)}, u32[]{:S(2)}) collective-permute-start(bf16[896,1536]{1,0:T(8,128)(2,1)S(1)} %collective-permute-done.1.rest_0_), channel_id=1, source_target_pairs={{16,8},{8,0},{17,9},{9,1},{18,10},{10,2},{19,11},{11,3},{20,12},{1... | collective-permute-start | bytes 8257544 | tf_op jit(solution)/shard_map/ppermute | solution.py:379
  78.7 114.4 %collective-permute-start.6 = (bf16[896,1536]{1,0:T(8,128)(2,1)}, bf16[896,1536]{1,0:T(8,128)(2,1)}, u32[]{:S(2)}, u32[]{:S(2)}) collective-permute-start(bf16[896,1536]{1,0:T(8,128)(2,1)} %collective-permute-done.rest_2_), channel_id=1, source_target_pairs={{8,16},{16,24},{9,17},{17,25},{10,18},{18,26},{11,19},{19,27},{12,... | collective-permute-start | bytes 8257544 | tf_op jit(solution)/shard_map/ppermute | solution.py:379
  105.8 28.1 %collective-permute-start.7 = (bf16[896,768]{1,0:T(8,128)(2,1)}, bf16[896,768]{1,0:T(8,128)(2,1)}, u32[]{:S(2)}, u32[]{:S(2)}) collective-permute-start(bf16[896,768]{1,0:T(8,128)(2,1)} %collective-permute-done.3.rest_3_), channel_id=1, source_target_pairs={{8,16},{16,24},{9,17},{17,25},{10,18},{18,26},{11,19},{19,27},{12,... | collective-permute-start | bytes 4128776 | tf_op jit(solution)/shard_map/ppermute | solution.py:379
  107.5 85.5 %collective-permute-start.5 = (bf16[896,768]{1,0:T(8,128)(2,1)}, bf16[896,768]{1,0:T(8,128)(2,1)}, u32[]{:S(2)}, u32[]{:S(2)}) collective-permute-start(bf16[896,768]{1,0:T(8,128)(2,1)} %collective-permute-done.2.rest_1_), channel_id=1, source_target_pairs={{16,8},{8,0},{17,9},{9,1},{18,10},{10,2},{19,11},{11,3},{20,12},{1... | collective-permute-start | bytes 4128776 | tf_op jit(solution)/shard_map/ppermute | solution.py:379
  204.0 25.0 %all-to-all-start = ((bf16[8,112,896]{2,1,0:T(8,128)(2,1)}), bf16[8,112,896]{2,1,0:T(8,128)(2,1)S(1)}, u32[]{:S(2)}, u32[]{:S(2)}) async-start(bf16[8,112,896]{2,1,0:T(8,128)(2,1)} %bitcast.31), calls=%async_computation.2 | async-start | bytes 3211264 | tf_op jit(solution)/shard_map/all_to_all | solution.py:396
  207.7 29.2 %copy-start.15 = (bf16[1,112,896]{2,1,0:T(8,128)(2,1)S(1)}, bf16[1,112,896]{2,1,0:T(8,128)(2,1)}, u32[]{:S(2)}) copy-start(bf16[1,112,896]{2,1,0:T(8,128)(2,1)} %reduce-scatter.3.cloned.1.call-done) | copy-start | bytes 602116
  207.7 105.7 %all-gather.4.cloned.1.call-start = ((), (), s32[]{:S(2)}) async-start(), calls=%async_computation.5 | async-start | bytes 7225344 | tf_op jit(solution)/shard_map/all_gather | solution.py:413
  208.6 22.0 %collective-permute-start.9 = (bf16[112,896]{1,0:T(8,128)(2,1)}, bf16[112,896]{1,0:T(8,128)(2,1)S(1)}, u32[]{:S(2)}, u32[]{:S(2)}) collective-permute-start(bf16[112,896]{1,0:T(8,128)(2,1)} %get-tuple-element.43), channel_id=1, source_target_pairs={{8,16},{16,24},{9,17},{17,25},{10,18},{18,26},{11,19},{19,27},{12,... | collective-permute-start | bytes 602120 | tf_op jit(solution)/shard_map/ppermute | solution.py:379
  209.3 21.3 %collective-permute-start.8 = (bf16[112,896]{1,0:T(8,128)(2,1)}, bf16[112,896]{1,0:T(8,128)(2,1)S(1)}, u32[]{:S(2)}, u32[]{:S(2)}) collective-permute-start(bf16[112,896]{1,0:T(8,128)(2,1)} %get-tuple-element.44), channel_id=1, source_target_pairs={{16,8},{8,0},{17,9},{9,1},{18,10},{10,2},{19,11},{11,3},{20,12},{1... | collective-permute-start | bytes 602120 | tf_op jit(solution)/shard_map/ppermute | solution.py:379
  229.3 52.9 %copy-start.13 = (bf16[112,896]{1,0:T(8,128)(2,1)}, bf16[112,896]{1,0:T(8,128)(2,1)S(1)}, u32[]{:S(2)}) copy-start(bf16[112,896]{1,0:T(8,128)(2,1)S(1)} %reduce_sum.12) | copy-start | bytes 602116
  229.3 7.6 %collective-permute-start.10 = (bf16[1,112,896]{2,1,0:T(8,128)(2,1)S(1)}, bf16[1,112,896]{2,1,0:T(8,128)(2,1)S(1)}, u32[]{:S(2)}, u32[]{:S(2)}) collective-permute-start(bf16[1,112,896]{2,1,0:T(8,128)(2,1)S(1)} %bitcast.32), channel_id=1, source_target_pairs={{8,0},{16,24},{9,1},{17,25},{10,2},{18,26},{11,3},{19,27},{12,4},{... | collective-permute-start | bytes 602120 | tf_op jit(solution)/shard_map/ppermute | solution.py:379
  236.9 43.8 %copy-start.12 = (bf16[1,112,896]{2,1,0:T(8,128)(2,1)}, bf16[1,112,896]{2,1,0:T(8,128)(2,1)S(1)}, u32[]{:S(2)}) copy-start(bf16[1,112,896]{2,1,0:T(8,128)(2,1)S(1)} %collective-permute-done.10.end) | copy-start | bytes 602116
  238.1 42.6 %copy-start.2 = (bf16[4,112,896]{2,1,0:T(8,128)(2,1)}, bf16[4,112,896]{2,1,0:T(8,128)(2,1)S(1)}, u32[]{:S(2)}) copy-start(bf16[4,112,896]{2,1,0:T(8,128)(2,1)S(1)} %get-tuple-element.39.own) | copy-start | bytes 2408452
  238.2 144.8 %all-gather.6.cloned.1.call-start = ((), (), s32[]{:S(2)}) async-start(), calls=%async_computation.6 | async-start | bytes 8257536 | tf_op jit(solution)/shard_map/all_gather | solution.py:425
  238.2 17.5 %collective-permute-start.12 = (bf16[4,112,896]{2,1,0:T(8,128)(2,1)S(1)}, bf16[4,112,896]{2,1,0:T(8,128)(2,1)S(1)}, u32[]{:S(2)}, u32[]{:S(2)}) collective-permute-start(bf16[4,112,896]{2,1,0:T(8,128)(2,1)S(1)} %get-tuple-element.39.own), channel_id=1, source_target_pairs={{24,16},{16,8},{8,0},{25,17},{17,9},{9,1},{26,18},{18,10},{10,2},{... | collective-permute-start | bytes 2408456 | tf_op jit(solution)/shard_map/ppermute | solution.py:379
  239.5 17.4 %collective-permute-start.11 = (bf16[4,112,896]{2,1,0:T(8,128)(2,1)S(1)}, bf16[4,112,896]{2,1,0:T(8,128)(2,1)S(1)}, u32[]{:S(2)}, u32[]{:S(2)}) collective-permute-start(bf16[4,112,896]{2,1,0:T(8,128)(2,1)S(1)} %get-tuple-element.39.own), channel_id=1, source_target_pairs={{0,8},{8,16},{16,24},{1,9},{9,17},{17,25},{2,10},{10,18},{18,26},{... | collective-permute-start | bytes 2408456 | tf_op jit(solution)/shard_map/ppermute | solution.py:379
  255.7 25.0 %copy-start.6 = (bf16[4,112,896]{2,1,0:T(8,128)(2,1)}, bf16[4,112,896]{2,1,0:T(8,128)(2,1)S(1)}, u32[]{:S(2)}) copy-start(bf16[4,112,896]{2,1,0:T(8,128)(2,1)S(1)} %collective-permute-done.12.l1) | copy-start | bytes 2408452
  256.9 18.4 %collective-permute-start.15 = (bf16[4,112,896]{2,1,0:T(8,128)(2,1)S(1)}, bf16[4,112,896]{2,1,0:T(8,128)(2,1)S(1)}, u32[]{:S(2)}, u32[]{:S(2)}) collective-permute-start(bf16[4,112,896]{2,1,0:T(8,128)(2,1)S(1)} %collective-permute-done.12.l1), channel_id=1, source_target_pairs={{16,8},{8,0},{17,9},{9,1},{18,10},{10,2},{19,11},{11,3},{20,12},{1... | collective-permute-start | bytes 2408456 | tf_op jit(solution)/shard_map/ppermute | solution.py:379
  258.2 18.4 %collective-permute-start.13 = (bf16[4,112,896]{2,1,0:T(8,128)(2,1)S(1)}, bf16[4,112,896]{2,1,0:T(8,128)(2,1)S(1)}, u32[]{:S(2)}, u32[]{:S(2)}) collective-permute-start(bf16[4,112,896]{2,1,0:T(8,128)(2,1)S(1)} %collective-permute-done.11.r1), channel_id=1, source_target_pairs={{8,16},{16,24},{9,17},{17,25},{10,18},{18,26},{11,19},{19,27},{12,... | collective-permute-start | bytes 2408456 | tf_op jit(solution)/shard_map/ppermute | solution.py:379
  275.3 26.9 %collective-permute-start.16 = (bf16[4,112,896]{2,1,0:T(8,128)(2,1)S(1)}, bf16[4,112,896]{2,1,0:T(8,128)(2,1)S(1)}, u32[]{:S(2)}, u32[]{:S(2)}) collective-permute-start(bf16[4,112,896]{2,1,0:T(8,128)(2,1)S(1)} %collective-permute-done.15.l2), channel_id=1, source_target_pairs={{8,0},{9,1},{10,2},{11,3},{12,4},{13,5},{14,6},{15,7}} | collective-permute-start | bytes 2408456 | tf_op jit(solution)/shard_map/ppermute | solution.py:379
  276.6 26.4 %collective-permute-start.14 = (bf16[4,112,896]{2,1,0:T(8,128)(2,1)S(1)}, bf16[4,112,896]{2,1,0:T(8,128)(2,1)S(1)}, u32[]{:S(2)}, u32[]{:S(2)}) collective-permute-start(bf16[4,112,896]{2,1,0:T(8,128)(2,1)S(1)} %collective-permute-done.13.r2), channel_id=1, source_target_pairs={{16,24},{17,25},{18,26},{19,27},{20,28},{21,29},{22,30},{23,31}} | collective-permute-start | bytes 2408456 | tf_op jit(solution)/shard_map/ppermute | solution.py:379
  280.8 21.4 %collective-permute-start.18 = (bf16[896,256]{1,0:T(8,128)(2,1)S(1)}, bf16[896,256]{1,0:T(8,128)(2,1)S(1)}, u32[]{:S(2)}, u32[]{:S(2)}) collective-permute-start(bf16[896,256]{1,0:T(8,128)(2,1)S(1)} %slice.32), channel_id=1, source_target_pairs={{8,0},{16,24},{9,1},{17,25},{10,2},{18,26},{11,3},{19,27},{12,4},{... | collective-permute-start | bytes 1376264 | tf_op jit(solution)/shard_map/ppermute | solution.py:379
  282.1 2.3 collective-permute-start.17
  303.0 54.9 %collective-permute-start.19 = (bf16[896,1280]{1,0:T(8,128)(2,1)}, bf16[896,1280]{1,0:T(8,128)(2,1)S(1)}, u32[]{:S(2)}, u32[]{:S(2)}) collective-permute-start(bf16[896,1280]{1,0:T(8,128)(2,1)} %slice.33), channel_id=1, source_target_pairs={{8,0},{16,24},{9,1},{17,25},{10,2},{18,26},{11,3},{19,27},{12,4},{... | collective-permute-start | bytes 6881288 | tf_op jit(solution)/shard_map/ppermute | solution.py:379
  323.8 76.5 %collective-permute-start.20 = (bf16[896,768]{1,0:T(8,128)(2,1)}, bf16[896,768]{1,0:T(8,128)(2,1)}, u32[]{:S(2)}, u32[]{:S(2)}) collective-permute-start(bf16[896,768]{1,0:T(8,128)(2,1)} %add.19), channel_id=1, source_target_pairs={{8,0},{16,24},{9,1},{17,25},{10,2},{18,26},{11,3},{19,27},{12,4},{... | collective-permute-start | bytes 4128776 | tf_op jit(solution)/shard_map/ppermute | solution.py:379
  (11 other events, 85.5 us)
Sparse Core Ops, SparseCore 0:
  24.3 38.0 reduce-scatter.2
  134.0 69.9 reduce-scatter.4
  238.3 46.3 all-gather.3
  324.0 58.9 all-gather.5

commit v13 on v11

--- a/solution.py
+++ b/solution.py
@@ -165,7 +165,7 @@
         out_shape=jax.ShapeDtypeStruct((4 * part, 4 * rows), jnp.bfloat16),
         in_specs=[scalars()] + [whole()] * len(others),
         out_specs=whole(),
-        compiler_params=pltpu.CompilerParams(vmem_limit_bytes=24 * 2**20),
+        compiler_params=pltpu.CompilerParams(vmem_limit_bytes=56 * 2**20),
         cost_estimate=pl.CostEstimate(
             flops=16 * part * rows, bytes_accessed=2 * 44 * part * rows, transcendentals=0
         ),
@@ -380,36 +380,40 @@
     r2 = [send(piece, right[1:]) for piece in r1]
     l2 = [send(piece, left[1:]) for piece in l1]
 
+    across = [l2[0] + r2[0]]
+    far_marks = [0, 512, *marks[1:]]
+    head = across[0][:, :512]
+    head, across[0], l2[1], r2[1] = lax.optimization_barrier((head, across[0], l2[1], r2[1]))
+    across.append(l2[1] + r2[1])
+
     first = scatter(near_blocks(x, l1, r1, marks))
     corner = corner_block(place, l1, r1, l2, r2, marks)
     corner, first = lax.optimization_barrier((corner, first))
-    corner = scatter(corner)
-
+    shares = lax.all_to_all(corner.reshape(n_col, -1, corner.shape[2]), "col", 0, 0)
+    corner = shares.astype(jnp.float32).sum(0, keepdims=True).astype(jnp.bfloat16)
+
+    def send_on(value, *after):
+        return send(lax.optimization_barrier((value, *after))[0], [(1, 0), (2, 3)])
+
+    far = [send_on(head)]
     second = send(first[2], left[1:]) + send(first[3], right[1:])
+    second, far[0] = lax.optimization_barrier((second, far[0]))
     tile = jnp.stack([own[0], first[0], second, first[1]])
     tr1, tl1 = send(tile, right), send(tile, left)
 
-    across = [a + b for a, b in zip(l2, r2)]
-    far_marks = [0, 256, *marks[1:]]
-
-    def send_on(value, *after):
-        return send(lax.optimization_barrier((value, *after))[0], [(1, 0), (2, 3)])
-
-    far = [send_on(across[0][:, :256], tile)]
-    corner, tr1, tl1, far[0] = lax.optimization_barrier((corner, tr1, tl1, far[0]))
     end = send(corner, [(1, 0), (2, 3)])
     pair = send(corner, [(1, 2), (2, 1)])
+    end, tr1, tl1 = lax.optimization_barrier((end, tr1, tl1))
     zero = jnp.zeros_like(end)
     added = [zero, jnp.where(z == 3, end, zero), zero, jnp.where(z == 0, end, zero)]
     panel = lax.all_gather(tile + jnp.concatenate(added), "col", axis=1, tiled=True)
 
-    end, tr1, tl1 = lax.optimization_barrier((end, tr1, tl1))
     tr2, tl2 = send(tr1, right[1:]), send(tl1, left[1:])
     tr3, tl3 = send(tr2, right[2:]), send(tl2, left[2:])
-    far.append(arrived(send_on(across[0][:, 256:], tr3, tl3, pair)))
-
-    rights = strips(place, tile, tl1, tr3, tl2, tr2, tr1, tl3, corner, pair, end)
-    factor = square(place, panel, rights)
+    far.append(arrived(send_on(across[0][:, 512:], tr3, tl3, pair)))
+
+    strip = strips(place, tile, tl1, tr3, tl2, tr2, tr1, tl3, corner, pair, end)
+    factor = square(place, panel, strip)
     far.append(send_on(across[1], factor))
     factor = lax.all_gather(factor, "col", axis=0, tiled=False)
     near = [l1, r1, across]

time: 402 us -> 403 us (level)
  waiting for transfers between devices: 255 us -> 244 us
  starting transfers between devices: 37.9 us -> 43.2 us
  other arithmetic: 9.44 us -> 14.1 us
    ppermute x21, waiting for transfers between devices: 200 us -> 180 us  [send(): return lax.ppermute(value, 'row', pairs)]
    all_gather x1, waiting for transfers between devices: 14.1 us -> 25.1 us  [per_device_line(): factor = lax.all_gather(factor, 'col', axis=0, tiled=False)]
    all_to_all x0 -> x1, starting transfers between devices: none -> 4.43 us  [per_device_line(): lax.all_to_all(corner.reshape(n_col, -1, corner.shape[2]), 'col', 0, 0)]
    reduce_scatter x3 -> x2, waiting for transfers between devices: 39.9 us -> 38.6 us  [scatter(): return lax.psum_scatter(blocks, 'col', scatter_dimension=1, tiled=True)]
  transfers between devices with their start and end apart: 26 -> 26, of which waited for: 14 -> 14; matrix products, arithmetic and copies ran while one was open for 5% -> 5% of each run, Pallas kernels for 14% -> 15%
where the time goes in v13:
time: 403 us; the launch traced here: 402 us
  waiting for transfers between devices  244 us (61%)
  Pallas kernels  70.4 us (17%)
  starting transfers between devices  43.2 us (11%)
  other arithmetic  14.1 us (3%)
  between operations  13.5 us (3%)
  local copies, waits for them, and re-layouts  11.7 us (3%)
  matrix products  5.53 us (1%)
    ppermute x21, waiting for transfers between devices, send(): return lax.ppermute(value, 'row', pairs)  180 us
    ppermute x21, starting transfers between devices, send(): return lax.ppermute(value, 'row', pairs)  38.7 us
    reduce_scatter x2, waiting for transfers between devices, scatter(): return lax.psum_scatter(blocks, 'col', scatter_dimension=1, tiled=True)  38.6 us
    pallas_call x2, Pallas kernels, product(): pl.pallas_call(functools.partial(product_kernel, tuple(marks), ready), gr...  27.9 us
    all_gather x1, waiting for transfers between devices, per_device_line(): factor = lax.all_gather(factor, 'col', axis=0, tiled=False)  25.1 us
    pallas_call x1, Pallas kernels, near_blocks(): pl.pallas_call(functools.partial(near_kernel, marks), out_shape=jax.Shape...  24.9 us
    pallas_call x1, Pallas kernels, square(): pl.pallas_call(square_kernel, out_shape=jax.ShapeDtypeStruct((rows, depth...  10.8 us
  transfers between devices with their start and end apart: 26, of which 14 were waited for; matrix products, arithmetic and copies ran while one was open for 5% of the time, Pallas kernels for 15%

profile of v13, /device:TPU:0, one launch (start us, length us, event | category | flops | bytes accessed | tf_op | source)
XLA Modules:
  0.0 402.3 jit_solution(17425679026457579312)
XLA Ops:
  6.5 3.6 slice.24
  11.5 7.1 %collective-permute-start = (bf16[896,1536]{1,0:T(8,128)(2,1)}, bf16[896,1536]{1,0:T(8,128)(2,1)}, u32[]{:S(2)}, u32[]{:S(2)}) collective-permute-start(bf16[896,1536]{1,0:T(8,128)(2,1)} %slice.24), channel_id=1, source_target_pairs={{0,8},{8,16},{16,24},{1,9},{9,17},{17,25},{2,10},{10,18},{18,26},{... | collective-permute-start | bytes 8257544 | tf_op jit(solution)/shard_map/ppermute | solution.py:369
  18.6 5.5 %fusion = bf16[1,896,896]{2,1,0:T(8,128)(2,1)} fusion(bf16[896,2304]{1,0:T(8,128)(2,1)S(1)} %copy-done), kind=kOutput, calls=%fused_computation.1 | convolution fusion | flops 3700178944 | bytes 5734400 | tf_op jit(solution)/shard_map/dot_general | solution.py:20
  24.2 2.5 slice.25
  26.7 3.5 collective-permute-start.3
  31.4 30.9 %reduce-scatter.3.cloned.1.call-done = bf16[1,112,896]{2,1,0:T(8,128)(2,1)} async-done(((bf16[1,896,896]{2,1,0:T(8,128)(2,1)}), bf16[1,112,896]{2,1,0:T(8,128)(2,1)}) %reduce-scatter.3.cloned.1.call-update) | async-done | bytes 200720 | tf_op jit(solution)/shard_map/reduce_scatter | solution.py:372
  62.4 13.4 %collective-permute-done.1.rest_0_ = bf16[896,1536]{1,0:T(8,128)(2,1)S(1)} collective-permute-done((bf16[896,1536]{1,0:T(8,128)(2,1)}, bf16[896,1536]{1,0:T(8,128)(2,1)S(1)}, u32[]{:S(2)}, u32[]{:S(2)}) %collective-permute-start.1) | collective-permute-done | bytes 2752544 | tf_op jit(solution)/shard_map/ppermute | solution.py:369
  78.7 2.2 collective-permute-start.5
  81.5 24.3 %collective-permute-done.3.rest_3_ = bf16[896,768]{1,0:T(8,128)(2,1)} collective-permute-done((bf16[896,768]{1,0:T(8,128)(2,1)}, bf16[896,768]{1,0:T(8,128)(2,1)}, u32[]{:S(2)}, u32[]{:S(2)}) %collective-permute-start.3) | collective-permute-done | bytes 1376288 | tf_op jit(solution)/shard_map/ppermute | solution.py:369
  105.8 1.8 collective-permute-start.7
  109.0 24.9 %shard_map.18 = bf16[4,896,896]{2,1,0:T(8,128)(2,1)} custom-call(bf16[896,2304]{1,0:T(8,128)(2,1)} %x.1, bf16[896,1536]{1,0:T(8,128)(2,1)} %copy-done.4, bf16[896,768]{1,0:T(8,128)(2,1)} %collective-permute-done.2.rest_1_, bf16[896,1536]{1,0:T(8,128)(2,1)} %collective-permute-done.rest_2_, bf16[896,768]{1,0:T(8,128)(2,1)} %collective-permute-done.3.rest_3_), custom_call_target="tpu_custom_call" | custom-call | flops 14797504512 | bytes 12386304 | tf_op jit(solution)/shard_map/pallas_call | solution.py:84
  133.9 30.5 %collective-permute-done.4.rest_4_ = bf16[896,1536]{1,0:T(8,128)(2,1)} collective-permute-done((bf16[896,1536]{1,0:T(8,128)(2,1)S(1)}, bf16[896,1536]{1,0:T(8,128)(2,1)}, u32[]{:S(2)}, u32[]{:S(2)}) %collective-permute-start.4) | collective-permute-done | bytes 2752544 | tf_op jit(solution)/shard_map/ppermute | solution.py:369
  164.4 4.4 %add.16 = bf16[896,1536]{1,0:T(8,128)(2,1)S(1)} add(bf16[896,1536]{1,0:T(8,128)(2,1)} %collective-permute-done.4.rest_4_, bf16[896,1536]{1,0:T(8,128)(2,1)} %collective-permute-done.5.rest_6_) | non-fusion elementwise | flops 1376256 | bytes 8257536 | tf_op jit(solution)/shard_map/add | solution.py:383
  171.4 21.7 %collective-permute-done.6.rest_5_ = bf16[896,768]{1,0:T(8,128)(2,1)} collective-permute-done((bf16[896,768]{1,0:T(8,128)(2,1)}, bf16[896,768]{1,0:T(8,128)(2,1)}, u32[]{:S(2)}, u32[]{:S(2)}) %collective-permute-start.6) | collective-permute-done | bytes 1376288 | tf_op jit(solution)/shard_map/ppermute | solution.py:369
  194.3 2.0 shard_map.17
  196.4 7.7 %reduce-scatter.5.cloned.1.call-done = bf16[4,112,896]{2,1,0:T(8,128)(2,1)} async-done(((bf16[4,896,896]{2,1,0:T(8,128)(2,1)}), bf16[4,112,896]{2,1,0:T(8,128)(2,1)}) %reduce-scatter.5.cloned.1.call-update) | async-done | bytes 802832 | tf_op jit(solution)/shard_map/reduce_scatter | solution.py:372
  204.0 4.4 %all-to-all-start = ((bf16[8,112,896]{2,1,0:T(8,128)(2,1)}), bf16[8,112,896]{2,1,0:T(8,128)(2,1)}, u32[]{:S(2)}, u32[]{:S(2)}) async-start(bf16[8,112,896]{2,1,0:T(8,128)(2,1)} %bitcast.32), calls=%async_computation.2 | async-start | bytes 3211264 | tf_op jit(solution)/shard_map/all_to_all | solution.py:392
  210.6 15.9 %collective-permute-done.8 = bf16[112,896]{1,0:T(8,128)(2,1)S(1)} collective-permute-done((bf16[112,896]{1,0:T(8,128)(2,1)S(1)}, bf16[112,896]{1,0:T(8,128)(2,1)S(1)}, u32[]{:S(2)}, u32[]{:S(2)}) %collective-permute-start.8) | collective-permute-done | bytes 200736 | tf_op jit(solution)/shard_map/ppermute | solution.py:369
  228.3 5.5 %collective-permute-start.12 = (bf16[4,112,896]{2,1,0:T(8,128)(2,1)S(1)}, bf16[4,112,896]{2,1,0:T(8,128)(2,1)}, u32[]{:S(2)}, u32[]{:S(2)}) collective-permute-start(bf16[4,112,896]{2,1,0:T(8,128)(2,1)S(1)} %pad_maximum_fusion.own), channel_id=1, source_target_pairs={{0,8},{8,16},{16,24},{1,9},{9,17},{17,25},{2,10},{10,18},{18,26},{... | collective-permute-start | bytes 2408456 | tf_op jit(solution)/shard_map/ppermute | solution.py:369
  233.8 2.4 reduce_sum.12
  237.5 12.4 %collective-permute-done.13.l1 = bf16[4,112,896]{2,1,0:T(8,128)(2,1)} collective-permute-done((bf16[4,112,896]{2,1,0:T(8,128)(2,1)S(1)}, bf16[4,112,896]{2,1,0:T(8,128)(2,1)}, u32[]{:S(2)}, u32[]{:S(2)}) %collective-permute-start.13) | collective-permute-done | bytes 802848 | tf_op jit(solution)/shard_map/ppermute | solution.py:369
  249.8 2.9 collective-permute-done.11.end
  253.7 2.4 maximum_add_fusion
  258.2 18.6 %collective-permute-done.16.l2 = bf16[4,112,896]{2,1,0:T(8,128)(2,1)S(1)} collective-permute-done((bf16[4,112,896]{2,1,0:T(8,128)(2,1)}, bf16[4,112,896]{2,1,0:T(8,128)(2,1)S(1)}, u32[]{:S(2)}, u32[]{:S(2)}) %collective-permute-start.16) | collective-permute-done | bytes 802848 | tf_op jit(solution)/shard_map/ppermute | solution.py:369
  281.2 15.3 %collective-permute-done.17.l3 = bf16[4,112,896]{2,1,0:T(8,128)(2,1)S(1)} collective-permute-done((bf16[4,112,896]{2,1,0:T(8,128)(2,1)S(1)}, bf16[4,112,896]{2,1,0:T(8,128)(2,1)S(1)}, u32[]{:S(2)}, u32[]{:S(2)}) %collective-permute-start.17) | collective-permute-done | bytes 802848 | tf_op jit(solution)/shard_map/ppermute | solution.py:369
  297.7 3.2 add.19
  300.9 4.9 %shard_map.19.right = bf16[448,3584]{1,0:T(8,128)(2,1)} custom-call(s32[2]{0:T(128)} %pad_add_fusion.place, bf16[4,112,896]{2,1,0:T(8,128)(2,1)} %copy-done.3, bf16[4,112,896]{2,1,0:T(8,128)(2,1)} %collective-permute-done.13.l1, bf16[4,112,896]{2,1,0:T(8,128)(2,1)} %copy-done.12, bf16[4,112,896]{2,1,0:T(8,128)(2,1)} %copy-done.9, ...), custom_call_target="tpu_custom_call" | custom-call | flops 1605632 | bytes 8830976 | tf_op jit(solution)/shard_map/pallas_call | solution.py:163
  305.9 10.8 %shard_map.20 = bf16[896,448]{1,0:T(8,128)(2,1)} custom-call(s32[2]{0:T(128)} %pad_add_fusion.place, bf16[4,896,896]{2,1,0:T(8,128)(2,1)} %all-gather.4.cloned.1.call-done.panel, bf16[448,3584]{1,0:T(8,128)(2,1)} %shard_map.19.right), custom_call_target="tpu_custom_call" | custom-call | flops 2877292544 | bytes 8028160 | tf_op jit(solution)/shard_map/pallas_call | solution.py:206
  317.9 23.5 %collective-permute-done.19.value = bf16[896,1024]{1,0:T(8,128)(2,1)S(1)} collective-permute-done((bf16[896,1024]{1,0:T(8,128)(2,1)}, bf16[896,1024]{1,0:T(8,128)(2,1)S(1)}, u32[]{:S(2)}, u32[]{:S(2)}) %collective-permute-start.19) | collective-permute-done | bytes 1835040 | tf_op jit(solution)/shard_map/ppermute | solution.py:369
  342.7 25.1 %all-gather.6.cloned.1.call-done = bf16[7168,448]{1,0:T(8,128)(2,1)} async-done(((bf16[896,448]{1,0:T(8,128)(2,1)}), bf16[7168,448]{1,0:T(8,128)(2,1)}) %all-gather.6.cloned.1.call-update) | async-done | bytes 6422544 | tf_op jit(solution)/shard_map/all_gather | solution.py:418
  367.9 17.4 %shard_map.22 = (bf16[896,2304]{1,0:T(8,128)(2,1)}, bf16[896,3584]{1,0:T(8,128)(2,1)}) custom-call(s32[2]{0:T(128)} %pad_add_fusion.place, bf16[8,896,448]{2,1,0:T(8,128)(2,1)} %bitcast.27, bf16[8,112,2304]{2,1,0:T(8,128)(2,1)} %bitcast.24, bf16[8,112,1536]{2,1,0:T(8,128)(2,1)} %bitcast.28, bf16[8,112,1536]{2,1,0:T(8,128)(2,1)} %bitcast.11.rest_1_, ...), custom_call_target="tpu_custom_call" | custom-call | tf_op jit(solution)/shard_map/pallas_call | solution.py:330
  385.3 10.5 %shard_map.23 = bf16[896,2304]{1,0:T(8,128)(2,1)} custom-call(s32[2]{0:T(128)} %pad_add_fusion.place, bf16[896,3584]{1,0:T(8,128)(2,1)} %get-tuple-element.38.f, bf16[8,112,2304]{2,1,0:T(8,128)(2,1)} %bitcast.25, bf16[8,112,768]{2,1,0:T(8,128)(2,1)} %bitcast.15.rest_0_, bf16[8,112,768]{2,1,0:T(8,128)(2,1)} %bitcast.16.rest_1_, ...), custom_call_target="tpu_custom_call", output_to_operand_aliasing={{}: (7, {})} | custom-call | flops 4932501504 | bytes 8257536 | tf_op jit(solution)/shard_map/pallas_call | solution.py:330
  (78 shorter events, 27.8 us)
Async XLA Ops:
  6.5 55.8 %reduce-scatter.3.cloned.1.call-start = ((), (), s32[]{:S(2)}) async-start(), calls=%async_computation.3 | async-start | bytes 1806336 | tf_op jit(solution)/shard_map/reduce_scatter | solution.py:372
  10.2 65.6 %collective-permute-start.1 = (bf16[896,1536]{1,0:T(8,128)(2,1)}, bf16[896,1536]{1,0:T(8,128)(2,1)S(1)}, u32[]{:S(2)}, u32[]{:S(2)}) collective-permute-start(bf16[896,1536]{1,0:T(8,128)(2,1)} %slice.24), channel_id=1, source_target_pairs={{24,16},{16,8},{8,0},{25,17},{17,9},{9,1},{26,18},{18,10},{10,2},{... | collective-permute-start | bytes 8257544 | tf_op jit(solution)/shard_map/ppermute | solution.py:369
  11.5 65.9 %collective-permute-start = (bf16[896,1536]{1,0:T(8,128)(2,1)}, bf16[896,1536]{1,0:T(8,128)(2,1)}, u32[]{:S(2)}, u32[]{:S(2)}) collective-permute-start(bf16[896,1536]{1,0:T(8,128)(2,1)} %slice.24), channel_id=1, source_target_pairs={{0,8},{8,16},{16,24},{1,9},{9,17},{17,25},{2,10},{10,18},{18,26},{... | collective-permute-start | bytes 8257544 | tf_op jit(solution)/shard_map/ppermute | solution.py:369
  24.1 179.9 %reduce-scatter.5.cloned.1.call-start = ((), (), s32[]{:S(2)}) async-start(), calls=%async_computation.4 | async-start | bytes 7225344 | tf_op jit(solution)/shard_map/reduce_scatter | solution.py:372
  26.7 79.1 %collective-permute-start.3 = (bf16[896,768]{1,0:T(8,128)(2,1)}, bf16[896,768]{1,0:T(8,128)(2,1)}, u32[]{:S(2)}, u32[]{:S(2)}) collective-permute-start(bf16[896,768]{1,0:T(8,128)(2,1)} %slice.25), channel_id=1, source_target_pairs={{0,8},{8,16},{16,24},{1,9},{9,17},{17,25},{2,10},{10,18},{18,26},{... | collective-permute-start | bytes 4128776 | tf_op jit(solution)/shard_map/ppermute | solution.py:369
  30.2 77.4 %collective-permute-start.2 = (bf16[896,768]{1,0:T(8,128)(2,1)}, bf16[896,768]{1,0:T(8,128)(2,1)}, u32[]{:S(2)}, u32[]{:S(2)}) collective-permute-start(bf16[896,768]{1,0:T(8,128)(2,1)} %slice.25), channel_id=1, source_target_pairs={{24,16},{16,8},{8,0},{25,17},{17,9},{9,1},{26,18},{18,10},{10,2},{... | collective-permute-start | bytes 4128776 | tf_op jit(solution)/shard_map/ppermute | solution.py:369
  75.8 33.2 %copy-start.4 = (bf16[896,1536]{1,0:T(8,128)(2,1)}, bf16[896,1536]{1,0:T(8,128)(2,1)S(1)}, u32[]{:S(2)}) copy-start(bf16[896,1536]{1,0:T(8,128)(2,1)S(1)} %collective-permute-done.1.rest_0_) | copy-start | bytes 8257540
  77.4 87.0 %collective-permute-start.4 = (bf16[896,1536]{1,0:T(8,128)(2,1)S(1)}, bf16[896,1536]{1,0:T(8,128)(2,1)}, u32[]{:S(2)}, u32[]{:S(2)}) collective-permute-start(bf16[896,1536]{1,0:T(8,128)(2,1)S(1)} %collective-permute-done.1.rest_0_), channel_id=1, source_target_pairs={{16,8},{8,0},{17,9},{9,1},{18,10},{10,2},{19,11},{11,3},{20,12},{1... | collective-permute-start | bytes 8257544 | tf_op jit(solution)/shard_map/ppermute | solution.py:369
  78.7 85.7 %collective-permute-start.5 = (bf16[896,1536]{1,0:T(8,128)(2,1)}, bf16[896,1536]{1,0:T(8,128)(2,1)}, u32[]{:S(2)}, u32[]{:S(2)}) collective-permute-start(bf16[896,1536]{1,0:T(8,128)(2,1)} %collective-permute-done.rest_2_), channel_id=1, source_target_pairs={{8,16},{16,24},{9,17},{17,25},{10,18},{18,26},{11,19},{19,27},{12,... | collective-permute-start | bytes 8257544 | tf_op jit(solution)/shard_map/ppermute | solution.py:369
  105.8 65.6 %collective-permute-start.7 = (bf16[896,768]{1,0:T(8,128)(2,1)}, bf16[896,768]{1,0:T(8,128)(2,1)}, u32[]{:S(2)}, u32[]{:S(2)}) collective-permute-start(bf16[896,768]{1,0:T(8,128)(2,1)} %collective-permute-done.3.rest_3_), channel_id=1, source_target_pairs={{8,16},{16,24},{9,17},{17,25},{10,18},{18,26},{11,19},{19,27},{12,... | collective-permute-start | bytes 4128776 | tf_op jit(solution)/shard_map/ppermute | solution.py:369
  107.6 85.5 %collective-permute-start.6 = (bf16[896,768]{1,0:T(8,128)(2,1)}, bf16[896,768]{1,0:T(8,128)(2,1)}, u32[]{:S(2)}, u32[]{:S(2)}) collective-permute-start(bf16[896,768]{1,0:T(8,128)(2,1)} %collective-permute-done.2.rest_1_), channel_id=1, source_target_pairs={{16,8},{8,0},{17,9},{9,1},{18,10},{10,2},{19,11},{11,3},{20,12},{1... | collective-permute-start | bytes 4128776 | tf_op jit(solution)/shard_map/ppermute | solution.py:369
  193.1 33.5 %collective-permute-start.10 = (bf16[896,512]{1,0:T(8,128)(2,1)}, bf16[896,512]{1,0:T(8,128)(2,1)}, u32[]{:S(2)}, u32[]{:S(2)}) collective-permute-start(bf16[896,512]{1,0:T(8,128)(2,1)} %slice.32), channel_id=1, source_target_pairs={{8,0},{16,24},{9,1},{17,25},{10,2},{18,26},{11,3},{19,27},{12,4},{... | collective-permute-start | bytes 2752520 | tf_op jit(solution)/shard_map/ppermute | solution.py:369
  196.3 30.3 %copy-start.13 = (bf16[1,112,896]{2,1,0:T(8,128)(2,1)S(1)}, bf16[1,112,896]{2,1,0:T(8,128)(2,1)}, u32[]{:S(2)}) copy-start(bf16[1,112,896]{2,1,0:T(8,128)(2,1)} %reduce-scatter.3.cloned.1.call-done) | copy-start | bytes 602116
  204.0 29.8 %all-to-all-start = ((bf16[8,112,896]{2,1,0:T(8,128)(2,1)}), bf16[8,112,896]{2,1,0:T(8,128)(2,1)}, u32[]{:S(2)}, u32[]{:S(2)}) async-start(bf16[8,112,896]{2,1,0:T(8,128)(2,1)} %bitcast.32), calls=%async_computation.2 | async-start | bytes 3211264 | tf_op jit(solution)/shard_map/all_to_all | solution.py:392
  208.4 97.4 %all-gather.4.cloned.1.call-start = ((), (), s32[]{:S(2)}) async-start(), calls=%async_computation.5 | async-start | bytes 7225344 | tf_op jit(solution)/shard_map/all_gather | solution.py:409
  208.6 2.0 collective-permute-start.9
  209.3 17.2 %collective-permute-start.8 = (bf16[112,896]{1,0:T(8,128)(2,1)S(1)}, bf16[112,896]{1,0:T(8,128)(2,1)S(1)}, u32[]{:S(2)}, u32[]{:S(2)}) collective-permute-start(bf16[112,896]{1,0:T(8,128)(2,1)S(1)} %get-tuple-element.44), channel_id=1, source_target_pairs={{16,8},{8,0},{17,9},{9,1},{18,10},{10,2},{19,11},{11,3},{20,12},{1... | collective-permute-start | bytes 602120 | tf_op jit(solution)/shard_map/ppermute | solution.py:369
  226.7 29.4 %copy-start.3 = (bf16[4,112,896]{2,1,0:T(8,128)(2,1)}, bf16[4,112,896]{2,1,0:T(8,128)(2,1)S(1)}, u32[]{:S(2)}) copy-start(bf16[4,112,896]{2,1,0:T(8,128)(2,1)S(1)} %pad_maximum_fusion.own) | copy-start | bytes 2408452
  226.8 52.8 %copy-start.2 = (bf16[896,1536]{1,0:T(8,128)(2,1)S(1)}, bf16[896,1536]{1,0:T(8,128)(2,1)}, u32[]{:S(2)}) copy-start(bf16[896,1536]{1,0:T(8,128)(2,1)} %copy-done.1) | copy-start | bytes 8257540
  226.8 23.1 %collective-permute-start.13 = (bf16[4,112,896]{2,1,0:T(8,128)(2,1)S(1)}, bf16[4,112,896]{2,1,0:T(8,128)(2,1)}, u32[]{:S(2)}, u32[]{:S(2)}) collective-permute-start(bf16[4,112,896]{2,1,0:T(8,128)(2,1)S(1)} %pad_maximum_fusion.own), channel_id=1, source_target_pairs={{24,16},{16,8},{8,0},{25,17},{17,9},{9,1},{26,18},{18,10},{10,2},{... | collective-permute-start | bytes 2408456 | tf_op jit(solution)/shard_map/ppermute | solution.py:369
  228.3 21.5 %collective-permute-start.12 = (bf16[4,112,896]{2,1,0:T(8,128)(2,1)S(1)}, bf16[4,112,896]{2,1,0:T(8,128)(2,1)}, u32[]{:S(2)}, u32[]{:S(2)}) collective-permute-start(bf16[4,112,896]{2,1,0:T(8,128)(2,1)S(1)} %pad_maximum_fusion.own), channel_id=1, source_target_pairs={{0,8},{8,16},{16,24},{1,9},{9,17},{17,25},{2,10},{10,18},{18,26},{... | collective-permute-start | bytes 2408456 | tf_op jit(solution)/shard_map/ppermute | solution.py:369
  236.2 16.6 %collective-permute-start.11 = (bf16[1,112,896]{2,1,0:T(8,128)(2,1)}, bf16[1,112,896]{2,1,0:T(8,128)(2,1)}, u32[]{:S(2)}, u32[]{:S(2)}) collective-permute-start(bf16[1,112,896]{2,1,0:T(8,128)(2,1)} %bitcast.33), channel_id=1, source_target_pairs={{8,0},{16,24},{9,1},{17,25},{10,2},{18,26},{11,3},{19,27},{12,4},{... | collective-permute-start | bytes 602120 | tf_op jit(solution)/shard_map/ppermute | solution.py:369
  256.2 111.7 %all-gather.6.cloned.1.call-start = ((), (), s32[]{:S(2)}) async-start(), calls=%async_computation.6 | async-start | bytes 8257536 | tf_op jit(solution)/shard_map/all_gather | solution.py:418
  256.2 20.6 %collective-permute-start.16 = (bf16[4,112,896]{2,1,0:T(8,128)(2,1)}, bf16[4,112,896]{2,1,0:T(8,128)(2,1)S(1)}, u32[]{:S(2)}, u32[]{:S(2)}) collective-permute-start(bf16[4,112,896]{2,1,0:T(8,128)(2,1)} %collective-permute-done.13.l1), channel_id=1, source_target_pairs={{16,8},{8,0},{17,9},{9,1},{18,10},{10,2},{19,11},{11,3},{20,12},{1... | collective-permute-start | bytes 2408456 | tf_op jit(solution)/shard_map/ppermute | solution.py:369
  257.5 20.6 %collective-permute-start.14 = (bf16[4,112,896]{2,1,0:T(8,128)(2,1)}, bf16[4,112,896]{2,1,0:T(8,128)(2,1)S(1)}, u32[]{:S(2)}, u32[]{:S(2)}) collective-permute-start(bf16[4,112,896]{2,1,0:T(8,128)(2,1)} %collective-permute-done.12.r1), channel_id=1, source_target_pairs={{8,16},{16,24},{9,17},{17,25},{10,18},{18,26},{11,19},{19,27},{12,... | collective-permute-start | bytes 2408456 | tf_op jit(solution)/shard_map/ppermute | solution.py:369
  276.8 24.1 %copy-start.9 = (bf16[4,112,896]{2,1,0:T(8,128)(2,1)}, bf16[4,112,896]{2,1,0:T(8,128)(2,1)S(1)}, u32[]{:S(2)}) copy-start(bf16[4,112,896]{2,1,0:T(8,128)(2,1)S(1)} %collective-permute-done.16.l2) | copy-start | bytes 2408452
  276.8 19.6 %collective-permute-start.17 = (bf16[4,112,896]{2,1,0:T(8,128)(2,1)S(1)}, bf16[4,112,896]{2,1,0:T(8,128)(2,1)S(1)}, u32[]{:S(2)}, u32[]{:S(2)}) collective-permute-start(bf16[4,112,896]{2,1,0:T(8,128)(2,1)S(1)} %collective-permute-done.16.l2), channel_id=1, source_target_pairs={{8,0},{9,1},{10,2},{11,3},{12,4},{13,5},{14,6},{15,7}} | collective-permute-start | bytes 2408456 | tf_op jit(solution)/shard_map/ppermute | solution.py:369
  278.1 22.8 %copy-start.10 = (bf16[4,112,896]{2,1,0:T(8,128)(2,1)}, bf16[4,112,896]{2,1,0:T(8,128)(2,1)S(1)}, u32[]{:S(2)}) copy-start(bf16[4,112,896]{2,1,0:T(8,128)(2,1)S(1)} %collective-permute-done.14.r2) | copy-start | bytes 2408452
  278.1 18.3 %collective-permute-start.15 = (bf16[4,112,896]{2,1,0:T(8,128)(2,1)S(1)}, bf16[4,112,896]{2,1,0:T(8,128)(2,1)S(1)}, u32[]{:S(2)}, u32[]{:S(2)}) collective-permute-start(bf16[4,112,896]{2,1,0:T(8,128)(2,1)S(1)} %collective-permute-done.14.r2), channel_id=1, source_target_pairs={{16,24},{17,25},{18,26},{19,27},{20,28},{21,29},{22,30},{23,31}} | collective-permute-start | bytes 2408456 | tf_op jit(solution)/shard_map/ppermute | solution.py:369
  278.9 2.3 collective-permute-start.18
  296.4 45.0 %collective-permute-start.19 = (bf16[896,1024]{1,0:T(8,128)(2,1)}, bf16[896,1024]{1,0:T(8,128)(2,1)S(1)}, u32[]{:S(2)}, u32[]{:S(2)}) collective-permute-start(bf16[896,1024]{1,0:T(8,128)(2,1)} %slice.31), channel_id=1, source_target_pairs={{8,0},{16,24},{9,1},{17,25},{10,2},{18,26},{11,3},{19,27},{12,4},{... | collective-permute-start | bytes 5505032 | tf_op jit(solution)/shard_map/ppermute | solution.py:369
  316.6 68.6 %collective-permute-start.20 = (bf16[896,768]{1,0:T(8,128)(2,1)}, bf16[896,768]{1,0:T(8,128)(2,1)}, u32[]{:S(2)}, u32[]{:S(2)}) collective-permute-start(bf16[896,768]{1,0:T(8,128)(2,1)} %add.19), channel_id=1, source_target_pairs={{8,0},{16,24},{9,1},{17,25},{10,2},{18,26},{11,3},{19,27},{12,4},{... | collective-permute-start | bytes 4128776 | tf_op jit(solution)/shard_map/ppermute | solution.py:369
  (10 other events, 87.8 us)
Sparse Core Ops, SparseCore 0:
  24.3 38.0 reduce-scatter.2
  134.1 69.9 reduce-scatter.4
  256.3 47.9 all-gather.3
  316.8 51.0 all-gather.5

commit v14 on v13

--- a/solution.py
+++ b/solution.py
@@ -61,40 +61,73 @@
     return copies
 
 
-def near_kernel(marks, x, *rest):
-    n = len(marks) - 1
-    l1, r1 = rest[:n], rest[n : 2 * n]
-    out, held, sems = rest[2 * n :]
+def load_near(begin, x, l1, r1, held, sems):
+    rows, width = l1.shape
+    sources = (r1, x.at[:, begin : begin + width], l1)
+    copies = [
+        pltpu.make_async_copy(source, held.at[g * rows : (g + 1) * rows], sems.at[g])
+        for g, source in enumerate(sources)
+    ]
+    for copy in copies:
+        copy.start()
+    for copy in copies:
+        copy.wait()
+
+
+def near_first_kernel(x, l1, r1, out, held, sems):
     rows = x.shape[0]
-    copies = load_pieces([x], [0, marks[-1]], held.at[rows : 2 * rows], sems.at[0])
-    copies += load_pieces(l1, marks, held.at[2 * rows :], sems.at[1])
-    copies += load_pieces(r1, marks, held.at[:rows], sems.at[2])
-    for copy in copies:
-        copy.wait()
-    value = dot_rows(held[: 2 * rows], held[2 * rows :]).astype(out.dtype)
-    out[2] = value[:rows]
-    out[0] = value[rows:]
-    value = dot_rows(held[rows:], held[:rows]).astype(out.dtype)
-    out[1] = value[:rows]
-    out[3] = value[rows:]
-
-
-def near_blocks(x, l1, r1, marks):
-    rows, depth = x.shape
-    return pl.pallas_call(
-        functools.partial(near_kernel, marks),
-        out_shape=jax.ShapeDtypeStruct((4, rows, rows), jnp.bfloat16),
-        in_specs=[pl.BlockSpec(memory_space=pl.ANY)] * (1 + len(l1) + len(r1)),
+    load_near(0, x, l1, r1, held, sems)
+    out[0] = dot_rows(held[: 2 * rows], held[2 * rows :])
+    out[1] = dot_rows(held[rows:], held[:rows])
+
+
+def near_rest_kernel(begin, x, l1, r1, part, out, held, total, sems):
+    rows = x.shape[0]
+    copies = [pltpu.make_async_copy(part.at[g], total.at[g], sems.at[3 + g]) for g in range(2)]
+    for copy in copies:
+        copy.start()
+    load_near(begin, x, l1, r1, held, sems)
+    for g, (left, right, above, below) in enumerate(
+        (
+            (slice(0, 2 * rows), slice(2 * rows, 3 * rows), 2, 0),
+            (slice(rows, 3 * rows), slice(0, rows), 1, 3),
+        )
+    ):
+        value = dot_rows(held[left], held[right])
+        copies[g].wait()
+        value = (value + total[g]).astype(out.dtype)
+        out[above] = value[:rows]
+        out[below] = value[rows:]
+
+
+def near_call(kernel, shape, dtype, operands, scratch, share):
+    rows, width = operands[1].shape
+    return pl.pallas_call(
+        kernel,
+        out_shape=jax.ShapeDtypeStruct(shape, dtype),
+        in_specs=[pl.BlockSpec(memory_space=pl.ANY)] * len(operands),
         out_specs=whole(),
-        scratch_shapes=[
-            pltpu.VMEM((3 * rows, depth), jnp.bfloat16),
-            pltpu.SemaphoreType.DMA((3, len(l1))),
-        ],
+        scratch_shapes=[pltpu.VMEM((3 * rows, width), jnp.bfloat16), *scratch],
         compiler_params=pltpu.CompilerParams(vmem_limit_bytes=56 * 2**20),
         cost_estimate=pl.CostEstimate(
-            flops=8 * rows * rows * depth, bytes_accessed=6 * rows * depth, transcendentals=0
+            flops=share * 8 * rows * rows * width,
+            bytes_accessed=share * 6 * rows * width,
+            transcendentals=0,
         ),
-    )(x, *l1, *r1)
+    )(*operands)
+
+
+def near_first(x, l1, r1):
+    rows = x.shape[0]
+    sems = pltpu.SemaphoreType.DMA((3,))
+    return near_call(near_first_kernel, (2, 2 * rows, rows), jnp.float32, [x, l1, r1], [sems], 0)
+
+
+def near_rest(x, l1, r1, part):
+    rows = x.shape[0]
+    kernel = functools.partial(near_rest_kernel, x.shape[1] - l1.shape[1])
+    scratch = [pltpu.VMEM(part.shape, jnp.float32), pltpu.SemaphoreType.DMA((5,))]
+    return near_call(kernel, (4, rows, rows), jnp.bfloat16, [x, l1, r1, part], scratch, 1)
 
 
 def corner_kernel(marks, place, *rest):
@@ -165,7 +198,7 @@
         out_shape=jax.ShapeDtypeStruct((4 * part, 4 * rows), jnp.bfloat16),
         in_specs=[scalars()] + [whole()] * len(others),
         out_specs=whole(),
-        compiler_params=pltpu.CompilerParams(vmem_limit_bytes=56 * 2**20),
+        compiler_params=pltpu.CompilerParams(vmem_limit_bytes=24 * 2**20),
         cost_estimate=pl.CostEstimate(
             flops=16 * part * rows, bytes_accessed=2 * 44 * part * rows, transcendentals=0
         ),
@@ -344,20 +377,20 @@
     )(*operands)
 
 
-def arrived_kernel(value, out):
+def arrived_kernel(*refs):
     pass
 
 
-def arrived(value):
+def arrived(*values):
     outside = pl.BlockSpec(memory_space=pl.ANY)
     return pl.pallas_call(
         arrived_kernel,
-        out_shape=jax.ShapeDtypeStruct(value.shape, value.dtype),
-        in_specs=[outside],
-        out_specs=outside,
-        input_output_aliases={0: 0},
+        out_shape=[jax.ShapeDtypeStruct(value.shape, value.dtype) for value in values],
+        in_specs=[outside] * len(values),
+        out_specs=[outside] * len(values),
+        input_output_aliases={i: i for i in range(len(values))},
         cost_estimate=pl.CostEstimate(flops=2 * 10**11, bytes_accessed=0, transcendentals=0),
-    )(value)
+    )(*values)
 
 
 def per_device_line(n_col, x):
@@ -377,27 +410,28 @@
     l1 = [send(piece, left) for piece in xs]
     own = scatter(dot_rows(x, x).astype(jnp.bfloat16)[None])
     own, r1[0], l1[0] = lax.optimization_barrier((own, r1[0], l1[0]))
-    r2 = [send(piece, right[1:]) for piece in r1]
-    l2 = [send(piece, left[1:]) for piece in l1]
-
-    across = [l2[0] + r2[0]]
-    far_marks = [0, 512, *marks[1:]]
-    head = across[0][:, :512]
-    head, across[0], l2[1], r2[1] = lax.optimization_barrier((head, across[0], l2[1], r2[1]))
+    r2, l2 = [send(r1[0], right[1:])], [send(l1[0], left[1:])]
+
+    part = near_first(x, l1[0], r1[0])
+    part, r1[1], l1[1] = lax.optimization_barrier((part, r1[1], l1[1]))
+    r1[1], l1[1] = arrived(r1[1], l1[1])
+    r2.append(send(r1[1], right[1:]))
+    l2.append(send(l1[1], left[1:]))
+    first = scatter(near_rest(x, l1[1], r1[1], part))
+    across = list(arrived(l2[0] + r2[0]))
+    first, across[0] = lax.optimization_barrier((first, across[0]))
+    second = send(first[2], left[1:]) + send(first[3], right[1:])
+
+    second, l2[1], r2[1] = lax.optimization_barrier((second, l2[1], r2[1]))
     across.append(l2[1] + r2[1])
-
-    first = scatter(near_blocks(x, l1, r1, marks))
     corner = corner_block(place, l1, r1, l2, r2, marks)
-    corner, first = lax.optimization_barrier((corner, first))
+    corner, second = lax.optimization_barrier((corner, second))
     shares = lax.all_to_all(corner.reshape(n_col, -1, corner.shape[2]), "col", 0, 0)
     corner = shares.astype(jnp.float32).sum(0, keepdims=True).astype(jnp.bfloat16)
 
     def send_on(value, *after):
         return send(lax.optimization_barrier((value, *after))[0], [(1, 0), (2, 3)])
 
-    far = [send_on(head)]
-    second = send(first[2], left[1:]) + send(first[3], right[1:])
-    second, far[0] = lax.optimization_barrier((second, far[0]))
     tile = jnp.stack([own[0], first[0], second, first[1]])
     tr1, tl1 = send(tile, right), send(tile, left)
 
@@ -410,7 +444,7 @@
 
     tr2, tl2 = send(tr1, right[1:]), send(tl1, left[1:])
     tr3, tl3 = send(tr2, right[2:]), send(tl2, left[2:])
-    far.append(arrived(send_on(across[0][:, 512:], tr3, tl3, pair)))
+    far = list(arrived(send_on(across[0], tr3, tl3, pair)))
 
     strip = strips(place, tile, tl1, tr3, tl2, tr2, tr1, tl3, corner, pair, end)
     factor = square(place, panel, strip)
@@ -418,9 +452,9 @@
     factor = lax.all_gather(factor, "col", axis=0, tiled=False)
     near = [l1, r1, across]
     out, factor = product(
-        place, factor, x, [group[0] for group in near], far[:2], 256, far_marks[:3], None
-    )
-    (out,) = product(place, factor, x, [group[1] for group in near], far[2:], 256, marks[1:], out)
+        place, factor, x, [group[0] for group in near], far[:1], 256, marks[:2], None
+    )
+    (out,) = product(place, factor, x, [group[1] for group in near], far[1:], 256, marks[1:], out)
     return out
 
 

time: 403 us -> 404 us (level)
  waiting for transfers between devices: 244 us -> 235 us
  starting transfers between devices: 43.2 us -> 49 us
  Pallas kernels: 70.4 us -> 76 us
    all_gather x1, waiting for transfers between devices: 25.1 us -> 4.89 us  [per_device_line(): factor = lax.all_gather(factor, 'col', axis=0, tiled=False)]
    reduce_scatter x2, waiting for transfers between devices: 38.6 us -> 54 us  [scatter(): return lax.psum_scatter(blocks, 'col', scatter_dimension=1, tiled=True)]
    ppermute x21 -> x20, waiting for transfers between devices: 180 us -> 169 us  [send(): return lax.ppermute(value, 'row', pairs)]
    pallas_call x2 -> x5, Pallas kernels: 24.9 us -> 34.8 us  [the longest x2 34.8 us: near_call(): pl.pallas_call(kernel, out_shape=jax.ShapeDtypeStruct(shape, dtype), in_s...]
    all_to_all x1, waiting for transfers between devices: 0.01 us -> 7.31 us  [per_device_line(): lax.all_to_all(corner.reshape(n_col, -1, corner.shape[2]), 'col', 0, 0)]
    ppermute x21 -> x20, starting transfers between devices: 38.7 us -> 44.5 us  [send(): return lax.ppermute(value, 'row', pairs)]
  transfers between devices with their start and end apart: 26 -> 25, of which waited for: 14 -> 17; matrix products, arithmetic and copies ran while one was open for 5% -> 5% of each run, Pallas kernels for 15% -> 16%
where the time goes in v14:
time: 404 us; the launch traced here: 403 us
  waiting for transfers between devices  235 us (58%)
  Pallas kernels  76 us (19%)
  starting transfers between devices  49 us (12%)
  between operations  13.5 us (3%)
  other arithmetic  13.2 us (3%)
  local copies, waits for them, and re-layouts  9.94 us (2%)
  matrix products  5.58 us (1%)
    ppermute x20, waiting for transfers between devices, send(): return lax.ppermute(value, 'row', pairs)  169 us
    reduce_scatter x2, waiting for transfers between devices, scatter(): return lax.psum_scatter(blocks, 'col', scatter_dimension=1, tiled=True)  54 us
    ppermute x20, starting transfers between devices, send(): return lax.ppermute(value, 'row', pairs)  44.5 us
    pallas_call x2, Pallas kernels, near_call(): pl.pallas_call(kernel, out_shape=jax.ShapeDtypeStruct(shape, dtype), in_s...  34.8 us
    pallas_call x2, Pallas kernels, product(): pl.pallas_call(functools.partial(product_kernel, tuple(marks), ready), gr...  27.8 us
    pallas_call x1, Pallas kernels, square(): pl.pallas_call(square_kernel, out_shape=jax.ShapeDtypeStruct((rows, depth...  10.5 us
  transfers between devices with their start and end apart: 25, of which 17 were waited for; matrix products, arithmetic and copies ran while one was open for 5% of the time, Pallas kernels for 16%

profile of v14, /device:TPU:0, one launch (start us, length us, event | category | flops | bytes accessed | tf_op | source)
XLA Modules:
  0.0 402.6 jit_solution(9073498397559877504)
XLA Ops:
  6.5 3.6 slice.18
  10.2 5.1 %collective-permute-start = (bf16[896,1536]{1,0:T(8,128)(2,1)}, bf16[896,1536]{1,0:T(8,128)(2,1)S(1)}, u32[]{:S(2)}, u32[]{:S(2)}) collective-permute-start(bf16[896,1536]{1,0:T(8,128)(2,1)} %slice.18), channel_id=1, source_target_pairs={{0,8},{8,16},{16,24},{1,9},{9,17},{17,25},{2,10},{10,18},{18,26},{... | collective-permute-start | bytes 8257544 | tf_op jit(solution)/shard_map/ppermute | solution.py:402
  16.6 5.6 %fusion = bf16[1,896,896]{2,1,0:T(8,128)(2,1)} fusion(bf16[896,2304]{1,0:T(8,128)(2,1)S(1)} %copy-done.2), kind=kOutput, calls=%fused_computation.1 | convolution fusion | flops 3700178944 | bytes 5734400 | tf_op jit(solution)/shard_map/dot_general | solution.py:20
  22.2 2.5 slice.19
  24.8 5.6 %collective-permute-start.2 = (bf16[896,768]{1,0:T(8,128)(2,1)}, bf16[896,768]{1,0:T(8,128)(2,1)}, u32[]{:S(2)}, u32[]{:S(2)}) collective-permute-start(bf16[896,768]{1,0:T(8,128)(2,1)} %slice.19), channel_id=1, source_target_pairs={{0,8},{8,16},{16,24},{1,9},{9,17},{17,25},{2,10},{10,18},{18,26},{... | collective-permute-start | bytes 4128776 | tf_op jit(solution)/shard_map/ppermute | solution.py:402
  31.7 33.1 %reduce-scatter.3.cloned.1.call-done = bf16[1,112,896]{2,1,0:T(8,128)(2,1)} async-done(((bf16[1,896,896]{2,1,0:T(8,128)(2,1)}), bf16[1,112,896]{2,1,0:T(8,128)(2,1)}) %reduce-scatter.3.cloned.1.call-update) | async-done | bytes 200720 | tf_op jit(solution)/shard_map/reduce_scatter | solution.py:405
  64.8 10.6 %collective-permute-done.r1.rest_2_ = bf16[896,1536]{1,0:T(8,128)(2,1)S(1)} collective-permute-done((bf16[896,1536]{1,0:T(8,128)(2,1)}, bf16[896,1536]{1,0:T(8,128)(2,1)S(1)}, u32[]{:S(2)}, u32[]{:S(2)}) %collective-permute-start) | collective-permute-done | bytes 2752544 | tf_op jit(solution)/shard_map/ppermute | solution.py:402
  75.5 4.6 %collective-permute-done.1.l1.rest_0_ = bf16[896,1536]{1,0:T(8,128)(2,1)} collective-permute-done((bf16[896,1536]{1,0:T(8,128)(2,1)}, bf16[896,1536]{1,0:T(8,128)(2,1)}, u32[]{:S(2)}, u32[]{:S(2)}) %collective-permute-start.1) | collective-permute-done | bytes 2752544 | tf_op jit(solution)/shard_map/ppermute | solution.py:402
  81.6 19.7 %shard_map.17.part = f32[2,1792,896]{2,1,0:T(8,128)} custom-call(bf16[896,2304]{1,0:T(8,128)(2,1)} %x.3, bf16[896,1536]{1,0:T(8,128)(2,1)} %collective-permute-done.1.l1.rest_0_, bf16[896,1536]{1,0:T(8,128)(2,1)} %copy-done.3), custom_call_target="tpu_custom_call" | custom-call | tf_op jit(solution)/shard_map/pallas_call | solution.py:105
  101.3 2.3 collective-permute-start.5
  103.8 5.8 %collective-permute-done.3.refs_1_ = bf16[896,768]{1,0:T(8,128)(2,1)} collective-permute-done((bf16[896,768]{1,0:T(8,128)(2,1)}, bf16[896,768]{1,0:T(8,128)(2,1)}, u32[]{:S(2)}, u32[]{:S(2)}) %collective-permute-start.3) | collective-permute-done | bytes 1376288 | tf_op jit(solution)/shard_map/ppermute | solution.py:402
  112.6 15.0 %shard_map.19 = bf16[4,896,896]{2,1,0:T(8,128)(2,1)} custom-call(bf16[896,2304]{1,0:T(8,128)(2,1)} %x.3, bf16[896,768]{1,0:T(8,128)(2,1)} %get-tuple-element.32.l1.rest_1_, bf16[896,768]{1,0:T(8,128)(2,1)} %get-tuple-element.33.r1.rest_3_, f32[2,1792,896]{2,1,0:T(8,128)} %shard_map.17.part), custom_call_target="tpu_custom_call" | custom-call | flops 4932501504 | bytes 4128768 | tf_op jit(solution)/shard_map/pallas_call | solution.py:105
  127.7 40.9 %collective-permute-done.4.rest_4_ = bf16[896,1536]{1,0:T(8,128)(2,1)} collective-permute-done((bf16[896,1536]{1,0:T(8,128)(2,1)}, bf16[896,1536]{1,0:T(8,128)(2,1)}, u32[]{:S(2)}, u32[]{:S(2)}) %collective-permute-start.4) | collective-permute-done | bytes 2752544 | tf_op jit(solution)/shard_map/ppermute | solution.py:402
  168.6 4.8 %add.16.refs_0_ = bf16[896,1536]{1,0:T(8,128)(2,1)} add(bf16[896,1536]{1,0:T(8,128)(2,1)} %collective-permute-done.4.rest_4_, bf16[896,1536]{1,0:T(8,128)(2,1)} %collective-permute-done.5.rest_6_) | non-fusion elementwise | flops 1376256 | bytes 8257536 | tf_op jit(solution)/shard_map/add | solution.py:421
  173.4 20.9 %reduce-scatter.5.cloned.1.call-done = bf16[4,112,896]{2,1,0:T(8,128)(2,1)} async-done(((bf16[4,896,896]{2,1,0:T(8,128)(2,1)}), bf16[4,112,896]{2,1,0:T(8,128)(2,1)}) %reduce-scatter.5.cloned.1.call-update) | async-done | bytes 802832 | tf_op jit(solution)/shard_map/reduce_scatter | solution.py:405
  198.9 6.0 %collective-permute-done.6 = bf16[112,896]{1,0:T(8,128)(2,1)S(1)} collective-permute-done((bf16[112,896]{1,0:T(8,128)(2,1)S(1)}, bf16[112,896]{1,0:T(8,128)(2,1)S(1)}, u32[]{:S(2)}, u32[]{:S(2)}) %collective-permute-start.6) | collective-permute-done | bytes 200736 | tf_op jit(solution)/shard_map/ppermute | solution.py:402
  207.7 4.5 %all-to-all-start = ((bf16[8,112,896]{2,1,0:T(8,128)(2,1)}), bf16[8,112,896]{2,1,0:T(8,128)(2,1)}, u32[]{:S(2)}, u32[]{:S(2)}) async-start(bf16[8,112,896]{2,1,0:T(8,128)(2,1)} %bitcast.33), calls=%async_computation.2 | async-start | bytes 3211264 | tf_op jit(solution)/shard_map/all_to_all | solution.py:429
  212.4 12.6 %collective-permute-start.11 = (bf16[4,112,896]{2,1,0:T(8,128)(2,1)S(1)}, bf16[4,112,896]{2,1,0:T(8,128)(2,1)S(1)}, u32[]{:S(2)}, u32[]{:S(2)}) collective-permute-start(bf16[4,112,896]{2,1,0:T(8,128)(2,1)S(1)} %pad_maximum_fusion.own), channel_id=1, source_target_pairs={{0,8},{8,16},{16,24},{1,9},{9,17},{17,25},{2,10},{10,18},{18,26},{... | collective-permute-start | bytes 2408456 | tf_op jit(solution)/shard_map/ppermute | solution.py:402
  226.3 7.3 %all-to-all-done = bf16[8,112,896]{2,1,0:T(8,128)(2,1)} async-done(((bf16[8,112,896]{2,1,0:T(8,128)(2,1)}), bf16[8,112,896]{2,1,0:T(8,128)(2,1)}, u32[]{:S(2)}, u32[]{:S(2)}) %all-to-all-start) | async-done | bytes 1605664 | tf_op jit(solution)/shard_map/all_to_all | solution.py:429
  236.5 5.7 %collective-permute-done.11.r1 = bf16[4,112,896]{2,1,0:T(8,128)(2,1)S(1)} collective-permute-done((bf16[4,112,896]{2,1,0:T(8,128)(2,1)S(1)}, bf16[4,112,896]{2,1,0:T(8,128)(2,1)S(1)}, u32[]{:S(2)}, u32[]{:S(2)}) %collective-permute-start.11) | collective-permute-done | bytes 802848 | tf_op jit(solution)/shard_map/ppermute | solution.py:402
  242.3 5.7 %collective-permute-done.12.l1 = bf16[4,112,896]{2,1,0:T(8,128)(2,1)S(1)} collective-permute-done((bf16[4,112,896]{2,1,0:T(8,128)(2,1)S(1)}, bf16[4,112,896]{2,1,0:T(8,128)(2,1)S(1)}, u32[]{:S(2)}, u32[]{:S(2)}) %collective-permute-start.12) | collective-permute-done | bytes 802848 | tf_op jit(solution)/shard_map/ppermute | solution.py:402
  248.0 3.7 collective-permute-done.10.end
  251.8 2.1 maximum_add_fusion
  256.7 18.7 %collective-permute-done.15.l2 = bf16[4,112,896]{2,1,0:T(8,128)(2,1)S(1)} collective-permute-done((bf16[4,112,896]{2,1,0:T(8,128)(2,1)S(1)}, bf16[4,112,896]{2,1,0:T(8,128)(2,1)S(1)}, u32[]{:S(2)}, u32[]{:S(2)}) %collective-permute-start.15) | collective-permute-done | bytes 802848 | tf_op jit(solution)/shard_map/ppermute | solution.py:402
  277.4 17.7 %collective-permute-done.16.l3 = bf16[4,112,896]{2,1,0:T(8,128)(2,1)S(1)} collective-permute-done((bf16[4,112,896]{2,1,0:T(8,128)(2,1)S(1)}, bf16[4,112,896]{2,1,0:T(8,128)(2,1)S(1)}, u32[]{:S(2)}, u32[]{:S(2)}) %collective-permute-start.16) | collective-permute-done | bytes 802848 | tf_op jit(solution)/shard_map/ppermute | solution.py:402
  296.4 3.2 add.19
  302.2 10.5 %shard_map.23 = bf16[896,448]{1,0:T(8,128)(2,1)} custom-call(s32[2]{0:T(128)} %pad_add_fusion.place, bf16[4,896,896]{2,1,0:T(8,128)(2,1)} %all-gather.4.cloned.1.call-done.panel, bf16[448,3584]{1,0:T(8,128)(2,1)} %copy-done), custom_call_target="tpu_custom_call" | custom-call | flops 2877292544 | bytes 8028160 | tf_op jit(solution)/shard_map/pallas_call | solution.py:239
  314.1 45.9 %collective-permute-done.18.refs_0_ = bf16[896,1536]{1,0:T(8,128)(2,1)} collective-permute-done((bf16[896,1536]{1,0:T(8,128)(2,1)}, bf16[896,1536]{1,0:T(8,128)(2,1)}, u32[]{:S(2)}, u32[]{:S(2)}) %collective-permute-start.18) | collective-permute-done | bytes 2752544 | tf_op jit(solution)/shard_map/ppermute | solution.py:402
  359.9 4.9 %all-gather.6.cloned.1.call-done = bf16[7168,448]{1,0:T(8,128)(2,1)} async-done(((bf16[896,448]{1,0:T(8,128)(2,1)}), bf16[7168,448]{1,0:T(8,128)(2,1)}) %all-gather.6.cloned.1.call-update) | async-done | bytes 6422544 | tf_op jit(solution)/shard_map/all_gather | solution.py:452
  364.8 17.3 %shard_map.25 = (bf16[896,2304]{1,0:T(8,128)(2,1)}, bf16[896,3584]{1,0:T(8,128)(2,1)}) custom-call(s32[2]{0:T(128)} %pad_add_fusion.place, bf16[8,896,448]{2,1,0:T(8,128)(2,1)} %bitcast.30, bf16[8,112,2304]{2,1,0:T(8,128)(2,1)} %bitcast.26, bf16[8,112,1536]{2,1,0:T(8,128)(2,1)} %bitcast.10.rest_0_, bf16[8,112,1536]{2,1,0:T(8,128)(2,1)} %bitcast.29, ...), custom_call_target="tpu_custom_call" | custom-call | tf_op jit(solution)/shard_map/pallas_call | solution.py:363
  382.2 3.5 collective-permute-done.19
  385.6 10.5 %shard_map.26 = bf16[896,2304]{1,0:T(8,128)(2,1)} custom-call(s32[2]{0:T(128)} %pad_add_fusion.place, bf16[896,3584]{1,0:T(8,128)(2,1)} %get-tuple-element.46.f, bf16[8,112,2304]{2,1,0:T(8,128)(2,1)} %bitcast.27, bf16[8,112,768]{2,1,0:T(8,128)(2,1)} %bitcast.14.rest_0_, bf16[8,112,768]{2,1,0:T(8,128)(2,1)} %bitcast.15.rest_1_, ...), custom_call_target="tpu_custom_call", output_to_operand_aliasing={{}: (7, {})} | custom-call | flops 4932501504 | bytes 8257536 | tf_op jit(solution)/shard_map/pallas_call | solution.py:363
  (61 shorter events, 29.2 us)
Async XLA Ops:
  6.5 58.3 %reduce-scatter.3.cloned.1.call-start = ((), (), s32[]{:S(2)}) async-start(), calls=%async_computation.3 | async-start | bytes 1806336 | tf_op jit(solution)/shard_map/reduce_scatter | solution.py:405
  6.5 10.0 %copy-start.2 = (bf16[896,2304]{1,0:T(8,128)(2,1)S(1)}, bf16[896,2304]{1,0:T(8,128)(2,1)}, u32[]{:S(2)}) copy-start(bf16[896,2304]{1,0:T(8,128)(2,1)} %x.3) | copy-start | bytes 12386308
  10.2 65.3 %collective-permute-start = (bf16[896,1536]{1,0:T(8,128)(2,1)}, bf16[896,1536]{1,0:T(8,128)(2,1)S(1)}, u32[]{:S(2)}, u32[]{:S(2)}) collective-permute-start(bf16[896,1536]{1,0:T(8,128)(2,1)} %slice.18), channel_id=1, source_target_pairs={{0,8},{8,16},{16,24},{1,9},{9,17},{17,25},{2,10},{10,18},{18,26},{... | collective-permute-start | bytes 8257544 | tf_op jit(solution)/shard_map/ppermute | solution.py:402
  15.3 64.8 %collective-permute-start.1 = (bf16[896,1536]{1,0:T(8,128)(2,1)}, bf16[896,1536]{1,0:T(8,128)(2,1)}, u32[]{:S(2)}, u32[]{:S(2)}) collective-permute-start(bf16[896,1536]{1,0:T(8,128)(2,1)} %slice.18), channel_id=1, source_target_pairs={{24,16},{16,8},{8,0},{25,17},{17,9},{9,1},{26,18},{18,10},{10,2},{... | collective-permute-start | bytes 8257544 | tf_op jit(solution)/shard_map/ppermute | solution.py:402
  22.2 172.1 %reduce-scatter.5.cloned.1.call-start = ((), (), s32[]{:S(2)}) async-start(), calls=%async_computation.4 | async-start | bytes 7225344 | tf_op jit(solution)/shard_map/reduce_scatter | solution.py:405
  24.8 79.1 %collective-permute-start.2 = (bf16[896,768]{1,0:T(8,128)(2,1)}, bf16[896,768]{1,0:T(8,128)(2,1)}, u32[]{:S(2)}, u32[]{:S(2)}) collective-permute-start(bf16[896,768]{1,0:T(8,128)(2,1)} %slice.19), channel_id=1, source_target_pairs={{0,8},{8,16},{16,24},{1,9},{9,17},{17,25},{2,10},{10,18},{18,26},{... | collective-permute-start | bytes 4128776 | tf_op jit(solution)/shard_map/ppermute | solution.py:402
  30.4 79.2 %collective-permute-start.3 = (bf16[896,768]{1,0:T(8,128)(2,1)}, bf16[896,768]{1,0:T(8,128)(2,1)}, u32[]{:S(2)}, u32[]{:S(2)}) collective-permute-start(bf16[896,768]{1,0:T(8,128)(2,1)} %slice.19), channel_id=1, source_target_pairs={{24,16},{16,8},{8,0},{25,17},{17,9},{9,1},{26,18},{18,10},{10,2},{... | collective-permute-start | bytes 4128776 | tf_op jit(solution)/shard_map/ppermute | solution.py:402
  75.5 6.1 %copy-start.3 = (bf16[896,1536]{1,0:T(8,128)(2,1)}, bf16[896,1536]{1,0:T(8,128)(2,1)S(1)}, u32[]{:S(2)}) copy-start(bf16[896,1536]{1,0:T(8,128)(2,1)S(1)} %collective-permute-done.r1.rest_2_) | copy-start | bytes 8257540
  80.1 88.5 %collective-permute-start.4 = (bf16[896,1536]{1,0:T(8,128)(2,1)}, bf16[896,1536]{1,0:T(8,128)(2,1)}, u32[]{:S(2)}, u32[]{:S(2)}) collective-permute-start(bf16[896,1536]{1,0:T(8,128)(2,1)} %collective-permute-done.1.l1.rest_0_), channel_id=1, source_target_pairs={{16,8},{8,0},{17,9},{9,1},{18,10},{10,2},{19,11},{11,3},{20,12},{1... | collective-permute-start | bytes 8257544 | tf_op jit(solution)/shard_map/ppermute | solution.py:402
  101.3 67.3 %collective-permute-start.5 = (bf16[896,1536]{1,0:T(8,128)(2,1)}, bf16[896,1536]{1,0:T(8,128)(2,1)}, u32[]{:S(2)}, u32[]{:S(2)}) collective-permute-start(bf16[896,1536]{1,0:T(8,128)(2,1)} %copy-done.3), channel_id=1, source_target_pairs={{8,16},{16,24},{9,17},{17,25},{10,18},{18,26},{11,19},{19,27},{12,... | collective-permute-start | bytes 8257544 | tf_op jit(solution)/shard_map/ppermute | solution.py:402
  109.6 96.1 %collective-permute-start.8 = (bf16[896,768]{1,0:T(8,128)(2,1)}, bf16[896,768]{1,0:T(8,128)(2,1)}, u32[]{:S(2)}, u32[]{:S(2)}) collective-permute-start(bf16[896,768]{1,0:T(8,128)(2,1)} %get-tuple-element.32.l1.rest_1_), channel_id=1, source_target_pairs={{16,8},{8,0},{17,9},{9,1},{18,10},{10,2},{19,11},{11,3},{20,12},{1... | collective-permute-start | bytes 4128776 | tf_op jit(solution)/shard_map/ppermute | solution.py:402
  110.9 94.8 %collective-permute-start.9 = (bf16[896,768]{1,0:T(8,128)(2,1)}, bf16[896,768]{1,0:T(8,128)(2,1)}, u32[]{:S(2)}, u32[]{:S(2)}) collective-permute-start(bf16[896,768]{1,0:T(8,128)(2,1)} %get-tuple-element.33.r1.rest_3_), channel_id=1, source_target_pairs={{8,16},{16,24},{9,17},{17,25},{10,18},{18,26},{11,19},{19,27},{12,... | collective-permute-start | bytes 4128776 | tf_op jit(solution)/shard_map/ppermute | solution.py:402
  196.3 8.6 %collective-permute-start.6 = (bf16[112,896]{1,0:T(8,128)(2,1)S(1)}, bf16[112,896]{1,0:T(8,128)(2,1)S(1)}, u32[]{:S(2)}, u32[]{:S(2)}) collective-permute-start(bf16[112,896]{1,0:T(8,128)(2,1)S(1)} %get-tuple-element.52), channel_id=1, source_target_pairs={{16,8},{8,0},{17,9},{9,1},{18,10},{10,2},{19,11},{11,3},{20,12},{1... | collective-permute-start | bytes 602120 | tf_op jit(solution)/shard_map/ppermute | solution.py:402
  197.6 7.3 %collective-permute-start.7 = (bf16[112,896]{1,0:T(8,128)(2,1)S(1)}, bf16[112,896]{1,0:T(8,128)(2,1)S(1)}, u32[]{:S(2)}, u32[]{:S(2)}) collective-permute-start(bf16[112,896]{1,0:T(8,128)(2,1)S(1)} %get-tuple-element.51), channel_id=1, source_target_pairs={{8,16},{16,24},{9,17},{17,25},{10,18},{18,26},{11,19},{19,27},{12,... | collective-permute-start | bytes 602120 | tf_op jit(solution)/shard_map/ppermute | solution.py:402
  207.7 4.5 %copy-start.4 = (bf16[1,112,896]{2,1,0:T(8,128)(2,1)S(1)}, bf16[1,112,896]{2,1,0:T(8,128)(2,1)}, u32[]{:S(2)}) copy-start(bf16[1,112,896]{2,1,0:T(8,128)(2,1)} %get-tuple-element.49) | copy-start | bytes 602116
  207.7 4.5 %copy-start.5 = (bf16[1,112,896]{2,1,0:T(8,128)(2,1)S(1)}, bf16[1,112,896]{2,1,0:T(8,128)(2,1)}, u32[]{:S(2)}) copy-start(bf16[1,112,896]{2,1,0:T(8,128)(2,1)} %get-tuple-element.50) | copy-start | bytes 602116
  207.7 4.5 %copy-start.6 = (bf16[112,896]{1,0:T(8,128)(2,1)S(1)}, bf16[112,896]{1,0:T(8,128)(2,1)}, u32[]{:S(2)}) copy-start(bf16[112,896]{1,0:T(8,128)(2,1)} %add.17) | copy-start | bytes 602116
  207.7 4.5 %copy-start.7 = (bf16[1,112,896]{2,1,0:T(8,128)(2,1)S(1)}, bf16[1,112,896]{2,1,0:T(8,128)(2,1)}, u32[]{:S(2)}) copy-start(bf16[1,112,896]{2,1,0:T(8,128)(2,1)} %reduce-scatter.3.cloned.1.call-done) | copy-start | bytes 602116
  207.7 25.8 %all-to-all-start = ((bf16[8,112,896]{2,1,0:T(8,128)(2,1)}), bf16[8,112,896]{2,1,0:T(8,128)(2,1)}, u32[]{:S(2)}, u32[]{:S(2)}) async-start(bf16[8,112,896]{2,1,0:T(8,128)(2,1)} %bitcast.33), calls=%async_computation.2 | async-start | bytes 3211264 | tf_op jit(solution)/shard_map/all_to_all | solution.py:429
  212.2 90.1 %all-gather.4.cloned.1.call-start = ((), (), s32[]{:S(2)}) async-start(), calls=%async_computation.5 | async-start | bytes 7225344 | tf_op jit(solution)/shard_map/all_gather | solution.py:443
  212.4 29.9 %collective-permute-start.11 = (bf16[4,112,896]{2,1,0:T(8,128)(2,1)S(1)}, bf16[4,112,896]{2,1,0:T(8,128)(2,1)S(1)}, u32[]{:S(2)}, u32[]{:S(2)}) collective-permute-start(bf16[4,112,896]{2,1,0:T(8,128)(2,1)S(1)} %pad_maximum_fusion.own), channel_id=1, source_target_pairs={{0,8},{8,16},{16,24},{1,9},{9,17},{17,25},{2,10},{10,18},{18,26},{... | collective-permute-start | bytes 2408456 | tf_op jit(solution)/shard_map/ppermute | solution.py:402
  225.0 23.0 %collective-permute-start.12 = (bf16[4,112,896]{2,1,0:T(8,128)(2,1)S(1)}, bf16[4,112,896]{2,1,0:T(8,128)(2,1)S(1)}, u32[]{:S(2)}, u32[]{:S(2)}) collective-permute-start(bf16[4,112,896]{2,1,0:T(8,128)(2,1)S(1)} %pad_maximum_fusion.own), channel_id=1, source_target_pairs={{24,16},{16,8},{8,0},{25,17},{17,9},{9,1},{26,18},{18,10},{10,2},{... | collective-permute-start | bytes 2408456 | tf_op jit(solution)/shard_map/ppermute | solution.py:402
  235.2 16.5 %collective-permute-start.10 = (bf16[1,112,896]{2,1,0:T(8,128)(2,1)S(1)}, bf16[1,112,896]{2,1,0:T(8,128)(2,1)S(1)}, u32[]{:S(2)}, u32[]{:S(2)}) collective-permute-start(bf16[1,112,896]{2,1,0:T(8,128)(2,1)S(1)} %bitcast.23), channel_id=1, source_target_pairs={{8,0},{16,24},{9,1},{17,25},{10,2},{18,26},{11,3},{19,27},{12,4},{... | collective-permute-start | bytes 602120 | tf_op jit(solution)/shard_map/ppermute | solution.py:402
  253.8 45.7 %copy-start.1 = (s32[2]{0:T(128)S(1)}, s32[2]{0:T(128)}, u32[]{:S(2)}) copy-start(s32[2]{0:T(128)} %pad_add_fusion.place) | copy-start | bytes 28
  253.9 111.0 %all-gather.6.cloned.1.call-start = ((), (), s32[]{:S(2)}) async-start(), calls=%async_computation.6 | async-start | bytes 8257536 | tf_op jit(solution)/shard_map/all_gather | solution.py:452
  253.9 2.0 collective-permute-start.13
  254.6 20.8 %collective-permute-start.15 = (bf16[4,112,896]{2,1,0:T(8,128)(2,1)S(1)}, bf16[4,112,896]{2,1,0:T(8,128)(2,1)S(1)}, u32[]{:S(2)}, u32[]{:S(2)}) collective-permute-start(bf16[4,112,896]{2,1,0:T(8,128)(2,1)S(1)} %collective-permute-done.12.l1), channel_id=1, source_target_pairs={{16,8},{8,0},{17,9},{9,1},{18,10},{10,2},{19,11},{11,3},{20,12},{1... | collective-permute-start | bytes 2408456 | tf_op jit(solution)/shard_map/ppermute | solution.py:402
  255.9 21.4 %collective-permute-start.14 = (bf16[4,112,896]{2,1,0:T(8,128)(2,1)S(1)}, bf16[4,112,896]{2,1,0:T(8,128)(2,1)S(1)}, u32[]{:S(2)}, u32[]{:S(2)}) collective-permute-start(bf16[4,112,896]{2,1,0:T(8,128)(2,1)S(1)} %collective-permute-done.13.r2), channel_id=1, source_target_pairs={{16,24},{17,25},{18,26},{19,27},{20,28},{21,29},{22,30},{23,31}} | collective-permute-start | bytes 2408456 | tf_op jit(solution)/shard_map/ppermute | solution.py:402
  275.4 19.7 %collective-permute-start.16 = (bf16[4,112,896]{2,1,0:T(8,128)(2,1)S(1)}, bf16[4,112,896]{2,1,0:T(8,128)(2,1)S(1)}, u32[]{:S(2)}, u32[]{:S(2)}) collective-permute-start(bf16[4,112,896]{2,1,0:T(8,128)(2,1)S(1)} %collective-permute-done.15.l2), channel_id=1, source_target_pairs={{8,0},{9,1},{10,2},{11,3},{12,4},{13,5},{14,6},{15,7}} | collective-permute-start | bytes 2408456 | tf_op jit(solution)/shard_map/ppermute | solution.py:402
  276.7 0.7 collective-permute-start.17
  295.1 64.8 %collective-permute-start.18 = (bf16[896,1536]{1,0:T(8,128)(2,1)}, bf16[896,1536]{1,0:T(8,128)(2,1)}, u32[]{:S(2)}, u32[]{:S(2)}) collective-permute-start(bf16[896,1536]{1,0:T(8,128)(2,1)} %shard_map.20), channel_id=1, source_target_pairs={{8,0},{16,24},{9,1},{17,25},{10,2},{18,26},{11,3},{19,27},{12,4},{... | collective-permute-start | bytes 8257544 | tf_op jit(solution)/shard_map/ppermute | solution.py:402
  312.8 72.9 %collective-permute-start.19 = (bf16[896,768]{1,0:T(8,128)(2,1)}, bf16[896,768]{1,0:T(8,128)(2,1)}, u32[]{:S(2)}, u32[]{:S(2)}) collective-permute-start(bf16[896,768]{1,0:T(8,128)(2,1)} %add.19), channel_id=1, source_target_pairs={{8,0},{16,24},{9,1},{17,25},{10,2},{18,26},{11,3},{19,27},{12,4},{... | collective-permute-start | bytes 4128776 | tf_op jit(solution)/shard_map/ppermute | solution.py:402
  (1 other events, 1.7 us)
Sparse Core Ops, SparseCore 0:
  22.3 42.4 reduce-scatter.2
  127.8 66.4 reduce-scatter.4
  254.0 45.5 all-gather.3
  312.9 51.8 all-gather.5

commit v15 on v14

--- a/solution.py
+++ b/solution.py
@@ -418,33 +418,37 @@
     r2.append(send(r1[1], right[1:]))
     l2.append(send(l1[1], left[1:]))
     first = scatter(near_rest(x, l1[1], r1[1], part))
-    across = list(arrived(l2[0] + r2[0]))
-    first, across[0] = lax.optimization_barrier((first, across[0]))
-    second = send(first[2], left[1:]) + send(first[3], right[1:])
-
-    second, l2[1], r2[1] = lax.optimization_barrier((second, l2[1], r2[1]))
+
+    across = [l2[0] + r2[0]]
+    far_marks = [0, 512, *marks[1:]]
+    head = across[0][:, :512]
+    head, across[0], l2[1], r2[1] = lax.optimization_barrier((head, across[0], l2[1], r2[1]))
     across.append(l2[1] + r2[1])
+
+    def send_on(value, *after):
+        return send(lax.optimization_barrier((value, *after))[0], [(1, 0), (2, 3)])
+
     corner = corner_block(place, l1, r1, l2, r2, marks)
-    corner, second = lax.optimization_barrier((corner, second))
+    corner, first = lax.optimization_barrier((corner, first))
     shares = lax.all_to_all(corner.reshape(n_col, -1, corner.shape[2]), "col", 0, 0)
     corner = shares.astype(jnp.float32).sum(0, keepdims=True).astype(jnp.bfloat16)
 
-    def send_on(value, *after):
-        return send(lax.optimization_barrier((value, *after))[0], [(1, 0), (2, 3)])
-
+    far = [send_on(head)]
+    second = send(first[2], left[1:]) + send(first[3], right[1:])
+    second, far[0] = lax.optimization_barrier((second, far[0]))
     tile = jnp.stack([own[0], first[0], second, first[1]])
     tr1, tl1 = send(tile, right), send(tile, left)
 
     end = send(corner, [(1, 0), (2, 3)])
     pair = send(corner, [(1, 2), (2, 1)])
-    end, tr1, tl1 = lax.optimization_barrier((end, tr1, tl1))
+    end, tr1, tl1, across[1] = lax.optimization_barrier((end, tr1, tl1, across[1]))
     zero = jnp.zeros_like(end)
     added = [zero, jnp.where(z == 3, end, zero), zero, jnp.where(z == 0, end, zero)]
     panel = lax.all_gather(tile + jnp.concatenate(added), "col", axis=1, tiled=True)
 
     tr2, tl2 = send(tr1, right[1:]), send(tl1, left[1:])
     tr3, tl3 = send(tr2, right[2:]), send(tl2, left[2:])
-    far = list(arrived(send_on(across[0], tr3, tl3, pair)))
+    far += arrived(send_on(across[0][:, 512:], tr3, tl3, pair))
 
     strip = strips(place, tile, tl1, tr3, tl2, tr2, tr1, tl3, corner, pair, end)
     factor = square(place, panel, strip)
@@ -452,9 +456,9 @@
     factor = lax.all_gather(factor, "col", axis=0, tiled=False)
     near = [l1, r1, across]
     out, factor = product(
-        place, factor, x, [group[0] for group in near], far[:1], 256, marks[:2], None
-    )
-    (out,) = product(place, factor, x, [group[1] for group in near], far[1:], 256, marks[1:], out)
+        place, factor, x, [group[0] for group in near], far[:2], 256, far_marks[:3], None
+    )
+    (out,) = product(place, factor, x, [group[1] for group in near], far[2:], 256, marks[1:], out)
     return out
 
 

time: 404 us -> 396 us (0.980)
  starting transfers between devices: 49 us -> 41.2 us
  local copies, waits for them, and re-layouts: 9.94 us -> 14.3 us
    reduce_scatter x2, waiting for transfers between devices: 54 us -> 33 us  [scatter(): return lax.psum_scatter(blocks, 'col', scatter_dimension=1, tiled=True)]
    all_gather x1, waiting for transfers between devices: 4.89 us -> 20 us  [per_device_line(): factor = lax.all_gather(factor, 'col', axis=0, tiled=False)]
    ppermute x20 -> x21, waiting for transfers between devices: 169 us -> 180 us  [send(): return lax.ppermute(value, 'row', pairs)]
    ppermute x20 -> x21, starting transfers between devices: 44.5 us -> 36.6 us  [send(): return lax.ppermute(value, 'row', pairs)]
    all_to_all x1, waiting for transfers between devices: 7.31 us -> 0.01 us  [per_device_line(): lax.all_to_all(corner.reshape(n_col, -1, corner.shape[2]), 'col', 0, 0)]
    slice x0 -> x2, local copies, waits for them, and re-layouts: none -> 4.44 us  [the longest x1 3.43 us: per_device_line(): far += arrived(send_on(across[0][:, 512:], tr3, tl3, pair))]
  transfers between devices with their start and end apart: 25 -> 26, of which waited for: 17 -> 16; matrix products, arithmetic and copies ran while one was open for 5% -> 5% of each run, Pallas kernels for 16% -> 17%
where the time goes in v15:
time: 396 us; the launch traced here: 395 us
  waiting for transfers between devices  234 us (59%)
  Pallas kernels  76.2 us (19%)
  starting transfers between devices  41.2 us (10%)
  local copies, waits for them, and re-layouts  14.3 us (4%)
  between operations  13.5 us (3%)
  other arithmetic  10.2 us (3%)
  matrix products  5.56 us (1%)
    ppermute x21, waiting for transfers between devices, send(): return lax.ppermute(value, 'row', pairs)  180 us
    ppermute x21, starting transfers between devices, send(): return lax.ppermute(value, 'row', pairs)  36.6 us
    pallas_call x2, Pallas kernels, near_call(): pl.pallas_call(kernel, out_shape=jax.ShapeDtypeStruct(shape, dtype), in_s...  34.8 us
    reduce_scatter x2, waiting for transfers between devices, scatter(): return lax.psum_scatter(blocks, 'col', scatter_dimension=1, tiled=True)  33 us
    pallas_call x2, Pallas kernels, product(): pl.pallas_call(functools.partial(product_kernel, tuple(marks), ready), gr...  27.9 us
    all_gather x1, waiting for transfers between devices, per_device_line(): factor = lax.all_gather(factor, 'col', axis=0, tiled=False)  20 us
    pallas_call x1, Pallas kernels, square(): pl.pallas_call(square_kernel, out_shape=jax.ShapeDtypeStruct((rows, depth...  10.6 us
  transfers between devices with their start and end apart: 26, of which 16 were waited for; matrix products, arithmetic and copies ran while one was open for 5% of the time, Pallas kernels for 17%

profile of v15, /device:TPU:0, one launch (start us, length us, event | category | flops | bytes accessed | tf_op | source)
XLA Modules:
  0.0 394.7 jit_solution(6344327583560321905)
XLA Ops:
  6.5 3.6 slice.24
  10.2 5.1 %collective-permute-start = (bf16[896,1536]{1,0:T(8,128)(2,1)}, bf16[896,1536]{1,0:T(8,128)(2,1)S(1)}, u32[]{:S(2)}, u32[]{:S(2)}) collective-permute-start(bf16[896,1536]{1,0:T(8,128)(2,1)} %slice.24), channel_id=1, source_target_pairs={{0,8},{8,16},{16,24},{1,9},{9,17},{17,25},{2,10},{10,18},{18,26},{... | collective-permute-start | bytes 8257544 | tf_op jit(solution)/shard_map/ppermute | solution.py:402
  16.6 5.6 %fusion = bf16[1,896,896]{2,1,0:T(8,128)(2,1)} fusion(bf16[896,2304]{1,0:T(8,128)(2,1)S(1)} %copy-done.2), kind=kOutput, calls=%fused_computation.1 | convolution fusion | flops 3700178944 | bytes 5734400 | tf_op jit(solution)/shard_map/dot_general | solution.py:20
  22.2 2.6 slice.25
  24.8 5.6 %collective-permute-start.2 = (bf16[896,768]{1,0:T(8,128)(2,1)}, bf16[896,768]{1,0:T(8,128)(2,1)}, u32[]{:S(2)}, u32[]{:S(2)}) collective-permute-start(bf16[896,768]{1,0:T(8,128)(2,1)} %slice.25), channel_id=1, source_target_pairs={{0,8},{8,16},{16,24},{1,9},{9,17},{17,25},{2,10},{10,18},{18,26},{... | collective-permute-start | bytes 4128776 | tf_op jit(solution)/shard_map/ppermute | solution.py:402
  31.7 33.0 %reduce-scatter.3.cloned.1.call-done = bf16[1,112,896]{2,1,0:T(8,128)(2,1)} async-done(((bf16[1,896,896]{2,1,0:T(8,128)(2,1)}), bf16[1,112,896]{2,1,0:T(8,128)(2,1)}) %reduce-scatter.3.cloned.1.call-update) | async-done | bytes 200720 | tf_op jit(solution)/shard_map/reduce_scatter | solution.py:405
  64.8 10.7 %collective-permute-done.r1.rest_2_ = bf16[896,1536]{1,0:T(8,128)(2,1)S(1)} collective-permute-done((bf16[896,1536]{1,0:T(8,128)(2,1)}, bf16[896,1536]{1,0:T(8,128)(2,1)S(1)}, u32[]{:S(2)}, u32[]{:S(2)}) %collective-permute-start) | collective-permute-done | bytes 2752544 | tf_op jit(solution)/shard_map/ppermute | solution.py:402
  75.5 4.6 %collective-permute-done.1.l1.rest_0_ = bf16[896,1536]{1,0:T(8,128)(2,1)} collective-permute-done((bf16[896,1536]{1,0:T(8,128)(2,1)}, bf16[896,1536]{1,0:T(8,128)(2,1)}, u32[]{:S(2)}, u32[]{:S(2)}) %collective-permute-start.1) | collective-permute-done | bytes 2752544 | tf_op jit(solution)/shard_map/ppermute | solution.py:402
  81.6 19.7 %shard_map.17.part = f32[2,1792,896]{2,1,0:T(8,128)} custom-call(bf16[896,2304]{1,0:T(8,128)(2,1)} %x.3, bf16[896,1536]{1,0:T(8,128)(2,1)} %collective-permute-done.1.l1.rest_0_, bf16[896,1536]{1,0:T(8,128)(2,1)} %copy-done.4), custom_call_target="tpu_custom_call" | custom-call | tf_op jit(solution)/shard_map/pallas_call | solution.py:105
  101.3 2.2 collective-permute-start.5
  103.8 5.8 %collective-permute-done.3.refs_1_ = bf16[896,768]{1,0:T(8,128)(2,1)} collective-permute-done((bf16[896,768]{1,0:T(8,128)(2,1)}, bf16[896,768]{1,0:T(8,128)(2,1)}, u32[]{:S(2)}, u32[]{:S(2)}) %collective-permute-start.3) | collective-permute-done | bytes 1376288 | tf_op jit(solution)/shard_map/ppermute | solution.py:402
  112.5 15.0 %shard_map.20 = bf16[4,896,896]{2,1,0:T(8,128)(2,1)} custom-call(bf16[896,2304]{1,0:T(8,128)(2,1)} %x.3, bf16[896,768]{1,0:T(8,128)(2,1)} %get-tuple-element.34.rest_1_.l1, bf16[896,768]{1,0:T(8,128)(2,1)} %get-tuple-element.35.rest_3_.r1, f32[2,1792,896]{2,1,0:T(8,128)} %shard_map.17.part), custom_call_target="tpu_custom_call" | custom-call | flops 4932501504 | bytes 4128768 | tf_op jit(solution)/shard_map/pallas_call | solution.py:105
  127.6 41.0 %collective-permute-done.4.rest_4_ = bf16[896,1536]{1,0:T(8,128)(2,1)} collective-permute-done((bf16[896,1536]{1,0:T(8,128)(2,1)}, bf16[896,1536]{1,0:T(8,128)(2,1)}, u32[]{:S(2)}, u32[]{:S(2)}) %collective-permute-start.4) | collective-permute-done | bytes 2752544 | tf_op jit(solution)/shard_map/ppermute | solution.py:402
  168.6 3.3 add.16
  174.5 22.0 %collective-permute-done.6.rest_5_ = bf16[896,768]{1,0:T(8,128)(2,1)S(1)} collective-permute-done((bf16[896,768]{1,0:T(8,128)(2,1)}, bf16[896,768]{1,0:T(8,128)(2,1)S(1)}, u32[]{:S(2)}, u32[]{:S(2)}) %collective-permute-start.6) | collective-permute-done | bytes 1376288 | tf_op jit(solution)/shard_map/ppermute | solution.py:402
  198.0 2.0 shard_map.19
  200.1 4.4 %all-to-all-start = ((bf16[8,112,896]{2,1,0:T(8,128)(2,1)}), bf16[8,112,896]{2,1,0:T(8,128)(2,1)}, u32[]{:S(2)}, u32[]{:S(2)}) async-start(bf16[8,112,896]{2,1,0:T(8,128)(2,1)} %bitcast.34), calls=%async_computation.2 | async-start | bytes 3211264 | tf_op jit(solution)/shard_map/all_to_all | solution.py:433
  206.9 16.9 %collective-permute-done.8 = bf16[112,896]{1,0:T(8,128)(2,1)S(1)} collective-permute-done((bf16[112,896]{1,0:T(8,128)(2,1)S(1)}, bf16[112,896]{1,0:T(8,128)(2,1)S(1)}, u32[]{:S(2)}, u32[]{:S(2)}) %collective-permute-start.8) | collective-permute-done | bytes 200736 | tf_op jit(solution)/shard_map/ppermute | solution.py:402
  224.0 4.1 %collective-permute-start.12 = (bf16[4,112,896]{2,1,0:T(8,128)(2,1)S(1)}, bf16[4,112,896]{2,1,0:T(8,128)(2,1)S(1)}, u32[]{:S(2)}, u32[]{:S(2)}) collective-permute-start(bf16[4,112,896]{2,1,0:T(8,128)(2,1)S(1)} %pad_maximum_fusion.own), channel_id=1, source_target_pairs={{0,8},{8,16},{16,24},{1,9},{9,17},{17,25},{2,10},{10,18},{18,26},{... | collective-permute-start | bytes 2408456 | tf_op jit(solution)/shard_map/ppermute | solution.py:402
  232.4 3.2 add.18
  235.6 8.9 %collective-permute-done.12.r1 = bf16[4,112,896]{2,1,0:T(8,128)(2,1)S(1)} collective-permute-done((bf16[4,112,896]{2,1,0:T(8,128)(2,1)S(1)}, bf16[4,112,896]{2,1,0:T(8,128)(2,1)S(1)}, u32[]{:S(2)}, u32[]{:S(2)}) %collective-permute-start.12) | collective-permute-done | bytes 802848 | tf_op jit(solution)/shard_map/ppermute | solution.py:402
  244.6 6.7 %collective-permute-done.13.l1 = bf16[4,112,896]{2,1,0:T(8,128)(2,1)S(1)} collective-permute-done((bf16[4,112,896]{2,1,0:T(8,128)(2,1)S(1)}, bf16[4,112,896]{2,1,0:T(8,128)(2,1)S(1)}, u32[]{:S(2)}, u32[]{:S(2)}) %collective-permute-start.13) | collective-permute-done | bytes 802848 | tf_op jit(solution)/shard_map/ppermute | solution.py:402
  251.3 2.6 collective-permute-done.11.end
  257.9 18.0 %collective-permute-done.16.l2 = bf16[4,112,896]{2,1,0:T(8,128)(2,1)S(1)} collective-permute-done((bf16[4,112,896]{2,1,0:T(8,128)(2,1)S(1)}, bf16[4,112,896]{2,1,0:T(8,128)(2,1)S(1)}, u32[]{:S(2)}, u32[]{:S(2)}) %collective-permute-start.16) | collective-permute-done | bytes 802848 | tf_op jit(solution)/shard_map/ppermute | solution.py:402
  277.9 3.4 slice.31
  281.3 13.7 %collective-permute-done.17.l3 = bf16[4,112,896]{2,1,0:T(8,128)(2,1)S(1)} collective-permute-done((bf16[4,112,896]{2,1,0:T(8,128)(2,1)S(1)}, bf16[4,112,896]{2,1,0:T(8,128)(2,1)S(1)}, u32[]{:S(2)}, u32[]{:S(2)}) %collective-permute-start.17) | collective-permute-done | bytes 802848 | tf_op jit(solution)/shard_map/ppermute | solution.py:402
  297.3 1.7 copy-done
  299.5 10.6 %shard_map.22 = bf16[896,448]{1,0:T(8,128)(2,1)} custom-call(s32[2]{0:T(128)} %pad_add_fusion.place, bf16[4,896,896]{2,1,0:T(8,128)(2,1)} %all-gather.4.cloned.1.call-done.panel, bf16[448,3584]{1,0:T(8,128)(2,1)} %copy-done), custom_call_target="tpu_custom_call" | custom-call | flops 2877292544 | bytes 8028160 | tf_op jit(solution)/shard_map/pallas_call | solution.py:239
  311.4 28.8 %collective-permute-done.19.refs_0_ = bf16[896,1024]{1,0:T(8,128)(2,1)} collective-permute-done((bf16[896,1024]{1,0:T(8,128)(2,1)}, bf16[896,1024]{1,0:T(8,128)(2,1)}, u32[]{:S(2)}, u32[]{:S(2)}) %collective-permute-start.19) | collective-permute-done | bytes 1835040 | tf_op jit(solution)/shard_map/ppermute | solution.py:402
  340.2 20.0 %all-gather.6.cloned.1.call-done = bf16[7168,448]{1,0:T(8,128)(2,1)} async-done(((bf16[896,448]{1,0:T(8,128)(2,1)}), bf16[7168,448]{1,0:T(8,128)(2,1)}) %all-gather.6.cloned.1.call-update) | async-done | bytes 6422544 | tf_op jit(solution)/shard_map/all_gather | solution.py:456
  360.2 17.4 %shard_map.24 = (bf16[896,2304]{1,0:T(8,128)(2,1)}, bf16[896,3584]{1,0:T(8,128)(2,1)}) custom-call(s32[2]{0:T(128)} %pad_add_fusion.place, bf16[8,896,448]{2,1,0:T(8,128)(2,1)} %bitcast.31, bf16[8,112,2304]{2,1,0:T(8,128)(2,1)} %bitcast.27, bf16[8,112,1536]{2,1,0:T(8,128)(2,1)} %bitcast.10.rest_0_, bf16[8,112,1536]{2,1,0:T(8,128)(2,1)} %bitcast.30, ...), custom_call_target="tpu_custom_call" | custom-call | tf_op jit(solution)/shard_map/pallas_call | solution.py:363
  377.6 10.5 %shard_map.25 = bf16[896,2304]{1,0:T(8,128)(2,1)} custom-call(s32[2]{0:T(128)} %pad_add_fusion.place, bf16[896,3584]{1,0:T(8,128)(2,1)} %get-tuple-element.49.f, bf16[8,112,2304]{2,1,0:T(8,128)(2,1)} %bitcast.28, bf16[8,112,768]{2,1,0:T(8,128)(2,1)} %bitcast.15.rest_0_, bf16[8,112,768]{2,1,0:T(8,128)(2,1)} %bitcast.16.rest_1_, ...), custom_call_target="tpu_custom_call", output_to_operand_aliasing={{}: (7, {})} | custom-call | flops 4932501504 | bytes 8257536 | tf_op jit(solution)/shard_map/pallas_call | solution.py:363
  (68 shorter events, 28.2 us)
Async XLA Ops:
  6.5 58.2 %reduce-scatter.3.cloned.1.call-start = ((), (), s32[]{:S(2)}) async-start(), calls=%async_computation.3 | async-start | bytes 1806336 | tf_op jit(solution)/shard_map/reduce_scatter | solution.py:405
  6.5 10.0 %copy-start.2 = (bf16[896,2304]{1,0:T(8,128)(2,1)S(1)}, bf16[896,2304]{1,0:T(8,128)(2,1)}, u32[]{:S(2)}) copy-start(bf16[896,2304]{1,0:T(8,128)(2,1)} %x.3) | copy-start | bytes 12386308
  10.2 65.3 %collective-permute-start = (bf16[896,1536]{1,0:T(8,128)(2,1)}, bf16[896,1536]{1,0:T(8,128)(2,1)S(1)}, u32[]{:S(2)}, u32[]{:S(2)}) collective-permute-start(bf16[896,1536]{1,0:T(8,128)(2,1)} %slice.24), channel_id=1, source_target_pairs={{0,8},{8,16},{16,24},{1,9},{9,17},{17,25},{2,10},{10,18},{18,26},{... | collective-permute-start | bytes 8257544 | tf_op jit(solution)/shard_map/ppermute | solution.py:402
  15.3 64.8 %collective-permute-start.1 = (bf16[896,1536]{1,0:T(8,128)(2,1)}, bf16[896,1536]{1,0:T(8,128)(2,1)}, u32[]{:S(2)}, u32[]{:S(2)}) collective-permute-start(bf16[896,1536]{1,0:T(8,128)(2,1)} %slice.24), channel_id=1, source_target_pairs={{24,16},{16,8},{8,0},{25,17},{17,9},{9,1},{26,18},{18,10},{10,2},{... | collective-permute-start | bytes 8257544 | tf_op jit(solution)/shard_map/ppermute | solution.py:402
  22.2 177.9 %reduce-scatter.5.cloned.1.call-start = ((), (), s32[]{:S(2)}) async-start(), calls=%async_computation.4 | async-start | bytes 7225344 | tf_op jit(solution)/shard_map/reduce_scatter | solution.py:405
  24.8 79.0 %collective-permute-start.2 = (bf16[896,768]{1,0:T(8,128)(2,1)}, bf16[896,768]{1,0:T(8,128)(2,1)}, u32[]{:S(2)}, u32[]{:S(2)}) collective-permute-start(bf16[896,768]{1,0:T(8,128)(2,1)} %slice.25), channel_id=1, source_target_pairs={{0,8},{8,16},{16,24},{1,9},{9,17},{17,25},{2,10},{10,18},{18,26},{... | collective-permute-start | bytes 4128776 | tf_op jit(solution)/shard_map/ppermute | solution.py:402
  30.5 79.1 %collective-permute-start.3 = (bf16[896,768]{1,0:T(8,128)(2,1)}, bf16[896,768]{1,0:T(8,128)(2,1)}, u32[]{:S(2)}, u32[]{:S(2)}) collective-permute-start(bf16[896,768]{1,0:T(8,128)(2,1)} %slice.25), channel_id=1, source_target_pairs={{24,16},{16,8},{8,0},{25,17},{17,9},{9,1},{26,18},{18,10},{10,2},{... | collective-permute-start | bytes 4128776 | tf_op jit(solution)/shard_map/ppermute | solution.py:402
  75.5 6.1 %copy-start.4 = (bf16[896,1536]{1,0:T(8,128)(2,1)}, bf16[896,1536]{1,0:T(8,128)(2,1)S(1)}, u32[]{:S(2)}) copy-start(bf16[896,1536]{1,0:T(8,128)(2,1)S(1)} %collective-permute-done.r1.rest_2_) | copy-start | bytes 8257540
  80.1 88.5 %collective-permute-start.4 = (bf16[896,1536]{1,0:T(8,128)(2,1)}, bf16[896,1536]{1,0:T(8,128)(2,1)}, u32[]{:S(2)}, u32[]{:S(2)}) collective-permute-start(bf16[896,1536]{1,0:T(8,128)(2,1)} %collective-permute-done.1.l1.rest_0_), channel_id=1, source_target_pairs={{16,8},{8,0},{17,9},{9,1},{18,10},{10,2},{19,11},{11,3},{20,12},{1... | collective-permute-start | bytes 8257544 | tf_op jit(solution)/shard_map/ppermute | solution.py:402
  101.3 67.3 %collective-permute-start.5 = (bf16[896,1536]{1,0:T(8,128)(2,1)}, bf16[896,1536]{1,0:T(8,128)(2,1)}, u32[]{:S(2)}, u32[]{:S(2)}) collective-permute-start(bf16[896,1536]{1,0:T(8,128)(2,1)} %copy-done.4), channel_id=1, source_target_pairs={{8,16},{16,24},{9,17},{17,25},{10,18},{18,26},{11,19},{19,27},{12,... | collective-permute-start | bytes 8257544 | tf_op jit(solution)/shard_map/ppermute | solution.py:402
  109.6 86.9 %collective-permute-start.6 = (bf16[896,768]{1,0:T(8,128)(2,1)}, bf16[896,768]{1,0:T(8,128)(2,1)S(1)}, u32[]{:S(2)}, u32[]{:S(2)}) collective-permute-start(bf16[896,768]{1,0:T(8,128)(2,1)} %get-tuple-element.34.rest_1_.l1), channel_id=1, source_target_pairs={{16,8},{8,0},{17,9},{9,1},{18,10},{10,2},{19,11},{11,3},{20,12},{1... | collective-permute-start | bytes 4128776 | tf_op jit(solution)/shard_map/ppermute | solution.py:402
  110.9 85.6 %collective-permute-start.7 = (bf16[896,768]{1,0:T(8,128)(2,1)}, bf16[896,768]{1,0:T(8,128)(2,1)S(1)}, u32[]{:S(2)}, u32[]{:S(2)}) collective-permute-start(bf16[896,768]{1,0:T(8,128)(2,1)} %get-tuple-element.35.rest_3_.r1), channel_id=1, source_target_pairs={{8,16},{16,24},{9,17},{17,25},{10,18},{18,26},{11,19},{19,27},{12,... | collective-permute-start | bytes 4128776 | tf_op jit(solution)/shard_map/ppermute | solution.py:402
  196.5 27.4 %collective-permute-start.10 = (bf16[896,512]{1,0:T(8,128)(2,1)}, bf16[896,512]{1,0:T(8,128)(2,1)}, u32[]{:S(2)}, u32[]{:S(2)}) collective-permute-start(bf16[896,512]{1,0:T(8,128)(2,1)} %slice.32), channel_id=1, source_target_pairs={{8,0},{16,24},{9,1},{17,25},{10,2},{18,26},{11,3},{19,27},{12,4},{... | collective-permute-start | bytes 2752520 | tf_op jit(solution)/shard_map/ppermute | solution.py:402
  200.0 23.9 %copy-start.7 = (bf16[1,112,896]{2,1,0:T(8,128)(2,1)S(1)}, bf16[1,112,896]{2,1,0:T(8,128)(2,1)}, u32[]{:S(2)}) copy-start(bf16[1,112,896]{2,1,0:T(8,128)(2,1)} %reduce-scatter.3.cloned.1.call-done) | copy-start | bytes 602116
  200.1 4.5 %copy-start.9 = (bf16[4,112,896]{2,1,0:T(8,128)(2,1)S(1)}, bf16[4,112,896]{2,1,0:T(8,128)(2,1)}, u32[]{:S(2)}) copy-start(bf16[4,112,896]{2,1,0:T(8,128)(2,1)} %reduce-scatter.5.cloned.1.call-done) | copy-start | bytes 2408452
  200.1 29.4 %all-to-all-start = ((bf16[8,112,896]{2,1,0:T(8,128)(2,1)}), bf16[8,112,896]{2,1,0:T(8,128)(2,1)}, u32[]{:S(2)}, u32[]{:S(2)}) async-start(bf16[8,112,896]{2,1,0:T(8,128)(2,1)} %bitcast.34), calls=%async_computation.2 | async-start | bytes 3211264 | tf_op jit(solution)/shard_map/all_to_all | solution.py:433
  204.5 95.0 %all-gather.4.cloned.1.call-start = ((), (), s32[]{:S(2)}) async-start(), calls=%async_computation.5 | async-start | bytes 7225344 | tf_op jit(solution)/shard_map/all_gather | solution.py:447
  204.6 19.2 %collective-permute-start.8 = (bf16[112,896]{1,0:T(8,128)(2,1)S(1)}, bf16[112,896]{1,0:T(8,128)(2,1)S(1)}, u32[]{:S(2)}, u32[]{:S(2)}) collective-permute-start(bf16[112,896]{1,0:T(8,128)(2,1)S(1)} %get-tuple-element.56), channel_id=1, source_target_pairs={{16,8},{8,0},{17,9},{9,1},{18,10},{10,2},{19,11},{11,3},{20,12},{1... | collective-permute-start | bytes 602120 | tf_op jit(solution)/shard_map/ppermute | solution.py:402
  205.9 17.9 %collective-permute-start.9 = (bf16[112,896]{1,0:T(8,128)(2,1)S(1)}, bf16[112,896]{1,0:T(8,128)(2,1)S(1)}, u32[]{:S(2)}, u32[]{:S(2)}) collective-permute-start(bf16[112,896]{1,0:T(8,128)(2,1)S(1)} %get-tuple-element.55), channel_id=1, source_target_pairs={{8,16},{16,24},{9,17},{17,25},{10,18},{18,26},{11,19},{19,27},{12,... | collective-permute-start | bytes 602120 | tf_op jit(solution)/shard_map/ppermute | solution.py:402
  224.0 20.6 %collective-permute-start.12 = (bf16[4,112,896]{2,1,0:T(8,128)(2,1)S(1)}, bf16[4,112,896]{2,1,0:T(8,128)(2,1)S(1)}, u32[]{:S(2)}, u32[]{:S(2)}) collective-permute-start(bf16[4,112,896]{2,1,0:T(8,128)(2,1)S(1)} %pad_maximum_fusion.own), channel_id=1, source_target_pairs={{0,8},{8,16},{16,24},{1,9},{9,17},{17,25},{2,10},{10,18},{18,26},{... | collective-permute-start | bytes 2408456 | tf_op jit(solution)/shard_map/ppermute | solution.py:402
  228.1 23.1 %collective-permute-start.13 = (bf16[4,112,896]{2,1,0:T(8,128)(2,1)S(1)}, bf16[4,112,896]{2,1,0:T(8,128)(2,1)S(1)}, u32[]{:S(2)}, u32[]{:S(2)}) collective-permute-start(bf16[4,112,896]{2,1,0:T(8,128)(2,1)S(1)} %pad_maximum_fusion.own), channel_id=1, source_target_pairs={{24,16},{16,8},{8,0},{25,17},{17,9},{9,1},{26,18},{18,10},{10,2},{... | collective-permute-start | bytes 2408456 | tf_op jit(solution)/shard_map/ppermute | solution.py:402
  231.1 22.7 %collective-permute-start.11 = (bf16[1,112,896]{2,1,0:T(8,128)(2,1)S(1)}, bf16[1,112,896]{2,1,0:T(8,128)(2,1)S(1)}, u32[]{:S(2)}, u32[]{:S(2)}) collective-permute-start(bf16[1,112,896]{2,1,0:T(8,128)(2,1)S(1)} %bitcast.24), channel_id=1, source_target_pairs={{8,0},{16,24},{9,1},{17,25},{10,2},{18,26},{11,3},{19,27},{12,4},{... | collective-permute-start | bytes 602120 | tf_op jit(solution)/shard_map/ppermute | solution.py:402
  232.4 21.5 %copy-start.8 = (bf16[1,112,896]{2,1,0:T(8,128)(2,1)S(1)}, bf16[1,112,896]{2,1,0:T(8,128)(2,1)}, u32[]{:S(2)}) copy-start(bf16[1,112,896]{2,1,0:T(8,128)(2,1)} %reduce-scatter.3.cloned.1.call-done) | copy-start | bytes 602116
  255.0 41.3 %copy-start.1 = (s32[2]{0:T(128)S(1)}, s32[2]{0:T(128)}, u32[]{:S(2)}) copy-start(s32[2]{0:T(128)} %pad_add_fusion.place) | copy-start | bytes 28
  255.1 105.1 %all-gather.6.cloned.1.call-start = ((), (), s32[]{:S(2)}) async-start(), calls=%async_computation.6 | async-start | bytes 8257536 | tf_op jit(solution)/shard_map/all_gather | solution.py:456
  255.1 2.0 collective-permute-start.14
  255.8 20.1 %collective-permute-start.16 = (bf16[4,112,896]{2,1,0:T(8,128)(2,1)S(1)}, bf16[4,112,896]{2,1,0:T(8,128)(2,1)S(1)}, u32[]{:S(2)}, u32[]{:S(2)}) collective-permute-start(bf16[4,112,896]{2,1,0:T(8,128)(2,1)S(1)} %collective-permute-done.13.l1), channel_id=1, source_target_pairs={{16,8},{8,0},{17,9},{9,1},{18,10},{10,2},{19,11},{11,3},{20,12},{1... | collective-permute-start | bytes 2408456 | tf_op jit(solution)/shard_map/ppermute | solution.py:402
  257.2 24.2 %collective-permute-start.15 = (bf16[4,112,896]{2,1,0:T(8,128)(2,1)S(1)}, bf16[4,112,896]{2,1,0:T(8,128)(2,1)S(1)}, u32[]{:S(2)}, u32[]{:S(2)}) collective-permute-start(bf16[4,112,896]{2,1,0:T(8,128)(2,1)S(1)} %collective-permute-done.14.r2), channel_id=1, source_target_pairs={{16,24},{17,25},{18,26},{19,27},{20,28},{21,29},{22,30},{23,31}} | collective-permute-start | bytes 2408456 | tf_op jit(solution)/shard_map/ppermute | solution.py:402
  275.9 19.1 %collective-permute-start.17 = (bf16[4,112,896]{2,1,0:T(8,128)(2,1)S(1)}, bf16[4,112,896]{2,1,0:T(8,128)(2,1)S(1)}, u32[]{:S(2)}, u32[]{:S(2)}) collective-permute-start(bf16[4,112,896]{2,1,0:T(8,128)(2,1)S(1)} %collective-permute-done.16.l2), channel_id=1, source_target_pairs={{8,0},{9,1},{10,2},{11,3},{12,4},{13,5},{14,6},{15,7}} | collective-permute-start | bytes 2408456 | tf_op jit(solution)/shard_map/ppermute | solution.py:402
  277.2 4.1 %collective-permute-start.18 = (bf16[1,112,896]{2,1,0:T(8,128)(2,1)S(1)}, bf16[1,112,896]{2,1,0:T(8,128)(2,1)S(1)}, u32[]{:S(2)}, u32[]{:S(2)}) collective-permute-start(bf16[1,112,896]{2,1,0:T(8,128)(2,1)S(1)} %bitcast.25), channel_id=1, source_target_pairs={{8,16},{16,8},{9,17},{17,9},{10,18},{18,10},{11,19},{19,11},{12,20... | collective-permute-start | bytes 602120 | tf_op jit(solution)/shard_map/ppermute | solution.py:402
  295.1 45.1 %collective-permute-start.19 = (bf16[896,1024]{1,0:T(8,128)(2,1)}, bf16[896,1024]{1,0:T(8,128)(2,1)}, u32[]{:S(2)}, u32[]{:S(2)}) collective-permute-start(bf16[896,1024]{1,0:T(8,128)(2,1)} %slice.31), channel_id=1, source_target_pairs={{8,0},{16,24},{9,1},{17,25},{10,2},{18,26},{11,3},{19,27},{12,4},{... | collective-permute-start | bytes 5505032 | tf_op jit(solution)/shard_map/ppermute | solution.py:402
  310.1 67.5 %collective-permute-start.20 = (bf16[896,768]{1,0:T(8,128)(2,1)}, bf16[896,768]{1,0:T(8,128)(2,1)}, u32[]{:S(2)}, u32[]{:S(2)}) collective-permute-start(bf16[896,768]{1,0:T(8,128)(2,1)} %add.18), channel_id=1, source_target_pairs={{8,0},{16,24},{9,1},{17,25},{10,2},{18,26},{11,3},{19,27},{12,4},{... | collective-permute-start | bytes 4128776 | tf_op jit(solution)/shard_map/ppermute | solution.py:402
  (4 other events, 6.1 us)
Sparse Core Ops, SparseCore 0:
  22.3 42.4 reduce-scatter.2
  127.7 65.4 reduce-scatter.4
  255.2 44.2 all-gather.3
  310.2 49.9 all-gather.5

commit v16 on v15

--- a/solution.py
+++ b/solution.py
@@ -165,6 +165,9 @@
             flops=128 * rows * rows * depth, bytes_accessed=8 * rows * depth, transcendentals=0
         ),
     )(place, *l1, *r1, *l2, *r2)
+
+
+block_order = (1, 3, 0, 2)
 
 
 def strips_kernel(place, own, l1, r3, l2, r2, r1, l3, corner, pair, end, out):
@@ -187,7 +190,7 @@
                 value = value + jnp.where((z + e) % 4 == 0, low, zero)
             if block == 1:
                 value = value + jnp.where((z + e) % 4 == 3, high, zero)
-            place_of = (block + e) % 4 * rows
+            place_of = block_order.index((block + e) % 4) * rows
             out[e * part : (e + 1) * part, place_of : place_of + rows] = value
 
 
@@ -208,14 +211,17 @@
 def square_kernel(place, panel, right, out, held, strip, sems):
     z = place[0]
     rows, part = panel.shape[1], right.shape[0] // 4
-    copies = [pltpu.make_async_copy(right, strip, sems.at[4])]
-    for d in range(4):
-        columns = held.at[:, d * rows : (d + 1) * rows]
-        copies.append(pltpu.make_async_copy(panel.at[d], columns, sems.at[d]))
-    for copy in copies:
-        copy.start()
-    for copy in copies:
-        copy.wait()
+    half = 2 * rows
+    loads = [pltpu.make_async_copy(right, strip, sems.at[4])]
+    for i, d in enumerate(block_order):
+        columns = held.at[:, i * rows : (i + 1) * rows]
+        loads.append(pltpu.make_async_copy(panel.at[d], columns, sems.at[d]))
+    for load in loads:
+        load.start()
+    for load in loads[:3]:
+        load.wait()
+    total = dot_rows(held[:, :half], strip[:, :half])
+    own = slice(half, half + rows)
     for plane, block, e in ((0, 3, 3), (3, 1, 1)):
 
         @pl.when(z == plane)
@@ -223,14 +229,17 @@
             index = lax.broadcasted_iota(jnp.int32, (part, rows), 0) + place[1] * part
             other = lax.broadcasted_iota(jnp.int32, (part, rows), 1)
             pick = jnp.where(index == other, 1.0, 0.0).astype(jnp.bfloat16)
-            far = dot_rows(pick, held[:, block * rows : (block + 1) * rows]).astype(strip.dtype)
-            strip[e * part : (e + 1) * part, :rows] += far
-
-    total = dot_rows(held[...], strip[...])
+            at = block_order.index(block) * rows
+            far = dot_rows(pick, held[:, at : at + rows]).astype(strip.dtype)
+            strip[e * part : (e + 1) * part, own] += far
+
+    for load in loads[3:]:
+        load.wait()
+    total = total + dot_rows(held[:, half:], strip[:, half:])
     index = lax.broadcasted_iota(jnp.int32, (rows, rows), 0)
     other = lax.broadcasted_iota(jnp.int32, (rows, rows), 1)
     unit = jnp.where(index == other, 1.0, 0.0).astype(jnp.bfloat16)
-    out[...] = (coef_b * dot_rows(unit, strip[:, :rows]) + coef_c * total).astype(out.dtype)
+    out[...] = (coef_b * dot_rows(unit, strip[:, own]) + coef_c * total).astype(out.dtype)
 
 
 def square(place, panel, right):
@@ -292,38 +301,57 @@
     slot = lax.rem(step, 2)
     if ready:
         f_sems = rest[-1]
-        loads = [pltpu.make_async_copy(f, whole_f, f_sems.at[0])]
+        pair = 2 * depth
+        parts = [slice(q * pair, (q + 1) * pair) for q in range(n_col // 2)]
+        loads = [
+            pltpu.make_async_copy(f.at[:, part_of], whole_f.at[:, part_of], f_sems.at[q])
+            for q, part_of in enumerate(parts)
+        ]
     else:
         held_f, f_sems = rest[2], rest[-1]
         loads = [pltpu.make_async_copy(f.at[c], held_f.at[c], f_sems.at[c]) for c in range(n_col)]
         save = pltpu.make_async_copy(whole_f, rest[1], f_sems.at[n_col])
 
+    def arrive():
+        for d in range(4):
+            copy(x, 0, slot, d).wait()
+
+    def finish(total):
+        own = wide[slot, :, :part, :].reshape(rows, width).astype(jnp.float32)
+        out[...] = (math.sqrt(N) * (coef_a * own + total)).astype(out.dtype)
+
     @pl.when(step == 0)
     def _():
-        for one in loads:
-            one.start()
         fetch(0, 0)
-        if ready:
-            loads[0].wait()
-        else:
-            for c in range(n_col):
-                loads[c].wait()
-                whole_f[:, c * depth : (c + 1) * depth] = held_f[c]
+        for load in loads:
+            load.start()
+        if n_tile > 1:
+            fetch(1, 1)
+        arrive()
+        total = jnp.zeros((rows, width), jnp.float32)
+        for i, load in enumerate(loads):
+            load.wait()
+            if ready:
+                left = whole_f[:, parts[i]]
+                right = wide[0, 2 * i : 2 * i + 2].reshape(pair, width)
+            else:
+                left, right = held_f[i], wide[0, i]
+                whole_f[:, i * depth : (i + 1) * depth] = left
+            total = total + jnp.dot(left, right, preferred_element_type=jnp.float32)
+        if not ready:
             save.start()
-
-    @pl.when(step + 1 < n_tile)
+        finish(total)
+
+    @pl.when(step > 0)
     def _():
-        fetch(step + 1, 1 - slot)
-
-    for d in range(4):
-        copy(x, 0, slot, d).wait()
-    total = jnp.dot(
-        whole_f[...],
-        wide[slot].reshape(n_col * depth, width),
-        preferred_element_type=jnp.float32,
-    )
-    own = wide[slot, :, :part, :].reshape(rows, width).astype(jnp.float32)
-    out[...] = (math.sqrt(N) * (coef_a * own + total)).astype(out.dtype)
+        @pl.when(step + 1 < n_tile)
+        def _():
+            fetch(step + 1, 1 - slot)
+
+        arrive()
+        right = wide[slot].reshape(n_col * depth, width)
+        finish(jnp.dot(whole_f[...], right, preferred_element_type=jnp.float32))
+
     if not ready:
 
         @pl.when(step == n_tile - 1)

time: 396 us -> 400 us (1.010)
  transfers between devices with their start and end apart: 26 -> 26, of which waited for: 16 -> 15; matrix products, arithmetic and copies ran while one was open for 5% -> 5% of each run, Pallas kernels for 17% -> 17%
where the time goes in v16:
time: 400 us; the launch traced here: 397 us
  waiting for transfers between devices  234 us (58%)
  Pallas kernels  77.4 us (19%)
  starting transfers between devices  41.7 us (10%)
  local copies, waits for them, and re-layouts  14.3 us (4%)
  between operations  13.8 us (3%)
  other arithmetic  10.2 us (3%)
  matrix products  5.56 us (1%)
    ppermute x21, waiting for transfers between devices, send(): return lax.ppermute(value, 'row', pairs)  180 us
    ppermute x21, starting transfers between devices, send(): return lax.ppermute(value, 'row', pairs)  37.1 us
    pallas_call x2, Pallas kernels, near_call(): pl.pallas_call(kernel, out_shape=jax.ShapeDtypeStruct(shape, dtype), in_s...  34.8 us
    reduce_scatter x2, waiting for transfers between devices, scatter(): return lax.psum_scatter(blocks, 'col', scatter_dimension=1, tiled=True)  33.1 us
    pallas_call x2, Pallas kernels, product(): pl.pallas_call(functools.partial(product_kernel, tuple(marks), ready), gr...  29.7 us
    all_gather x1, waiting for transfers between devices, per_device_line(): factor = lax.all_gather(factor, 'col', axis=0, tiled=False)  20 us
    pallas_call x1, Pallas kernels, square(): pl.pallas_call(square_kernel, out_shape=jax.ShapeDtypeStruct((rows, depth...  9.96 us
  transfers between devices with their start and end apart: 26, of which 15 were waited for; matrix products, arithmetic and copies ran while one was open for 5% of the time, Pallas kernels for 17%

profile of v16, /device:TPU:0, one launch (start us, length us, event | category | flops | bytes accessed | tf_op | source)
XLA Modules:
  0.0 396.7 jit_solution(6296700630164398750)
XLA Ops:
  6.5 3.6 slice.24
  10.2 5.1 %collective-permute-start = (bf16[896,1536]{1,0:T(8,128)(2,1)}, bf16[896,1536]{1,0:T(8,128)(2,1)S(1)}, u32[]{:S(2)}, u32[]{:S(2)}) collective-permute-start(bf16[896,1536]{1,0:T(8,128)(2,1)} %slice.24), channel_id=1, source_target_pairs={{0,8},{8,16},{16,24},{1,9},{9,17},{17,25},{2,10},{10,18},{18,26},{... | collective-permute-start | bytes 8257544 | tf_op jit(solution)/shard_map/ppermute | solution.py:430
  16.6 5.6 %fusion = bf16[1,896,896]{2,1,0:T(8,128)(2,1)} fusion(bf16[896,2304]{1,0:T(8,128)(2,1)S(1)} %copy-done.2), kind=kOutput, calls=%fused_computation.1 | convolution fusion | flops 3700178944 | bytes 5734400 | tf_op jit(solution)/shard_map/dot_general | solution.py:20
  22.2 2.6 slice.25
  24.8 5.6 %collective-permute-start.2 = (bf16[896,768]{1,0:T(8,128)(2,1)}, bf16[896,768]{1,0:T(8,128)(2,1)}, u32[]{:S(2)}, u32[]{:S(2)}) collective-permute-start(bf16[896,768]{1,0:T(8,128)(2,1)} %slice.25), channel_id=1, source_target_pairs={{0,8},{8,16},{16,24},{1,9},{9,17},{17,25},{2,10},{10,18},{18,26},{... | collective-permute-start | bytes 4128776 | tf_op jit(solution)/shard_map/ppermute | solution.py:430
  31.7 33.0 %reduce-scatter.3.cloned.1.call-done = bf16[1,112,896]{2,1,0:T(8,128)(2,1)} async-done(((bf16[1,896,896]{2,1,0:T(8,128)(2,1)}), bf16[1,112,896]{2,1,0:T(8,128)(2,1)}) %reduce-scatter.3.cloned.1.call-update) | async-done | bytes 200720 | tf_op jit(solution)/shard_map/reduce_scatter | solution.py:433
  64.8 10.7 %collective-permute-done.r1.rest_2_ = bf16[896,1536]{1,0:T(8,128)(2,1)S(1)} collective-permute-done((bf16[896,1536]{1,0:T(8,128)(2,1)}, bf16[896,1536]{1,0:T(8,128)(2,1)S(1)}, u32[]{:S(2)}, u32[]{:S(2)}) %collective-permute-start) | collective-permute-done | bytes 2752544 | tf_op jit(solution)/shard_map/ppermute | solution.py:430
  75.5 4.6 %collective-permute-done.1.l1.rest_0_ = bf16[896,1536]{1,0:T(8,128)(2,1)} collective-permute-done((bf16[896,1536]{1,0:T(8,128)(2,1)}, bf16[896,1536]{1,0:T(8,128)(2,1)}, u32[]{:S(2)}, u32[]{:S(2)}) %collective-permute-start.1) | collective-permute-done | bytes 2752544 | tf_op jit(solution)/shard_map/ppermute | solution.py:430
  80.1 1.8 collective-permute-start.4
  81.9 19.7 %shard_map.17.part = f32[2,1792,896]{2,1,0:T(8,128)} custom-call(bf16[896,2304]{1,0:T(8,128)(2,1)} %x.3, bf16[896,1536]{1,0:T(8,128)(2,1)} %collective-permute-done.1.l1.rest_0_, bf16[896,1536]{1,0:T(8,128)(2,1)} %copy-done.4), custom_call_target="tpu_custom_call" | custom-call | tf_op jit(solution)/shard_map/pallas_call | solution.py:105
  101.6 2.2 collective-permute-start.5
  103.8 5.8 %collective-permute-done.3.refs_1_ = bf16[896,768]{1,0:T(8,128)(2,1)} collective-permute-done((bf16[896,768]{1,0:T(8,128)(2,1)}, bf16[896,768]{1,0:T(8,128)(2,1)}, u32[]{:S(2)}, u32[]{:S(2)}) %collective-permute-start.3) | collective-permute-done | bytes 1376288 | tf_op jit(solution)/shard_map/ppermute | solution.py:430
  112.5 15.0 %shard_map.20 = bf16[4,896,896]{2,1,0:T(8,128)(2,1)} custom-call(bf16[896,2304]{1,0:T(8,128)(2,1)} %x.3, bf16[896,768]{1,0:T(8,128)(2,1)} %get-tuple-element.34.rest_1_.l1, bf16[896,768]{1,0:T(8,128)(2,1)} %get-tuple-element.35.rest_3_.r1, f32[2,1792,896]{2,1,0:T(8,128)} %shard_map.17.part), custom_call_target="tpu_custom_call" | custom-call | flops 4932501504 | bytes 4128768 | tf_op jit(solution)/shard_map/pallas_call | solution.py:105
  127.5 41.0 %collective-permute-done.4.rest_4_ = bf16[896,1536]{1,0:T(8,128)(2,1)} collective-permute-done((bf16[896,1536]{1,0:T(8,128)(2,1)}, bf16[896,1536]{1,0:T(8,128)(2,1)}, u32[]{:S(2)}, u32[]{:S(2)}) %collective-permute-start.4) | collective-permute-done | bytes 2752544 | tf_op jit(solution)/shard_map/ppermute | solution.py:430
  168.6 3.3 add.16
  174.5 22.0 %collective-permute-done.6.rest_5_ = bf16[896,768]{1,0:T(8,128)(2,1)S(1)} collective-permute-done((bf16[896,768]{1,0:T(8,128)(2,1)}, bf16[896,768]{1,0:T(8,128)(2,1)S(1)}, u32[]{:S(2)}, u32[]{:S(2)}) %collective-permute-start.6) | collective-permute-done | bytes 1376288 | tf_op jit(solution)/shard_map/ppermute | solution.py:430
  198.0 2.0 shard_map.19
  200.1 4.4 %all-to-all-start = ((bf16[8,112,896]{2,1,0:T(8,128)(2,1)}), bf16[8,112,896]{2,1,0:T(8,128)(2,1)}, u32[]{:S(2)}, u32[]{:S(2)}) async-start(bf16[8,112,896]{2,1,0:T(8,128)(2,1)} %bitcast.34), calls=%async_computation.2 | async-start | bytes 3211264 | tf_op jit(solution)/shard_map/all_to_all | solution.py:461
  206.8 17.0 %collective-permute-done.8 = bf16[112,896]{1,0:T(8,128)(2,1)S(1)} collective-permute-done((bf16[112,896]{1,0:T(8,128)(2,1)S(1)}, bf16[112,896]{1,0:T(8,128)(2,1)S(1)}, u32[]{:S(2)}, u32[]{:S(2)}) %collective-permute-start.8) | collective-permute-done | bytes 200736 | tf_op jit(solution)/shard_map/ppermute | solution.py:430
  224.0 4.1 %collective-permute-start.12 = (bf16[4,112,896]{2,1,0:T(8,128)(2,1)S(1)}, bf16[4,112,896]{2,1,0:T(8,128)(2,1)S(1)}, u32[]{:S(2)}, u32[]{:S(2)}) collective-permute-start(bf16[4,112,896]{2,1,0:T(8,128)(2,1)S(1)} %pad_maximum_fusion.own), channel_id=1, source_target_pairs={{0,8},{8,16},{16,24},{1,9},{9,17},{17,25},{2,10},{10,18},{18,26},{... | collective-permute-start | bytes 2408456 | tf_op jit(solution)/shard_map/ppermute | solution.py:430
  232.4 3.2 add.18
  235.6 8.9 %collective-permute-done.12.r1 = bf16[4,112,896]{2,1,0:T(8,128)(2,1)S(1)} collective-permute-done((bf16[4,112,896]{2,1,0:T(8,128)(2,1)S(1)}, bf16[4,112,896]{2,1,0:T(8,128)(2,1)S(1)}, u32[]{:S(2)}, u32[]{:S(2)}) %collective-permute-start.12) | collective-permute-done | bytes 802848 | tf_op jit(solution)/shard_map/ppermute | solution.py:430
  244.6 6.7 %collective-permute-done.13.l1 = bf16[4,112,896]{2,1,0:T(8,128)(2,1)S(1)} collective-permute-done((bf16[4,112,896]{2,1,0:T(8,128)(2,1)S(1)}, bf16[4,112,896]{2,1,0:T(8,128)(2,1)S(1)}, u32[]{:S(2)}, u32[]{:S(2)}) %collective-permute-start.13) | collective-permute-done | bytes 802848 | tf_op jit(solution)/shard_map/ppermute | solution.py:430
  251.3 2.6 collective-permute-done.11.end
  257.9 18.0 %collective-permute-done.16.l2 = bf16[4,112,896]{2,1,0:T(8,128)(2,1)S(1)} collective-permute-done((bf16[4,112,896]{2,1,0:T(8,128)(2,1)S(1)}, bf16[4,112,896]{2,1,0:T(8,128)(2,1)S(1)}, u32[]{:S(2)}, u32[]{:S(2)}) %collective-permute-start.16) | collective-permute-done | bytes 802848 | tf_op jit(solution)/shard_map/ppermute | solution.py:430
  277.9 3.4 slice.31
  281.3 13.7 %collective-permute-done.17.l3 = bf16[4,112,896]{2,1,0:T(8,128)(2,1)S(1)} collective-permute-done((bf16[4,112,896]{2,1,0:T(8,128)(2,1)S(1)}, bf16[4,112,896]{2,1,0:T(8,128)(2,1)S(1)}, u32[]{:S(2)}, u32[]{:S(2)}) %collective-permute-start.17) | collective-permute-done | bytes 802848 | tf_op jit(solution)/shard_map/ppermute | solution.py:430
  299.5 10.0 %shard_map.22 = bf16[896,448]{1,0:T(8,128)(2,1)} custom-call(s32[2]{0:T(128)} %pad_add_fusion.place, bf16[4,896,896]{2,1,0:T(8,128)(2,1)} %all-gather.4.cloned.1.call-done.panel, bf16[448,3584]{1,0:T(8,128)(2,1)} %copy-done), custom_call_target="tpu_custom_call" | custom-call | flops 2877292544 | bytes 8028160 | tf_op jit(solution)/shard_map/pallas_call | solution.py:248
  311.0 29.2 %collective-permute-done.19.refs_0_ = bf16[896,1024]{1,0:T(8,128)(2,1)} collective-permute-done((bf16[896,1024]{1,0:T(8,128)(2,1)}, bf16[896,1024]{1,0:T(8,128)(2,1)}, u32[]{:S(2)}, u32[]{:S(2)}) %collective-permute-start.19) | collective-permute-done | bytes 1835040 | tf_op jit(solution)/shard_map/ppermute | solution.py:430
  340.2 20.0 %all-gather.6.cloned.1.call-done = bf16[7168,448]{1,0:T(8,128)(2,1)} async-done(((bf16[896,448]{1,0:T(8,128)(2,1)}), bf16[7168,448]{1,0:T(8,128)(2,1)}) %all-gather.6.cloned.1.call-update) | async-done | bytes 6422544 | tf_op jit(solution)/shard_map/all_gather | solution.py:484
  360.2 18.1 %shard_map.24 = (bf16[896,2304]{1,0:T(8,128)(2,1)}, bf16[896,3584]{1,0:T(8,128)(2,1)}) custom-call(s32[2]{0:T(128)} %pad_add_fusion.place, bf16[8,896,448]{2,1,0:T(8,128)(2,1)} %bitcast.31, bf16[8,112,2304]{2,1,0:T(8,128)(2,1)} %bitcast.27, bf16[8,112,1536]{2,1,0:T(8,128)(2,1)} %bitcast.10.rest_0_, bf16[8,112,1536]{2,1,0:T(8,128)(2,1)} %bitcast.30, ...), custom_call_target="tpu_custom_call" | custom-call | tf_op jit(solution)/shard_map/pallas_call | solution.py:391
  378.3 11.6 %shard_map.25 = bf16[896,2304]{1,0:T(8,128)(2,1)} custom-call(s32[2]{0:T(128)} %pad_add_fusion.place, bf16[896,3584]{1,0:T(8,128)(2,1)} %get-tuple-element.49.f, bf16[8,112,2304]{2,1,0:T(8,128)(2,1)} %bitcast.28, bf16[8,112,768]{2,1,0:T(8,128)(2,1)} %bitcast.15.rest_0_, bf16[8,112,768]{2,1,0:T(8,128)(2,1)} %bitcast.16.rest_1_, ...), custom_call_target="tpu_custom_call", output_to_operand_aliasing={{}: (7, {})} | custom-call | flops 4932501504 | bytes 8257536 | tf_op jit(solution)/shard_map/pallas_call | solution.py:391
  (68 shorter events, 28.3 us)
Async XLA Ops:
  6.5 58.3 %reduce-scatter.3.cloned.1.call-start = ((), (), s32[]{:S(2)}) async-start(), calls=%async_computation.3 | async-start | bytes 1806336 | tf_op jit(solution)/shard_map/reduce_scatter | solution.py:433
  6.5 10.0 %copy-start.2 = (bf16[896,2304]{1,0:T(8,128)(2,1)S(1)}, bf16[896,2304]{1,0:T(8,128)(2,1)}, u32[]{:S(2)}) copy-start(bf16[896,2304]{1,0:T(8,128)(2,1)} %x.3) | copy-start | bytes 12386308
  10.2 65.3 %collective-permute-start = (bf16[896,1536]{1,0:T(8,128)(2,1)}, bf16[896,1536]{1,0:T(8,128)(2,1)S(1)}, u32[]{:S(2)}, u32[]{:S(2)}) collective-permute-start(bf16[896,1536]{1,0:T(8,128)(2,1)} %slice.24), channel_id=1, source_target_pairs={{0,8},{8,16},{16,24},{1,9},{9,17},{17,25},{2,10},{10,18},{18,26},{... | collective-permute-start | bytes 8257544 | tf_op jit(solution)/shard_map/ppermute | solution.py:430
  15.3 64.8 %collective-permute-start.1 = (bf16[896,1536]{1,0:T(8,128)(2,1)}, bf16[896,1536]{1,0:T(8,128)(2,1)}, u32[]{:S(2)}, u32[]{:S(2)}) collective-permute-start(bf16[896,1536]{1,0:T(8,128)(2,1)} %slice.24), channel_id=1, source_target_pairs={{24,16},{16,8},{8,0},{25,17},{17,9},{9,1},{26,18},{18,10},{10,2},{... | collective-permute-start | bytes 8257544 | tf_op jit(solution)/shard_map/ppermute | solution.py:430
  22.2 177.9 %reduce-scatter.5.cloned.1.call-start = ((), (), s32[]{:S(2)}) async-start(), calls=%async_computation.4 | async-start | bytes 7225344 | tf_op jit(solution)/shard_map/reduce_scatter | solution.py:433
  24.8 79.0 %collective-permute-start.2 = (bf16[896,768]{1,0:T(8,128)(2,1)}, bf16[896,768]{1,0:T(8,128)(2,1)}, u32[]{:S(2)}, u32[]{:S(2)}) collective-permute-start(bf16[896,768]{1,0:T(8,128)(2,1)} %slice.25), channel_id=1, source_target_pairs={{0,8},{8,16},{16,24},{1,9},{9,17},{17,25},{2,10},{10,18},{18,26},{... | collective-permute-start | bytes 4128776 | tf_op jit(solution)/shard_map/ppermute | solution.py:430
  30.5 79.1 %collective-permute-start.3 = (bf16[896,768]{1,0:T(8,128)(2,1)}, bf16[896,768]{1,0:T(8,128)(2,1)}, u32[]{:S(2)}, u32[]{:S(2)}) collective-permute-start(bf16[896,768]{1,0:T(8,128)(2,1)} %slice.25), channel_id=1, source_target_pairs={{24,16},{16,8},{8,0},{25,17},{17,9},{9,1},{26,18},{18,10},{10,2},{... | collective-permute-start | bytes 4128776 | tf_op jit(solution)/shard_map/ppermute | solution.py:430
  75.5 6.4 %copy-start.4 = (bf16[896,1536]{1,0:T(8,128)(2,1)}, bf16[896,1536]{1,0:T(8,128)(2,1)S(1)}, u32[]{:S(2)}) copy-start(bf16[896,1536]{1,0:T(8,128)(2,1)S(1)} %collective-permute-done.r1.rest_2_) | copy-start | bytes 8257540
  80.1 88.5 %collective-permute-start.4 = (bf16[896,1536]{1,0:T(8,128)(2,1)}, bf16[896,1536]{1,0:T(8,128)(2,1)}, u32[]{:S(2)}, u32[]{:S(2)}) collective-permute-start(bf16[896,1536]{1,0:T(8,128)(2,1)} %collective-permute-done.1.l1.rest_0_), channel_id=1, source_target_pairs={{16,8},{8,0},{17,9},{9,1},{18,10},{10,2},{19,11},{11,3},{20,12},{1... | collective-permute-start | bytes 8257544 | tf_op jit(solution)/shard_map/ppermute | solution.py:430
  101.6 66.9 %collective-permute-start.5 = (bf16[896,1536]{1,0:T(8,128)(2,1)}, bf16[896,1536]{1,0:T(8,128)(2,1)}, u32[]{:S(2)}, u32[]{:S(2)}) collective-permute-start(bf16[896,1536]{1,0:T(8,128)(2,1)} %copy-done.4), channel_id=1, source_target_pairs={{8,16},{16,24},{9,17},{17,25},{10,18},{18,26},{11,19},{19,27},{12,... | collective-permute-start | bytes 8257544 | tf_op jit(solution)/shard_map/ppermute | solution.py:430
  109.6 86.9 %collective-permute-start.6 = (bf16[896,768]{1,0:T(8,128)(2,1)}, bf16[896,768]{1,0:T(8,128)(2,1)S(1)}, u32[]{:S(2)}, u32[]{:S(2)}) collective-permute-start(bf16[896,768]{1,0:T(8,128)(2,1)} %get-tuple-element.34.rest_1_.l1), channel_id=1, source_target_pairs={{16,8},{8,0},{17,9},{9,1},{18,10},{10,2},{19,11},{11,3},{20,12},{1... | collective-permute-start | bytes 4128776 | tf_op jit(solution)/shard_map/ppermute | solution.py:430
  110.9 85.6 %collective-permute-start.7 = (bf16[896,768]{1,0:T(8,128)(2,1)}, bf16[896,768]{1,0:T(8,128)(2,1)S(1)}, u32[]{:S(2)}, u32[]{:S(2)}) collective-permute-start(bf16[896,768]{1,0:T(8,128)(2,1)} %get-tuple-element.35.rest_3_.r1), channel_id=1, source_target_pairs={{8,16},{16,24},{9,17},{17,25},{10,18},{18,26},{11,19},{19,27},{12,... | collective-permute-start | bytes 4128776 | tf_op jit(solution)/shard_map/ppermute | solution.py:430
  196.5 27.4 %collective-permute-start.10 = (bf16[896,512]{1,0:T(8,128)(2,1)}, bf16[896,512]{1,0:T(8,128)(2,1)}, u32[]{:S(2)}, u32[]{:S(2)}) collective-permute-start(bf16[896,512]{1,0:T(8,128)(2,1)} %slice.32), channel_id=1, source_target_pairs={{8,0},{16,24},{9,1},{17,25},{10,2},{18,26},{11,3},{19,27},{12,4},{... | collective-permute-start | bytes 2752520 | tf_op jit(solution)/shard_map/ppermute | solution.py:430
  200.0 23.9 %copy-start.7 = (bf16[1,112,896]{2,1,0:T(8,128)(2,1)S(1)}, bf16[1,112,896]{2,1,0:T(8,128)(2,1)}, u32[]{:S(2)}) copy-start(bf16[1,112,896]{2,1,0:T(8,128)(2,1)} %reduce-scatter.3.cloned.1.call-done) | copy-start | bytes 602116
  200.1 4.5 %copy-start.9 = (bf16[4,112,896]{2,1,0:T(8,128)(2,1)S(1)}, bf16[4,112,896]{2,1,0:T(8,128)(2,1)}, u32[]{:S(2)}) copy-start(bf16[4,112,896]{2,1,0:T(8,128)(2,1)} %reduce-scatter.5.cloned.1.call-done) | copy-start | bytes 2408452
  200.1 29.4 %all-to-all-start = ((bf16[8,112,896]{2,1,0:T(8,128)(2,1)}), bf16[8,112,896]{2,1,0:T(8,128)(2,1)}, u32[]{:S(2)}, u32[]{:S(2)}) async-start(bf16[8,112,896]{2,1,0:T(8,128)(2,1)} %bitcast.34), calls=%async_computation.2 | async-start | bytes 3211264 | tf_op jit(solution)/shard_map/all_to_all | solution.py:461
  204.5 95.0 %all-gather.4.cloned.1.call-start = ((), (), s32[]{:S(2)}) async-start(), calls=%async_computation.5 | async-start | bytes 7225344 | tf_op jit(solution)/shard_map/all_gather | solution.py:475
  204.6 19.2 %collective-permute-start.8 = (bf16[112,896]{1,0:T(8,128)(2,1)S(1)}, bf16[112,896]{1,0:T(8,128)(2,1)S(1)}, u32[]{:S(2)}, u32[]{:S(2)}) collective-permute-start(bf16[112,896]{1,0:T(8,128)(2,1)S(1)} %get-tuple-element.56), channel_id=1, source_target_pairs={{16,8},{8,0},{17,9},{9,1},{18,10},{10,2},{19,11},{11,3},{20,12},{1... | collective-permute-start | bytes 602120 | tf_op jit(solution)/shard_map/ppermute | solution.py:430
  205.9 17.9 %collective-permute-start.9 = (bf16[112,896]{1,0:T(8,128)(2,1)S(1)}, bf16[112,896]{1,0:T(8,128)(2,1)S(1)}, u32[]{:S(2)}, u32[]{:S(2)}) collective-permute-start(bf16[112,896]{1,0:T(8,128)(2,1)S(1)} %get-tuple-element.55), channel_id=1, source_target_pairs={{8,16},{16,24},{9,17},{17,25},{10,18},{18,26},{11,19},{19,27},{12,... | collective-permute-start | bytes 602120 | tf_op jit(solution)/shard_map/ppermute | solution.py:430
  224.0 20.6 %collective-permute-start.12 = (bf16[4,112,896]{2,1,0:T(8,128)(2,1)S(1)}, bf16[4,112,896]{2,1,0:T(8,128)(2,1)S(1)}, u32[]{:S(2)}, u32[]{:S(2)}) collective-permute-start(bf16[4,112,896]{2,1,0:T(8,128)(2,1)S(1)} %pad_maximum_fusion.own), channel_id=1, source_target_pairs={{0,8},{8,16},{16,24},{1,9},{9,17},{17,25},{2,10},{10,18},{18,26},{... | collective-permute-start | bytes 2408456 | tf_op jit(solution)/shard_map/ppermute | solution.py:430
  228.1 23.1 %collective-permute-start.13 = (bf16[4,112,896]{2,1,0:T(8,128)(2,1)S(1)}, bf16[4,112,896]{2,1,0:T(8,128)(2,1)S(1)}, u32[]{:S(2)}, u32[]{:S(2)}) collective-permute-start(bf16[4,112,896]{2,1,0:T(8,128)(2,1)S(1)} %pad_maximum_fusion.own), channel_id=1, source_target_pairs={{24,16},{16,8},{8,0},{25,17},{17,9},{9,1},{26,18},{18,10},{10,2},{... | collective-permute-start | bytes 2408456 | tf_op jit(solution)/shard_map/ppermute | solution.py:430
  231.1 22.7 %collective-permute-start.11 = (bf16[1,112,896]{2,1,0:T(8,128)(2,1)S(1)}, bf16[1,112,896]{2,1,0:T(8,128)(2,1)S(1)}, u32[]{:S(2)}, u32[]{:S(2)}) collective-permute-start(bf16[1,112,896]{2,1,0:T(8,128)(2,1)S(1)} %bitcast.24), channel_id=1, source_target_pairs={{8,0},{16,24},{9,1},{17,25},{10,2},{18,26},{11,3},{19,27},{12,4},{... | collective-permute-start | bytes 602120 | tf_op jit(solution)/shard_map/ppermute | solution.py:430
  232.4 21.5 %copy-start.8 = (bf16[1,112,896]{2,1,0:T(8,128)(2,1)S(1)}, bf16[1,112,896]{2,1,0:T(8,128)(2,1)}, u32[]{:S(2)}) copy-start(bf16[1,112,896]{2,1,0:T(8,128)(2,1)} %reduce-scatter.3.cloned.1.call-done) | copy-start | bytes 602116
  255.0 41.3 %copy-start.1 = (s32[2]{0:T(128)S(1)}, s32[2]{0:T(128)}, u32[]{:S(2)}) copy-start(s32[2]{0:T(128)} %pad_add_fusion.place) | copy-start | bytes 28
  255.1 105.1 %all-gather.6.cloned.1.call-start = ((), (), s32[]{:S(2)}) async-start(), calls=%async_computation.6 | async-start | bytes 8257536 | tf_op jit(solution)/shard_map/all_gather | solution.py:484
  255.1 2.0 collective-permute-start.14
  255.8 20.1 %collective-permute-start.16 = (bf16[4,112,896]{2,1,0:T(8,128)(2,1)S(1)}, bf16[4,112,896]{2,1,0:T(8,128)(2,1)S(1)}, u32[]{:S(2)}, u32[]{:S(2)}) collective-permute-start(bf16[4,112,896]{2,1,0:T(8,128)(2,1)S(1)} %collective-permute-done.13.l1), channel_id=1, source_target_pairs={{16,8},{8,0},{17,9},{9,1},{18,10},{10,2},{19,11},{11,3},{20,12},{1... | collective-permute-start | bytes 2408456 | tf_op jit(solution)/shard_map/ppermute | solution.py:430
  257.2 24.2 %collective-permute-start.15 = (bf16[4,112,896]{2,1,0:T(8,128)(2,1)S(1)}, bf16[4,112,896]{2,1,0:T(8,128)(2,1)S(1)}, u32[]{:S(2)}, u32[]{:S(2)}) collective-permute-start(bf16[4,112,896]{2,1,0:T(8,128)(2,1)S(1)} %collective-permute-done.14.r2), channel_id=1, source_target_pairs={{16,24},{17,25},{18,26},{19,27},{20,28},{21,29},{22,30},{23,31}} | collective-permute-start | bytes 2408456 | tf_op jit(solution)/shard_map/ppermute | solution.py:430
  275.9 19.1 %collective-permute-start.17 = (bf16[4,112,896]{2,1,0:T(8,128)(2,1)S(1)}, bf16[4,112,896]{2,1,0:T(8,128)(2,1)S(1)}, u32[]{:S(2)}, u32[]{:S(2)}) collective-permute-start(bf16[4,112,896]{2,1,0:T(8,128)(2,1)S(1)} %collective-permute-done.16.l2), channel_id=1, source_target_pairs={{8,0},{9,1},{10,2},{11,3},{12,4},{13,5},{14,6},{15,7}} | collective-permute-start | bytes 2408456 | tf_op jit(solution)/shard_map/ppermute | solution.py:430
  277.2 4.1 %collective-permute-start.18 = (bf16[1,112,896]{2,1,0:T(8,128)(2,1)S(1)}, bf16[1,112,896]{2,1,0:T(8,128)(2,1)S(1)}, u32[]{:S(2)}, u32[]{:S(2)}) collective-permute-start(bf16[1,112,896]{2,1,0:T(8,128)(2,1)S(1)} %bitcast.25), channel_id=1, source_target_pairs={{8,16},{16,8},{9,17},{17,9},{10,18},{18,10},{11,19},{19,11},{12,20... | collective-permute-start | bytes 602120 | tf_op jit(solution)/shard_map/ppermute | solution.py:430
  295.1 45.1 %collective-permute-start.19 = (bf16[896,1024]{1,0:T(8,128)(2,1)}, bf16[896,1024]{1,0:T(8,128)(2,1)}, u32[]{:S(2)}, u32[]{:S(2)}) collective-permute-start(bf16[896,1024]{1,0:T(8,128)(2,1)} %slice.31), channel_id=1, source_target_pairs={{8,0},{16,24},{9,1},{17,25},{10,2},{18,26},{11,3},{19,27},{12,4},{... | collective-permute-start | bytes 5505032 | tf_op jit(solution)/shard_map/ppermute | solution.py:430
  309.5 68.9 %collective-permute-start.20 = (bf16[896,768]{1,0:T(8,128)(2,1)}, bf16[896,768]{1,0:T(8,128)(2,1)}, u32[]{:S(2)}, u32[]{:S(2)}) collective-permute-start(bf16[896,768]{1,0:T(8,128)(2,1)} %add.18), channel_id=1, source_target_pairs={{8,0},{16,24},{9,1},{17,25},{10,2},{18,26},{11,3},{19,27},{12,4},{... | collective-permute-start | bytes 4128776 | tf_op jit(solution)/shard_map/ppermute | solution.py:430
  (4 other events, 6.1 us)
Sparse Core Ops, SparseCore 0:
  22.3 42.4 reduce-scatter.2
  127.7 65.4 reduce-scatter.4
  255.2 44.2 all-gather.3
  309.6 50.5 all-gather.5

commit v17 on v15

--- a/solution.py
+++ b/solution.py
@@ -49,16 +49,6 @@
 
 def scalars():
     return pl.BlockSpec(memory_space=pltpu.SMEM)
-
-
-def load_pieces(pieces, marks, target, sem):
-    copies = [
-        pltpu.make_async_copy(piece, target.at[:, low:high], sem.at[p])
-        for p, (piece, low, high) in enumerate(zip(pieces, marks, marks[1:]))
-    ]
-    for copy in copies:
-        copy.start()
-    return copies
 
 
 def load_near(begin, x, l1, r1, held, sems):
@@ -130,41 +120,53 @@
     return near_call(kernel, (4, rows, rows), jnp.bfloat16, [x, l1, r1, part], scratch, 1)
 
 
-def corner_kernel(marks, place, *rest):
-    n = len(marks) - 1
-    l1, r1, l2, r2 = (rest[g * n : (g + 1) * n] for g in range(4))
-    out, held, sems = rest[4 * n :]
+def corner_kernel(place, l1, r1, l2, r2, *rest):
+    *part, out, held, total, sems = rest
     for plane, one, other in ((1, r1, l2), (2, l1, r2)):
 
         @pl.when(place[0] == plane)
         def _(one=one, other=other):
-            copies = load_pieces(one, marks, held.at[0], sems.at[0])
-            copies += load_pieces(other, marks, held.at[1], sems.at[1])
+            copies = [
+                pltpu.make_async_copy(one, held.at[0], sems.at[0]),
+                pltpu.make_async_copy(other, held.at[1], sems.at[1]),
+            ]
+            if part:
+                copies.append(pltpu.make_async_copy(part[0].at[0], total, sems.at[2]))
             for copy in copies:
+                copy.start()
+            for copy in copies[:2]:
                 copy.wait()
-            out[0] = dot_rows(held[0], held[1]).astype(out.dtype)
+            value = dot_rows(held[0], held[1])
+            if part:
+                copies[2].wait()
+                value = value + total[...]
+            out[0] = value.astype(out.dtype)
 
     @pl.when(jnp.logical_or(place[0] == 0, place[0] == 3))
     def _():
         out[...] = jnp.zeros_like(out)
 
 
-def corner_block(place, l1, r1, l2, r2, marks):
-    rows, depth = l1[0].shape[0], marks[-1]
-    return pl.pallas_call(
-        functools.partial(corner_kernel, marks),
-        out_shape=jax.ShapeDtypeStruct((1, rows, rows), jnp.bfloat16),
-        in_specs=[scalars()] + [pl.BlockSpec(memory_space=pl.ANY)] * (4 * len(l1)),
+def corner_block(place, l1, r1, l2, r2, *part):
+    rows, width = l1.shape
+    operands = [l1, r1, l2, r2, *part]
+    return pl.pallas_call(
+        corner_kernel,
+        out_shape=jax.ShapeDtypeStruct((1, rows, rows), jnp.bfloat16 if part else jnp.float32),
+        in_specs=[scalars()] + [pl.BlockSpec(memory_space=pl.ANY)] * len(operands),
         out_specs=whole(),
         scratch_shapes=[
-            pltpu.VMEM((2, rows, depth), jnp.bfloat16),
-            pltpu.SemaphoreType.DMA((2, len(l1))),
+            pltpu.VMEM((2, rows, width), jnp.bfloat16),
+            pltpu.VMEM((rows, rows), jnp.float32),
+            pltpu.SemaphoreType.DMA((3,)),
         ],
         compiler_params=pltpu.CompilerParams(vmem_limit_bytes=56 * 2**20),
         cost_estimate=pl.CostEstimate(
-            flops=128 * rows * rows * depth, bytes_accessed=8 * rows * depth, transcendentals=0
+            flops=256 * rows * rows * width if part else 0,
+            bytes_accessed=8 * rows * width if part else 0,
+            transcendentals=0,
         ),
-    )(place, *l1, *r1, *l2, *r2)
+    )(place, *operands)
 
 
 def strips_kernel(place, own, l1, r3, l2, r2, r1, l3, corner, pair, end, out):
@@ -422,13 +424,16 @@
     across = [l2[0] + r2[0]]
     far_marks = [0, 512, *marks[1:]]
     head = across[0][:, :512]
-    head, across[0], l2[1], r2[1] = lax.optimization_barrier((head, across[0], l2[1], r2[1]))
+    part = corner_block(place, l1[0], r1[0], l2[0], r2[0])
+    part, head, across[0], l2[1], r2[1] = lax.optimization_barrier(
+        (part, head, across[0], l2[1], r2[1])
+    )
     across.append(l2[1] + r2[1])
 
     def send_on(value, *after):
         return send(lax.optimization_barrier((value, *after))[0], [(1, 0), (2, 3)])
 
-    corner = corner_block(place, l1, r1, l2, r2, marks)
+    corner = corner_block(place, l1[1], r1[1], l2[1], r2[1], part)
     corner, first = lax.optimization_barrier((corner, first))
     shares = lax.all_to_all(corner.reshape(n_col, -1, corner.shape[2]), "col", 0, 0)
     corner = shares.astype(jnp.float32).sum(0, keepdims=True).astype(jnp.bfloat16)

time: 396 us -> 396 us (level)
  waiting for transfers between devices: 234 us -> 229 us
    ppermute x21, waiting for transfers between devices: 180 us -> 169 us  [send(): return lax.ppermute(value, 'row', pairs)]
  transfers between devices with their start and end apart: 26 -> 26, of which waited for: 16 -> 15; matrix products, arithmetic and copies ran while one was open for 5% -> 5% of each run, Pallas kernels for 17% -> 17%
where the time goes in v17:
time: 396 us; the launch traced here: 395 us
  waiting for transfers between devices  229 us (58%)
  Pallas kernels  79 us (20%)
  starting transfers between devices  42.2 us (11%)
  local copies, waits for them, and re-layouts  15.5 us (4%)
  between operations  13.5 us (3%)
  other arithmetic  10.2 us (3%)
  matrix products  5.54 us (1%)
    ppermute x21, waiting for transfers between devices, send(): return lax.ppermute(value, 'row', pairs)  169 us
    ppermute x21, starting transfers between devices, send(): return lax.ppermute(value, 'row', pairs)  37.7 us
    pallas_call x2, Pallas kernels, near_call(): pl.pallas_call(kernel, out_shape=jax.ShapeDtypeStruct(shape, dtype), in_s...  34.7 us
    reduce_scatter x2, waiting for transfers between devices, scatter(): return lax.psum_scatter(blocks, 'col', scatter_dimension=1, tiled=True)  31.1 us
    pallas_call x2, Pallas kernels, product(): pl.pallas_call(functools.partial(product_kernel, tuple(marks), ready), gr...  27.9 us
    all_gather x1, waiting for transfers between devices, per_device_line(): factor = lax.all_gather(factor, 'col', axis=0, tiled=False)  23.8 us
    pallas_call x1, Pallas kernels, square(): pl.pallas_call(square_kernel, out_shape=jax.ShapeDtypeStruct((rows, depth...  10.5 us
  transfers between devices with their start and end apart: 26, of which 15 were waited for; matrix products, arithmetic and copies ran while one was open for 5% of the time, Pallas kernels for 17%

profile of v17, /device:TPU:0, one launch (start us, length us, event | category | flops | bytes accessed | tf_op | source)
XLA Modules:
  0.0 394.8 jit_solution(14372205100098943285)
XLA Ops:
  6.5 3.6 slice.24
  11.5 7.1 %collective-permute-start = (bf16[896,1536]{1,0:T(8,128)(2,1)}, bf16[896,1536]{1,0:T(8,128)(2,1)}, u32[]{:S(2)}, u32[]{:S(2)}) collective-permute-start(bf16[896,1536]{1,0:T(8,128)(2,1)} %slice.24), channel_id=1, source_target_pairs={{0,8},{8,16},{16,24},{1,9},{9,17},{17,25},{2,10},{10,18},{18,26},{... | collective-permute-start | bytes 8257544 | tf_op jit(solution)/shard_map/ppermute | solution.py:404
  18.6 5.5 %fusion = bf16[1,896,896]{2,1,0:T(8,128)(2,1)} fusion(bf16[896,2304]{1,0:T(8,128)(2,1)S(1)} %copy-done.2), kind=kOutput, calls=%fused_computation.1 | convolution fusion | flops 3700178944 | bytes 5734400 | tf_op jit(solution)/shard_map/dot_general | solution.py:20
  24.2 2.6 slice.25
  28.1 4.6 %collective-permute-start.2 = (bf16[896,768]{1,0:T(8,128)(2,1)}, bf16[896,768]{1,0:T(8,128)(2,1)S(1)}, u32[]{:S(2)}, u32[]{:S(2)}) collective-permute-start(bf16[896,768]{1,0:T(8,128)(2,1)} %slice.25), channel_id=1, source_target_pairs={{0,8},{8,16},{16,24},{1,9},{9,17},{17,25},{2,10},{10,18},{18,26},{... | collective-permute-start | bytes 4128776 | tf_op jit(solution)/shard_map/ppermute | solution.py:404
  32.7 31.0 %reduce-scatter.3.cloned.1.call-done = bf16[1,112,896]{2,1,0:T(8,128)(2,1)} async-done(((bf16[1,896,896]{2,1,0:T(8,128)(2,1)}), bf16[1,112,896]{2,1,0:T(8,128)(2,1)}) %reduce-scatter.3.cloned.1.call-update) | async-done | bytes 200720 | tf_op jit(solution)/shard_map/reduce_scatter | solution.py:407
  63.8 12.1 %collective-permute-done.1.l1 = bf16[896,1536]{1,0:T(8,128)(2,1)} collective-permute-done((bf16[896,1536]{1,0:T(8,128)(2,1)}, bf16[896,1536]{1,0:T(8,128)(2,1)}, u32[]{:S(2)}, u32[]{:S(2)}) %collective-permute-start.1) | collective-permute-done | bytes 2752544 | tf_op jit(solution)/shard_map/ppermute | solution.py:404
  78.7 2.2 collective-permute-start.5
  80.9 19.7 %shard_map.17.part = f32[2,1792,896]{2,1,0:T(8,128)} custom-call(bf16[896,2304]{1,0:T(8,128)(2,1)} %x.3, bf16[896,1536]{1,0:T(8,128)(2,1)} %collective-permute-done.1.l1, bf16[896,1536]{1,0:T(8,128)(2,1)} %collective-permute-done.r1), custom_call_target="tpu_custom_call" | custom-call | tf_op jit(solution)/shard_map/pallas_call | solution.py:95
  100.6 4.7 %collective-permute-done.3.refs_1_ = bf16[896,768]{1,0:T(8,128)(2,1)S(1)} collective-permute-done((bf16[896,768]{1,0:T(8,128)(2,1)}, bf16[896,768]{1,0:T(8,128)(2,1)S(1)}, u32[]{:S(2)}, u32[]{:S(2)}) %collective-permute-start.3) | collective-permute-done | bytes 1376288 | tf_op jit(solution)/shard_map/ppermute | solution.py:404
  110.3 15.0 %shard_map.21 = bf16[4,896,896]{2,1,0:T(8,128)(2,1)} custom-call(bf16[896,2304]{1,0:T(8,128)(2,1)} %x.3, bf16[896,768]{1,0:T(8,128)(2,1)} %get-tuple-element.35.l1, bf16[896,768]{1,0:T(8,128)(2,1)} %get-tuple-element.36.r1, f32[2,1792,896]{2,1,0:T(8,128)} %shard_map.17.part), custom_call_target="tpu_custom_call" | custom-call | flops 4932501504 | bytes 4128768 | tf_op jit(solution)/shard_map/pallas_call | solution.py:95
  125.4 39.0 %collective-permute-done.4.l2 = bf16[896,1536]{1,0:T(8,128)(2,1)} collective-permute-done((bf16[896,1536]{1,0:T(8,128)(2,1)}, bf16[896,1536]{1,0:T(8,128)(2,1)}, u32[]{:S(2)}, u32[]{:S(2)}) %collective-permute-start.4) | collective-permute-done | bytes 2752544 | tf_op jit(solution)/shard_map/ppermute | solution.py:404
  164.4 3.3 add.16
  170.3 2.6 shard_map.19.rest_0_
  173.0 20.0 %collective-permute-done.6.l2 = bf16[896,768]{1,0:T(8,128)(2,1)S(1)} collective-permute-done((bf16[896,768]{1,0:T(8,128)(2,1)}, bf16[896,768]{1,0:T(8,128)(2,1)S(1)}, u32[]{:S(2)}, u32[]{:S(2)}) %collective-permute-start.6) | collective-permute-done | bytes 1376288 | tf_op jit(solution)/shard_map/ppermute | solution.py:404
  194.5 2.3 shard_map.20
  196.9 4.5 %all-to-all-start = ((bf16[8,112,896]{2,1,0:T(8,128)(2,1)}), bf16[8,112,896]{2,1,0:T(8,128)(2,1)}, u32[]{:S(2)}, u32[]{:S(2)}) async-start(bf16[8,112,896]{2,1,0:T(8,128)(2,1)} %bitcast.35), calls=%async_computation.2 | async-start | bytes 3211264 | tf_op jit(solution)/shard_map/all_to_all | solution.py:438
  203.4 21.1 %collective-permute-done.8 = bf16[112,896]{1,0:T(8,128)(2,1)S(1)} collective-permute-done((bf16[112,896]{1,0:T(8,128)(2,1)S(1)}, bf16[112,896]{1,0:T(8,128)(2,1)S(1)}, u32[]{:S(2)}, u32[]{:S(2)}) %collective-permute-start.8) | collective-permute-done | bytes 200736 | tf_op jit(solution)/shard_map/ppermute | solution.py:404
  226.1 4.6 %collective-permute-start.12 = (bf16[4,112,896]{2,1,0:T(8,128)(2,1)S(1)}, bf16[4,112,896]{2,1,0:T(8,128)(2,1)S(1)}, u32[]{:S(2)}, u32[]{:S(2)}) collective-permute-start(bf16[4,112,896]{2,1,0:T(8,128)(2,1)S(1)} %pad_maximum_fusion.own), channel_id=1, source_target_pairs={{0,8},{8,16},{16,24},{1,9},{9,17},{17,25},{2,10},{10,18},{18,26},{... | collective-permute-start | bytes 2408456 | tf_op jit(solution)/shard_map/ppermute | solution.py:404
  233.7 3.2 add.18
  236.9 10.6 %collective-permute-done.13.l1 = bf16[4,112,896]{2,1,0:T(8,128)(2,1)S(1)} collective-permute-done((bf16[4,112,896]{2,1,0:T(8,128)(2,1)S(1)}, bf16[4,112,896]{2,1,0:T(8,128)(2,1)S(1)}, u32[]{:S(2)}, u32[]{:S(2)}) %collective-permute-start.13) | collective-permute-done | bytes 802848 | tf_op jit(solution)/shard_map/ppermute | solution.py:404
  247.5 2.8 collective-permute-done.11.end
  253.6 18.3 %collective-permute-done.16.l2 = bf16[4,112,896]{2,1,0:T(8,128)(2,1)S(1)} collective-permute-done((bf16[4,112,896]{2,1,0:T(8,128)(2,1)S(1)}, bf16[4,112,896]{2,1,0:T(8,128)(2,1)S(1)}, u32[]{:S(2)}, u32[]{:S(2)}) %collective-permute-start.16) | collective-permute-done | bytes 802848 | tf_op jit(solution)/shard_map/ppermute | solution.py:404
  274.6 2.9 slice.31
  277.4 13.9 %collective-permute-done.17.l3 = bf16[4,112,896]{2,1,0:T(8,128)(2,1)S(1)} collective-permute-done((bf16[4,112,896]{2,1,0:T(8,128)(2,1)S(1)}, bf16[4,112,896]{2,1,0:T(8,128)(2,1)S(1)}, u32[]{:S(2)}, u32[]{:S(2)}) %collective-permute-start.17) | collective-permute-done | bytes 802848 | tf_op jit(solution)/shard_map/ppermute | solution.py:404
  293.6 1.7 copy-done
  295.3 4.4 %all-gather.4.cloned.1.call-done.panel = bf16[4,896,896]{2,1,0:T(8,128)(2,1)} async-done(((bf16[4,112,896]{2,1,0:T(8,128)(2,1)}), bf16[4,896,896]{2,1,0:T(8,128)(2,1)}) %all-gather.4.cloned.1.call-update) | async-done | bytes 6422544 | tf_op jit(solution)/shard_map/all_gather | solution.py:452
  299.7 10.5 %shard_map.23 = bf16[896,448]{1,0:T(8,128)(2,1)} custom-call(s32[2]{0:T(128)} %pad_add_fusion.place, bf16[4,896,896]{2,1,0:T(8,128)(2,1)} %all-gather.4.cloned.1.call-done.panel, bf16[448,3584]{1,0:T(8,128)(2,1)} %copy-done), custom_call_target="tpu_custom_call" | custom-call | flops 2877292544 | bytes 8028160 | tf_op jit(solution)/shard_map/pallas_call | solution.py:241
  311.5 25.0 %collective-permute-done.19.refs_0_ = bf16[896,1024]{1,0:T(8,128)(2,1)} collective-permute-done((bf16[896,1024]{1,0:T(8,128)(2,1)}, bf16[896,1024]{1,0:T(8,128)(2,1)}, u32[]{:S(2)}, u32[]{:S(2)}) %collective-permute-start.19) | collective-permute-done | bytes 1835040 | tf_op jit(solution)/shard_map/ppermute | solution.py:404
  336.5 23.8 %all-gather.6.cloned.1.call-done = bf16[7168,448]{1,0:T(8,128)(2,1)} async-done(((bf16[896,448]{1,0:T(8,128)(2,1)}), bf16[7168,448]{1,0:T(8,128)(2,1)}) %all-gather.6.cloned.1.call-update) | async-done | bytes 6422544 | tf_op jit(solution)/shard_map/all_gather | solution.py:461
  360.3 17.4 %shard_map.25 = (bf16[896,2304]{1,0:T(8,128)(2,1)}, bf16[896,3584]{1,0:T(8,128)(2,1)}) custom-call(s32[2]{0:T(128)} %pad_add_fusion.place, bf16[8,896,448]{2,1,0:T(8,128)(2,1)} %bitcast.30, bf16[8,112,2304]{2,1,0:T(8,128)(2,1)} %bitcast.27, bf16[8,112,1536]{2,1,0:T(8,128)(2,1)} %bitcast.10.rest_0_, bf16[8,112,1536]{2,1,0:T(8,128)(2,1)} %bitcast.11.rest_1_, ...), custom_call_target="tpu_custom_call" | custom-call | tf_op jit(solution)/shard_map/pallas_call | solution.py:365
  377.7 10.5 %shard_map.26 = bf16[896,2304]{1,0:T(8,128)(2,1)} custom-call(s32[2]{0:T(128)} %pad_add_fusion.place, bf16[896,3584]{1,0:T(8,128)(2,1)} %get-tuple-element.51.f, bf16[8,112,2304]{2,1,0:T(8,128)(2,1)} %bitcast.28, bf16[8,112,768]{2,1,0:T(8,128)(2,1)} %bitcast.31, bf16[8,112,768]{2,1,0:T(8,128)(2,1)} %bitcast.32, ...), custom_call_target="tpu_custom_call", output_to_operand_aliasing={{}: (7, {})} | custom-call | flops 4932501504 | bytes 8257536 | tf_op jit(solution)/shard_map/pallas_call | solution.py:365
  (71 shorter events, 30.6 us)
Async XLA Ops:
  6.5 57.2 %reduce-scatter.3.cloned.1.call-start = ((), (), s32[]{:S(2)}) async-start(), calls=%async_computation.3 | async-start | bytes 1806336 | tf_op jit(solution)/shard_map/reduce_scatter | solution.py:407
  6.5 12.0 %copy-start.2 = (bf16[896,2304]{1,0:T(8,128)(2,1)S(1)}, bf16[896,2304]{1,0:T(8,128)(2,1)}, u32[]{:S(2)}) copy-start(bf16[896,2304]{1,0:T(8,128)(2,1)} %x.3) | copy-start | bytes 12386308
  10.2 65.7 %collective-permute-start.1 = (bf16[896,1536]{1,0:T(8,128)(2,1)}, bf16[896,1536]{1,0:T(8,128)(2,1)}, u32[]{:S(2)}, u32[]{:S(2)}) collective-permute-start(bf16[896,1536]{1,0:T(8,128)(2,1)} %slice.24), channel_id=1, source_target_pairs={{24,16},{16,8},{8,0},{25,17},{17,9},{9,1},{26,18},{18,10},{10,2},{... | collective-permute-start | bytes 8257544 | tf_op jit(solution)/shard_map/ppermute | solution.py:404
  11.5 65.9 %collective-permute-start = (bf16[896,1536]{1,0:T(8,128)(2,1)}, bf16[896,1536]{1,0:T(8,128)(2,1)}, u32[]{:S(2)}, u32[]{:S(2)}) collective-permute-start(bf16[896,1536]{1,0:T(8,128)(2,1)} %slice.24), channel_id=1, source_target_pairs={{0,8},{8,16},{16,24},{1,9},{9,17},{17,25},{2,10},{10,18},{18,26},{... | collective-permute-start | bytes 8257544 | tf_op jit(solution)/shard_map/ppermute | solution.py:404
  24.1 172.7 %reduce-scatter.5.cloned.1.call-start = ((), (), s32[]{:S(2)}) async-start(), calls=%async_computation.4 | async-start | bytes 7225344 | tf_op jit(solution)/shard_map/reduce_scatter | solution.py:407
  26.8 78.5 %collective-permute-start.3 = (bf16[896,768]{1,0:T(8,128)(2,1)}, bf16[896,768]{1,0:T(8,128)(2,1)S(1)}, u32[]{:S(2)}, u32[]{:S(2)}) collective-permute-start(bf16[896,768]{1,0:T(8,128)(2,1)} %slice.25), channel_id=1, source_target_pairs={{24,16},{16,8},{8,0},{25,17},{17,9},{9,1},{26,18},{18,10},{10,2},{... | collective-permute-start | bytes 4128776 | tf_op jit(solution)/shard_map/ppermute | solution.py:404
  28.1 77.7 %collective-permute-start.2 = (bf16[896,768]{1,0:T(8,128)(2,1)}, bf16[896,768]{1,0:T(8,128)(2,1)S(1)}, u32[]{:S(2)}, u32[]{:S(2)}) collective-permute-start(bf16[896,768]{1,0:T(8,128)(2,1)} %slice.25), channel_id=1, source_target_pairs={{0,8},{8,16},{16,24},{1,9},{9,17},{17,25},{2,10},{10,18},{18,26},{... | collective-permute-start | bytes 4128776 | tf_op jit(solution)/shard_map/ppermute | solution.py:404
  77.4 87.0 %collective-permute-start.4 = (bf16[896,1536]{1,0:T(8,128)(2,1)}, bf16[896,1536]{1,0:T(8,128)(2,1)}, u32[]{:S(2)}, u32[]{:S(2)}) collective-permute-start(bf16[896,1536]{1,0:T(8,128)(2,1)} %collective-permute-done.1.l1), channel_id=1, source_target_pairs={{16,8},{8,0},{17,9},{9,1},{18,10},{10,2},{19,11},{11,3},{20,12},{1... | collective-permute-start | bytes 8257544 | tf_op jit(solution)/shard_map/ppermute | solution.py:404
  78.7 85.7 %collective-permute-start.5 = (bf16[896,1536]{1,0:T(8,128)(2,1)}, bf16[896,1536]{1,0:T(8,128)(2,1)}, u32[]{:S(2)}, u32[]{:S(2)}) collective-permute-start(bf16[896,1536]{1,0:T(8,128)(2,1)} %collective-permute-done.r1), channel_id=1, source_target_pairs={{8,16},{16,24},{9,17},{17,25},{10,18},{18,26},{11,19},{19,27},{12,... | collective-permute-start | bytes 8257544 | tf_op jit(solution)/shard_map/ppermute | solution.py:404
  107.4 85.5 %collective-permute-start.6 = (bf16[896,768]{1,0:T(8,128)(2,1)}, bf16[896,768]{1,0:T(8,128)(2,1)S(1)}, u32[]{:S(2)}, u32[]{:S(2)}) collective-permute-start(bf16[896,768]{1,0:T(8,128)(2,1)} %get-tuple-element.35.l1), channel_id=1, source_target_pairs={{16,8},{8,0},{17,9},{9,1},{18,10},{10,2},{19,11},{11,3},{20,12},{1... | collective-permute-start | bytes 4128776 | tf_op jit(solution)/shard_map/ppermute | solution.py:404
  108.7 84.2 %collective-permute-start.7 = (bf16[896,768]{1,0:T(8,128)(2,1)}, bf16[896,768]{1,0:T(8,128)(2,1)S(1)}, u32[]{:S(2)}, u32[]{:S(2)}) collective-permute-start(bf16[896,768]{1,0:T(8,128)(2,1)} %get-tuple-element.36.r1), channel_id=1, source_target_pairs={{8,16},{16,24},{9,17},{17,25},{10,18},{18,26},{11,19},{19,27},{12,... | collective-permute-start | bytes 4128776 | tf_op jit(solution)/shard_map/ppermute | solution.py:404
  193.0 31.7 %collective-permute-start.10 = (bf16[896,512]{1,0:T(8,128)(2,1)}, bf16[896,512]{1,0:T(8,128)(2,1)}, u32[]{:S(2)}, u32[]{:S(2)}) collective-permute-start(bf16[896,512]{1,0:T(8,128)(2,1)} %slice.32), channel_id=1, source_target_pairs={{8,0},{16,24},{9,1},{17,25},{10,2},{18,26},{11,3},{19,27},{12,4},{... | collective-permute-start | bytes 2752520 | tf_op jit(solution)/shard_map/ppermute | solution.py:404
  196.8 27.8 %copy-start.8 = (bf16[1,112,896]{2,1,0:T(8,128)(2,1)S(1)}, bf16[1,112,896]{2,1,0:T(8,128)(2,1)}, u32[]{:S(2)}) copy-start(bf16[1,112,896]{2,1,0:T(8,128)(2,1)} %reduce-scatter.3.cloned.1.call-done) | copy-start | bytes 602116
  196.8 4.5 %copy-start.10 = (bf16[4,112,896]{2,1,0:T(8,128)(2,1)S(1)}, bf16[4,112,896]{2,1,0:T(8,128)(2,1)}, u32[]{:S(2)}) copy-start(bf16[4,112,896]{2,1,0:T(8,128)(2,1)} %reduce-scatter.5.cloned.1.call-done) | copy-start | bytes 2408452
  196.9 33.8 %all-to-all-start = ((bf16[8,112,896]{2,1,0:T(8,128)(2,1)}), bf16[8,112,896]{2,1,0:T(8,128)(2,1)}, u32[]{:S(2)}, u32[]{:S(2)}) async-start(bf16[8,112,896]{2,1,0:T(8,128)(2,1)} %bitcast.35), calls=%async_computation.2 | async-start | bytes 3211264 | tf_op jit(solution)/shard_map/all_to_all | solution.py:438
  201.3 98.4 %all-gather.4.cloned.1.call-start = ((), (), s32[]{:S(2)}) async-start(), calls=%async_computation.5 | async-start | bytes 7225344 | tf_op jit(solution)/shard_map/all_gather | solution.py:452
  201.4 2.0 collective-permute-start.9
  202.1 22.4 %collective-permute-start.8 = (bf16[112,896]{1,0:T(8,128)(2,1)S(1)}, bf16[112,896]{1,0:T(8,128)(2,1)S(1)}, u32[]{:S(2)}, u32[]{:S(2)}) collective-permute-start(bf16[112,896]{1,0:T(8,128)(2,1)S(1)} %get-tuple-element.58), channel_id=1, source_target_pairs={{16,8},{8,0},{17,9},{9,1},{18,10},{10,2},{19,11},{11,3},{20,12},{1... | collective-permute-start | bytes 602120 | tf_op jit(solution)/shard_map/ppermute | solution.py:404
  224.8 22.7 %collective-permute-start.13 = (bf16[4,112,896]{2,1,0:T(8,128)(2,1)S(1)}, bf16[4,112,896]{2,1,0:T(8,128)(2,1)S(1)}, u32[]{:S(2)}, u32[]{:S(2)}) collective-permute-start(bf16[4,112,896]{2,1,0:T(8,128)(2,1)S(1)} %pad_maximum_fusion.own), channel_id=1, source_target_pairs={{24,16},{16,8},{8,0},{25,17},{17,9},{9,1},{26,18},{18,10},{10,2},{... | collective-permute-start | bytes 2408456 | tf_op jit(solution)/shard_map/ppermute | solution.py:404
  226.1 21.4 %collective-permute-start.12 = (bf16[4,112,896]{2,1,0:T(8,128)(2,1)S(1)}, bf16[4,112,896]{2,1,0:T(8,128)(2,1)S(1)}, u32[]{:S(2)}, u32[]{:S(2)}) collective-permute-start(bf16[4,112,896]{2,1,0:T(8,128)(2,1)S(1)} %pad_maximum_fusion.own), channel_id=1, source_target_pairs={{0,8},{8,16},{16,24},{1,9},{9,17},{17,25},{2,10},{10,18},{18,26},{... | collective-permute-start | bytes 2408456 | tf_op jit(solution)/shard_map/ppermute | solution.py:404
  232.3 17.9 %collective-permute-start.11 = (bf16[1,112,896]{2,1,0:T(8,128)(2,1)S(1)}, bf16[1,112,896]{2,1,0:T(8,128)(2,1)S(1)}, u32[]{:S(2)}, u32[]{:S(2)}) collective-permute-start(bf16[1,112,896]{2,1,0:T(8,128)(2,1)S(1)} %bitcast.24), channel_id=1, source_target_pairs={{8,0},{16,24},{9,1},{17,25},{10,2},{18,26},{11,3},{19,27},{12,4},{... | collective-permute-start | bytes 602120 | tf_op jit(solution)/shard_map/ppermute | solution.py:404
  233.6 16.7 %copy-start.9 = (bf16[1,112,896]{2,1,0:T(8,128)(2,1)S(1)}, bf16[1,112,896]{2,1,0:T(8,128)(2,1)}, u32[]{:S(2)}) copy-start(bf16[1,112,896]{2,1,0:T(8,128)(2,1)} %reduce-scatter.3.cloned.1.call-done) | copy-start | bytes 602116
  251.5 41.1 %copy-start.1 = (s32[2]{0:T(128)S(1)}, s32[2]{0:T(128)}, u32[]{:S(2)}) copy-start(s32[2]{0:T(128)} %pad_add_fusion.place) | copy-start | bytes 28
  251.5 108.8 %all-gather.6.cloned.1.call-start = ((), (), s32[]{:S(2)}) async-start(), calls=%async_computation.6 | async-start | bytes 8257536 | tf_op jit(solution)/shard_map/all_gather | solution.py:461
  251.6 20.3 %collective-permute-start.16 = (bf16[4,112,896]{2,1,0:T(8,128)(2,1)S(1)}, bf16[4,112,896]{2,1,0:T(8,128)(2,1)S(1)}, u32[]{:S(2)}, u32[]{:S(2)}) collective-permute-start(bf16[4,112,896]{2,1,0:T(8,128)(2,1)S(1)} %collective-permute-done.13.l1), channel_id=1, source_target_pairs={{16,8},{8,0},{17,9},{9,1},{18,10},{10,2},{19,11},{11,3},{20,12},{1... | collective-permute-start | bytes 2408456 | tf_op jit(solution)/shard_map/ppermute | solution.py:404
  252.9 20.3 %collective-permute-start.14 = (bf16[4,112,896]{2,1,0:T(8,128)(2,1)S(1)}, bf16[4,112,896]{2,1,0:T(8,128)(2,1)S(1)}, u32[]{:S(2)}, u32[]{:S(2)}) collective-permute-start(bf16[4,112,896]{2,1,0:T(8,128)(2,1)S(1)} %collective-permute-done.12.r1), channel_id=1, source_target_pairs={{8,16},{16,24},{9,17},{17,25},{10,18},{18,26},{11,19},{19,27},{12,... | collective-permute-start | bytes 2408456 | tf_op jit(solution)/shard_map/ppermute | solution.py:404
  271.9 19.5 %collective-permute-start.17 = (bf16[4,112,896]{2,1,0:T(8,128)(2,1)S(1)}, bf16[4,112,896]{2,1,0:T(8,128)(2,1)S(1)}, u32[]{:S(2)}, u32[]{:S(2)}) collective-permute-start(bf16[4,112,896]{2,1,0:T(8,128)(2,1)S(1)} %collective-permute-done.16.l2), channel_id=1, source_target_pairs={{8,0},{9,1},{10,2},{11,3},{12,4},{13,5},{14,6},{15,7}} | collective-permute-start | bytes 2408456 | tf_op jit(solution)/shard_map/ppermute | solution.py:404
  273.2 18.2 %collective-permute-start.15 = (bf16[4,112,896]{2,1,0:T(8,128)(2,1)S(1)}, bf16[4,112,896]{2,1,0:T(8,128)(2,1)S(1)}, u32[]{:S(2)}, u32[]{:S(2)}) collective-permute-start(bf16[4,112,896]{2,1,0:T(8,128)(2,1)S(1)} %collective-permute-done.14.r2), channel_id=1, source_target_pairs={{16,24},{17,25},{18,26},{19,27},{20,28},{21,29},{22,30},{23,31}} | collective-permute-start | bytes 2408456 | tf_op jit(solution)/shard_map/ppermute | solution.py:404
  273.9 3.6 collective-permute-start.18
  291.3 45.1 %collective-permute-start.19 = (bf16[896,1024]{1,0:T(8,128)(2,1)}, bf16[896,1024]{1,0:T(8,128)(2,1)}, u32[]{:S(2)}, u32[]{:S(2)}) collective-permute-start(bf16[896,1024]{1,0:T(8,128)(2,1)} %slice.31), channel_id=1, source_target_pairs={{8,0},{16,24},{9,1},{17,25},{10,2},{18,26},{11,3},{19,27},{12,4},{... | collective-permute-start | bytes 5505032 | tf_op jit(solution)/shard_map/ppermute | solution.py:404
  293.6 1.7 copy-start
  310.2 67.5 %collective-permute-start.20 = (bf16[896,768]{1,0:T(8,128)(2,1)}, bf16[896,768]{1,0:T(8,128)(2,1)}, u32[]{:S(2)}, u32[]{:S(2)}) collective-permute-start(bf16[896,768]{1,0:T(8,128)(2,1)} %add.18), channel_id=1, source_target_pairs={{8,0},{16,24},{9,1},{17,25},{10,2},{18,26},{11,3},{19,27},{12,4},{... | collective-permute-start | bytes 4128776 | tf_op jit(solution)/shard_map/ppermute | solution.py:404
  (5 other events, 6.6 us)
Sparse Core Ops, SparseCore 0:
  24.3 39.4 reduce-scatter.2
  125.5 68.1 reduce-scatter.4
  251.6 48.0 all-gather.3
  310.3 49.9 all-gather.5

commit v18 on v17

--- a/solution.py
+++ b/solution.py
@@ -422,8 +422,8 @@
     first = scatter(near_rest(x, l1[1], r1[1], part))
 
     across = [l2[0] + r2[0]]
-    far_marks = [0, 512, *marks[1:]]
-    head = across[0][:, :512]
+    far_marks = [0, 256, *marks[1:]]
+    head = across[0][:, :256]
     part = corner_block(place, l1[0], r1[0], l2[0], r2[0])
     part, head, across[0], l2[1], r2[1] = lax.optimization_barrier(
         (part, head, across[0], l2[1], r2[1])
@@ -453,7 +453,7 @@
 
     tr2, tl2 = send(tr1, right[1:]), send(tl1, left[1:])
     tr3, tl3 = send(tr2, right[2:]), send(tl2, left[2:])
-    far += arrived(send_on(across[0][:, 512:], tr3, tl3, pair))
+    far += arrived(send_on(across[0][:, 256:], tr3, tl3, pair))
 
     strip = strips(place, tile, tl1, tr3, tl2, tr2, tr1, tl3, corner, pair, end)
     factor = square(place, panel, strip)

time: 396 us -> 398 us (level)
    all_gather x1, waiting for transfers between devices: 23.8 us -> 14.4 us  [per_device_line(): factor = lax.all_gather(factor, 'col', axis=0, tiled=False)]
    ppermute x21, waiting for transfers between devices: 169 us -> 178 us  [send(): return lax.ppermute(value, 'row', pairs)]
    unnamed x22 -> x26, local copies, waits for them, and re-layouts: 5.26 us -> 7.98 us
where the time goes in v18:
time: 398 us; the launch traced here: 397 us
  waiting for transfers between devices  229 us (58%)
  Pallas kernels  79 us (20%)
  starting transfers between devices  42.3 us (11%)
  local copies, waits for them, and re-layouts  18.3 us (5%)
  between operations  13.6 us (3%)
  other arithmetic  10.2 us (3%)
  matrix products  5.54 us (1%)
    ppermute x21, waiting for transfers between devices, send(): return lax.ppermute(value, 'row', pairs)  178 us
    ppermute x21, starting transfers between devices, send(): return lax.ppermute(value, 'row', pairs)  37.7 us
    pallas_call x2, Pallas kernels, near_call(): pl.pallas_call(kernel, out_shape=jax.ShapeDtypeStruct(shape, dtype), in_s...  34.7 us
    reduce_scatter x2, waiting for transfers between devices, scatter(): return lax.psum_scatter(blocks, 'col', scatter_dimension=1, tiled=True)  31.1 us
    pallas_call x2, Pallas kernels, product(): pl.pallas_call(functools.partial(product_kernel, tuple(marks), ready), gr...  27.9 us
    all_gather x1, waiting for transfers between devices, per_device_line(): factor = lax.all_gather(factor, 'col', axis=0, tiled=False)  14.4 us
    pallas_call x1, Pallas kernels, square(): pl.pallas_call(square_kernel, out_shape=jax.ShapeDtypeStruct((rows, depth...  10.5 us
    unnamed x26, local copies, waits for them, and re-layouts  7.98 us
  transfers between devices with their start and end apart: 26, of which 15 were waited for; matrix products, arithmetic and copies ran while one was open for 5% of the time, Pallas kernels for 17%

profile of v18, /device:TPU:0, one launch (start us, length us, event | category | flops | bytes accessed | tf_op | source)
XLA Modules:
  0.0 397.2 jit_solution(5097503974862370196)
XLA Ops:
  6.5 3.6 slice.24
  11.5 7.1 %collective-permute-start = (bf16[896,1536]{1,0:T(8,128)(2,1)}, bf16[896,1536]{1,0:T(8,128)(2,1)}, u32[]{:S(2)}, u32[]{:S(2)}) collective-permute-start(bf16[896,1536]{1,0:T(8,128)(2,1)} %slice.24), channel_id=1, source_target_pairs={{0,8},{8,16},{16,24},{1,9},{9,17},{17,25},{2,10},{10,18},{18,26},{... | collective-permute-start | bytes 8257544 | tf_op jit(solution)/shard_map/ppermute | solution.py:404
  18.6 5.5 %fusion = bf16[1,896,896]{2,1,0:T(8,128)(2,1)} fusion(bf16[896,2304]{1,0:T(8,128)(2,1)S(1)} %copy-done.2), kind=kOutput, calls=%fused_computation.1 | convolution fusion | flops 3700178944 | bytes 5734400 | tf_op jit(solution)/shard_map/dot_general | solution.py:20
  24.2 2.6 slice.25
  28.1 4.6 %collective-permute-start.2 = (bf16[896,768]{1,0:T(8,128)(2,1)}, bf16[896,768]{1,0:T(8,128)(2,1)S(1)}, u32[]{:S(2)}, u32[]{:S(2)}) collective-permute-start(bf16[896,768]{1,0:T(8,128)(2,1)} %slice.25), channel_id=1, source_target_pairs={{0,8},{8,16},{16,24},{1,9},{9,17},{17,25},{2,10},{10,18},{18,26},{... | collective-permute-start | bytes 4128776 | tf_op jit(solution)/shard_map/ppermute | solution.py:404
  32.7 31.0 %reduce-scatter.3.cloned.1.call-done = bf16[1,112,896]{2,1,0:T(8,128)(2,1)} async-done(((bf16[1,896,896]{2,1,0:T(8,128)(2,1)}), bf16[1,112,896]{2,1,0:T(8,128)(2,1)}) %reduce-scatter.3.cloned.1.call-update) | async-done | bytes 200720 | tf_op jit(solution)/shard_map/reduce_scatter | solution.py:407
  63.7 12.2 %collective-permute-done.1.l1 = bf16[896,1536]{1,0:T(8,128)(2,1)} collective-permute-done((bf16[896,1536]{1,0:T(8,128)(2,1)}, bf16[896,1536]{1,0:T(8,128)(2,1)}, u32[]{:S(2)}, u32[]{:S(2)}) %collective-permute-start.1) | collective-permute-done | bytes 2752544 | tf_op jit(solution)/shard_map/ppermute | solution.py:404
  78.7 2.2 collective-permute-start.5
  80.9 19.7 %shard_map.17.part = f32[2,1792,896]{2,1,0:T(8,128)} custom-call(bf16[896,2304]{1,0:T(8,128)(2,1)} %x.3, bf16[896,1536]{1,0:T(8,128)(2,1)} %collective-permute-done.1.l1, bf16[896,1536]{1,0:T(8,128)(2,1)} %collective-permute-done.r1), custom_call_target="tpu_custom_call" | custom-call | tf_op jit(solution)/shard_map/pallas_call | solution.py:95
  100.6 4.7 %collective-permute-done.3.refs_1_ = bf16[896,768]{1,0:T(8,128)(2,1)S(1)} collective-permute-done((bf16[896,768]{1,0:T(8,128)(2,1)}, bf16[896,768]{1,0:T(8,128)(2,1)S(1)}, u32[]{:S(2)}, u32[]{:S(2)}) %collective-permute-start.3) | collective-permute-done | bytes 1376288 | tf_op jit(solution)/shard_map/ppermute | solution.py:404
  110.3 15.0 %shard_map.21 = bf16[4,896,896]{2,1,0:T(8,128)(2,1)} custom-call(bf16[896,2304]{1,0:T(8,128)(2,1)} %x.3, bf16[896,768]{1,0:T(8,128)(2,1)} %get-tuple-element.35.l1, bf16[896,768]{1,0:T(8,128)(2,1)} %get-tuple-element.36.r1, f32[2,1792,896]{2,1,0:T(8,128)} %shard_map.17.part), custom_call_target="tpu_custom_call" | custom-call | flops 4932501504 | bytes 4128768 | tf_op jit(solution)/shard_map/pallas_call | solution.py:95
  125.4 39.0 %collective-permute-done.4.l2 = bf16[896,1536]{1,0:T(8,128)(2,1)} collective-permute-done((bf16[896,1536]{1,0:T(8,128)(2,1)}, bf16[896,1536]{1,0:T(8,128)(2,1)}, u32[]{:S(2)}, u32[]{:S(2)}) %collective-permute-start.4) | collective-permute-done | bytes 2752544 | tf_op jit(solution)/shard_map/ppermute | solution.py:404
  164.4 3.3 add.16
  170.1 2.6 shard_map.19.rest_0_
  172.8 20.2 %collective-permute-done.6.l2 = bf16[896,768]{1,0:T(8,128)(2,1)S(1)} collective-permute-done((bf16[896,768]{1,0:T(8,128)(2,1)}, bf16[896,768]{1,0:T(8,128)(2,1)S(1)}, u32[]{:S(2)}, u32[]{:S(2)}) %collective-permute-start.6) | collective-permute-done | bytes 1376288 | tf_op jit(solution)/shard_map/ppermute | solution.py:404
  195.2 2.3 shard_map.20
  197.5 4.4 %all-to-all-start = ((bf16[8,112,896]{2,1,0:T(8,128)(2,1)}), bf16[8,112,896]{2,1,0:T(8,128)(2,1)}, u32[]{:S(2)}, u32[]{:S(2)}) async-start(bf16[8,112,896]{2,1,0:T(8,128)(2,1)} %bitcast.35), calls=%async_computation.2 | async-start | bytes 3211264 | tf_op jit(solution)/shard_map/all_to_all | solution.py:438
  205.4 19.4 %collective-permute-done.8 = bf16[112,896]{1,0:T(8,128)(2,1)S(1)} collective-permute-done((bf16[112,896]{1,0:T(8,128)(2,1)S(1)}, bf16[112,896]{1,0:T(8,128)(2,1)S(1)}, u32[]{:S(2)}, u32[]{:S(2)}) %collective-permute-start.8) | collective-permute-done | bytes 200736 | tf_op jit(solution)/shard_map/ppermute | solution.py:404
  227.0 4.6 %collective-permute-start.12 = (bf16[4,112,896]{2,1,0:T(8,128)(2,1)S(1)}, bf16[4,112,896]{2,1,0:T(8,128)(2,1)S(1)}, u32[]{:S(2)}, u32[]{:S(2)}) collective-permute-start(bf16[4,112,896]{2,1,0:T(8,128)(2,1)S(1)} %pad_maximum_fusion.own), channel_id=1, source_target_pairs={{0,8},{8,16},{16,24},{1,9},{9,17},{17,25},{2,10},{10,18},{18,26},{... | collective-permute-start | bytes 2408456 | tf_op jit(solution)/shard_map/ppermute | solution.py:404
  234.6 3.2 add.18
  237.9 10.6 %collective-permute-done.13.l1 = bf16[4,112,896]{2,1,0:T(8,128)(2,1)S(1)} collective-permute-done((bf16[4,112,896]{2,1,0:T(8,128)(2,1)S(1)}, bf16[4,112,896]{2,1,0:T(8,128)(2,1)S(1)}, u32[]{:S(2)}, u32[]{:S(2)}) %collective-permute-start.13) | collective-permute-done | bytes 802848 | tf_op jit(solution)/shard_map/ppermute | solution.py:404
  248.5 3.1 collective-permute-done.11.end
  254.9 18.6 %collective-permute-done.16.l2 = bf16[4,112,896]{2,1,0:T(8,128)(2,1)S(1)} collective-permute-done((bf16[4,112,896]{2,1,0:T(8,128)(2,1)S(1)}, bf16[4,112,896]{2,1,0:T(8,128)(2,1)S(1)}, u32[]{:S(2)}, u32[]{:S(2)}) %collective-permute-start.16) | collective-permute-done | bytes 802848 | tf_op jit(solution)/shard_map/ppermute | solution.py:404
  276.2 3.2 slice.31
  279.4 13.9 %collective-permute-done.17.l3 = bf16[4,112,896]{2,1,0:T(8,128)(2,1)S(1)} collective-permute-done((bf16[4,112,896]{2,1,0:T(8,128)(2,1)S(1)}, bf16[4,112,896]{2,1,0:T(8,128)(2,1)S(1)}, u32[]{:S(2)}, u32[]{:S(2)}) %collective-permute-start.17) | collective-permute-done | bytes 802848 | tf_op jit(solution)/shard_map/ppermute | solution.py:404
  295.7 1.7 copy-done
  297.3 4.7 %all-gather.4.cloned.1.call-done.panel = bf16[4,896,896]{2,1,0:T(8,128)(2,1)} async-done(((bf16[4,112,896]{2,1,0:T(8,128)(2,1)}), bf16[4,896,896]{2,1,0:T(8,128)(2,1)}) %all-gather.4.cloned.1.call-update) | async-done | bytes 6422544 | tf_op jit(solution)/shard_map/all_gather | solution.py:452
  302.0 10.5 %shard_map.23 = bf16[896,448]{1,0:T(8,128)(2,1)} custom-call(s32[2]{0:T(128)} %pad_add_fusion.place, bf16[4,896,896]{2,1,0:T(8,128)(2,1)} %all-gather.4.cloned.1.call-done.panel, bf16[448,3584]{1,0:T(8,128)(2,1)} %copy-done), custom_call_target="tpu_custom_call" | custom-call | flops 2877292544 | bytes 8028160 | tf_op jit(solution)/shard_map/pallas_call | solution.py:241
  313.9 34.5 %collective-permute-done.19.refs_0_ = bf16[896,1280]{1,0:T(8,128)(2,1)} collective-permute-done((bf16[896,1280]{1,0:T(8,128)(2,1)}, bf16[896,1280]{1,0:T(8,128)(2,1)}, u32[]{:S(2)}, u32[]{:S(2)}) %collective-permute-start.19) | collective-permute-done | bytes 2293792 | tf_op jit(solution)/shard_map/ppermute | solution.py:404
  348.4 14.4 %all-gather.6.cloned.1.call-done = bf16[7168,448]{1,0:T(8,128)(2,1)} async-done(((bf16[896,448]{1,0:T(8,128)(2,1)}), bf16[7168,448]{1,0:T(8,128)(2,1)}) %all-gather.6.cloned.1.call-update) | async-done | bytes 6422544 | tf_op jit(solution)/shard_map/all_gather | solution.py:461
  362.8 17.4 %shard_map.25 = (bf16[896,2304]{1,0:T(8,128)(2,1)}, bf16[896,3584]{1,0:T(8,128)(2,1)}) custom-call(s32[2]{0:T(128)} %pad_add_fusion.place, bf16[8,896,448]{2,1,0:T(8,128)(2,1)} %bitcast.30, bf16[8,112,2304]{2,1,0:T(8,128)(2,1)} %bitcast.27, bf16[8,112,1536]{2,1,0:T(8,128)(2,1)} %bitcast.10.rest_0_, bf16[8,112,1536]{2,1,0:T(8,128)(2,1)} %bitcast.11.rest_1_, ...), custom_call_target="tpu_custom_call" | custom-call | tf_op jit(solution)/shard_map/pallas_call | solution.py:365
  380.2 10.5 %shard_map.26 = bf16[896,2304]{1,0:T(8,128)(2,1)} custom-call(s32[2]{0:T(128)} %pad_add_fusion.place, bf16[896,3584]{1,0:T(8,128)(2,1)} %get-tuple-element.51.f, bf16[8,112,2304]{2,1,0:T(8,128)(2,1)} %bitcast.28, bf16[8,112,768]{2,1,0:T(8,128)(2,1)} %bitcast.31, bf16[8,112,768]{2,1,0:T(8,128)(2,1)} %bitcast.32, ...), custom_call_target="tpu_custom_call", output_to_operand_aliasing={{}: (7, {})} | custom-call | flops 4932501504 | bytes 8257536 | tf_op jit(solution)/shard_map/pallas_call | solution.py:365
  (75 shorter events, 33.2 us)
Async XLA Ops:
  6.5 57.2 %reduce-scatter.3.cloned.1.call-start = ((), (), s32[]{:S(2)}) async-start(), calls=%async_computation.3 | async-start | bytes 1806336 | tf_op jit(solution)/shard_map/reduce_scatter | solution.py:407
  6.5 12.1 %copy-start.2 = (bf16[896,2304]{1,0:T(8,128)(2,1)S(1)}, bf16[896,2304]{1,0:T(8,128)(2,1)}, u32[]{:S(2)}) copy-start(bf16[896,2304]{1,0:T(8,128)(2,1)} %x.3) | copy-start | bytes 12386308
  10.2 65.7 %collective-permute-start.1 = (bf16[896,1536]{1,0:T(8,128)(2,1)}, bf16[896,1536]{1,0:T(8,128)(2,1)}, u32[]{:S(2)}, u32[]{:S(2)}) collective-permute-start(bf16[896,1536]{1,0:T(8,128)(2,1)} %slice.24), channel_id=1, source_target_pairs={{24,16},{16,8},{8,0},{25,17},{17,9},{9,1},{26,18},{18,10},{10,2},{... | collective-permute-start | bytes 8257544 | tf_op jit(solution)/shard_map/ppermute | solution.py:404
  11.5 65.9 %collective-permute-start = (bf16[896,1536]{1,0:T(8,128)(2,1)}, bf16[896,1536]{1,0:T(8,128)(2,1)}, u32[]{:S(2)}, u32[]{:S(2)}) collective-permute-start(bf16[896,1536]{1,0:T(8,128)(2,1)} %slice.24), channel_id=1, source_target_pairs={{0,8},{8,16},{16,24},{1,9},{9,17},{17,25},{2,10},{10,18},{18,26},{... | collective-permute-start | bytes 8257544 | tf_op jit(solution)/shard_map/ppermute | solution.py:404
  24.2 173.3 %reduce-scatter.5.cloned.1.call-start = ((), (), s32[]{:S(2)}) async-start(), calls=%async_computation.4 | async-start | bytes 7225344 | tf_op jit(solution)/shard_map/reduce_scatter | solution.py:407
  26.8 78.5 %collective-permute-start.3 = (bf16[896,768]{1,0:T(8,128)(2,1)}, bf16[896,768]{1,0:T(8,128)(2,1)S(1)}, u32[]{:S(2)}, u32[]{:S(2)}) collective-permute-start(bf16[896,768]{1,0:T(8,128)(2,1)} %slice.25), channel_id=1, source_target_pairs={{24,16},{16,8},{8,0},{25,17},{17,9},{9,1},{26,18},{18,10},{10,2},{... | collective-permute-start | bytes 4128776 | tf_op jit(solution)/shard_map/ppermute | solution.py:404
  28.1 77.7 %collective-permute-start.2 = (bf16[896,768]{1,0:T(8,128)(2,1)}, bf16[896,768]{1,0:T(8,128)(2,1)S(1)}, u32[]{:S(2)}, u32[]{:S(2)}) collective-permute-start(bf16[896,768]{1,0:T(8,128)(2,1)} %slice.25), channel_id=1, source_target_pairs={{0,8},{8,16},{16,24},{1,9},{9,17},{17,25},{2,10},{10,18},{18,26},{... | collective-permute-start | bytes 4128776 | tf_op jit(solution)/shard_map/ppermute | solution.py:404
  77.4 87.0 %collective-permute-start.4 = (bf16[896,1536]{1,0:T(8,128)(2,1)}, bf16[896,1536]{1,0:T(8,128)(2,1)}, u32[]{:S(2)}, u32[]{:S(2)}) collective-permute-start(bf16[896,1536]{1,0:T(8,128)(2,1)} %collective-permute-done.1.l1), channel_id=1, source_target_pairs={{16,8},{8,0},{17,9},{9,1},{18,10},{10,2},{19,11},{11,3},{20,12},{1... | collective-permute-start | bytes 8257544 | tf_op jit(solution)/shard_map/ppermute | solution.py:404
  78.7 85.7 %collective-permute-start.5 = (bf16[896,1536]{1,0:T(8,128)(2,1)}, bf16[896,1536]{1,0:T(8,128)(2,1)}, u32[]{:S(2)}, u32[]{:S(2)}) collective-permute-start(bf16[896,1536]{1,0:T(8,128)(2,1)} %collective-permute-done.r1), channel_id=1, source_target_pairs={{8,16},{16,24},{9,17},{17,25},{10,18},{18,26},{11,19},{19,27},{12,... | collective-permute-start | bytes 8257544 | tf_op jit(solution)/shard_map/ppermute | solution.py:404
  107.4 85.5 %collective-permute-start.6 = (bf16[896,768]{1,0:T(8,128)(2,1)}, bf16[896,768]{1,0:T(8,128)(2,1)S(1)}, u32[]{:S(2)}, u32[]{:S(2)}) collective-permute-start(bf16[896,768]{1,0:T(8,128)(2,1)} %get-tuple-element.35.l1), channel_id=1, source_target_pairs={{16,8},{8,0},{17,9},{9,1},{18,10},{10,2},{19,11},{11,3},{20,12},{1... | collective-permute-start | bytes 4128776 | tf_op jit(solution)/shard_map/ppermute | solution.py:404
  108.7 84.2 %collective-permute-start.7 = (bf16[896,768]{1,0:T(8,128)(2,1)}, bf16[896,768]{1,0:T(8,128)(2,1)S(1)}, u32[]{:S(2)}, u32[]{:S(2)}) collective-permute-start(bf16[896,768]{1,0:T(8,128)(2,1)} %get-tuple-element.36.r1), channel_id=1, source_target_pairs={{8,16},{16,24},{9,17},{17,25},{10,18},{18,26},{11,19},{19,27},{12,... | collective-permute-start | bytes 4128776 | tf_op jit(solution)/shard_map/ppermute | solution.py:404
  197.4 4.6 %copy-start.11 = (bf16[896,256]{1,0:T(8,128)(2,1)S(1)}, bf16[896,256]{1,0:T(8,128)(2,1)}, u32[]{:S(2)}) copy-start(bf16[896,256]{1,0:T(8,128)(2,1)} %slice.32) | copy-start | bytes 1376260
  197.4 28.2 %copy-start.8 = (bf16[1,112,896]{2,1,0:T(8,128)(2,1)S(1)}, bf16[1,112,896]{2,1,0:T(8,128)(2,1)}, u32[]{:S(2)}) copy-start(bf16[1,112,896]{2,1,0:T(8,128)(2,1)} %reduce-scatter.3.cloned.1.call-done) | copy-start | bytes 602116
  197.5 5.8 %copy-start.10 = (bf16[4,112,896]{2,1,0:T(8,128)(2,1)S(1)}, bf16[4,112,896]{2,1,0:T(8,128)(2,1)}, u32[]{:S(2)}) copy-start(bf16[4,112,896]{2,1,0:T(8,128)(2,1)} %reduce-scatter.5.cloned.1.call-done) | copy-start | bytes 2408452
  197.5 34.2 %all-to-all-start = ((bf16[8,112,896]{2,1,0:T(8,128)(2,1)}), bf16[8,112,896]{2,1,0:T(8,128)(2,1)}, u32[]{:S(2)}, u32[]{:S(2)}) async-start(bf16[8,112,896]{2,1,0:T(8,128)(2,1)} %bitcast.35), calls=%async_computation.2 | async-start | bytes 3211264 | tf_op jit(solution)/shard_map/all_to_all | solution.py:438
  201.9 100.1 %all-gather.4.cloned.1.call-start = ((), (), s32[]{:S(2)}) async-start(), calls=%async_computation.5 | async-start | bytes 7225344 | tf_op jit(solution)/shard_map/all_gather | solution.py:452
  202.0 22.8 %collective-permute-start.10 = (bf16[896,256]{1,0:T(8,128)(2,1)S(1)}, bf16[896,256]{1,0:T(8,128)(2,1)S(1)}, u32[]{:S(2)}, u32[]{:S(2)}) collective-permute-start(bf16[896,256]{1,0:T(8,128)(2,1)S(1)} %copy-done.11), channel_id=1, source_target_pairs={{8,0},{16,24},{9,1},{17,25},{10,2},{18,26},{11,3},{19,27},{12,4},{... | collective-permute-start | bytes 1376264 | tf_op jit(solution)/shard_map/ppermute | solution.py:404
  203.4 2.0 collective-permute-start.9
  204.1 20.7 %collective-permute-start.8 = (bf16[112,896]{1,0:T(8,128)(2,1)S(1)}, bf16[112,896]{1,0:T(8,128)(2,1)S(1)}, u32[]{:S(2)}, u32[]{:S(2)}) collective-permute-start(bf16[112,896]{1,0:T(8,128)(2,1)S(1)} %get-tuple-element.58), channel_id=1, source_target_pairs={{16,8},{8,0},{17,9},{9,1},{18,10},{10,2},{19,11},{11,3},{20,12},{1... | collective-permute-start | bytes 602120 | tf_op jit(solution)/shard_map/ppermute | solution.py:404
  225.7 22.7 %collective-permute-start.13 = (bf16[4,112,896]{2,1,0:T(8,128)(2,1)S(1)}, bf16[4,112,896]{2,1,0:T(8,128)(2,1)S(1)}, u32[]{:S(2)}, u32[]{:S(2)}) collective-permute-start(bf16[4,112,896]{2,1,0:T(8,128)(2,1)S(1)} %pad_maximum_fusion.own), channel_id=1, source_target_pairs={{24,16},{16,8},{8,0},{25,17},{17,9},{9,1},{26,18},{18,10},{10,2},{... | collective-permute-start | bytes 2408456 | tf_op jit(solution)/shard_map/ppermute | solution.py:404
  227.0 21.4 %collective-permute-start.12 = (bf16[4,112,896]{2,1,0:T(8,128)(2,1)S(1)}, bf16[4,112,896]{2,1,0:T(8,128)(2,1)S(1)}, u32[]{:S(2)}, u32[]{:S(2)}) collective-permute-start(bf16[4,112,896]{2,1,0:T(8,128)(2,1)S(1)} %pad_maximum_fusion.own), channel_id=1, source_target_pairs={{0,8},{8,16},{16,24},{1,9},{9,17},{17,25},{2,10},{10,18},{18,26},{... | collective-permute-start | bytes 2408456 | tf_op jit(solution)/shard_map/ppermute | solution.py:404
  233.3 18.3 %collective-permute-start.11 = (bf16[1,112,896]{2,1,0:T(8,128)(2,1)S(1)}, bf16[1,112,896]{2,1,0:T(8,128)(2,1)S(1)}, u32[]{:S(2)}, u32[]{:S(2)}) collective-permute-start(bf16[1,112,896]{2,1,0:T(8,128)(2,1)S(1)} %bitcast.24), channel_id=1, source_target_pairs={{8,0},{16,24},{9,1},{17,25},{10,2},{18,26},{11,3},{19,27},{12,4},{... | collective-permute-start | bytes 602120 | tf_op jit(solution)/shard_map/ppermute | solution.py:404
  234.6 17.0 %copy-start.9 = (bf16[1,112,896]{2,1,0:T(8,128)(2,1)S(1)}, bf16[1,112,896]{2,1,0:T(8,128)(2,1)}, u32[]{:S(2)}) copy-start(bf16[1,112,896]{2,1,0:T(8,128)(2,1)} %reduce-scatter.3.cloned.1.call-done) | copy-start | bytes 602116
  252.8 41.9 %copy-start.1 = (s32[2]{0:T(128)S(1)}, s32[2]{0:T(128)}, u32[]{:S(2)}) copy-start(s32[2]{0:T(128)} %pad_add_fusion.place) | copy-start | bytes 28
  252.8 110.0 %all-gather.6.cloned.1.call-start = ((), (), s32[]{:S(2)}) async-start(), calls=%async_computation.6 | async-start | bytes 8257536 | tf_op jit(solution)/shard_map/all_gather | solution.py:461
  252.9 20.7 %collective-permute-start.16 = (bf16[4,112,896]{2,1,0:T(8,128)(2,1)S(1)}, bf16[4,112,896]{2,1,0:T(8,128)(2,1)S(1)}, u32[]{:S(2)}, u32[]{:S(2)}) collective-permute-start(bf16[4,112,896]{2,1,0:T(8,128)(2,1)S(1)} %collective-permute-done.13.l1), channel_id=1, source_target_pairs={{16,8},{8,0},{17,9},{9,1},{18,10},{10,2},{19,11},{11,3},{20,12},{1... | collective-permute-start | bytes 2408456 | tf_op jit(solution)/shard_map/ppermute | solution.py:404
  254.2 20.7 %collective-permute-start.14 = (bf16[4,112,896]{2,1,0:T(8,128)(2,1)S(1)}, bf16[4,112,896]{2,1,0:T(8,128)(2,1)S(1)}, u32[]{:S(2)}, u32[]{:S(2)}) collective-permute-start(bf16[4,112,896]{2,1,0:T(8,128)(2,1)S(1)} %collective-permute-done.12.r1), channel_id=1, source_target_pairs={{8,16},{16,24},{9,17},{17,25},{10,18},{18,26},{11,19},{19,27},{12,... | collective-permute-start | bytes 2408456 | tf_op jit(solution)/shard_map/ppermute | solution.py:404
  273.5 19.8 %collective-permute-start.17 = (bf16[4,112,896]{2,1,0:T(8,128)(2,1)S(1)}, bf16[4,112,896]{2,1,0:T(8,128)(2,1)S(1)}, u32[]{:S(2)}, u32[]{:S(2)}) collective-permute-start(bf16[4,112,896]{2,1,0:T(8,128)(2,1)S(1)} %collective-permute-done.16.l2), channel_id=1, source_target_pairs={{8,0},{9,1},{10,2},{11,3},{12,4},{13,5},{14,6},{15,7}} | collective-permute-start | bytes 2408456 | tf_op jit(solution)/shard_map/ppermute | solution.py:404
  274.8 18.5 %collective-permute-start.15 = (bf16[4,112,896]{2,1,0:T(8,128)(2,1)S(1)}, bf16[4,112,896]{2,1,0:T(8,128)(2,1)S(1)}, u32[]{:S(2)}, u32[]{:S(2)}) collective-permute-start(bf16[4,112,896]{2,1,0:T(8,128)(2,1)S(1)} %collective-permute-done.14.r2), channel_id=1, source_target_pairs={{16,24},{17,25},{18,26},{19,27},{20,28},{21,29},{22,30},{23,31}} | collective-permute-start | bytes 2408456 | tf_op jit(solution)/shard_map/ppermute | solution.py:404
  275.6 3.9 collective-permute-start.18
  293.4 55.0 %collective-permute-start.19 = (bf16[896,1280]{1,0:T(8,128)(2,1)}, bf16[896,1280]{1,0:T(8,128)(2,1)}, u32[]{:S(2)}, u32[]{:S(2)}) collective-permute-start(bf16[896,1280]{1,0:T(8,128)(2,1)} %slice.31), channel_id=1, source_target_pairs={{8,0},{16,24},{9,1},{17,25},{10,2},{18,26},{11,3},{19,27},{12,4},{... | collective-permute-start | bytes 6881288 | tf_op jit(solution)/shard_map/ppermute | solution.py:404
  312.6 67.6 %collective-permute-start.20 = (bf16[896,768]{1,0:T(8,128)(2,1)}, bf16[896,768]{1,0:T(8,128)(2,1)}, u32[]{:S(2)}, u32[]{:S(2)}) collective-permute-start(bf16[896,768]{1,0:T(8,128)(2,1)} %add.18), channel_id=1, source_target_pairs={{8,0},{16,24},{9,1},{17,25},{10,2},{18,26},{11,3},{19,27},{12,4},{... | collective-permute-start | bytes 4128776 | tf_op jit(solution)/shard_map/ppermute | solution.py:404
  (7 other events, 8.4 us)
Sparse Core Ops, SparseCore 0:
  24.3 39.4 reduce-scatter.2
  125.5 68.1 reduce-scatter.4
  252.9 49.0 all-gather.3
  312.7 50.0 all-gather.5
